TPU v7x, 32 devices: a whole 2x2x4 slice. The times are simulated.
32 devices in a mesh: dp: 4 (over y, x), seq: 8 (over z, core).
Axes of the slice: x: 2, y: 2, z: 4, core: 2. Of those that a mesh axis runs over, the one named last changes fastest.
Arguments:
- queries: bfloat16 [4, 192, 2048], P('dp', 'seq'), may hold values from -18 to 18
- keys: bfloat16 [4, 2048, 2048], P('dp', 'seq'), may hold values from -18 to 18
- values: bfloat16 [4, 2048, 2048], P('dp', 'seq'), may hold values from -6 to 6
- attn_out: bfloat16 [4, 192, 2048], P('dp', 'seq'), may hold values from -3 to 3
- out_grad: bfloat16 [4, 192, 2048], P('dp', 'seq'), may hold values from -12 to 12
- loss_mask: int32 [4, 192], P('dp', 'seq'), may hold values from 0 to 1, as said below
- input_lengths: int32 [4, 1, 4], P('dp'), may hold values from 1 to 1024, 2048 in all within a row
- target_lengths: int32 [4, 1, 4], P('dp'), may hold values from 1 to 96, 192 in all within a row
Outputs:
- grad_queries: bfloat16 [4, 192, 2048], P('dp', 'seq')
- grad_keys: bfloat16 [4, 2048, 2048], P('dp', 'seq')
- grad_values: bfloat16 [4, 2048, 2048], P('dp', 'seq')
Inputs may be any that keep to these rules, and one draw needn't show every extreme that they name: `loss_mask`: the first of each device's 24 target rows carries loss.
All inputs are finite; a program needn't handle non-finite values.
Results may differ from a plain program's by a relative error of at most 0.0095.
Values may be sent and summed in bfloat16 or wider, within the bound.
No kernel may reach another device: no remote copies, remote signals or barrier semaphores. Data moves between devices by JAX's collectives and lax.ppermute only.
A program may use at most 128 MiB of HBM per device.

v0:
```python
import jax
import jax.numpy as jnp
from jax import lax
from jax.sharding import PartitionSpec as P

HEADS = 8
HEAD_SIZE = 256


def swapped(block, axis, apart):
    count = lax.axis_size(axis)
    route = []
    for low in range(count):
        high = low | 1 << apart
        if high != low and high < count:
            route += [(low, high), (high, low)]
    return lax.ppermute(block, axis, route)


def for_sending(shard):
    return jax.tree.map(lambda a: a.astype(jnp.bfloat16) if a.dtype == jnp.float32 else a, shard)


def document_ids(lengths, positions):
    doc_ends = jnp.cumsum(lengths)
    return jnp.sum((positions[:, None] >= doc_ends[None, :]).astype(jnp.int32), axis=1)


def score_block(query_rows, key_rows):
    query_heads = query_rows.reshape(query_rows.shape[0], HEADS, HEAD_SIZE)
    key_heads = key_rows.reshape(key_rows.shape[0], HEADS, HEAD_SIZE)
    return jnp.einsum(
        "rhd,ehd->hre", query_heads, key_heads, preferred_element_type=jnp.float32
    ) * HEAD_SIZE ** (-0.5)


def partial_stats(scores, allowed):
    masked_scores = jnp.where(allowed[None], scores, -1e30)
    row_top = jnp.max(masked_scores, axis=2)
    row_total = jnp.sum(
        jnp.where(allowed[None], jnp.exp(scores - row_top[:, :, None]), 0.0), axis=2
    )
    return (row_top, row_total)


def combine_stats(row_top, row_total, bit_count):
    for bit_number in range(bit_count):
        other_top, other_total = swapped((row_top, row_total), "seq", bit_number)
        new_top = jnp.maximum(row_top, other_top)
        row_total = row_total * jnp.exp(row_top - new_top) + other_total * jnp.exp(
            other_top - new_top
        )
        row_top = new_top
    return row_top + jnp.log(row_total)


def tile_grads(scores, allowed, log_total, query_rows, grad_rows, delta_rows, key_rows, value_rows):
    dec_count = query_rows.shape[0]
    enc_count = key_rows.shape[0]
    inverse_root = HEAD_SIZE ** (-0.5)
    query_heads = query_rows.reshape(dec_count, HEADS, HEAD_SIZE)
    grad_heads = grad_rows.reshape(dec_count, HEADS, HEAD_SIZE)
    key_heads = key_rows.reshape(enc_count, HEADS, HEAD_SIZE)
    value_heads = value_rows.reshape(enc_count, HEADS, HEAD_SIZE)
    probs = jnp.where(allowed[None], jnp.exp(scores - log_total[:, :, None]), 0.0)
    dprob = jnp.einsum("rhd,ehd->hre", grad_heads, value_heads, preferred_element_type=jnp.float32)
    dscore = probs * (dprob - delta_rows.astype(jnp.float32).T[:, :, None])
    probs_low = probs.astype(jnp.bfloat16)
    dscore_low = dscore.astype(jnp.bfloat16)
    dvalue = jnp.einsum(
        "hre,rhd->ehd", probs_low, grad_heads, preferred_element_type=jnp.float32
    ).reshape(enc_count, HEADS * HEAD_SIZE)
    dkey = (
        jnp.einsum(
            "hre,rhd->ehd", dscore_low, query_heads, preferred_element_type=jnp.float32
        ).reshape(enc_count, HEADS * HEAD_SIZE)
        * inverse_root
    )
    dquery = (
        jnp.einsum(
            "hre,ehd->rhd", dscore_low, key_heads, preferred_element_type=jnp.float32
        ).reshape(dec_count, HEADS * HEAD_SIZE)
        * inverse_root
    )
    return (dquery, dkey, dvalue)


def local(queries, keys, values, attn_out, out_grad, loss_mask, input_lengths, target_lengths):
    query_rows = queries[0]
    key_rows = keys[0]
    value_rows = values[0]
    dec_local = query_rows.shape[0]
    enc_local = key_rows.shape[0]
    seq_count = lax.axis_size("seq")
    bit_count = seq_count.bit_length() - 1
    local_index = lax.axis_index("seq")
    group_rows = seq_count * dec_local
    mask_rows = loss_mask[0]
    count = lax.psum(jnp.sum(mask_rows).astype(jnp.float32), ("dp", "seq"))
    factor = jnp.float32(dec_local * lax.axis_size("dp") * seq_count) / count
    masked = out_grad[0] * mask_rows[:, None].astype(jnp.bfloat16)
    delta = jnp.sum(
        (masked.astype(jnp.float32) * attn_out[0].astype(jnp.float32)).reshape(
            dec_local, HEADS, HEAD_SIZE
        ),
        axis=2,
    ).astype(jnp.bfloat16)
    collected = (query_rows, masked, delta)
    for bit_number in range(bit_count):
        partner = jax.tree.map(
            lambda part, own: part.astype(own.dtype),
            swapped(for_sending(collected), "seq", bit_number),
            collected,
        )
        upper = local_index >> bit_number & 1 == 1
        collected = tuple(
            (
                jnp.where(
                    upper,
                    jnp.concatenate([theirs, own_part], 0),
                    jnp.concatenate([own_part, theirs], 0),
                )
                for own_part, theirs in zip(collected, partner)
            )
        )
    block_query, block_grad, block_delta = collected
    input_lens = input_lengths[0, 0]
    target_lens = target_lengths[0, 0]
    enc_doc = document_ids(
        input_lens, local_index * enc_local + jnp.arange(enc_local, dtype=jnp.int32)
    )
    dec_doc = document_ids(target_lens, jnp.arange(group_rows, dtype=jnp.int32))
    allowed = dec_doc[:, None] == enc_doc[None, :]
    scores = score_block(block_query, key_rows)
    row_top, row_total = partial_stats(scores, allowed)
    log_total = combine_stats(row_top, row_total, bit_count)
    dquery, dkey, dvalue = tile_grads(
        scores, allowed, log_total, block_query, block_grad, block_delta, key_rows, value_rows
    )
    summed = dquery
    for bit_number in reversed(range(bit_count)):
        half_rows = summed.shape[0] // 2
        lower_half = summed[:half_rows]
        upper_half = summed[half_rows:]
        upper = local_index >> bit_number & 1 == 1
        outgoing = jnp.where(upper, lower_half, upper_half)
        kept = jnp.where(upper, upper_half, lower_half)
        summed = kept + swapped(outgoing, "seq", bit_number)
    grad_queries = (factor * summed).astype(jnp.bfloat16)[None]
    grad_keys = (factor * dkey).astype(jnp.bfloat16)[None]
    grad_values = (factor * dvalue).astype(jnp.bfloat16)[None]
    return (grad_queries, grad_keys, grad_values)


def solution(mesh):
    return jax.shard_map(
        local,
        mesh=mesh,
        in_specs=(
            P("dp", "seq", None),
            P("dp", "seq", None),
            P("dp", "seq", None),
            P("dp", "seq", None),
            P("dp", "seq", None),
            P("dp", "seq"),
            P("dp", None, None),
            P("dp", None, None),
        ),
        out_specs=(P("dp", "seq", None), P("dp", "seq", None), P("dp", "seq", None)),
        check_vma=False,
    )
```

profile of v0, /device:TPU:0, one launch (start us, length us, event | category | flops | bytes accessed | tf_op | source)
XLA Modules:
  0.0 152.6 jit_solution(10765149074181876483)
XLA Ops:
  0.7 1.4 fusion.17
  2.1 1.0 bitcast_multiply_fusion
  3.0 0.5 collective-permute-start.9
  3.6 0.9 copy.88
  4.5 0.9 copy.90
  5.4 0.2 fusion.8
  5.6 0.5 collective-permute-start.12
  6.1 0.8 reduce-window.17
  7.0 0.8 reduce-window.16
  8.0 2.7 %collective-permute-start.13 = (bf16[48,8]{0,1:T(8,128)(2,1)S(1)}, bf16[48,8]{0,1:T(8,128)(2,1)S(1)}, u32[]{:S(2)}, u32[]{:S(2)}) collective-permute-start(bf16[48,8]{0,1:T(8,128)(2,1)S(1)} %maximum_select_fusion.15), channel_id=1, source_target_pairs={{0,2},{2,0},{1,3},{3,1},{4,6},{6,4},{5,7},{7,5},{8,10},{10,8},{9,1... | collective-permute-start | bytes 2312 | tf_op jit(solution)/shard_map/ppermute | solution.py:17
  10.8 1.5 collective-permute-done.13
  12.3 3.0 %collective-permute-start.14 = (bf16[96,8]{0,1:T(8,128)(2,1)S(1)}, bf16[96,8]{0,1:T(8,128)(2,1)S(1)}, u32[]{:S(2)}, u32[]{:S(2)}) collective-permute-start(bf16[96,8]{0,1:T(8,128)(2,1)S(1)} %maximum_select_fusion.16), channel_id=1, source_target_pairs={{0,4},{4,0},{1,5},{5,1},{2,6},{6,2},{3,7},{7,3},{8,12},{12,8},{9,1... | collective-permute-start | bytes 4616 | tf_op jit(solution)/shard_map/ppermute | solution.py:17
  15.4 1.0 maximum_select_fusion.6
  16.4 1.6 %collective-permute-start.1 = (bf16[48,2048]{1,0:T(8,128)(2,1)S(1)}, bf16[48,2048]{1,0:T(8,128)(2,1)S(1)}, u32[]{:S(2)}, u32[]{:S(2)}) collective-permute-start(bf16[48,2048]{1,0:T(8,128)(2,1)S(1)} %maximum_select_fusion.6), channel_id=1, source_target_pairs={{0,2},{2,0},{1,3},{3,1},{4,6},{6,4},{5,7},{7,5},{8,10},{10,8},{9,1... | collective-permute-start | bytes 589832 | tf_op jit(solution)/shard_map/ppermute | solution.py:17
  18.0 0.1 broadcast_compare_fusion
  18.2 0.3 copy.87
  18.5 0.3 copy.89
  19.0 3.2 %collective-permute-done.1 = bf16[48,2048]{1,0:T(8,128)(2,1)S(1)} collective-permute-done((bf16[48,2048]{1,0:T(8,128)(2,1)S(1)}, bf16[48,2048]{1,0:T(8,128)(2,1)S(1)}, u32[]{:S(2)}, u32[]{:S(2)}) %collective-permute-start.1) | collective-permute-done | bytes 196640 | tf_op jit(solution)/shard_map/ppermute | solution.py:17
  22.3 0.4 collective-permute-start.2
  22.7 1.7 %collective-permute-start.10 = (bf16[48,2048]{1,0:T(8,128)(2,1)S(1)}, bf16[48,2048]{1,0:T(8,128)(2,1)S(1)}, u32[]{:S(2)}, u32[]{:S(2)}) collective-permute-start(bf16[48,2048]{1,0:T(8,128)(2,1)S(1)} %maximum_select_fusion.8), channel_id=1, source_target_pairs={{0,2},{2,0},{1,3},{3,1},{4,6},{6,4},{5,7},{7,5},{8,10},{10,8},{9,1... | collective-permute-start | bytes 589832 | tf_op jit(solution)/shard_map/ppermute | solution.py:17
  24.4 0.2 maximum_select_fusion.3
  24.6 15.8 %collective-permute-done.2 = bf16[96,2048]{1,0:T(8,128)(2,1)S(1)} collective-permute-done((bf16[96,2048]{1,0:T(8,128)(2,1)S(1)}, bf16[96,2048]{1,0:T(8,128)(2,1)S(1)}, u32[]{:S(2)}, u32[]{:S(2)}) %collective-permute-start.2) | collective-permute-done | bytes 393248 | tf_op jit(solution)/shard_map/ppermute | solution.py:17
  40.5 0.8 select_reduce_fusion.1
  41.4 0.7 select_reduce_fusion
  42.1 0.6 collective-permute-start.6
  42.8 0.7 collective-permute-done.6
  43.5 1.6 %collective-permute-start.7 = (f32[8,192]{1,0:T(8,128)S(1)}, f32[8,192]{1,0:T(8,128)S(1)}, u32[]{:S(2)}, u32[]{:S(2)}) collective-permute-start(f32[8,192]{1,0:T(8,128)S(1)} %get-tuple-element.14), channel_id=1, source_target_pairs={{0,2},{2,0},{1,3},{3,1},{4,6},{6,4},{5,7},{7,5},{8,10},{10,8},{9,1... | collective-permute-start | bytes 18440 | tf_op jit(solution)/shard_map/ppermute | solution.py:17
  45.1 0.5 collective-permute-start.4
  45.7 6.3 %collective-permute-done.7 = f32[8,192]{1,0:T(8,128)S(1)} collective-permute-done((f32[8,192]{1,0:T(8,128)S(1)}, f32[8,192]{1,0:T(8,128)S(1)}, u32[]{:S(2)}, u32[]{:S(2)}) %collective-permute-start.7) | collective-permute-done | bytes 6176 | tf_op jit(solution)/shard_map/ppermute | solution.py:17
  52.0 2.7 %collective-permute-start.8 = (f32[8,192]{1,0:T(8,128)S(1)}, f32[8,192]{1,0:T(8,128)S(1)}, u32[]{:S(2)}, u32[]{:S(2)}) collective-permute-start(f32[8,192]{1,0:T(8,128)S(1)} %get-tuple-element.12), channel_id=1, source_target_pairs={{0,4},{4,0},{1,5},{5,1},{2,6},{6,2},{3,7},{7,3},{8,12},{12,8},{9,1... | collective-permute-start | bytes 18440 | tf_op jit(solution)/shard_map/ppermute | solution.py:17
  54.7 0.3 collective-permute-start.5
  55.0 0.2 maximum_select_fusion.5
  55.2 7.4 %collective-permute-done.11 = bf16[96,2048]{1,0:T(8,128)(2,1)S(1)} collective-permute-done((bf16[96,2048]{1,0:T(8,128)(2,1)S(1)}, bf16[96,2048]{1,0:T(8,128)(2,1)S(1)}, u32[]{:S(2)}, u32[]{:S(2)}) %collective-permute-start.11) | collective-permute-done | bytes 393248 | tf_op jit(solution)/shard_map/ppermute | solution.py:17
  62.6 0.1 collective-permute-done.8
  62.9 1.0 multiply_convert_fusion.2
  63.9 0.4 multiply_bitcast_fusion
  64.3 0.5 copy-done.2
  64.8 0.1 select_bitcast_fusion
  65.2 36.7 %collective-permute-done.15 = f32[96,2048]{1,0:T(8,128)S(1)} collective-permute-done((f32[96,2048]{1,0:T(8,128)S(1)}, f32[96,2048]{1,0:T(8,128)S(1)}, u32[]{:S(2)}, u32[]{:S(2)}) %collective-permute-start.15) | collective-permute-done | bytes 786464 | tf_op jit(solution)/shard_map/ppermute | solution.py:17
  101.9 0.8 slice_select_fusion
  103.4 40.7 %psum.7 = f32[]{:T(128)} all-reduce(f32[]{:T(128)S(6)} %convert_element_type.84), channel_id=1, replica_groups=mesh['dp'=4,'seq'=8] {'dp','seq'}, use_global_device_ids=true, to_apply=%region_1.0 | all-reduce | flops 1 | bytes 8 | tf_op jit(solution)/shard_map/psum | solution.py:99
  144.9 2.2 %multiply_convert_fusion = bf16[8,256,256]{2,1,0:T(8,128)(2,1)S(1)} fusion(f32[]{:T(128)S(6)} %div.3, f32[8,192,256]{2,1,0:T(8,128)S(1)} %get-tuple-element.23, f32[8,192]{1,0:T(8,128)S(1)} %log_add_fusion, pred[192,256]{1,0:T(8,128)(4,1)S(1)} %broadcast_compare_fusion, bf16[96,8,256]{2,0,1:T(8,128)(2,1)} %copy-done.10, bf16[96,8,256]{2,0,1:T(8,128)(2,1)} %bitcast.87, ...), kind=kOutput, calls=%fused_computation | convolution fusion | flops 207093760 | bytes 3463173 | tf_op jit(solution)/shard_map/hre,rhd->ehd/dot_general | solution.py:70
  147.1 1.4 copy.77
  148.5 1.2 select_add_fusion
  149.8 0.1 copy-done.9
  150.0 0.5 multiply_convert_fusion.1
  150.5 1.4 copy.76
  151.9 0.7 fusion.9
  (62 shorter events, 1.8 us)
Async XLA Ops:
  0.6 17.5 %copy-start.7 = (bf16[1,24,2048]{2,1,0:T(8,128)(2,1)S(1)}, bf16[1,24,2048]{2,1,0:T(8,128)(2,1)}, u32[]{:S(2)}) copy-start(bf16[1,24,2048]{2,1,0:T(8,128)(2,1)} %param.8) | copy-start | bytes 294916
  0.6 17.6 %copy-start = (bf16[1,256,2048]{2,1,0:T(8,128)(2,1)S(1)}, bf16[1,256,2048]{2,1,0:T(8,128)(2,1)}, u32[]{:S(2)}) copy-start(bf16[1,256,2048]{2,1,0:T(8,128)(2,1)} %param.9) | copy-start | bytes 3145732
  3.0 15.9 %collective-permute-start.9 = (bf16[24,2048]{1,0:T(8,128)(2,1)S(1)}, bf16[24,2048]{1,0:T(8,128)(2,1)S(1)}, u32[]{:S(2)}, u32[]{:S(2)}) collective-permute-start(bf16[24,2048]{1,0:T(8,128)(2,1)S(1)} %bitcast_multiply_fusion), channel_id=1, source_target_pairs={{0,1},{1,0},{2,3},{3,2},{4,5},{5,4},{6,7},{7,6},{8,9},{9,8},{10,11... | collective-permute-start | bytes 294920 | tf_op jit(solution)/shard_map/ppermute | solution.py:17
  3.5 11.8 %collective-permute-start = (bf16[24,2048]{1,0:T(8,128)(2,1)}, bf16[24,2048]{1,0:T(8,128)(2,1)S(1)}, u32[]{:S(2)}, u32[]{:S(2)}) collective-permute-start(bf16[24,2048]{1,0:T(8,128)(2,1)} %bitcast.91), channel_id=1, source_target_pairs={{0,1},{1,0},{2,3},{3,2},{4,5},{5,4},{6,7},{7,6},{8,9},{9,8},{10,11... | collective-permute-start | bytes 294920 | tf_op jit(solution)/shard_map/ppermute | solution.py:17
  5.6 12.9 %copy-start.1 = (bf16[1,256,2048]{2,1,0:T(8,128)(2,1)S(1)}, bf16[1,256,2048]{2,1,0:T(8,128)(2,1)}, u32[]{:S(2)}) copy-start(bf16[1,256,2048]{2,1,0:T(8,128)(2,1)} %param.10) | copy-start | bytes 3145732
  5.6 2.2 %collective-permute-start.12 = (bf16[24,8]{0,1:T(8,128)(2,1)S(1)}, bf16[24,8]{0,1:T(8,128)(2,1)S(1)}, u32[]{:S(2)}, u32[]{:S(2)}) collective-permute-start(bf16[24,8]{0,1:T(8,128)(2,1)S(1)} %get-tuple-element.16), channel_id=1, source_target_pairs={{0,1},{1,0},{2,3},{3,2},{4,5},{5,4},{6,7},{7,6},{8,9},{9,8},{10,11... | collective-permute-start | bytes 1160 | tf_op jit(solution)/shard_map/ppermute | solution.py:17
  8.0 4.3 %collective-permute-start.13 = (bf16[48,8]{0,1:T(8,128)(2,1)S(1)}, bf16[48,8]{0,1:T(8,128)(2,1)S(1)}, u32[]{:S(2)}, u32[]{:S(2)}) collective-permute-start(bf16[48,8]{0,1:T(8,128)(2,1)S(1)} %maximum_select_fusion.15), channel_id=1, source_target_pairs={{0,2},{2,0},{1,3},{3,1},{4,6},{6,4},{5,7},{7,5},{8,10},{10,8},{9,1... | collective-permute-start | bytes 2312 | tf_op jit(solution)/shard_map/ppermute | solution.py:17
  12.3 6.5 %collective-permute-start.14 = (bf16[96,8]{0,1:T(8,128)(2,1)S(1)}, bf16[96,8]{0,1:T(8,128)(2,1)S(1)}, u32[]{:S(2)}, u32[]{:S(2)}) collective-permute-start(bf16[96,8]{0,1:T(8,128)(2,1)S(1)} %maximum_select_fusion.16), channel_id=1, source_target_pairs={{0,4},{4,0},{1,5},{5,1},{2,6},{6,2},{3,7},{7,3},{8,12},{12,8},{9,1... | collective-permute-start | bytes 4616 | tf_op jit(solution)/shard_map/ppermute | solution.py:17
  16.4 5.8 %collective-permute-start.1 = (bf16[48,2048]{1,0:T(8,128)(2,1)S(1)}, bf16[48,2048]{1,0:T(8,128)(2,1)S(1)}, u32[]{:S(2)}, u32[]{:S(2)}) collective-permute-start(bf16[48,2048]{1,0:T(8,128)(2,1)S(1)} %maximum_select_fusion.6), channel_id=1, source_target_pairs={{0,2},{2,0},{1,3},{3,1},{4,6},{6,4},{5,7},{7,5},{8,10},{10,8},{9,1... | collective-permute-start | bytes 589832 | tf_op jit(solution)/shard_map/ppermute | solution.py:17
  22.3 18.2 %collective-permute-start.2 = (bf16[96,2048]{1,0:T(8,128)(2,1)S(1)}, bf16[96,2048]{1,0:T(8,128)(2,1)S(1)}, u32[]{:S(2)}, u32[]{:S(2)}) collective-permute-start(bf16[96,2048]{1,0:T(8,128)(2,1)S(1)} %maximum_select_fusion.2), channel_id=1, source_target_pairs={{0,4},{4,0},{1,5},{5,1},{2,6},{6,2},{3,7},{7,3},{8,12},{12,8},{9,1... | collective-permute-start | bytes 1179656 | tf_op jit(solution)/shard_map/ppermute | solution.py:17
  22.7 19.9 %collective-permute-start.10 = (bf16[48,2048]{1,0:T(8,128)(2,1)S(1)}, bf16[48,2048]{1,0:T(8,128)(2,1)S(1)}, u32[]{:S(2)}, u32[]{:S(2)}) collective-permute-start(bf16[48,2048]{1,0:T(8,128)(2,1)S(1)} %maximum_select_fusion.8), channel_id=1, source_target_pairs={{0,2},{2,0},{1,3},{3,1},{4,6},{6,4},{5,7},{7,5},{8,10},{10,8},{9,1... | collective-permute-start | bytes 589832 | tf_op jit(solution)/shard_map/ppermute | solution.py:17
  24.6 16.7 %copy-start.8 = (bf16[96,8,256]{2,0,1:T(8,128)(2,1)}, bf16[96,8,256]{2,0,1:T(8,128)(2,1)S(1)}, u32[]{:S(2)}) copy-start(bf16[96,8,256]{2,0,1:T(8,128)(2,1)S(1)} %maximum_select_fusion.3) | copy-start | bytes 1179652
  40.5 0.9 copy-start.4
  41.3 2.1 %collective-permute-start.3 = (f32[8,192]{1,0:T(8,128)S(1)}, f32[8,192]{1,0:T(8,128)S(1)}, u32[]{:S(2)}, u32[]{:S(2)}) collective-permute-start(f32[8,192]{1,0:T(8,128)S(1)} %get-tuple-element.22), channel_id=1, source_target_pairs={{0,1},{1,0},{2,3},{3,2},{4,5},{5,4},{6,7},{7,6},{8,9},{9,8},{10,11... | collective-permute-start | bytes 18440 | tf_op jit(solution)/shard_map/ppermute | solution.py:17
  42.1 1.4 collective-permute-start.6
  42.7 19.9 %collective-permute-start.11 = (bf16[96,2048]{1,0:T(8,128)(2,1)S(1)}, bf16[96,2048]{1,0:T(8,128)(2,1)S(1)}, u32[]{:S(2)}, u32[]{:S(2)}) collective-permute-start(bf16[96,2048]{1,0:T(8,128)(2,1)S(1)} %maximum_select_fusion.4), channel_id=1, source_target_pairs={{0,4},{4,0},{1,5},{5,1},{2,6},{6,2},{3,7},{7,3},{8,12},{12,8},{9,1... | collective-permute-start | bytes 1179656 | tf_op jit(solution)/shard_map/ppermute | solution.py:17
  43.5 8.5 %collective-permute-start.7 = (f32[8,192]{1,0:T(8,128)S(1)}, f32[8,192]{1,0:T(8,128)S(1)}, u32[]{:S(2)}, u32[]{:S(2)}) collective-permute-start(f32[8,192]{1,0:T(8,128)S(1)} %get-tuple-element.14), channel_id=1, source_target_pairs={{0,2},{2,0},{1,3},{3,1},{4,6},{6,4},{5,7},{7,5},{8,10},{10,8},{9,1... | collective-permute-start | bytes 18440 | tf_op jit(solution)/shard_map/ppermute | solution.py:17
  45.1 7.0 %collective-permute-start.4 = (f32[8,192]{1,0:T(8,128)S(1)}, f32[8,192]{1,0:T(8,128)S(1)}, u32[]{:S(2)}, u32[]{:S(2)}) collective-permute-start(f32[8,192]{1,0:T(8,128)S(1)} %get-tuple-element.15), channel_id=1, source_target_pairs={{0,2},{2,0},{1,3},{3,1},{4,6},{6,4},{5,7},{7,5},{8,10},{10,8},{9,1... | collective-permute-start | bytes 18440 | tf_op jit(solution)/shard_map/ppermute | solution.py:17
  52.0 10.7 %collective-permute-start.8 = (f32[8,192]{1,0:T(8,128)S(1)}, f32[8,192]{1,0:T(8,128)S(1)}, u32[]{:S(2)}, u32[]{:S(2)}) collective-permute-start(f32[8,192]{1,0:T(8,128)S(1)} %get-tuple-element.12), channel_id=1, source_target_pairs={{0,4},{4,0},{1,5},{5,1},{2,6},{6,2},{3,7},{7,3},{8,12},{12,8},{9,1... | collective-permute-start | bytes 18440 | tf_op jit(solution)/shard_map/ppermute | solution.py:17
  54.7 8.1 %collective-permute-start.5 = (f32[8,192]{1,0:T(8,128)S(1)}, f32[8,192]{1,0:T(8,128)S(1)}, u32[]{:S(2)}, u32[]{:S(2)}) collective-permute-start(f32[8,192]{1,0:T(8,128)S(1)} %get-tuple-element.13), channel_id=1, source_target_pairs={{0,4},{4,0},{1,5},{5,1},{2,6},{6,2},{3,7},{7,3},{8,12},{12,8},{9,1... | collective-permute-start | bytes 18440 | tf_op jit(solution)/shard_map/ppermute | solution.py:17
  55.2 8.7 %copy-start.10 = (bf16[96,8,256]{2,0,1:T(8,128)(2,1)}, bf16[96,8,256]{2,0,1:T(8,128)(2,1)S(1)}, u32[]{:S(2)}) copy-start(bf16[96,8,256]{2,0,1:T(8,128)(2,1)S(1)} %maximum_select_fusion.5) | copy-start | bytes 1179652
  62.6 1.3 copy-start.6
  63.9 0.9 copy-start.2
  65.0 36.8 %collective-permute-start.15 = (f32[96,2048]{1,0:T(8,128)S(1)}, f32[96,2048]{1,0:T(8,128)S(1)}, u32[]{:S(2)}, u32[]{:S(2)}) collective-permute-start(f32[96,2048]{1,0:T(8,128)S(1)} %bitcast.77), channel_id=1, source_target_pairs={{0,4},{4,0},{1,5},{5,1},{2,6},{6,2},{3,7},{7,3},{8,12},{12,8},{9,1... | collective-permute-start | bytes 2359304 | tf_op jit(solution)/shard_map/ppermute | solution.py:17
  102.8 45.7 %collective-permute-start.16 = (f32[48,2048]{1,0:T(8,128)}, f32[48,2048]{1,0:T(8,128)}, u32[]{:S(2)}, u32[]{:S(2)}) collective-permute-start(f32[48,2048]{1,0:T(8,128)} %slice_select_fusion), channel_id=1, source_target_pairs={{0,2},{2,0},{1,3},{3,1},{4,6},{6,4},{5,7},{7,5},{8,10},{10,8},{9,1... | collective-permute-start | bytes 1179656 | tf_op jit(solution)/shard_map/ppermute | solution.py:17
  148.5 1.3 copy-start.3
  148.5 1.3 copy-start.5
  148.5 1.5 copy-start.9
  149.7 2.2 %collective-permute-start.17 = (f32[24,2048]{1,0:T(8,128)S(1)}, f32[24,2048]{1,0:T(8,128)S(1)}, u32[]{:S(2)}, u32[]{:S(2)}) collective-permute-start(f32[24,2048]{1,0:T(8,128)S(1)} %slice_select_fusion.1), channel_id=1, source_target_pairs={{0,1},{1,0},{2,3},{3,2},{4,5},{5,4},{6,7},{7,6},{8,9},{9,8},{10,11... | collective-permute-start | bytes 589832 | tf_op jit(solution)/shard_map/ppermute | solution.py:17
where the time goes:
time: 153 us
  waiting for transfers between devices  71.8 us (47%)
  blocking collectives  40.7 us (27%)
  starting transfers between devices  16.5 us (11%)
  other arithmetic  9.93 us (6%)
  local copies, waits for them, and re-layouts  6.23 us (4%)
  matrix products  5.03 us (3%)
  between operations  2.37 us (2%)
    ppermute x18, waiting for transfers between devices, swapped(): return lax.ppermute(block, axis, route)  71.8 us
    psum x1, blocking collectives, local(): count = lax.psum(jnp.sum(mask_rows).astype(jnp.float32), ('dp', 'seq'))  40.7 us
    ppermute x18, starting transfers between devices, swapped(): return lax.ppermute(block, axis, route)  16.5 us
    unnamed x29, local copies, waits for them, and re-layouts  5.97 us
  transfers between devices with their start and end apart: 18, of which 10 were waited for; matrix products, arithmetic and copies ran while one was open for 9% of the time, Pallas kernels for 0%

commit v1 on v0

v1 whole, which is shorter than its diff:
```python
import functools
import jax
import jax.numpy as jnp
from jax import lax
from jax.experimental import pallas as pl
from jax.experimental.pallas import tpu as pltpu
from jax.sharding import PartitionSpec as P

HEADS = 8
HEAD_SIZE = 256
HALF_HEADS = HEADS // 2
HALF = HALF_HEADS * HEAD_SIZE
EXTRA = 128
ROOT = HEAD_SIZE**-0.5
NEVER = -1e30
VMEM_LIMIT = 24 * 1024 * 1024
F32 = jnp.float32
BF16 = jnp.bfloat16
ANY = pl.BlockSpec(memory_space=pl.ANY)
VMEM = pl.BlockSpec(memory_space=pltpu.VMEM)
SMEM = pl.BlockSpec(memory_space=pltpu.SMEM)
NT = (((1,), (1,)), ((), ()))
TN = (((0,), (0,)), ((), ()))
NN = (((1,), (0,)), ((), ()))


def dot(a, b, dims):
    return lax.dot_general(a, b, dims, preferred_element_type=F32)


def position():
    me = lax.axis_index("seq")
    return me >> 1, me & 1


def to_sibling(block):
    count = lax.axis_size("seq")
    return lax.ppermute(block, "seq", [(i, i ^ 1) for i in range(count)])


def across(block, apart):
    count = lax.axis_size("seq")
    return lax.ppermute(block, "seq", [(i, i ^ (2 * apart)) for i in range(count)])


def after(block, *others):
    return lax.optimization_barrier((block, *others))


def kernel_call(
    body, out_shape, in_specs, out_specs, scratch, flops, moved, name, vmem_limit=VMEM_LIMIT
):
    return pl.pallas_call(
        body,
        out_shape=out_shape,
        in_specs=in_specs,
        out_specs=out_specs,
        scratch_shapes=scratch,
        compiler_params=pltpu.CompilerParams(vmem_limit_bytes=vmem_limit),
        cost_estimate=pl.CostEstimate(flops=flops, bytes_accessed=moved, transcendentals=0),
        name=name,
    )


def prepare_kernel(
    grad_ref, out_ref, mask_ref, send_ref, keep_ref, grad_held, out_held, mask_held, sems
):
    _, core = position()
    rows = grad_ref.shape[0]
    copies = start_all(
        [(mask_ref, mask_held), (grad_ref, grad_held), (out_ref, out_held)], sems
    )
    copies[0].wait()
    mask_row = mask_held[...].astype(F32)
    here = lax.broadcasted_iota(jnp.int32, (rows, rows), 0) == lax.broadcasted_iota(
        jnp.int32, (rows, rows), 1
    )
    mask = jnp.sum(jnp.where(here, mask_row, 0.0), axis=1, keepdims=True)
    lane = lax.broadcasted_iota(jnp.int32, (rows, EXTRA), 1)
    for copy in copies[1:]:
        copy.wait()
    masked = grad_held[...].astype(F32) * mask
    products = masked * out_held[...].astype(F32)
    grad_held[...] = masked.astype(BF16)
    halves = []
    for half in range(2):
        extra = jnp.where(lane == HALF_HEADS, mask, 0.0)
        for head in range(HALF_HEADS):
            first = half * HALF + head * HEAD_SIZE
            delta = jnp.sum(products[:, first : first + HEAD_SIZE], axis=1, keepdims=True)
            extra = jnp.where(lane == head, delta, extra)
        halves.append(extra)
    for ref, half in ((send_ref, 1 - core), (keep_ref, core)):
        ref[:, :HALF] = grad_held[:, pl.ds(pl.multiple_of(half * HALF, HALF), HALF)]
        ref[:, HALF:] = jnp.where(half == 0, halves[0], halves[1]).astype(BF16)


def in_core_order(own, other, core):
    own, other = own.astype(F32), other.astype(F32)
    joined = jnp.where(
        core == 0, jnp.concatenate([own, other], 0), jnp.concatenate([other, own], 0)
    )
    return joined.astype(BF16)


def join_queries_kernel(own_ref, other_ref, joined_ref):
    _, core = position()
    mine = pl.ds(pl.multiple_of(core * HALF, HALF), HALF)
    joined_ref[...] = in_core_order(own_ref[:, mine], other_ref[:, mine], core)


def join_cotangents_kernel(own_ref, other_ref, joined_ref, delta_ref, count_ref):
    _, core = position()
    joined_ref[...] = in_core_order(own_ref[:, :HALF], other_ref[:, :HALF], core)
    extra = jnp.transpose(in_core_order(own_ref[:, HALF:], other_ref[:, HALF:], core).astype(F32))
    delta_ref[...] = extra[: delta_ref.shape[0]]
    count = jnp.sum(extra[HALF_HEADS : HALF_HEADS + 1], axis=1, keepdims=True)
    count_ref[...] = jnp.broadcast_to(count, count_ref.shape)


def document_of(positions, lengths_ref):
    end = 0
    document = jnp.zeros_like(positions)
    for i in range(lengths_ref.shape[1]):
        end = end + lengths_ref[0, i]
        document += (positions >= end).astype(jnp.int32)
    return document


def setup_kernel(offsets, in_ref, target_ref, key_ref, k_ref, bias_own, bias_other):
    chip, core = position()
    mine = pl.ds(pl.multiple_of(core * HALF, HALF), HALF)
    k_ref[...] = key_ref[:, mine]
    enc_rows, dec_rows = bias_own.shape
    block = dec_rows // len(offsets)
    lane = lax.broadcasted_iota(jnp.int32, (1, dec_rows), 1)
    dec = lane + chip * block
    for j, offset in enumerate(offsets[1:], 1):
        dec = jnp.where(lane >= j * block, lane + ((chip ^ offset) - j) * block, dec)
    dec = document_of(dec, target_ref)
    for ref, side in ((bias_own, core), (bias_other, 1 - core)):
        enc = lax.broadcasted_iota(jnp.int32, (enc_rows, 1), 0) + (2 * chip + side) * enc_rows
        ref[...] = jnp.where(document_of(enc, in_ref) == dec, 0.0, NEVER)


def start_all(pairs, sems):
    copies = [pltpu.make_async_copy(a, b, sems.at[i]) for i, (a, b) in enumerate(pairs)]
    for copy in copies:
        copy.start()
    return copies


def rows_of(blocks, head):
    columns = slice(head * HEAD_SIZE, (head + 1) * HEAD_SIZE)
    return jnp.concatenate([block[:, columns] for block in blocks], 0)


def tile_of(ref, head):
    first = head * HEAD_SIZE
    if ref.shape[1] == HALF:
        return ref[:, first : first + HEAD_SIZE]
    _, core = position()
    return ref[:, pl.ds(pl.multiple_of(core * HALF + first, HEAD_SIZE), HEAD_SIZE)]


def scores_kernel(offsets, delta_ref, bias_own, bias_other, key_ref, other_ref, *refs):
    count_ref, refs = refs[0], refs[1:]
    blocks, (stats_ref,) = refs[: len(offsets)], refs[len(offsets) :]
    rows = blocks[0].shape[0]
    dec_rows = rows * len(offsets)
    stats_ref[...] = jnp.broadcast_to(count_ref[0:1, 0:1], stats_ref.shape)
    stats_ref[HALF_HEADS:, :rows] = delta_ref[:HALF_HEADS]
    for head in range(HALF_HEADS):
        q = rows_of(blocks, head)
        scores = [
            dot(tile_of(k, head), q, NT) * ROOT + bias[...]
            for k, bias in ((key_ref, bias_own), (other_ref, bias_other))
        ]
        top = functools.reduce(jnp.maximum, [jnp.max(s, axis=0, keepdims=True) for s in scores])
        top = jnp.maximum(top, -1e20)
        total = sum(jnp.sum(jnp.exp(s - top), axis=0, keepdims=True) for s in scores)
        stats_ref[head : head + 1, :dec_rows] = jnp.where(
            total > 0, top + jnp.log(jnp.maximum(total, 1e-30)), NEVER
        )


def gathered_stats(offsets, stats, rows):
    logs = []
    for sender, ref in zip(offsets, stats):
        order = [offsets.index(offset ^ sender) for offset in offsets]
        logs.append(
            jnp.concatenate([ref[:HALF_HEADS, j * rows : (j + 1) * rows] for j in order], 1)
        )
    top = functools.reduce(jnp.maximum, logs)
    log_total = top + jnp.log(sum(jnp.exp(log - top) for log in logs))
    delta = jnp.concatenate([ref[HALF_HEADS:, :rows] for ref in stats], 1)
    last = stats[0].shape[1] - 1
    return log_total, delta, sum(ref[0:1, last:] for ref in stats)


def grads_kernel(offsets, bias_own, bias_other, *refs):
    chips = len(offsets)
    stats, refs = refs[:chips], refs[chips:]
    q_blocks, refs = refs[:chips], refs[chips:]
    g_blocks, refs = refs[:chips], refs[chips:]
    (key_ref, key_other, value_ref, value_other), refs = refs[:4], refs[4:]
    dq_blocks, (keep_ref, send_ref, count_ref) = refs[:chips], refs[chips:]
    rows = q_blocks[0].shape[0]
    log_total, delta, count = gathered_stats(offsets, stats, rows)
    count_ref[...] = jnp.broadcast_to(count, count_ref.shape)
    for head in range(HALF_HEADS):
        columns = slice(head * HEAD_SIZE, (head + 1) * HEAD_SIZE)
        value_columns = slice(HALF + columns.start, HALF + columns.stop)
        line = slice(head, head + 1)
        q, g = rows_of(q_blocks, head), rows_of(g_blocks, head)
        dq = 0.0
        for key, value, bias, out_ref in (
            (key_ref, value_ref, bias_own, keep_ref),
            (key_other, value_other, bias_other, send_ref),
        ):
            k, v = tile_of(key, head), tile_of(value, head)
            probs = jnp.exp(dot(k, q, NT) * ROOT + bias[...] - log_total[line])
            dscore = (probs * (dot(v, g, NT) - delta[line])).astype(BF16)
            dq += dot(dscore, k, TN)
            out_ref[:, columns] = (dot(dscore, q, NN) * ROOT).astype(BF16)
            out_ref[:, value_columns] = dot(probs.astype(BF16), g, NN).astype(BF16)
        dq = (dq * ROOT).astype(BF16)
        for j, block in enumerate(dq_blocks):
            block[:, columns] = dq[j * rows : (j + 1) * rows]


def key_end_kernel(rows_in_all, keep_ref, other_ref, *refs):
    counts, (dk_ref, dv_ref, factor_ref) = refs[:2], refs[2:]
    _, core = position()
    factor = rows_in_all / (counts[0][0:1, 0:1] + counts[1][0:1, 0:1])
    factor_ref[...] = jnp.broadcast_to(factor, factor_ref.shape)
    for ref, side in ((keep_ref, core), (other_ref, 1 - core)):
        columns = pl.ds(pl.multiple_of(side * HALF, HALF), HALF)
        dk_ref[:, columns] = (ref[:, :HALF].astype(F32) * factor).astype(BF16)
        dv_ref[:, columns] = (ref[:, HALF:].astype(F32) * factor).astype(BF16)


def query_end_kernel(factor_ref, *refs):
    parts, (send_ref, keep_ref) = refs[:-2], refs[-2:]
    _, core = position()
    summed = factor_ref[0:1, 0:1] * sum(part[...].astype(F32) for part in parts)
    half = summed.shape[0] // 2
    low, high = summed[:half], summed[half:]
    send_ref[...] = jnp.where(core == 0, high, low).astype(BF16)
    keep_ref[...] = jnp.where(core == 0, low, high).astype(BF16)


def in_order(own, other, core, axis):
    return jnp.where(
        core == 0, jnp.concatenate([own, other], axis), jnp.concatenate([other, own], axis)
    )


def local(queries, keys, values, attn_out, out_grad, loss_mask, input_lengths, target_lengths):
    query_rows, key_rows, value_rows = queries[0], keys[0], values[0]
    dec_local, enc_local = query_rows.shape[0], key_rows.shape[0]
    chips = lax.axis_size("seq") // 2
    data_groups = lax.axis_size("dp")
    _, core = position()
    dec_rows = 2 * chips * dec_local
    enc_rows = 2 * enc_local
    block = (2 * dec_local, HALF)
    lengths = (input_lengths[0], target_lengths[0])

    def shaped(*shape, dtype=BF16):
        return jax.ShapeDtypeStruct(shape, dtype)

    def gather(block):
        blocks = [block]
        apart = chips // 2
        while apart > 1:
            blocks += [across(one, apart) for one in blocks]
            apart //= 2
        return blocks, across(block, 1)

    def forwarded(blocks):
        return [across(one, 1) for one in blocks[1:]]

    offsets = [0]
    apart = chips // 2
    while apart:
        offsets += [offset ^ apart for offset in offsets]
        apart //= 2

    features = HEADS * HEAD_SIZE
    sent = shaped(dec_local, HALF + EXTRA)
    block = shaped(2 * dec_local, HALF)

    with jax.named_scope("sibling_exchange"):
        q_recv = to_sibling(query_rows)
        g_send, g_keep = kernel_call(
            prepare_kernel,
            (sent, sent),
            [ANY] * 3,
            (VMEM, VMEM),
            [
                pltpu.VMEM((dec_local, features), BF16),
                pltpu.VMEM((dec_local, features), BF16),
                pltpu.VMEM((1, dec_local), jnp.int32),
                pltpu.SemaphoreType.DMA((3,)),
            ],
            10**5,
            10**6,
            "prepare",
            60 * 1024 * 1024,
        )(out_grad[0], attn_out[0], loss_mask)
        g_recv = to_sibling(g_send)

    with jax.named_scope("query_gather"):
        q_recv, _ = after(q_recv, g_keep)
        q_block = kernel_call(
            join_queries_kernel, block, [VMEM, VMEM], VMEM, [], 10**5, 10**5, "join_queries"
        )(query_rows, q_recv)
        q_far, q_near = gather(q_block)

    with jax.named_scope("key_exchange"):
        k_recv = to_sibling(after(key_rows, q_block)[0])
        v_recv = to_sibling(after(value_rows, q_block)[0])

    with jax.named_scope("setup"):
        half_rows = shaped(enc_local, HALF)
        bias = shaped(enc_local, dec_rows, dtype=F32)
        k_own, bias_own, bias_other = kernel_call(
            functools.partial(setup_kernel, offsets),
            (half_rows, bias, bias),
            [SMEM] * 2 + [VMEM],
            (VMEM,) * 3,
            [],
            10**6,
            2**22,
            "setup",
        )(*lengths, after(key_rows, q_block)[0])

    with jax.named_scope("cotangent_gather"):
        small = shaped(8, 2 * dec_local, dtype=F32)
        g_block, delta, count = kernel_call(
            join_cotangents_kernel,
            (block, small, shaped(8, EXTRA, dtype=F32)),
            [VMEM, VMEM],
            (VMEM,) * 3,
            [],
            10**5,
            10**5,
            "join_cotangents",
        )(g_keep, g_recv)

    def over_groups(count, apart):
        return lax.ppermute(count, "dp", [(i, i ^ apart) for i in range(data_groups)])

    with jax.named_scope("mask_count"):
        apart = 1
        while apart < data_groups // 2:
            count = count + after(over_groups(count, apart), bias_own)[0]
            apart *= 2
        rows_in_all = float(data_groups * dec_rows)

    with jax.named_scope("query_forward"):
        q_far = [q_far[0], *(after(one, bias_own, count)[0] for one in q_far[1:])]
        q_blocks = [*q_far, q_near, *forwarded(q_far)]

    with jax.named_scope("cotangent_gather"):
        g_far, g_near = gather(after(g_block, *q_far, q_near)[0])

    with jax.named_scope("scores"):
        width = (dec_rows // 128 + 1) * 128
        stats = kernel_call(
            functools.partial(scores_kernel, offsets),
            shaped(2 * HALF_HEADS, width, dtype=F32),
            [VMEM] * (chips + 6),
            VMEM,
            [],
            2 * dec_rows * enc_rows * HALF,
            2 * (dec_rows + enc_rows) * HALF,
            "scores",
        )(delta, bias_own, bias_other, k_own, k_recv, count, *q_blocks)

    with jax.named_scope("cotangent_forward"):
        g_far = [g_far[0], *(after(one, stats)[0] for one in g_far[1:])]
        g_blocks = [*g_far, g_near, *forwarded(g_far)]

    with jax.named_scope("stats_exchange"):
        all_stats = [stats] + [across(stats, offset) for offset in offsets[1:]]

    with jax.named_scope("grads"):
        both = shaped(enc_local, 2 * HALF)
        *dq_blocks, dkv_keep, dkv_send, count = kernel_call(
            functools.partial(grads_kernel, offsets),
            (block,) * chips + (both, both, shaped(8, EXTRA, dtype=F32)),
            [VMEM] * (3 * chips + 6),
            (VMEM,) * (chips + 3),
            [],
            10 * dec_rows * enc_rows * HALF,
            4 * (dec_rows + 2 * enc_rows) * HALF,
            "grads",
        )(bias_own, bias_other, *all_stats, *q_blocks, *g_blocks, k_own, k_recv, value_rows, v_recv)

    with jax.named_scope("query_grad_sum"):
        parts = [dq_blocks[0]]
        for j in sorted(range(1, chips), key=lambda j: -offsets[j]):
            parts.append(across(dq_blocks[j], offsets[j]))

    with jax.named_scope("key_grad_end"):
        dkv_recv = to_sibling(dkv_send)
        counts = (count, over_groups(count, data_groups // 2))
        whole = shaped(enc_local, features)
        grad_keys, grad_values, factor = kernel_call(
            functools.partial(key_end_kernel, rows_in_all),
            (whole, whole, shaped(8, EXTRA, dtype=F32)),
            [VMEM] * 4,
            (VMEM, VMEM, VMEM),
            [],
            10**6,
            2**22,
            "key_end",
        )(dkv_keep, dkv_recv, *counts)

    with jax.named_scope("query_grad_end"):
        half = shaped(dec_local, HALF)
        dq_send, dq_keep = kernel_call(
            query_end_kernel,
            (half, half),
            [VMEM] * (chips + 1),
            (VMEM, VMEM),
            [],
            10**5,
            10**6,
            "query_end",
        )(factor, *parts)
        grad_queries = in_order(dq_keep, to_sibling(dq_send), core, 1)

    return grad_queries[None], grad_keys[None], grad_values[None]


def solution(mesh):
    return jax.shard_map(
        local,
        mesh=mesh,
        in_specs=(
            P("dp", "seq", None),
            P("dp", "seq", None),
            P("dp", "seq", None),
            P("dp", "seq", None),
            P("dp", "seq", None),
            P("dp", "seq"),
            P("dp", None, None),
            P("dp", None, None),
        ),
        out_specs=(P("dp", "seq", None), P("dp", "seq", None), P("dp", "seq", None)),
        check_vma=False,
    )
```

time: 153 us -> 47.1 us (0.31)
  waiting for transfers between devices: 71.8 us -> 13.9 us
  blocking collectives: 40.7 us -> 0 us
  other arithmetic: 9.93 us -> 0.67 us
  Pallas kernels: 0 us -> 8.1 us
  starting transfers between devices: 16.5 us -> 21.6 us
  matrix products: 5.03 us -> 0 us
  local copies, waits for them, and re-layouts: 6.23 us -> 1.91 us
  between operations: 2.37 us -> 0.77 us
    ppermute x18 -> x20, waiting for transfers between devices: 71.8 us -> 13.9 us  [the longest x12 9.35 us: across(): lax.ppermute(block, 'seq', [(i, i ^ 2 * apart) for i in range(count)])]
    psum x1 -> x0, blocking collectives: 40.7 us -> none  [local(): count = lax.psum(jnp.sum(mask_rows).astype(jnp.float32), ('dp', 'seq'))]
    pallas_call x0 -> x8, Pallas kernels: none -> 8.1 us  [the longest x1 2.59 us: local(): kernel_call(functools.partial(grads_kernel, offsets), (block,) * chips +...]
    ppermute x18 -> x20, starting transfers between devices: 16.5 us -> 21.6 us  [the longest x12 17.3 us: across(): lax.ppermute(block, 'seq', [(i, i ^ 2 * apart) for i in range(count)])]
    dot_general x5 -> x0, matrix products: 5.03 us -> none  [the longest x1 2.2 us: tile_grads(): jnp.einsum('hre,rhd->ehd', probs_low, grad_heads, preferred_element_type=...]
    unnamed x29 -> x14, local copies, waits for them, and re-layouts: 5.97 us -> 1.91 us
    reduce_sum x5 -> x0, other arithmetic: 2.41 us -> none  [the longest x1 1.4 us: local(): count = lax.psum(jnp.sum(mask_rows).astype(jnp.float32), ('dp', 'seq'))]
    select_n x12 -> x1, other arithmetic: 2.62 us -> 0.66 us  [in_order(): jnp.where(core == 0, jnp.concatenate([own, other], axis), jnp.concatenate...]
  transfers between devices with their start and end apart: 18 -> 20, of which waited for: 10 -> 8; matrix products, arithmetic and copies ran while one was open for 9% -> 0% of each run, Pallas kernels for 0% -> 12%
where the time goes in v1:
time: 47.1 us; the launch traced here: 46.9 us
  starting transfers between devices  21.6 us (46%)
  waiting for transfers between devices  13.9 us (30%)
  Pallas kernels  8.1 us (17%)
  local copies, waits for them, and re-layouts  1.91 us (4%)
  between operations  0.77 us (2%)
  other arithmetic  0.67 us (1%)
    ppermute x12, starting transfers between devices, across(): lax.ppermute(block, 'seq', [(i, i ^ 2 * apart) for i in range(count)])  17.3 us
    ppermute x12, waiting for transfers between devices, across(): lax.ppermute(block, 'seq', [(i, i ^ 2 * apart) for i in range(count)])  9.35 us
    ppermute x2, starting transfers between devices, over_groups(): lax.ppermute(count, 'dp', [(i, i ^ apart) for i in range(data_groups)])  3.01 us
    pallas_call x1, Pallas kernels, local(): kernel_call(functools.partial(grads_kernel, offsets), (block,) * chips +...  2.59 us
    ppermute x6, waiting for transfers between devices, to_sibling(): return lax.ppermute(block, 'seq', [(i, i ^ 1) for i in range(count)])  2.44 us
    ppermute x2, waiting for transfers between devices, over_groups(): lax.ppermute(count, 'dp', [(i, i ^ apart) for i in range(data_groups)])  2.09 us
    unnamed x14, local copies, waits for them, and re-layouts  1.91 us
    pallas_call x1, Pallas kernels, local(): kernel_call(functools.partial(key_end_kernel, rows_in_all), (whole, whole...  1.84 us
  transfers between devices with their start and end apart: 20, of which 8 were waited for; matrix products, arithmetic and copies ran while one was open for 0% of the time, Pallas kernels for 12%

profile of v1, /device:TPU:0, one launch (start us, length us, event | category | flops | bytes accessed | tf_op | source)
XLA Modules:
  0.0 46.9 jit_solution(9770933701696043803)
XLA Ops:
  0.6 0.5 %collective-permute-start = (bf16[24,2048]{1,0:T(8,128)(2,1)}, bf16[24,2048]{1,0:T(8,128)(2,1)S(1)}, u32[]{:S(2)}, u32[]{:S(2)}) collective-permute-start(bf16[24,2048]{1,0:T(8,128)(2,1)} %bitcast.15), channel_id=1, source_target_pairs={{0,1},{1,0},{2,3},{3,2},{4,5},{5,4},{6,7},{7,6},{8,9},{9,8},{10,11... | collective-permute-start | bytes 294920 | tf_op jit(solution)/shard_map/sibling_exchange/ppermute | solution.py:38
  1.2 1.8 %prepare.1 = (bf16[24,1152]{1,0:T(8,128)(2,1)}, bf16[24,1152]{1,0:T(8,128)(2,1)}) custom-call(bf16[24,2048]{1,0:T(8,128)(2,1)} %bitcast.20, bf16[24,2048]{1,0:T(8,128)(2,1)} %bitcast.21, s32[1,24]{1,0:T(1,128)} %mask_ref.1), custom_call_target="tpu_custom_call" | custom-call | flops 100000 | bytes 1000000 | tf_op jit(solution)/shard_map/sibling_exchange/prepare/pallas_call | solution.py:296
  2.9 0.0 collective-permute-done.other_ref
  3.0 0.0 copy-start.6
  3.0 0.0 copy-start.3
  3.0 0.1 collective-permute-start.2
  3.1 0.5 collective-permute-start.13
  3.6 3.7 %collective-permute-start.4 = (bf16[48,1024]{1,0:T(8,128)(2,1)S(1)}, bf16[48,1024]{1,0:T(8,128)(2,1)S(1)}, u32[]{:S(2)}, u32[]{:S(2)}) collective-permute-start(bf16[48,1024]{1,0:T(8,128)(2,1)S(1)} %join_queries.1.refs_1_.refs_4_), channel_id=1, source_target_pairs={{0,4},{1,5},{2,6},{3,7},{4,0},{5,1},{6,2},{7,3},{8,12},{9,13},{10,... | collective-permute-start | bytes 294920 | tf_op jit(solution)/shard_map/query_gather/ppermute | solution.py:43
  7.3 1.6 %collective-permute-start.5 = (bf16[48,1024]{1,0:T(8,128)(2,1)S(1)}, bf16[48,1024]{1,0:T(8,128)(2,1)S(1)}, u32[]{:S(2)}, u32[]{:S(2)}) collective-permute-start(bf16[48,1024]{1,0:T(8,128)(2,1)S(1)} %join_queries.1.refs_1_.refs_4_), channel_id=1, source_target_pairs={{0,2},{1,3},{2,0},{3,1},{4,6},{5,7},{6,4},{7,5},{8,10},{9,11},{10,... | collective-permute-start | bytes 294920 | tf_op jit(solution)/shard_map/query_gather/ppermute | solution.py:43
  8.8 0.0 collective-permute-start.1
  8.8 1.2 %collective-permute-done.1.other_ref = bf16[24,1152]{1,0:T(8,128)(2,1)S(1)} collective-permute-done((bf16[24,1152]{1,0:T(8,128)(2,1)S(1)}, bf16[24,1152]{1,0:T(8,128)(2,1)S(1)}, u32[]{:S(2)}, u32[]{:S(2)}) %collective-permute-start.1) | collective-permute-done | bytes 55328 | tf_op jit(solution)/shard_map/sibling_exchange/ppermute | solution.py:38
  10.1 0.2 join_cotangents.1
  10.2 1.5 %collective-permute-start.3 = (f32[8,128]{1,0:T(8,128)S(1)}, f32[8,128]{1,0:T(8,128)S(1)}, u32[]{:S(2)}, u32[]{:S(2)}) collective-permute-start(f32[8,128]{1,0:T(8,128)S(1)} %get-tuple-element.38), channel_id=1, source_target_pairs={{0,8},{8,0},{16,24},{24,16},{1,9},{9,1},{17,25},{25,17},{2,10},{10... | collective-permute-start | bytes 12296 | tf_op jit(solution)/shard_map/mask_count/ppermute | solution.py:353
  11.7 0.7 %copy-done.4 = s32[1,1,4]{2,1,0:T(1,128)S(1)} copy-done((s32[1,1,4]{2,1,0:T(1,128)S(1)}, s32[1,1,4]{2,1,0:T(1,128)}, u32[]{:S(2)}) %copy-start.4) | copy-done | bytes 40
  12.4 0.0 copy-done.5
  12.4 1.2 %copy-done.1 = bf16[1,256,2048]{2,1,0:T(8,128)(2,1)S(1)} copy-done((bf16[1,256,2048]{2,1,0:T(8,128)(2,1)S(1)}, bf16[1,256,2048]{2,1,0:T(8,128)(2,1)}, u32[]{:S(2)}) %copy-start.1) | copy-done | bytes 1048600
  13.6 0.7 %setup.1 = (bf16[256,1024]{1,0:T(8,128)(2,1)S(1)}, f32[256,192]{1,0:T(8,128)S(1)}, f32[256,192]{1,0:T(8,128)S(1)}) custom-call(s32[1,4]{1,0:T(1,128)S(1)} %bitcast.18, s32[1,4]{1,0:T(1,128)S(1)} %bitcast.19, bf16[256,2048]{1,0:T(8,128)(2,1)S(1)} %bitcast.14), custom_call_target="tpu_custom_call" | custom-call | flops 1000000 | bytes 4194304 | tf_op jit(solution)/shard_map/setup/setup/pallas_call | solution.py:328
  14.4 0.0 collective-permute-done.3
  14.4 0.5 %collective-permute-start.6 = (bf16[48,1024]{1,0:T(8,128)(2,1)S(1)}, bf16[48,1024]{1,0:T(8,128)(2,1)S(1)}, u32[]{:S(2)}, u32[]{:S(2)}) collective-permute-start(bf16[48,1024]{1,0:T(8,128)(2,1)S(1)} %collective-permute-done.4.refs_2_.refs_5_), channel_id=1, source_target_pairs={{0,2},{1,3},{2,0},{3,1},{4,6},{5,7},{6,4},{7,5},{8,10},{9,11},{10,... | collective-permute-start | bytes 294920 | tf_op jit(solution)/shard_map/query_forward/ppermute | solution.py:43
  14.9 0.0 collective-permute-done.5.refs_3_.refs_6_
  14.9 2.0 %collective-permute-start.10 = (bf16[48,1024]{1,0:T(8,128)(2,1)S(1)}, bf16[48,1024]{1,0:T(8,128)(2,1)S(1)}, u32[]{:S(2)}, u32[]{:S(2)}) collective-permute-start(bf16[48,1024]{1,0:T(8,128)(2,1)S(1)} %get-tuple-element.42.refs_8_), channel_id=1, source_target_pairs={{0,4},{1,5},{2,6},{3,7},{4,0},{5,1},{6,2},{7,3},{8,12},{9,13},{10,... | collective-permute-start | bytes 294920 | tf_op jit(solution)/shard_map/cotangent_gather/ppermute | solution.py:43
  16.9 0.6 %collective-permute-start.11 = (bf16[48,1024]{1,0:T(8,128)(2,1)S(1)}, bf16[48,1024]{1,0:T(8,128)(2,1)S(1)}, u32[]{:S(2)}, u32[]{:S(2)}) collective-permute-start(bf16[48,1024]{1,0:T(8,128)(2,1)S(1)} %get-tuple-element.42.refs_8_), channel_id=1, source_target_pairs={{0,2},{1,3},{2,0},{3,1},{4,6},{5,7},{6,4},{7,5},{8,10},{9,11},{10,... | collective-permute-start | bytes 294920 | tf_op jit(solution)/shard_map/cotangent_gather/ppermute | solution.py:43
  17.5 4.7 %collective-permute-done.6.refs_4_.refs_7_ = bf16[48,1024]{1,0:T(8,128)(2,1)S(1)} collective-permute-done((bf16[48,1024]{1,0:T(8,128)(2,1)S(1)}, bf16[48,1024]{1,0:T(8,128)(2,1)S(1)}, u32[]{:S(2)}, u32[]{:S(2)}) %collective-permute-start.6) | collective-permute-done | bytes 98336 | tf_op jit(solution)/shard_map/query_forward/ppermute | solution.py:43
  22.1 0.9 %scores.1.refs_0_ = f32[8,256]{1,0:T(8,128)S(1)} custom-call(f32[8,48]{1,0:T(8,128)S(1)} %get-tuple-element.36.delta_ref, f32[256,192]{1,0:T(8,128)S(1)} %get-tuple-element.33.bias_own, f32[256,192]{1,0:T(8,128)S(1)} %get-tuple-element.34.bias_other, bf16[256,1024]{1,0:T(8,128)(2,1)S(1)} %get-tuple-element.37.key_ref.refs_12_, ...), custom_call_target="tpu_custom_call" | custom-call | flops 201326592 | bytes 1441792 | tf_op jit(solution)/shard_map/scores/scores/pallas_call | solution.py:371
  23.0 0.0 collective-permute-done.10.refs_9_
  23.0 0.1 collective-permute-start.12
  23.1 2.0 %collective-permute-start.7 = (f32[8,256]{1,0:T(8,128)S(1)}, f32[8,256]{1,0:T(8,128)S(1)}, u32[]{:S(2)}, u32[]{:S(2)}) collective-permute-start(f32[8,256]{1,0:T(8,128)S(1)} %scores.1.refs_0_), channel_id=1, source_target_pairs={{0,4},{1,5},{2,6},{3,7},{4,0},{5,1},{6,2},{7,3},{8,12},{9,13},{10,... | collective-permute-start | bytes 24584 | tf_op jit(solution)/shard_map/stats_exchange/ppermute | solution.py:43
  25.1 0.4 collective-permute-start.8
  25.5 2.1 %collective-permute-start.9 = (f32[8,256]{1,0:T(8,128)S(1)}, f32[8,256]{1,0:T(8,128)S(1)}, u32[]{:S(2)}, u32[]{:S(2)}) collective-permute-start(f32[8,256]{1,0:T(8,128)S(1)} %scores.1.refs_0_), channel_id=1, source_target_pairs={{0,6},{1,7},{2,4},{3,5},{4,2},{5,3},{6,0},{7,1},{8,14},{9,15},{10,... | collective-permute-start | bytes 24584 | tf_op jit(solution)/shard_map/stats_exchange/ppermute | solution.py:43
  27.6 0.0 collective-permute-done.13.refs_15_
  27.6 0.2 collective-permute-done.7.refs_1_
  27.7 1.0 %collective-permute-done.8.refs_2_ = f32[8,256]{1,0:T(8,128)S(1)} collective-permute-done((f32[8,256]{1,0:T(8,128)S(1)}, f32[8,256]{1,0:T(8,128)S(1)}, u32[]{:S(2)}, u32[]{:S(2)}) %collective-permute-start.8) | collective-permute-done | bytes 8224 | tf_op jit(solution)/shard_map/stats_exchange/ppermute | solution.py:43
  28.7 2.2 %collective-permute-done.9.refs_3_ = f32[8,256]{1,0:T(8,128)S(1)} collective-permute-done((f32[8,256]{1,0:T(8,128)S(1)}, f32[8,256]{1,0:T(8,128)S(1)}, u32[]{:S(2)}, u32[]{:S(2)}) %collective-permute-start.9) | collective-permute-done | bytes 8224 | tf_op jit(solution)/shard_map/stats_exchange/ppermute | solution.py:43
  30.9 0.0 collective-permute-done.12.refs_11_
  31.0 2.6 %grads.1 = (bf16[48,1024]{1,0:T(8,128)(2,1)S(1)}, bf16[48,1024]{1,0:T(8,128)(2,1)S(1)}, bf16[48,1024]{1,0:T(8,128)(2,1)S(1)}, bf16[48,1024]{1,0:T(8,128)(2,1)S(1...) custom-call(f32[256,192]{1,0:T(8,128)S(1)} %get-tuple-element.33.bias_own, ...), custom_call_target="tpu_custom_call" | custom-call | flops 1006632960 | bytes 4980736 | tf_op jit(solution)/shard_map/grads/grads/pallas_call | solution.py:391
  33.5 0.1 collective-permute-start.14
  33.6 2.1 %collective-permute-start.16 = (bf16[48,1024]{1,0:T(8,128)(2,1)S(1)}, bf16[48,1024]{1,0:T(8,128)(2,1)S(1)}, u32[]{:S(2)}, u32[]{:S(2)}) collective-permute-start(bf16[48,1024]{1,0:T(8,128)(2,1)S(1)} %get-tuple-element.50), channel_id=1, source_target_pairs={{0,6},{1,7},{2,4},{3,5},{4,2},{5,3},{6,0},{7,1},{8,14},{9,15},{10,... | collective-permute-start | bytes 294920 | tf_op jit(solution)/shard_map/query_grad_sum/ppermute | solution.py:43
  35.8 2.3 %collective-permute-start.18 = (bf16[48,1024]{1,0:T(8,128)(2,1)S(1)}, bf16[48,1024]{1,0:T(8,128)(2,1)S(1)}, u32[]{:S(2)}, u32[]{:S(2)}) collective-permute-start(bf16[48,1024]{1,0:T(8,128)(2,1)S(1)} %get-tuple-element.52), channel_id=1, source_target_pairs={{0,2},{1,3},{2,0},{3,1},{4,6},{5,7},{6,4},{7,5},{8,10},{9,11},{10,... | collective-permute-start | bytes 294920 | tf_op jit(solution)/shard_map/query_grad_sum/ppermute | solution.py:43
  38.1 1.5 %collective-permute-start.15 = (f32[8,128]{1,0:T(8,128)S(1)}, f32[8,128]{1,0:T(8,128)S(1)}, u32[]{:S(2)}, u32[]{:S(2)}) collective-permute-start(f32[8,128]{1,0:T(8,128)S(1)} %get-tuple-element.47.refs_0_), channel_id=1, source_target_pairs={{0,16},{8,24},{16,0},{24,8},{1,17},{9,25},{17,1},{25,9},{2,18},{10... | collective-permute-start | bytes 12296 | tf_op jit(solution)/shard_map/key_grad_end/ppermute | solution.py:353
  39.6 2.1 %collective-permute-done.15.refs_1_ = f32[8,128]{1,0:T(8,128)S(1)} collective-permute-done((f32[8,128]{1,0:T(8,128)S(1)}, f32[8,128]{1,0:T(8,128)S(1)}, u32[]{:S(2)}, u32[]{:S(2)}) %collective-permute-start.15) | collective-permute-done | bytes 4128 | tf_op jit(solution)/shard_map/key_grad_end/ppermute | solution.py:353
  41.7 0.0 collective-permute-done.14.other_ref
  41.7 1.8 %key_end.1 = (bf16[256,2048]{1,0:T(8,128)(2,1)}, bf16[256,2048]{1,0:T(8,128)(2,1)}, f32[8,128]{1,0:T(8,128)S(1)}) custom-call(bf16[256,2048]{1,0:T(8,128)(2,1)S(1)} %get-tuple-element.45.keep_ref, bf16[256,2048]{1,0:T(8,128)(2,1)S(1)} %collective-permute-done.14.other_ref, f32[8,128]{1,0:T(8,128)S(1)} %get-tuple-element.47.refs_0_, ...), custom_call_target="tpu_custom_call" | custom-call | flops 1000000 | bytes 4194304 | tf_op jit(solution)/shard_map/key_grad_end/key_end/pallas_call | solution.py:411
  43.5 0.0 collective-permute-done.16.refs_1_
  43.5 1.3 %collective-permute-done.17.refs_2_ = bf16[48,1024]{1,0:T(8,128)(2,1)S(1)} collective-permute-done((bf16[48,1024]{1,0:T(8,128)(2,1)S(1)}, bf16[48,1024]{1,0:T(8,128)(2,1)S(1)}, u32[]{:S(2)}, u32[]{:S(2)}) %collective-permute-start.17) | collective-permute-done | bytes 98336 | tf_op jit(solution)/shard_map/query_grad_sum/ppermute | solution.py:43
  44.9 0.1 query_end.1
  44.9 0.1 collective-permute-start.19
  45.0 1.2 %collective-permute-done.19 = bf16[24,1024]{1,0:T(8,128)(2,1)S(1)} collective-permute-done((bf16[24,1024]{1,0:T(8,128)(2,1)S(1)}, bf16[24,1024]{1,0:T(8,128)(2,1)S(1)}, u32[]{:S(2)}, u32[]{:S(2)}) %collective-permute-start.19) | collective-permute-done | bytes 49184 | tf_op jit(solution)/shard_map/query_grad_end/ppermute | solution.py:38
  46.2 0.7 %maximum_select_fusion = bf16[1,24,2048]{2,1,0:T(8,128)(2,1)} fusion(bf16[1,24,1024]{2,1,0:T(8,128)(2,1)S(1)} %bitcast.22, bf16[1,24,1024]{2,1,0:T(8,128)(2,1)S(1)} %bitcast.17, pred[]{:T(512)S(6)} %eq.3), kind=kLoop, calls=%fused_computation | loop fusion | flops 442368 | bytes 196609 | tf_op jit(solution)/shard_map/query_grad_end/jit(_where)/select_n | solution.py:254
  (16 shorter events, 0.1 us)
Async XLA Ops:
  0.6 2.3 %collective-permute-start = (bf16[24,2048]{1,0:T(8,128)(2,1)}, bf16[24,2048]{1,0:T(8,128)(2,1)S(1)}, u32[]{:S(2)}, u32[]{:S(2)}) collective-permute-start(bf16[24,2048]{1,0:T(8,128)(2,1)} %bitcast.15), channel_id=1, source_target_pairs={{0,1},{1,0},{2,3},{3,2},{4,5},{5,4},{6,7},{7,6},{8,9},{9,8},{10,11... | collective-permute-start | bytes 294920 | tf_op jit(solution)/shard_map/sibling_exchange/ppermute | solution.py:38
  1.1 1.8 %copy-start.2 = (bf16[1,24,2048]{2,1,0:T(8,128)(2,1)S(1)}, bf16[1,24,2048]{2,1,0:T(8,128)(2,1)}, u32[]{:S(2)}) copy-start(bf16[1,24,2048]{2,1,0:T(8,128)(2,1)} %param.8) | copy-start | bytes 294916
  3.0 5.9 %copy-start.6 = (bf16[24,1152]{1,0:T(8,128)(2,1)S(1)}, bf16[24,1152]{1,0:T(8,128)(2,1)}, u32[]{:S(2)}) copy-start(bf16[24,1152]{1,0:T(8,128)(2,1)} %get-tuple-element.35) | copy-start | bytes 165892
  3.0 7.1 %copy-start.3 = (bf16[24,1152]{1,0:T(8,128)(2,1)S(1)}, bf16[24,1152]{1,0:T(8,128)(2,1)}, u32[]{:S(2)}) copy-start(bf16[24,1152]{1,0:T(8,128)(2,1)} %get-tuple-element.30.own_ref) | copy-start | bytes 165892
  3.0 19.1 %collective-permute-start.2 = (bf16[256,2048]{1,0:T(8,128)(2,1)}, bf16[256,2048]{1,0:T(8,128)(2,1)S(1)}, u32[]{:S(2)}, u32[]{:S(2)}) collective-permute-start(bf16[256,2048]{1,0:T(8,128)(2,1)} %bitcast.13), channel_id=1, source_target_pairs={{0,1},{1,0},{2,3},{3,2},{4,5},{5,4},{6,7},{7,6},{8,9},{9,8},{10,11... | collective-permute-start | bytes 3145736 | tf_op jit(solution)/shard_map/key_exchange/ppermute | solution.py:38
  3.1 24.4 %collective-permute-start.13 = (bf16[256,2048]{1,0:T(8,128)(2,1)}, bf16[256,2048]{1,0:T(8,128)(2,1)S(1)}, u32[]{:S(2)}, u32[]{:S(2)}) collective-permute-start(bf16[256,2048]{1,0:T(8,128)(2,1)} %bitcast.11), channel_id=1, source_target_pairs={{0,1},{1,0},{2,3},{3,2},{4,5},{5,4},{6,7},{7,6},{8,9},{9,8},{10,11... | collective-permute-start | bytes 3145736 | tf_op jit(solution)/shard_map/key_exchange/ppermute | solution.py:38
  3.6 10.8 %collective-permute-start.4 = (bf16[48,1024]{1,0:T(8,128)(2,1)S(1)}, bf16[48,1024]{1,0:T(8,128)(2,1)S(1)}, u32[]{:S(2)}, u32[]{:S(2)}) collective-permute-start(bf16[48,1024]{1,0:T(8,128)(2,1)S(1)} %join_queries.1.refs_1_.refs_4_), channel_id=1, source_target_pairs={{0,4},{1,5},{2,6},{3,7},{4,0},{5,1},{6,2},{7,3},{8,12},{9,13},{10,... | collective-permute-start | bytes 294920 | tf_op jit(solution)/shard_map/query_gather/ppermute | solution.py:43
  7.3 7.6 %collective-permute-start.5 = (bf16[48,1024]{1,0:T(8,128)(2,1)S(1)}, bf16[48,1024]{1,0:T(8,128)(2,1)S(1)}, u32[]{:S(2)}, u32[]{:S(2)}) collective-permute-start(bf16[48,1024]{1,0:T(8,128)(2,1)S(1)} %join_queries.1.refs_1_.refs_4_), channel_id=1, source_target_pairs={{0,2},{1,3},{2,0},{3,1},{4,6},{5,7},{6,4},{7,5},{8,10},{9,11},{10,... | collective-permute-start | bytes 294920 | tf_op jit(solution)/shard_map/query_gather/ppermute | solution.py:43
  8.8 1.2 %collective-permute-start.1 = (bf16[24,1152]{1,0:T(8,128)(2,1)S(1)}, bf16[24,1152]{1,0:T(8,128)(2,1)S(1)}, u32[]{:S(2)}, u32[]{:S(2)}) collective-permute-start(bf16[24,1152]{1,0:T(8,128)(2,1)S(1)} %copy-done.6), channel_id=1, source_target_pairs={{0,1},{1,0},{2,3},{3,2},{4,5},{5,4},{6,7},{7,6},{8,9},{9,8},{10,11... | collective-permute-start | bytes 165896 | tf_op jit(solution)/shard_map/sibling_exchange/ppermute | solution.py:38
  10.2 4.1 %collective-permute-start.3 = (f32[8,128]{1,0:T(8,128)S(1)}, f32[8,128]{1,0:T(8,128)S(1)}, u32[]{:S(2)}, u32[]{:S(2)}) collective-permute-start(f32[8,128]{1,0:T(8,128)S(1)} %get-tuple-element.38), channel_id=1, source_target_pairs={{0,8},{8,0},{16,24},{24,16},{1,9},{9,1},{17,25},{25,17},{2,10},{10... | collective-permute-start | bytes 12296 | tf_op jit(solution)/shard_map/mask_count/ppermute | solution.py:353
  11.7 0.7 %copy-start.4 = (s32[1,1,4]{2,1,0:T(1,128)S(1)}, s32[1,1,4]{2,1,0:T(1,128)}, u32[]{:S(2)}) copy-start(s32[1,1,4]{2,1,0:T(1,128)} %param.14) | copy-start | bytes 52
  11.7 0.7 %copy-start.5 = (s32[1,1,4]{2,1,0:T(1,128)S(1)}, s32[1,1,4]{2,1,0:T(1,128)}, u32[]{:S(2)}) copy-start(s32[1,1,4]{2,1,0:T(1,128)} %param.15) | copy-start | bytes 52
  12.4 1.2 %copy-start.1 = (bf16[1,256,2048]{2,1,0:T(8,128)(2,1)S(1)}, bf16[1,256,2048]{2,1,0:T(8,128)(2,1)}, u32[]{:S(2)}) copy-start(bf16[1,256,2048]{2,1,0:T(8,128)(2,1)} %param.9) | copy-start | bytes 3145732
  14.4 7.7 %collective-permute-start.6 = (bf16[48,1024]{1,0:T(8,128)(2,1)S(1)}, bf16[48,1024]{1,0:T(8,128)(2,1)S(1)}, u32[]{:S(2)}, u32[]{:S(2)}) collective-permute-start(bf16[48,1024]{1,0:T(8,128)(2,1)S(1)} %collective-permute-done.4.refs_2_.refs_5_), channel_id=1, source_target_pairs={{0,2},{1,3},{2,0},{3,1},{4,6},{5,7},{6,4},{7,5},{8,10},{9,11},{10,... | collective-permute-start | bytes 294920 | tf_op jit(solution)/shard_map/query_forward/ppermute | solution.py:43
  14.9 8.1 %collective-permute-start.10 = (bf16[48,1024]{1,0:T(8,128)(2,1)S(1)}, bf16[48,1024]{1,0:T(8,128)(2,1)S(1)}, u32[]{:S(2)}, u32[]{:S(2)}) collective-permute-start(bf16[48,1024]{1,0:T(8,128)(2,1)S(1)} %get-tuple-element.42.refs_8_), channel_id=1, source_target_pairs={{0,4},{1,5},{2,6},{3,7},{4,0},{5,1},{6,2},{7,3},{8,12},{9,13},{10,... | collective-permute-start | bytes 294920 | tf_op jit(solution)/shard_map/cotangent_gather/ppermute | solution.py:43
  16.9 8.6 %collective-permute-start.11 = (bf16[48,1024]{1,0:T(8,128)(2,1)S(1)}, bf16[48,1024]{1,0:T(8,128)(2,1)S(1)}, u32[]{:S(2)}, u32[]{:S(2)}) collective-permute-start(bf16[48,1024]{1,0:T(8,128)(2,1)S(1)} %get-tuple-element.42.refs_8_), channel_id=1, source_target_pairs={{0,2},{1,3},{2,0},{3,1},{4,6},{5,7},{6,4},{7,5},{8,10},{9,11},{10,... | collective-permute-start | bytes 294920 | tf_op jit(solution)/shard_map/cotangent_gather/ppermute | solution.py:43
  22.1 8.8 %copy-start = (bf16[1,256,2048]{2,1,0:T(8,128)(2,1)S(1)}, bf16[1,256,2048]{2,1,0:T(8,128)(2,1)}, u32[]{:S(2)}) copy-start(bf16[1,256,2048]{2,1,0:T(8,128)(2,1)} %param.10) | copy-start | bytes 3145732
  23.0 7.9 %collective-permute-start.12 = (bf16[48,1024]{1,0:T(8,128)(2,1)S(1)}, bf16[48,1024]{1,0:T(8,128)(2,1)S(1)}, u32[]{:S(2)}, u32[]{:S(2)}) collective-permute-start(bf16[48,1024]{1,0:T(8,128)(2,1)S(1)} %collective-permute-done.10.refs_9_), channel_id=1, source_target_pairs={{0,2},{1,3},{2,0},{3,1},{4,6},{5,7},{6,4},{7,5},{8,10},{9,11},{10,... | collective-permute-start | bytes 294920 | tf_op jit(solution)/shard_map/cotangent_forward/ppermute | solution.py:43
  23.1 4.6 %collective-permute-start.7 = (f32[8,256]{1,0:T(8,128)S(1)}, f32[8,256]{1,0:T(8,128)S(1)}, u32[]{:S(2)}, u32[]{:S(2)}) collective-permute-start(f32[8,256]{1,0:T(8,128)S(1)} %scores.1.refs_0_), channel_id=1, source_target_pairs={{0,4},{1,5},{2,6},{3,7},{4,0},{5,1},{6,2},{7,3},{8,12},{9,13},{10,... | collective-permute-start | bytes 24584 | tf_op jit(solution)/shard_map/stats_exchange/ppermute | solution.py:43
  25.1 3.7 %collective-permute-start.8 = (f32[8,256]{1,0:T(8,128)S(1)}, f32[8,256]{1,0:T(8,128)S(1)}, u32[]{:S(2)}, u32[]{:S(2)}) collective-permute-start(f32[8,256]{1,0:T(8,128)S(1)} %scores.1.refs_0_), channel_id=1, source_target_pairs={{0,2},{1,3},{2,0},{3,1},{4,6},{5,7},{6,4},{7,5},{8,10},{9,11},{10,... | collective-permute-start | bytes 24584 | tf_op jit(solution)/shard_map/stats_exchange/ppermute | solution.py:43
  25.5 5.4 %collective-permute-start.9 = (f32[8,256]{1,0:T(8,128)S(1)}, f32[8,256]{1,0:T(8,128)S(1)}, u32[]{:S(2)}, u32[]{:S(2)}) collective-permute-start(f32[8,256]{1,0:T(8,128)S(1)} %scores.1.refs_0_), channel_id=1, source_target_pairs={{0,6},{1,7},{2,4},{3,5},{4,2},{5,3},{6,0},{7,1},{8,14},{9,15},{10,... | collective-permute-start | bytes 24584 | tf_op jit(solution)/shard_map/stats_exchange/ppermute | solution.py:43
  33.5 8.1 %collective-permute-start.14 = (bf16[256,2048]{1,0:T(8,128)(2,1)S(1)}, bf16[256,2048]{1,0:T(8,128)(2,1)S(1)}, u32[]{:S(2)}, u32[]{:S(2)}) collective-permute-start(bf16[256,2048]{1,0:T(8,128)(2,1)S(1)} %get-tuple-element.46), channel_id=1, source_target_pairs={{0,1},{1,0},{2,3},{3,2},{4,5},{5,4},{6,7},{7,6},{8,9},{9,8},{10,11... | collective-permute-start | bytes 3145736 | tf_op jit(solution)/shard_map/key_grad_end/ppermute | solution.py:38
  33.6 9.9 %collective-permute-start.16 = (bf16[48,1024]{1,0:T(8,128)(2,1)S(1)}, bf16[48,1024]{1,0:T(8,128)(2,1)S(1)}, u32[]{:S(2)}, u32[]{:S(2)}) collective-permute-start(bf16[48,1024]{1,0:T(8,128)(2,1)S(1)} %get-tuple-element.50), channel_id=1, source_target_pairs={{0,6},{1,7},{2,4},{3,5},{4,2},{5,3},{6,0},{7,1},{8,14},{9,15},{10,... | collective-permute-start | bytes 294920 | tf_op jit(solution)/shard_map/query_grad_sum/ppermute | solution.py:43
  35.8 9.1 %collective-permute-start.17 = (bf16[48,1024]{1,0:T(8,128)(2,1)S(1)}, bf16[48,1024]{1,0:T(8,128)(2,1)S(1)}, u32[]{:S(2)}, u32[]{:S(2)}) collective-permute-start(bf16[48,1024]{1,0:T(8,128)(2,1)S(1)} %get-tuple-element.51), channel_id=1, source_target_pairs={{0,4},{1,5},{2,6},{3,7},{4,0},{5,1},{6,2},{7,3},{8,12},{9,13},{10,... | collective-permute-start | bytes 294920 | tf_op jit(solution)/shard_map/query_grad_sum/ppermute | solution.py:43
  35.8 9.1 %collective-permute-start.18 = (bf16[48,1024]{1,0:T(8,128)(2,1)S(1)}, bf16[48,1024]{1,0:T(8,128)(2,1)S(1)}, u32[]{:S(2)}, u32[]{:S(2)}) collective-permute-start(bf16[48,1024]{1,0:T(8,128)(2,1)S(1)} %get-tuple-element.52), channel_id=1, source_target_pairs={{0,2},{1,3},{2,0},{3,1},{4,6},{5,7},{6,4},{7,5},{8,10},{9,11},{10,... | collective-permute-start | bytes 294920 | tf_op jit(solution)/shard_map/query_grad_sum/ppermute | solution.py:43
  38.1 3.6 %collective-permute-start.15 = (f32[8,128]{1,0:T(8,128)S(1)}, f32[8,128]{1,0:T(8,128)S(1)}, u32[]{:S(2)}, u32[]{:S(2)}) collective-permute-start(f32[8,128]{1,0:T(8,128)S(1)} %get-tuple-element.47.refs_0_), channel_id=1, source_target_pairs={{0,16},{8,24},{16,0},{24,8},{1,17},{9,25},{17,1},{25,9},{2,18},{10... | collective-permute-start | bytes 12296 | tf_op jit(solution)/shard_map/key_grad_end/ppermute | solution.py:353
  44.9 1.3 %collective-permute-start.19 = (bf16[24,1024]{1,0:T(8,128)(2,1)S(1)}, bf16[24,1024]{1,0:T(8,128)(2,1)S(1)}, u32[]{:S(2)}, u32[]{:S(2)}) collective-permute-start(bf16[24,1024]{1,0:T(8,128)(2,1)S(1)} %get-tuple-element.54), channel_id=1, source_target_pairs={{0,1},{1,0},{2,3},{3,2},{4,5},{5,4},{6,7},{7,6},{8,9},{9,8},{10,11... | collective-permute-start | bytes 147464 | tf_op jit(solution)/shard_map/query_grad_end/ppermute | solution.py:38

commit v2 on v1

--- a/solution.py
+++ b/solution.py
@@ -118,6 +118,12 @@
     count_ref[...] = jnp.broadcast_to(count, count_ref.shape)
 
 
+def split_kernel(rows_ref, own_ref, send_ref):
+    _, core = position()
+    for ref, half in ((own_ref, core), (send_ref, 1 - core)):
+        ref[...] = rows_ref[:, pl.ds(pl.multiple_of(half * HALF, HALF), HALF)]
+
+
 def document_of(positions, lengths_ref):
     end = 0
     document = jnp.zeros_like(positions)
@@ -127,10 +133,9 @@
     return document
 
 
-def setup_kernel(offsets, in_ref, target_ref, key_ref, k_ref, bias_own, bias_other):
+def setup_kernel(offsets, in_ref, target_ref, key_ref, k_ref, send_ref, bias_own, bias_other):
     chip, core = position()
-    mine = pl.ds(pl.multiple_of(core * HALF, HALF), HALF)
-    k_ref[...] = key_ref[:, mine]
+    split_kernel(key_ref, k_ref, send_ref)
     enc_rows, dec_rows = bias_own.shape
     block = dec_rows // len(offsets)
     lane = lax.broadcasted_iota(jnp.int32, (1, dec_rows), 1)
@@ -155,12 +160,14 @@
     return jnp.concatenate([block[:, columns] for block in blocks], 0)
 
 
-def tile_of(ref, head):
-    first = head * HEAD_SIZE
-    if ref.shape[1] == HALF:
-        return ref[:, first : first + HEAD_SIZE]
-    _, core = position()
-    return ref[:, pl.ds(pl.multiple_of(core * HALF + first, HEAD_SIZE), HEAD_SIZE)]
+def value_columns_of(head):
+    _, core = position()
+    first = core * HALF + head * HEAD_SIZE
+    return pl.ds(pl.multiple_of(first, HEAD_SIZE), HEAD_SIZE)
+
+
+def columns_of(head):
+    return slice(head * HEAD_SIZE, (head + 1) * HEAD_SIZE)
 
 
 def scores_kernel(offsets, delta_ref, bias_own, bias_other, key_ref, other_ref, *refs):
@@ -173,7 +180,7 @@
     for head in range(HALF_HEADS):
         q = rows_of(blocks, head)
         scores = [
-            dot(tile_of(k, head), q, NT) * ROOT + bias[...]
+            dot(k[:, columns_of(head)], q, NT) * ROOT + bias[...]
             for k, bias in ((key_ref, bias_own), (other_ref, bias_other))
         ]
         top = functools.reduce(jnp.maximum, [jnp.max(s, axis=0, keepdims=True) for s in scores])
@@ -218,7 +225,7 @@
             (key_ref, value_ref, bias_own, keep_ref),
             (key_other, value_other, bias_other, send_ref),
         ):
-            k, v = tile_of(key, head), tile_of(value, head)
+            k, v = key[:, columns], value[:, value_columns_of(head)]
             probs = jnp.exp(dot(k, q, NT) * ROOT + bias[...] - log_total[line])
             dscore = (probs * (dot(v, g, NT) - delta[line])).astype(BF16)
             dq += dot(dscore, k, TN)
@@ -318,18 +325,14 @@
         )(query_rows, q_recv)
         q_far, q_near = gather(q_block)
 
-    with jax.named_scope("key_exchange"):
-        k_recv = to_sibling(after(key_rows, q_block)[0])
-        v_recv = to_sibling(after(value_rows, q_block)[0])
-
     with jax.named_scope("setup"):
         half_rows = shaped(enc_local, HALF)
         bias = shaped(enc_local, dec_rows, dtype=F32)
-        k_own, bias_own, bias_other = kernel_call(
+        k_own, k_send, bias_own, bias_other = kernel_call(
             functools.partial(setup_kernel, offsets),
-            (half_rows, bias, bias),
+            (half_rows, half_rows, bias, bias),
             [SMEM] * 2 + [VMEM],
-            (VMEM,) * 3,
+            (VMEM,) * 4,
             [],
             10**6,
             2**22,
@@ -360,11 +363,17 @@
         rows_in_all = float(data_groups * dec_rows)
 
     with jax.named_scope("query_forward"):
-        q_far = [q_far[0], *(after(one, bias_own, count)[0] for one in q_far[1:])]
+        q_far = [q_far[0], *(after(one, bias_own, count, q_near)[0] for one in q_far[1:])]
         q_blocks = [*q_far, q_near, *forwarded(q_far)]
 
     with jax.named_scope("cotangent_gather"):
-        g_far, g_near = gather(after(g_block, *q_far, q_near)[0])
+        sent = after(g_block, *q_far, q_near)[0]
+        g_blocks = [g_block] + [across(sent, offset) for offset in offsets[1:]]
+
+    with jax.named_scope("key_exchange"):
+        v_recv = to_sibling(value_rows)
+        k_send, v_recv, *_ = after(k_send, v_recv, *q_far, q_near)
+        k_recv = to_sibling(k_send)
 
     with jax.named_scope("scores"):
         width = (dec_rows // 128 + 1) * 128
@@ -378,10 +387,6 @@
             2 * (dec_rows + enc_rows) * HALF,
             "scores",
         )(delta, bias_own, bias_other, k_own, k_recv, count, *q_blocks)
-
-    with jax.named_scope("cotangent_forward"):
-        g_far = [g_far[0], *(after(one, stats)[0] for one in g_far[1:])]
-        g_blocks = [*g_far, g_near, *forwarded(g_far)]
 
     with jax.named_scope("stats_exchange"):
         all_stats = [stats] + [across(stats, offset) for offset in offsets[1:]]

time: 47.1 us -> 46.8 us (level)
  waiting for transfers between devices: 13.9 us -> 12 us
  starting transfers between devices: 21.6 us -> 23.2 us
    ppermute x12, waiting for transfers between devices: 9.35 us -> 6.65 us  [across(): lax.ppermute(block, 'seq', [(i, i ^ 2 * apart) for i in range(count)])]
    ppermute x12, starting transfers between devices: 17.3 us -> 19.4 us  [across(): lax.ppermute(block, 'seq', [(i, i ^ 2 * apart) for i in range(count)])]
    ppermute x6, waiting for transfers between devices: 2.44 us -> 3.23 us  [to_sibling(): return lax.ppermute(block, 'seq', [(i, i ^ 1) for i in range(count)])]
where the time goes in v2:
time: 46.8 us; the launch traced here: 46.6 us
  starting transfers between devices  23.2 us (50%)
  waiting for transfers between devices  12 us (26%)
  Pallas kernels  8.08 us (17%)
  local copies, waits for them, and re-layouts  1.91 us (4%)
  between operations  0.77 us (2%)
  other arithmetic  0.67 us (1%)
    ppermute x12, starting transfers between devices, across(): lax.ppermute(block, 'seq', [(i, i ^ 2 * apart) for i in range(count)])  19.4 us
    ppermute x12, waiting for transfers between devices, across(): lax.ppermute(block, 'seq', [(i, i ^ 2 * apart) for i in range(count)])  6.65 us
    ppermute x6, waiting for transfers between devices, to_sibling(): return lax.ppermute(block, 'seq', [(i, i ^ 1) for i in range(count)])  3.23 us
    ppermute x2, starting transfers between devices, over_groups(): lax.ppermute(count, 'dp', [(i, i ^ apart) for i in range(data_groups)])  3.02 us
    pallas_call x1, Pallas kernels, local(): kernel_call(functools.partial(grads_kernel, offsets), (block,) * chips +...  2.58 us
    ppermute x2, waiting for transfers between devices, over_groups(): lax.ppermute(count, 'dp', [(i, i ^ apart) for i in range(data_groups)])  2.08 us
    unnamed x14, local copies, waits for them, and re-layouts  1.91 us
    pallas_call x1, Pallas kernels, local(): kernel_call(functools.partial(key_end_kernel, rows_in_all), (whole, whole...  1.84 us
  transfers between devices with their start and end apart: 20, of which 8 were waited for; matrix products, arithmetic and copies ran while one was open for 0% of the time, Pallas kernels for 12%

profile of v2, /device:TPU:0, one launch (start us, length us, event | category | flops | bytes accessed | tf_op | source)
XLA Modules:
  0.0 46.6 jit_solution(8827973049595436856)
XLA Ops:
  0.6 0.5 %collective-permute-start.2 = (bf16[256,2048]{1,0:T(8,128)(2,1)}, bf16[256,2048]{1,0:T(8,128)(2,1)S(1)}, u32[]{:S(2)}, u32[]{:S(2)}) collective-permute-start(bf16[256,2048]{1,0:T(8,128)(2,1)} %bitcast.11), channel_id=1, source_target_pairs={{0,1},{1,0},{2,3},{3,2},{4,5},{5,4},{6,7},{7,6},{8,9},{9,8},{10,11... | collective-permute-start | bytes 3145736 | tf_op jit(solution)/shard_map/key_exchange/ppermute | solution.py:38
  1.1 0.1 collective-permute-start
  1.2 1.8 %prepare.1 = (bf16[24,1152]{1,0:T(8,128)(2,1)}, bf16[24,1152]{1,0:T(8,128)(2,1)}) custom-call(bf16[24,2048]{1,0:T(8,128)(2,1)} %bitcast.19, bf16[24,2048]{1,0:T(8,128)(2,1)} %bitcast.20, s32[1,24]{1,0:T(1,128)} %mask_ref.1), custom_call_target="tpu_custom_call" | custom-call | flops 100000 | bytes 1000000 | tf_op jit(solution)/shard_map/sibling_exchange/prepare/pallas_call | solution.py:303
  3.0 0.8 %collective-permute-done.other_ref = bf16[24,2048]{1,0:T(8,128)(2,1)S(1)} collective-permute-done((bf16[24,2048]{1,0:T(8,128)(2,1)}, bf16[24,2048]{1,0:T(8,128)(2,1)S(1)}, u32[]{:S(2)}, u32[]{:S(2)}) %collective-permute-start) | collective-permute-done | bytes 98336 | tf_op jit(solution)/shard_map/sibling_exchange/ppermute | solution.py:38
  3.8 3.0 %collective-permute-start.5 = (bf16[48,1024]{1,0:T(8,128)(2,1)S(1)}, bf16[48,1024]{1,0:T(8,128)(2,1)S(1)}, u32[]{:S(2)}, u32[]{:S(2)}) collective-permute-start(bf16[48,1024]{1,0:T(8,128)(2,1)S(1)} %join_queries.1.refs_1_.refs_4_), channel_id=1, source_target_pairs={{0,2},{1,3},{2,0},{3,1},{4,6},{5,7},{6,4},{7,5},{8,10},{9,11},{10,... | collective-permute-start | bytes 294920 | tf_op jit(solution)/shard_map/query_gather/ppermute | solution.py:43
  6.8 2.6 %collective-permute-start.3 = (bf16[48,1024]{1,0:T(8,128)(2,1)S(1)}, bf16[48,1024]{1,0:T(8,128)(2,1)S(1)}, u32[]{:S(2)}, u32[]{:S(2)}) collective-permute-start(bf16[48,1024]{1,0:T(8,128)(2,1)S(1)} %join_queries.1.refs_1_.refs_4_), channel_id=1, source_target_pairs={{0,4},{1,5},{2,6},{3,7},{4,0},{5,1},{6,2},{7,3},{8,12},{9,13},{10,... | collective-permute-start | bytes 294920 | tf_op jit(solution)/shard_map/query_gather/ppermute | solution.py:43
  9.4 0.0 collective-permute-start.1
  9.4 1.2 %collective-permute-done.1.other_ref = bf16[24,1152]{1,0:T(8,128)(2,1)S(1)} collective-permute-done((bf16[24,1152]{1,0:T(8,128)(2,1)S(1)}, bf16[24,1152]{1,0:T(8,128)(2,1)S(1)}, u32[]{:S(2)}, u32[]{:S(2)}) %collective-permute-start.1) | collective-permute-done | bytes 55328 | tf_op jit(solution)/shard_map/sibling_exchange/ppermute | solution.py:38
  10.7 0.2 join_cotangents.1
  10.8 1.5 %collective-permute-start.4 = (f32[8,128]{1,0:T(8,128)S(1)}, f32[8,128]{1,0:T(8,128)S(1)}, u32[]{:S(2)}, u32[]{:S(2)}) collective-permute-start(f32[8,128]{1,0:T(8,128)S(1)} %get-tuple-element.40), channel_id=1, source_target_pairs={{0,8},{8,0},{16,24},{24,16},{1,9},{9,1},{17,25},{25,17},{2,10},{10... | collective-permute-start | bytes 12296 | tf_op jit(solution)/shard_map/mask_count/ppermute | solution.py:356
  12.3 0.7 %copy-done.4 = s32[1,1,4]{2,1,0:T(1,128)S(1)} copy-done((s32[1,1,4]{2,1,0:T(1,128)S(1)}, s32[1,1,4]{2,1,0:T(1,128)}, u32[]{:S(2)}) %copy-start.4) | copy-done | bytes 40
  13.0 0.0 copy-done.5
  13.0 1.2 %copy-done.1 = bf16[1,256,2048]{2,1,0:T(8,128)(2,1)S(1)} copy-done((bf16[1,256,2048]{2,1,0:T(8,128)(2,1)S(1)}, bf16[1,256,2048]{2,1,0:T(8,128)(2,1)}, u32[]{:S(2)}) %copy-start.1) | copy-done | bytes 1048600
  14.2 0.7 %setup.1 = (bf16[256,1024]{1,0:T(8,128)(2,1)S(1)}, bf16[256,1024]{1,0:T(8,128)(2,1)S(1)}, f32[256,192]{1,0:T(8,128)S(1)}, f32[256,192]{1,0:T(8,128)S(1)}) custom-call(s32[1,4]{1,0:T(1,128)S(1)} %bitcast.17, s32[1,4]{1,0:T(1,128)S(1)} %bitcast.18, bf16[256,2048]{1,0:T(8,128)(2,1)S(1)} %bitcast.13), custom_call_target="tpu_custom_call" | custom-call | flops 1000000 | bytes 4194304 | tf_op jit(solution)/shard_map/setup/setup/pallas_call | solution.py:331
  15.0 0.0 copy-start
  15.0 0.0 collective-permute-done.5.refs_3_.refs_6_
  15.0 0.0 collective-permute-done.2.refs_15_
  15.0 0.1 collective-permute-start.6
  15.1 0.5 %collective-permute-start.7 = (bf16[48,1024]{1,0:T(8,128)(2,1)S(1)}, bf16[48,1024]{1,0:T(8,128)(2,1)S(1)}, u32[]{:S(2)}, u32[]{:S(2)}) collective-permute-start(bf16[48,1024]{1,0:T(8,128)(2,1)S(1)} %collective-permute-done.3.refs_2_.refs_5_), channel_id=1, source_target_pairs={{0,2},{1,3},{2,0},{3,1},{4,6},{5,7},{6,4},{7,5},{8,10},{9,11},{10,... | collective-permute-start | bytes 294920 | tf_op jit(solution)/shard_map/query_forward/ppermute | solution.py:43
  15.6 1.9 %collective-permute-start.11 = (bf16[48,1024]{1,0:T(8,128)(2,1)S(1)}, bf16[48,1024]{1,0:T(8,128)(2,1)S(1)}, u32[]{:S(2)}, u32[]{:S(2)}) collective-permute-start(bf16[48,1024]{1,0:T(8,128)(2,1)S(1)} %get-tuple-element.45.refs_8_), channel_id=1, source_target_pairs={{0,4},{1,5},{2,6},{3,7},{4,0},{5,1},{6,2},{7,3},{8,12},{9,13},{10,... | collective-permute-start | bytes 294920 | tf_op jit(solution)/shard_map/cotangent_gather/ppermute | solution.py:43
  17.5 0.1 collective-permute-start.12
  17.6 2.4 %collective-permute-start.13 = (bf16[48,1024]{1,0:T(8,128)(2,1)S(1)}, bf16[48,1024]{1,0:T(8,128)(2,1)S(1)}, u32[]{:S(2)}, u32[]{:S(2)}) collective-permute-start(bf16[48,1024]{1,0:T(8,128)(2,1)S(1)} %get-tuple-element.45.refs_8_), channel_id=1, source_target_pairs={{0,6},{1,7},{2,4},{3,5},{4,2},{5,3},{6,0},{7,1},{8,14},{9,15},{10,... | collective-permute-start | bytes 294920 | tf_op jit(solution)/shard_map/cotangent_gather/ppermute | solution.py:43
  20.0 1.9 %collective-permute-done.7.refs_4_.refs_7_ = bf16[48,1024]{1,0:T(8,128)(2,1)S(1)} collective-permute-done((bf16[48,1024]{1,0:T(8,128)(2,1)S(1)}, bf16[48,1024]{1,0:T(8,128)(2,1)S(1)}, u32[]{:S(2)}, u32[]{:S(2)}) %collective-permute-start.7) | collective-permute-done | bytes 98336 | tf_op jit(solution)/shard_map/query_forward/ppermute | solution.py:43
  21.9 0.0 collective-permute-done.6.other_ref.refs_13_
  21.9 0.9 %scores.1.refs_0_ = f32[8,256]{1,0:T(8,128)S(1)} custom-call(f32[8,48]{1,0:T(8,128)S(1)} %get-tuple-element.37.delta_ref, f32[256,192]{1,0:T(8,128)S(1)} %get-tuple-element.34.bias_own, f32[256,192]{1,0:T(8,128)S(1)} %get-tuple-element.35.bias_other, bf16[256,1024]{1,0:T(8,128)(2,1)S(1)} %get-tuple-element.38.key_ref.refs_12_, ...), custom_call_target="tpu_custom_call" | custom-call | flops 201326592 | bytes 1441792 | tf_op jit(solution)/shard_map/scores/scores/pallas_call | solution.py:380
  22.8 2.3 %collective-permute-start.10 = (f32[8,256]{1,0:T(8,128)S(1)}, f32[8,256]{1,0:T(8,128)S(1)}, u32[]{:S(2)}, u32[]{:S(2)}) collective-permute-start(f32[8,256]{1,0:T(8,128)S(1)} %scores.1.refs_0_), channel_id=1, source_target_pairs={{0,6},{1,7},{2,4},{3,5},{4,2},{5,3},{6,0},{7,1},{8,14},{9,15},{10,... | collective-permute-start | bytes 24584 | tf_op jit(solution)/shard_map/stats_exchange/ppermute | solution.py:43
  25.2 0.0 collective-permute-done.11.refs_9_
  25.2 2.1 %collective-permute-start.9 = (f32[8,256]{1,0:T(8,128)S(1)}, f32[8,256]{1,0:T(8,128)S(1)}, u32[]{:S(2)}, u32[]{:S(2)}) collective-permute-start(f32[8,256]{1,0:T(8,128)S(1)} %scores.1.refs_0_), channel_id=1, source_target_pairs={{0,2},{1,3},{2,0},{3,1},{4,6},{5,7},{6,4},{7,5},{8,10},{9,11},{10,... | collective-permute-start | bytes 24584 | tf_op jit(solution)/shard_map/stats_exchange/ppermute | solution.py:43
  27.3 0.0 collective-permute-done.12.refs_10_
  27.3 0.0 collective-permute-done.13.refs_11_
  27.3 1.1 %collective-permute-done.10.refs_3_ = f32[8,256]{1,0:T(8,128)S(1)} collective-permute-done((f32[8,256]{1,0:T(8,128)S(1)}, f32[8,256]{1,0:T(8,128)S(1)}, u32[]{:S(2)}, u32[]{:S(2)}) %collective-permute-start.10) | collective-permute-done | bytes 8224 | tf_op jit(solution)/shard_map/stats_exchange/ppermute | solution.py:43
  28.3 1.4 %collective-permute-done.8.refs_1_ = f32[8,256]{1,0:T(8,128)S(1)} collective-permute-done((f32[8,256]{1,0:T(8,128)S(1)}, f32[8,256]{1,0:T(8,128)S(1)}, u32[]{:S(2)}, u32[]{:S(2)}) %collective-permute-start.8) | collective-permute-done | bytes 8224 | tf_op jit(solution)/shard_map/stats_exchange/ppermute | solution.py:43
  29.7 2.6 %grads.1 = (bf16[48,1024]{1,0:T(8,128)(2,1)S(1)}, bf16[48,1024]{1,0:T(8,128)(2,1)S(1)}, bf16[48,1024]{1,0:T(8,128)(2,1)S(1)}, bf16[48,1024]{1,0:T(8,128)(2,1)S(1...) custom-call(f32[256,192]{1,0:T(8,128)S(1)} %get-tuple-element.34.bias_own, ...), custom_call_target="tpu_custom_call" | custom-call | flops 1006632960 | bytes 4980736 | tf_op jit(solution)/shard_map/grads/grads/pallas_call | solution.py:396
  32.3 0.1 collective-permute-start.14
  32.4 1.6 %collective-permute-start.16 = (bf16[48,1024]{1,0:T(8,128)(2,1)S(1)}, bf16[48,1024]{1,0:T(8,128)(2,1)S(1)}, u32[]{:S(2)}, u32[]{:S(2)}) collective-permute-start(bf16[48,1024]{1,0:T(8,128)(2,1)S(1)} %get-tuple-element.52), channel_id=1, source_target_pairs={{0,6},{1,7},{2,4},{3,5},{4,2},{5,3},{6,0},{7,1},{8,14},{9,15},{10,... | collective-permute-start | bytes 294920 | tf_op jit(solution)/shard_map/query_grad_sum/ppermute | solution.py:43
  34.0 1.1 %collective-permute-start.17 = (bf16[48,1024]{1,0:T(8,128)(2,1)S(1)}, bf16[48,1024]{1,0:T(8,128)(2,1)S(1)}, u32[]{:S(2)}, u32[]{:S(2)}) collective-permute-start(bf16[48,1024]{1,0:T(8,128)(2,1)S(1)} %get-tuple-element.53), channel_id=1, source_target_pairs={{0,4},{1,5},{2,6},{3,7},{4,0},{5,1},{6,2},{7,3},{8,12},{9,13},{10,... | collective-permute-start | bytes 294920 | tf_op jit(solution)/shard_map/query_grad_sum/ppermute | solution.py:43
  35.1 1.7 %collective-permute-start.18 = (bf16[48,1024]{1,0:T(8,128)(2,1)S(1)}, bf16[48,1024]{1,0:T(8,128)(2,1)S(1)}, u32[]{:S(2)}, u32[]{:S(2)}) collective-permute-start(bf16[48,1024]{1,0:T(8,128)(2,1)S(1)} %get-tuple-element.54), channel_id=1, source_target_pairs={{0,2},{1,3},{2,0},{3,1},{4,6},{5,7},{6,4},{7,5},{8,10},{9,11},{10,... | collective-permute-start | bytes 294920 | tf_op jit(solution)/shard_map/query_grad_sum/ppermute | solution.py:43
  36.8 1.5 %collective-permute-start.15 = (f32[8,128]{1,0:T(8,128)S(1)}, f32[8,128]{1,0:T(8,128)S(1)}, u32[]{:S(2)}, u32[]{:S(2)}) collective-permute-start(f32[8,128]{1,0:T(8,128)S(1)} %get-tuple-element.49.refs_0_), channel_id=1, source_target_pairs={{0,16},{8,24},{16,0},{24,8},{1,17},{9,25},{17,1},{25,9},{2,18},{10... | collective-permute-start | bytes 12296 | tf_op jit(solution)/shard_map/key_grad_end/ppermute | solution.py:356
  38.4 2.1 %collective-permute-done.15.refs_1_ = f32[8,128]{1,0:T(8,128)S(1)} collective-permute-done((f32[8,128]{1,0:T(8,128)S(1)}, f32[8,128]{1,0:T(8,128)S(1)}, u32[]{:S(2)}, u32[]{:S(2)}) %collective-permute-start.15) | collective-permute-done | bytes 4128 | tf_op jit(solution)/shard_map/key_grad_end/ppermute | solution.py:356
  40.4 0.0 collective-permute-done.14.other_ref
  40.4 1.8 %key_end.1 = (bf16[256,2048]{1,0:T(8,128)(2,1)}, bf16[256,2048]{1,0:T(8,128)(2,1)}, f32[8,128]{1,0:T(8,128)S(1)}) custom-call(bf16[256,2048]{1,0:T(8,128)(2,1)S(1)} %get-tuple-element.47.keep_ref, bf16[256,2048]{1,0:T(8,128)(2,1)S(1)} %collective-permute-done.14.other_ref, f32[8,128]{1,0:T(8,128)S(1)} %get-tuple-element.49.refs_0_, ...), custom_call_target="tpu_custom_call" | custom-call | flops 1000000 | bytes 4194304 | tf_op jit(solution)/shard_map/key_grad_end/key_end/pallas_call | solution.py:416
  42.3 0.0 collective-permute-done.16.refs_1_
  42.3 2.3 %collective-permute-done.17.refs_2_ = bf16[48,1024]{1,0:T(8,128)(2,1)S(1)} collective-permute-done((bf16[48,1024]{1,0:T(8,128)(2,1)S(1)}, bf16[48,1024]{1,0:T(8,128)(2,1)S(1)}, u32[]{:S(2)}, u32[]{:S(2)}) %collective-permute-start.17) | collective-permute-done | bytes 98336 | tf_op jit(solution)/shard_map/query_grad_sum/ppermute | solution.py:43
  44.6 0.0 collective-permute-done.18.refs_3_
  44.6 0.1 query_end.1
  44.7 0.1 collective-permute-start.19
  44.8 1.2 %collective-permute-done.19 = bf16[24,1024]{1,0:T(8,128)(2,1)S(1)} collective-permute-done((bf16[24,1024]{1,0:T(8,128)(2,1)S(1)}, bf16[24,1024]{1,0:T(8,128)(2,1)S(1)}, u32[]{:S(2)}, u32[]{:S(2)}) %collective-permute-start.19) | collective-permute-done | bytes 49184 | tf_op jit(solution)/shard_map/query_grad_end/ppermute | solution.py:38
  46.0 0.7 %maximum_select_fusion = bf16[1,24,2048]{2,1,0:T(8,128)(2,1)} fusion(bf16[1,24,1024]{2,1,0:T(8,128)(2,1)S(1)} %bitcast.21, bf16[1,24,1024]{2,1,0:T(8,128)(2,1)S(1)} %bitcast.16, pred[]{:T(512)S(6)} %eq.3), kind=kLoop, calls=%fused_computation | loop fusion | flops 442368 | bytes 196609 | tf_op jit(solution)/shard_map/query_grad_end/jit(_where)/select_n | solution.py:261
  (16 shorter events, 0.1 us)
Async XLA Ops:
  0.6 14.4 %collective-permute-start.2 = (bf16[256,2048]{1,0:T(8,128)(2,1)}, bf16[256,2048]{1,0:T(8,128)(2,1)S(1)}, u32[]{:S(2)}, u32[]{:S(2)}) collective-permute-start(bf16[256,2048]{1,0:T(8,128)(2,1)} %bitcast.11), channel_id=1, source_target_pairs={{0,1},{1,0},{2,3},{3,2},{4,5},{5,4},{6,7},{7,6},{8,9},{9,8},{10,11... | collective-permute-start | bytes 3145736 | tf_op jit(solution)/shard_map/key_exchange/ppermute | solution.py:38
  1.1 2.6 %collective-permute-start = (bf16[24,2048]{1,0:T(8,128)(2,1)}, bf16[24,2048]{1,0:T(8,128)(2,1)S(1)}, u32[]{:S(2)}, u32[]{:S(2)}) collective-permute-start(bf16[24,2048]{1,0:T(8,128)(2,1)} %bitcast.14), channel_id=1, source_target_pairs={{0,1},{1,0},{2,3},{3,2},{4,5},{5,4},{6,7},{7,6},{8,9},{9,8},{10,11... | collective-permute-start | bytes 294920 | tf_op jit(solution)/shard_map/sibling_exchange/ppermute | solution.py:38
  1.2 2.6 %copy-start.2 = (bf16[1,24,2048]{2,1,0:T(8,128)(2,1)S(1)}, bf16[1,24,2048]{2,1,0:T(8,128)(2,1)}, u32[]{:S(2)}) copy-start(bf16[1,24,2048]{2,1,0:T(8,128)(2,1)} %param.8) | copy-start | bytes 294916
  3.8 5.6 %copy-start.6 = (bf16[24,1152]{1,0:T(8,128)(2,1)S(1)}, bf16[24,1152]{1,0:T(8,128)(2,1)}, u32[]{:S(2)}) copy-start(bf16[24,1152]{1,0:T(8,128)(2,1)} %get-tuple-element.36) | copy-start | bytes 165892
  3.8 6.9 %copy-start.3 = (bf16[24,1152]{1,0:T(8,128)(2,1)S(1)}, bf16[24,1152]{1,0:T(8,128)(2,1)}, u32[]{:S(2)}) copy-start(bf16[24,1152]{1,0:T(8,128)(2,1)} %get-tuple-element.31.own_ref) | copy-start | bytes 165892
  3.8 11.2 %collective-permute-start.5 = (bf16[48,1024]{1,0:T(8,128)(2,1)S(1)}, bf16[48,1024]{1,0:T(8,128)(2,1)S(1)}, u32[]{:S(2)}, u32[]{:S(2)}) collective-permute-start(bf16[48,1024]{1,0:T(8,128)(2,1)S(1)} %join_queries.1.refs_1_.refs_4_), channel_id=1, source_target_pairs={{0,2},{1,3},{2,0},{3,1},{4,6},{5,7},{6,4},{7,5},{8,10},{9,11},{10,... | collective-permute-start | bytes 294920 | tf_op jit(solution)/shard_map/query_gather/ppermute | solution.py:43
  6.8 8.2 %collective-permute-start.3 = (bf16[48,1024]{1,0:T(8,128)(2,1)S(1)}, bf16[48,1024]{1,0:T(8,128)(2,1)S(1)}, u32[]{:S(2)}, u32[]{:S(2)}) collective-permute-start(bf16[48,1024]{1,0:T(8,128)(2,1)S(1)} %join_queries.1.refs_1_.refs_4_), channel_id=1, source_target_pairs={{0,4},{1,5},{2,6},{3,7},{4,0},{5,1},{6,2},{7,3},{8,12},{9,13},{10,... | collective-permute-start | bytes 294920 | tf_op jit(solution)/shard_map/query_gather/ppermute | solution.py:43
  9.4 1.2 %collective-permute-start.1 = (bf16[24,1152]{1,0:T(8,128)(2,1)S(1)}, bf16[24,1152]{1,0:T(8,128)(2,1)S(1)}, u32[]{:S(2)}, u32[]{:S(2)}) collective-permute-start(bf16[24,1152]{1,0:T(8,128)(2,1)S(1)} %copy-done.6), channel_id=1, source_target_pairs={{0,1},{1,0},{2,3},{3,2},{4,5},{5,4},{6,7},{7,6},{8,9},{9,8},{10,11... | collective-permute-start | bytes 165896 | tf_op jit(solution)/shard_map/sibling_exchange/ppermute | solution.py:38
  10.8 4.1 %collective-permute-start.4 = (f32[8,128]{1,0:T(8,128)S(1)}, f32[8,128]{1,0:T(8,128)S(1)}, u32[]{:S(2)}, u32[]{:S(2)}) collective-permute-start(f32[8,128]{1,0:T(8,128)S(1)} %get-tuple-element.40), channel_id=1, source_target_pairs={{0,8},{8,0},{16,24},{24,16},{1,9},{9,1},{17,25},{25,17},{2,10},{10... | collective-permute-start | bytes 12296 | tf_op jit(solution)/shard_map/mask_count/ppermute | solution.py:356
  12.3 0.7 %copy-start.4 = (s32[1,1,4]{2,1,0:T(1,128)S(1)}, s32[1,1,4]{2,1,0:T(1,128)}, u32[]{:S(2)}) copy-start(s32[1,1,4]{2,1,0:T(1,128)} %param.14) | copy-start | bytes 52
  12.3 0.7 %copy-start.5 = (s32[1,1,4]{2,1,0:T(1,128)S(1)}, s32[1,1,4]{2,1,0:T(1,128)}, u32[]{:S(2)}) copy-start(s32[1,1,4]{2,1,0:T(1,128)} %param.15) | copy-start | bytes 52
  13.0 1.2 %copy-start.1 = (bf16[1,256,2048]{2,1,0:T(8,128)(2,1)S(1)}, bf16[1,256,2048]{2,1,0:T(8,128)(2,1)}, u32[]{:S(2)}) copy-start(bf16[1,256,2048]{2,1,0:T(8,128)(2,1)} %param.9) | copy-start | bytes 3145732
  15.0 14.8 %copy-start = (bf16[1,256,2048]{2,1,0:T(8,128)(2,1)S(1)}, bf16[1,256,2048]{2,1,0:T(8,128)(2,1)}, u32[]{:S(2)}) copy-start(bf16[1,256,2048]{2,1,0:T(8,128)(2,1)} %param.10) | copy-start | bytes 3145732
  15.0 6.9 %collective-permute-start.6 = (bf16[256,1024]{1,0:T(8,128)(2,1)S(1)}, bf16[256,1024]{1,0:T(8,128)(2,1)S(1)}, u32[]{:S(2)}, u32[]{:S(2)}) collective-permute-start(bf16[256,1024]{1,0:T(8,128)(2,1)S(1)} %get-tuple-element.43), channel_id=1, source_target_pairs={{0,1},{1,0},{2,3},{3,2},{4,5},{5,4},{6,7},{7,6},{8,9},{9,8},{10,11... | collective-permute-start | bytes 1572872 | tf_op jit(solution)/shard_map/key_exchange/ppermute | solution.py:38
  15.1 6.8 %collective-permute-start.7 = (bf16[48,1024]{1,0:T(8,128)(2,1)S(1)}, bf16[48,1024]{1,0:T(8,128)(2,1)S(1)}, u32[]{:S(2)}, u32[]{:S(2)}) collective-permute-start(bf16[48,1024]{1,0:T(8,128)(2,1)S(1)} %collective-permute-done.3.refs_2_.refs_5_), channel_id=1, source_target_pairs={{0,2},{1,3},{2,0},{3,1},{4,6},{5,7},{6,4},{7,5},{8,10},{9,11},{10,... | collective-permute-start | bytes 294920 | tf_op jit(solution)/shard_map/query_forward/ppermute | solution.py:43
  15.6 9.6 %collective-permute-start.11 = (bf16[48,1024]{1,0:T(8,128)(2,1)S(1)}, bf16[48,1024]{1,0:T(8,128)(2,1)S(1)}, u32[]{:S(2)}, u32[]{:S(2)}) collective-permute-start(bf16[48,1024]{1,0:T(8,128)(2,1)S(1)} %get-tuple-element.45.refs_8_), channel_id=1, source_target_pairs={{0,4},{1,5},{2,6},{3,7},{4,0},{5,1},{6,2},{7,3},{8,12},{9,13},{10,... | collective-permute-start | bytes 294920 | tf_op jit(solution)/shard_map/cotangent_gather/ppermute | solution.py:43
  17.5 9.8 %collective-permute-start.12 = (bf16[48,1024]{1,0:T(8,128)(2,1)S(1)}, bf16[48,1024]{1,0:T(8,128)(2,1)S(1)}, u32[]{:S(2)}, u32[]{:S(2)}) collective-permute-start(bf16[48,1024]{1,0:T(8,128)(2,1)S(1)} %get-tuple-element.45.refs_8_), channel_id=1, source_target_pairs={{0,2},{1,3},{2,0},{3,1},{4,6},{5,7},{6,4},{7,5},{8,10},{9,11},{10,... | collective-permute-start | bytes 294920 | tf_op jit(solution)/shard_map/cotangent_gather/ppermute | solution.py:43
  17.6 9.7 %collective-permute-start.13 = (bf16[48,1024]{1,0:T(8,128)(2,1)S(1)}, bf16[48,1024]{1,0:T(8,128)(2,1)S(1)}, u32[]{:S(2)}, u32[]{:S(2)}) collective-permute-start(bf16[48,1024]{1,0:T(8,128)(2,1)S(1)} %get-tuple-element.45.refs_8_), channel_id=1, source_target_pairs={{0,6},{1,7},{2,4},{3,5},{4,2},{5,3},{6,0},{7,1},{8,14},{9,15},{10,... | collective-permute-start | bytes 294920 | tf_op jit(solution)/shard_map/cotangent_gather/ppermute | solution.py:43
  22.8 5.5 %collective-permute-start.10 = (f32[8,256]{1,0:T(8,128)S(1)}, f32[8,256]{1,0:T(8,128)S(1)}, u32[]{:S(2)}, u32[]{:S(2)}) collective-permute-start(f32[8,256]{1,0:T(8,128)S(1)} %scores.1.refs_0_), channel_id=1, source_target_pairs={{0,6},{1,7},{2,4},{3,5},{4,2},{5,3},{6,0},{7,1},{8,14},{9,15},{10,... | collective-permute-start | bytes 24584 | tf_op jit(solution)/shard_map/stats_exchange/ppermute | solution.py:43
  25.2 4.5 %collective-permute-start.8 = (f32[8,256]{1,0:T(8,128)S(1)}, f32[8,256]{1,0:T(8,128)S(1)}, u32[]{:S(2)}, u32[]{:S(2)}) collective-permute-start(f32[8,256]{1,0:T(8,128)S(1)} %scores.1.refs_0_), channel_id=1, source_target_pairs={{0,4},{1,5},{2,6},{3,7},{4,0},{5,1},{6,2},{7,3},{8,12},{9,13},{10,... | collective-permute-start | bytes 24584 | tf_op jit(solution)/shard_map/stats_exchange/ppermute | solution.py:43
  25.2 4.5 %collective-permute-start.9 = (f32[8,256]{1,0:T(8,128)S(1)}, f32[8,256]{1,0:T(8,128)S(1)}, u32[]{:S(2)}, u32[]{:S(2)}) collective-permute-start(f32[8,256]{1,0:T(8,128)S(1)} %scores.1.refs_0_), channel_id=1, source_target_pairs={{0,2},{1,3},{2,0},{3,1},{4,6},{5,7},{6,4},{7,5},{8,10},{9,11},{10,... | collective-permute-start | bytes 24584 | tf_op jit(solution)/shard_map/stats_exchange/ppermute | solution.py:43
  32.3 8.1 %collective-permute-start.14 = (bf16[256,2048]{1,0:T(8,128)(2,1)S(1)}, bf16[256,2048]{1,0:T(8,128)(2,1)S(1)}, u32[]{:S(2)}, u32[]{:S(2)}) collective-permute-start(bf16[256,2048]{1,0:T(8,128)(2,1)S(1)} %get-tuple-element.48), channel_id=1, source_target_pairs={{0,1},{1,0},{2,3},{3,2},{4,5},{5,4},{6,7},{7,6},{8,9},{9,8},{10,11... | collective-permute-start | bytes 3145736 | tf_op jit(solution)/shard_map/key_grad_end/ppermute | solution.py:38
  32.4 9.9 %collective-permute-start.16 = (bf16[48,1024]{1,0:T(8,128)(2,1)S(1)}, bf16[48,1024]{1,0:T(8,128)(2,1)S(1)}, u32[]{:S(2)}, u32[]{:S(2)}) collective-permute-start(bf16[48,1024]{1,0:T(8,128)(2,1)S(1)} %get-tuple-element.52), channel_id=1, source_target_pairs={{0,6},{1,7},{2,4},{3,5},{4,2},{5,3},{6,0},{7,1},{8,14},{9,15},{10,... | collective-permute-start | bytes 294920 | tf_op jit(solution)/shard_map/query_grad_sum/ppermute | solution.py:43
  34.0 10.6 %collective-permute-start.17 = (bf16[48,1024]{1,0:T(8,128)(2,1)S(1)}, bf16[48,1024]{1,0:T(8,128)(2,1)S(1)}, u32[]{:S(2)}, u32[]{:S(2)}) collective-permute-start(bf16[48,1024]{1,0:T(8,128)(2,1)S(1)} %get-tuple-element.53), channel_id=1, source_target_pairs={{0,4},{1,5},{2,6},{3,7},{4,0},{5,1},{6,2},{7,3},{8,12},{9,13},{10,... | collective-permute-start | bytes 294920 | tf_op jit(solution)/shard_map/query_grad_sum/ppermute | solution.py:43
  35.1 9.4 %collective-permute-start.18 = (bf16[48,1024]{1,0:T(8,128)(2,1)S(1)}, bf16[48,1024]{1,0:T(8,128)(2,1)S(1)}, u32[]{:S(2)}, u32[]{:S(2)}) collective-permute-start(bf16[48,1024]{1,0:T(8,128)(2,1)S(1)} %get-tuple-element.54), channel_id=1, source_target_pairs={{0,2},{1,3},{2,0},{3,1},{4,6},{5,7},{6,4},{7,5},{8,10},{9,11},{10,... | collective-permute-start | bytes 294920 | tf_op jit(solution)/shard_map/query_grad_sum/ppermute | solution.py:43
  36.8 3.6 %collective-permute-start.15 = (f32[8,128]{1,0:T(8,128)S(1)}, f32[8,128]{1,0:T(8,128)S(1)}, u32[]{:S(2)}, u32[]{:S(2)}) collective-permute-start(f32[8,128]{1,0:T(8,128)S(1)} %get-tuple-element.49.refs_0_), channel_id=1, source_target_pairs={{0,16},{8,24},{16,0},{24,8},{1,17},{9,25},{17,1},{25,9},{2,18},{10... | collective-permute-start | bytes 12296 | tf_op jit(solution)/shard_map/key_grad_end/ppermute | solution.py:356
  44.7 1.3 %collective-permute-start.19 = (bf16[24,1024]{1,0:T(8,128)(2,1)S(1)}, bf16[24,1024]{1,0:T(8,128)(2,1)S(1)}, u32[]{:S(2)}, u32[]{:S(2)}) collective-permute-start(bf16[24,1024]{1,0:T(8,128)(2,1)S(1)} %get-tuple-element.56), channel_id=1, source_target_pairs={{0,1},{1,0},{2,3},{3,2},{4,5},{5,4},{6,7},{7,6},{8,9},{9,8},{10,11... | collective-permute-start | bytes 147464 | tf_op jit(solution)/shard_map/query_grad_end/ppermute | solution.py:38

commit v3 on v2

--- a/solution.py
+++ b/solution.py
@@ -319,7 +319,8 @@
         g_recv = to_sibling(g_send)
 
     with jax.named_scope("query_gather"):
-        q_recv, _ = after(q_recv, g_keep)
+        v_recv = to_sibling(value_rows)
+        q_recv, _, v_recv = after(q_recv, g_keep, v_recv)
         q_block = kernel_call(
             join_queries_kernel, block, [VMEM, VMEM], VMEM, [], 10**5, 10**5, "join_queries"
         )(query_rows, q_recv)
@@ -350,7 +351,7 @@
             10**5,
             10**5,
             "join_cotangents",
-        )(g_keep, g_recv)
+        )(g_keep, after(g_recv, q_block)[0])
 
     def over_groups(count, apart):
         return lax.ppermute(count, "dp", [(i, i ^ apart) for i in range(data_groups)])
@@ -358,22 +359,22 @@
     with jax.named_scope("mask_count"):
         apart = 1
         while apart < data_groups // 2:
+            count = after(count, q_block)[0]
             count = count + after(over_groups(count, apart), bias_own)[0]
             apart *= 2
         rows_in_all = float(data_groups * dec_rows)
 
-    with jax.named_scope("query_forward"):
-        q_far = [q_far[0], *(after(one, bias_own, count, q_near)[0] for one in q_far[1:])]
+    with jax.named_scope("cotangent_gather"):
+        g_far, g_near = gather(g_block)
+
+    with jax.named_scope("forward"):
+        held = (bias_own, count, q_near, g_near, *g_far[1:])
+        q_far = [q_far[0], *(after(one, *held)[0] for one in q_far[1:])]
         q_blocks = [*q_far, q_near, *forwarded(q_far)]
-
-    with jax.named_scope("cotangent_gather"):
-        sent = after(g_block, *q_far, q_near)[0]
-        g_blocks = [g_block] + [across(sent, offset) for offset in offsets[1:]]
+        g_blocks = [*g_far, g_near, *forwarded(g_far)]
 
     with jax.named_scope("key_exchange"):
-        v_recv = to_sibling(value_rows)
-        k_send, v_recv, *_ = after(k_send, v_recv, *q_far, q_near)
-        k_recv = to_sibling(k_send)
+        k_recv = to_sibling(after(k_send, *q_far, q_near)[0])
 
     with jax.named_scope("scores"):
         width = (dec_rows // 128 + 1) * 128

time: 46.8 us -> 49.7 us (1.062)
  waiting for transfers between devices: 12 us -> 16.6 us
  starting transfers between devices: 23.2 us -> 21.5 us
    ppermute x12, waiting for transfers between devices: 6.65 us -> 12.2 us  [across(): lax.ppermute(block, 'seq', [(i, i ^ 2 * apart) for i in range(count)])]
    ppermute x12, starting transfers between devices: 19.4 us -> 16.9 us  [across(): lax.ppermute(block, 'seq', [(i, i ^ 2 * apart) for i in range(count)])]
    ppermute x6, waiting for transfers between devices: 3.23 us -> 2.27 us  [to_sibling(): return lax.ppermute(block, 'seq', [(i, i ^ 1) for i in range(count)])]
    unnamed x14 -> x12, local copies, waits for them, and re-layouts: 1.91 us -> 1.91 us
  transfers between devices with their start and end apart: 20 -> 20, of which waited for: 8 -> 11; matrix products, arithmetic and copies ran while one was open for 0% -> 0% of each run, Pallas kernels for 12% -> 11%
where the time goes in v3:
time: 49.7 us; the launch traced here: 49.5 us
  starting transfers between devices  21.5 us (43%)
  waiting for transfers between devices  16.6 us (33%)
  Pallas kernels  8.08 us (16%)
  local copies, waits for them, and re-layouts  1.91 us (4%)
  between operations  0.73 us (1%)
  other arithmetic  0.67 us (1%)
    ppermute x12, starting transfers between devices, across(): lax.ppermute(block, 'seq', [(i, i ^ 2 * apart) for i in range(count)])  16.9 us
    ppermute x12, waiting for transfers between devices, across(): lax.ppermute(block, 'seq', [(i, i ^ 2 * apart) for i in range(count)])  12.2 us
    ppermute x2, starting transfers between devices, over_groups(): lax.ppermute(count, 'dp', [(i, i ^ apart) for i in range(data_groups)])  3.33 us
    pallas_call x1, Pallas kernels, local(): kernel_call(functools.partial(grads_kernel, offsets), (block,) * chips +...  2.58 us
    ppermute x6, waiting for transfers between devices, to_sibling(): return lax.ppermute(block, 'seq', [(i, i ^ 1) for i in range(count)])  2.27 us
    ppermute x2, waiting for transfers between devices, over_groups(): lax.ppermute(count, 'dp', [(i, i ^ apart) for i in range(data_groups)])  2.09 us
    unnamed x12, local copies, waits for them, and re-layouts  1.91 us
    pallas_call x1, Pallas kernels, local(): kernel_call(functools.partial(key_end_kernel, rows_in_all), (whole, whole...  1.84 us
  transfers between devices with their start and end apart: 20, of which 11 were waited for; matrix products, arithmetic and copies ran while one was open for 0% of the time, Pallas kernels for 11%

profile of v3, /device:TPU:0, one launch (start us, length us, event | category | flops | bytes accessed | tf_op | source)
XLA Modules:
  0.0 49.5 jit_solution(2904380220893825081)
XLA Ops:
  0.6 0.5 %collective-permute-start.1 = (bf16[256,2048]{1,0:T(8,128)(2,1)}, bf16[256,2048]{1,0:T(8,128)(2,1)S(1)}, u32[]{:S(2)}, u32[]{:S(2)}) collective-permute-start(bf16[256,2048]{1,0:T(8,128)(2,1)} %bitcast.11), channel_id=1, source_target_pairs={{0,1},{1,0},{2,3},{3,2},{4,5},{5,4},{6,7},{7,6},{8,9},{9,8},{10,11... | collective-permute-start | bytes 3145736 | tf_op jit(solution)/shard_map/query_gather/ppermute | solution.py:38
  1.1 0.1 collective-permute-start
  1.2 1.8 %prepare.1 = (bf16[24,1152]{1,0:T(8,128)(2,1)}, bf16[24,1152]{1,0:T(8,128)(2,1)}) custom-call(bf16[24,2048]{1,0:T(8,128)(2,1)} %bitcast.19, bf16[24,2048]{1,0:T(8,128)(2,1)} %bitcast.20, s32[1,24]{1,0:T(1,128)} %mask_ref.1), custom_call_target="tpu_custom_call" | custom-call | flops 100000 | bytes 1000000 | tf_op jit(solution)/shard_map/sibling_exchange/prepare/pallas_call | solution.py:303
  3.0 0.5 %collective-permute-start.2 = (bf16[24,1152]{1,0:T(8,128)(2,1)}, bf16[24,1152]{1,0:T(8,128)(2,1)S(1)}, u32[]{:S(2)}, u32[]{:S(2)}) collective-permute-start(bf16[24,1152]{1,0:T(8,128)(2,1)} %get-tuple-element.37), channel_id=1, source_target_pairs={{0,1},{1,0},{2,3},{3,2},{4,5},{5,4},{6,7},{7,6},{8,9},{9,8},{10,11... | collective-permute-start | bytes 165896 | tf_op jit(solution)/shard_map/sibling_exchange/ppermute | solution.py:38
  3.5 0.3 collective-permute-done.other_ref
  3.8 0.0 collective-permute-done.1.refs_15_
  3.8 0.8 %collective-permute-done.2.other_ref = bf16[24,1152]{1,0:T(8,128)(2,1)S(1)} collective-permute-done((bf16[24,1152]{1,0:T(8,128)(2,1)}, bf16[24,1152]{1,0:T(8,128)(2,1)S(1)}, u32[]{:S(2)}, u32[]{:S(2)}) %collective-permute-start.2) | collective-permute-done | bytes 55328 | tf_op jit(solution)/shard_map/sibling_exchange/ppermute | solution.py:38
  4.6 0.2 join_cotangents.1
  4.8 4.0 %collective-permute-start.7 = (bf16[48,1024]{1,0:T(8,128)(2,1)S(1)}, bf16[48,1024]{1,0:T(8,128)(2,1)S(1)}, u32[]{:S(2)}, u32[]{:S(2)}) collective-permute-start(bf16[48,1024]{1,0:T(8,128)(2,1)S(1)} %get-tuple-element.45.refs_8_), channel_id=1, source_target_pairs={{0,4},{1,5},{2,6},{3,7},{4,0},{5,1},{6,2},{7,3},{8,12},{9,13},{10,... | collective-permute-start | bytes 294920 | tf_op jit(solution)/shard_map/cotangent_gather/ppermute | solution.py:43
  8.7 1.6 %collective-permute-start.6 = (bf16[48,1024]{1,0:T(8,128)(2,1)S(1)}, bf16[48,1024]{1,0:T(8,128)(2,1)S(1)}, u32[]{:S(2)}, u32[]{:S(2)}) collective-permute-start(bf16[48,1024]{1,0:T(8,128)(2,1)S(1)} %get-tuple-element.45.refs_8_), channel_id=1, source_target_pairs={{0,2},{1,3},{2,0},{3,1},{4,6},{5,7},{6,4},{7,5},{8,10},{9,11},{10,... | collective-permute-start | bytes 294920 | tf_op jit(solution)/shard_map/cotangent_gather/ppermute | solution.py:43
  10.3 0.4 collective-permute-start.5
  10.8 0.0 collective-permute-start.3
  10.8 1.8 %collective-permute-start.4 = (f32[8,128]{1,0:T(8,128)S(1)}, f32[8,128]{1,0:T(8,128)S(1)}, u32[]{:S(2)}, u32[]{:S(2)}) collective-permute-start(f32[8,128]{1,0:T(8,128)S(1)} %get-tuple-element.43), channel_id=1, source_target_pairs={{0,8},{8,0},{16,24},{24,16},{1,9},{9,1},{17,25},{25,17},{2,10},{10... | collective-permute-start | bytes 12296 | tf_op jit(solution)/shard_map/mask_count/ppermute | solution.py:357
  12.6 0.7 %copy-done.4 = s32[1,1,4]{2,1,0:T(1,128)S(1)} copy-done((s32[1,1,4]{2,1,0:T(1,128)S(1)}, s32[1,1,4]{2,1,0:T(1,128)}, u32[]{:S(2)}) %copy-start.4) | copy-done | bytes 40
  13.2 0.0 copy-done.5
  13.3 1.2 %copy-done.1 = bf16[1,256,2048]{2,1,0:T(8,128)(2,1)S(1)} copy-done((bf16[1,256,2048]{2,1,0:T(8,128)(2,1)S(1)}, bf16[1,256,2048]{2,1,0:T(8,128)(2,1)}, u32[]{:S(2)}) %copy-start.1) | copy-done | bytes 1048600
  14.5 0.7 %setup.1 = (bf16[256,1024]{1,0:T(8,128)(2,1)S(1)}, bf16[256,1024]{1,0:T(8,128)(2,1)S(1)}, f32[256,192]{1,0:T(8,128)S(1)}, f32[256,192]{1,0:T(8,128)S(1)}) custom-call(s32[1,4]{1,0:T(1,128)S(1)} %bitcast.17, s32[1,4]{1,0:T(1,128)S(1)} %bitcast.18, bf16[256,2048]{1,0:T(8,128)(2,1)S(1)} %bitcast.13), custom_call_target="tpu_custom_call" | custom-call | flops 1000000 | bytes 4194304 | tf_op jit(solution)/shard_map/setup/setup/pallas_call | solution.py:332
  15.2 0.0 copy-start
  15.2 0.0 collective-permute-done.4
  15.3 0.0 collective-permute-done.7.refs_9_
  15.3 2.1 %collective-permute-done.6.refs_10_ = bf16[48,1024]{1,0:T(8,128)(2,1)S(1)} collective-permute-done((bf16[48,1024]{1,0:T(8,128)(2,1)S(1)}, bf16[48,1024]{1,0:T(8,128)(2,1)S(1)}, u32[]{:S(2)}, u32[]{:S(2)}) %collective-permute-start.6) | collective-permute-done | bytes 98336 | tf_op jit(solution)/shard_map/cotangent_gather/ppermute | solution.py:43
  17.3 1.1 %collective-permute-done.5.refs_3_.refs_6_ = bf16[48,1024]{1,0:T(8,128)(2,1)S(1)} collective-permute-done((bf16[48,1024]{1,0:T(8,128)(2,1)S(1)}, bf16[48,1024]{1,0:T(8,128)(2,1)S(1)}, u32[]{:S(2)}, u32[]{:S(2)}) %collective-permute-start.5) | collective-permute-done | bytes 98336 | tf_op jit(solution)/shard_map/query_gather/ppermute | solution.py:43
  18.5 0.0 collective-permute-done.3.refs_2_.refs_5_
  18.5 0.0 collective-permute-start.8
  18.5 1.3 %collective-permute-start.9 = (bf16[48,1024]{1,0:T(8,128)(2,1)S(1)}, bf16[48,1024]{1,0:T(8,128)(2,1)S(1)}, u32[]{:S(2)}, u32[]{:S(2)}) collective-permute-start(bf16[48,1024]{1,0:T(8,128)(2,1)S(1)} %collective-permute-done.3.refs_2_.refs_5_), channel_id=1, source_target_pairs={{0,2},{1,3},{2,0},{3,1},{4,6},{5,7},{6,4},{7,5},{8,10},{9,11},{10,... | collective-permute-start | bytes 294920 | tf_op jit(solution)/shard_map/forward/ppermute | solution.py:43
  19.8 0.7 %collective-permute-start.13 = (bf16[48,1024]{1,0:T(8,128)(2,1)S(1)}, bf16[48,1024]{1,0:T(8,128)(2,1)S(1)}, u32[]{:S(2)}, u32[]{:S(2)}) collective-permute-start(bf16[48,1024]{1,0:T(8,128)(2,1)S(1)} %collective-permute-done.7.refs_9_), channel_id=1, source_target_pairs={{0,2},{1,3},{2,0},{3,1},{4,6},{5,7},{6,4},{7,5},{8,10},{9,11},{10,... | collective-permute-start | bytes 294920 | tf_op jit(solution)/shard_map/forward/ppermute | solution.py:43
  20.5 3.6 %collective-permute-done.9.refs_4_.refs_7_ = bf16[48,1024]{1,0:T(8,128)(2,1)S(1)} collective-permute-done((bf16[48,1024]{1,0:T(8,128)(2,1)S(1)}, bf16[48,1024]{1,0:T(8,128)(2,1)S(1)}, u32[]{:S(2)}, u32[]{:S(2)}) %collective-permute-start.9) | collective-permute-done | bytes 98336 | tf_op jit(solution)/shard_map/forward/ppermute | solution.py:43
  24.1 0.0 collective-permute-done.8.other_ref.refs_13_
  24.1 0.9 %scores.1.refs_0_ = f32[8,256]{1,0:T(8,128)S(1)} custom-call(f32[8,48]{1,0:T(8,128)S(1)} %get-tuple-element.39.delta_ref, f32[256,192]{1,0:T(8,128)S(1)} %get-tuple-element.35.bias_own, f32[256,192]{1,0:T(8,128)S(1)} %get-tuple-element.36.bias_other, bf16[256,1024]{1,0:T(8,128)(2,1)S(1)} %get-tuple-element.40.key_ref.refs_12_, ...), custom_call_target="tpu_custom_call" | custom-call | flops 201326592 | bytes 1441792 | tf_op jit(solution)/shard_map/scores/scores/pallas_call | solution.py:381
  25.0 2.4 %collective-permute-start.10 = (f32[8,256]{1,0:T(8,128)S(1)}, f32[8,256]{1,0:T(8,128)S(1)}, u32[]{:S(2)}, u32[]{:S(2)}) collective-permute-start(f32[8,256]{1,0:T(8,128)S(1)} %scores.1.refs_0_), channel_id=1, source_target_pairs={{0,4},{1,5},{2,6},{3,7},{4,0},{5,1},{6,2},{7,3},{8,12},{9,13},{10,... | collective-permute-start | bytes 24584 | tf_op jit(solution)/shard_map/stats_exchange/ppermute | solution.py:43
  27.4 0.7 %collective-permute-start.11 = (f32[8,256]{1,0:T(8,128)S(1)}, f32[8,256]{1,0:T(8,128)S(1)}, u32[]{:S(2)}, u32[]{:S(2)}) collective-permute-start(f32[8,256]{1,0:T(8,128)S(1)} %scores.1.refs_0_), channel_id=1, source_target_pairs={{0,2},{1,3},{2,0},{3,1},{4,6},{5,7},{6,4},{7,5},{8,10},{9,11},{10,... | collective-permute-start | bytes 24584 | tf_op jit(solution)/shard_map/stats_exchange/ppermute | solution.py:43
  28.1 1.3 %collective-permute-start.12 = (f32[8,256]{1,0:T(8,128)S(1)}, f32[8,256]{1,0:T(8,128)S(1)}, u32[]{:S(2)}, u32[]{:S(2)}) collective-permute-start(f32[8,256]{1,0:T(8,128)S(1)} %scores.1.refs_0_), channel_id=1, source_target_pairs={{0,6},{1,7},{2,4},{3,5},{4,2},{5,3},{6,0},{7,1},{8,14},{9,15},{10,... | collective-permute-start | bytes 24584 | tf_op jit(solution)/shard_map/stats_exchange/ppermute | solution.py:43
  29.4 0.2 collective-permute-done.10.refs_1_
  29.6 1.5 %collective-permute-done.11.refs_2_ = f32[8,256]{1,0:T(8,128)S(1)} collective-permute-done((f32[8,256]{1,0:T(8,128)S(1)}, f32[8,256]{1,0:T(8,128)S(1)}, u32[]{:S(2)}, u32[]{:S(2)}) %collective-permute-start.11) | collective-permute-done | bytes 8224 | tf_op jit(solution)/shard_map/stats_exchange/ppermute | solution.py:43
  31.0 2.5 %collective-permute-done.12.refs_3_ = f32[8,256]{1,0:T(8,128)S(1)} collective-permute-done((f32[8,256]{1,0:T(8,128)S(1)}, f32[8,256]{1,0:T(8,128)S(1)}, u32[]{:S(2)}, u32[]{:S(2)}) %collective-permute-start.12) | collective-permute-done | bytes 8224 | tf_op jit(solution)/shard_map/stats_exchange/ppermute | solution.py:43
  33.5 2.6 %grads.1 = (bf16[48,1024]{1,0:T(8,128)(2,1)S(1)}, bf16[48,1024]{1,0:T(8,128)(2,1)S(1)}, bf16[48,1024]{1,0:T(8,128)(2,1)S(1)}, bf16[48,1024]{1,0:T(8,128)(2,1)S(1...) custom-call(f32[256,192]{1,0:T(8,128)S(1)} %get-tuple-element.35.bias_own, ...), custom_call_target="tpu_custom_call" | custom-call | flops 1006632960 | bytes 4980736 | tf_op jit(solution)/shard_map/grads/grads/pallas_call | solution.py:397
  36.1 0.1 collective-permute-start.14
  36.2 1.4 %collective-permute-start.16 = (bf16[48,1024]{1,0:T(8,128)(2,1)S(1)}, bf16[48,1024]{1,0:T(8,128)(2,1)S(1)}, u32[]{:S(2)}, u32[]{:S(2)}) collective-permute-start(bf16[48,1024]{1,0:T(8,128)(2,1)S(1)} %get-tuple-element.54), channel_id=1, source_target_pairs={{0,6},{1,7},{2,4},{3,5},{4,2},{5,3},{6,0},{7,1},{8,14},{9,15},{10,... | collective-permute-start | bytes 294920 | tf_op jit(solution)/shard_map/query_grad_sum/ppermute | solution.py:43
  37.6 3.0 %collective-permute-start.18 = (bf16[48,1024]{1,0:T(8,128)(2,1)S(1)}, bf16[48,1024]{1,0:T(8,128)(2,1)S(1)}, u32[]{:S(2)}, u32[]{:S(2)}) collective-permute-start(bf16[48,1024]{1,0:T(8,128)(2,1)S(1)} %get-tuple-element.56), channel_id=1, source_target_pairs={{0,2},{1,3},{2,0},{3,1},{4,6},{5,7},{6,4},{7,5},{8,10},{9,11},{10,... | collective-permute-start | bytes 294920 | tf_op jit(solution)/shard_map/query_grad_sum/ppermute | solution.py:43
  40.7 1.5 %collective-permute-start.15 = (f32[8,128]{1,0:T(8,128)S(1)}, f32[8,128]{1,0:T(8,128)S(1)}, u32[]{:S(2)}, u32[]{:S(2)}) collective-permute-start(f32[8,128]{1,0:T(8,128)S(1)} %get-tuple-element.51.refs_0_), channel_id=1, source_target_pairs={{0,16},{8,24},{16,0},{24,8},{1,17},{9,25},{17,1},{25,9},{2,18},{10... | collective-permute-start | bytes 12296 | tf_op jit(solution)/shard_map/key_grad_end/ppermute | solution.py:357
  42.2 2.1 %collective-permute-done.15.refs_1_ = f32[8,128]{1,0:T(8,128)S(1)} collective-permute-done((f32[8,128]{1,0:T(8,128)S(1)}, f32[8,128]{1,0:T(8,128)S(1)}, u32[]{:S(2)}, u32[]{:S(2)}) %collective-permute-start.15) | collective-permute-done | bytes 4128 | tf_op jit(solution)/shard_map/key_grad_end/ppermute | solution.py:357
  44.3 1.8 %key_end.1 = (bf16[256,2048]{1,0:T(8,128)(2,1)}, bf16[256,2048]{1,0:T(8,128)(2,1)}, f32[8,128]{1,0:T(8,128)S(1)}) custom-call(bf16[256,2048]{1,0:T(8,128)(2,1)S(1)} %get-tuple-element.49.keep_ref, bf16[256,2048]{1,0:T(8,128)(2,1)S(1)} %collective-permute-done.14.other_ref, f32[8,128]{1,0:T(8,128)S(1)} %get-tuple-element.51.refs_0_, ...), custom_call_target="tpu_custom_call" | custom-call | flops 1000000 | bytes 4194304 | tf_op jit(solution)/shard_map/key_grad_end/key_end/pallas_call | solution.py:417
  46.1 1.3 %collective-permute-done.17.refs_2_ = bf16[48,1024]{1,0:T(8,128)(2,1)S(1)} collective-permute-done((bf16[48,1024]{1,0:T(8,128)(2,1)S(1)}, bf16[48,1024]{1,0:T(8,128)(2,1)S(1)}, u32[]{:S(2)}, u32[]{:S(2)}) %collective-permute-start.17) | collective-permute-done | bytes 98336 | tf_op jit(solution)/shard_map/query_grad_sum/ppermute | solution.py:43
  47.4 0.0 collective-permute-done.18.refs_3_
  47.4 0.1 query_end.1
  47.5 0.1 collective-permute-start.19
  47.6 1.2 %collective-permute-done.19 = bf16[24,1024]{1,0:T(8,128)(2,1)S(1)} collective-permute-done((bf16[24,1024]{1,0:T(8,128)(2,1)S(1)}, bf16[24,1024]{1,0:T(8,128)(2,1)S(1)}, u32[]{:S(2)}, u32[]{:S(2)}) %collective-permute-start.19) | collective-permute-done | bytes 49184 | tf_op jit(solution)/shard_map/query_grad_end/ppermute | solution.py:38
  48.8 0.7 %maximum_select_fusion = bf16[1,24,2048]{2,1,0:T(8,128)(2,1)} fusion(bf16[1,24,1024]{2,1,0:T(8,128)(2,1)S(1)} %bitcast.21, bf16[1,24,1024]{2,1,0:T(8,128)(2,1)S(1)} %bitcast.16, pred[]{:T(512)S(6)} %eq.3), kind=kLoop, calls=%fused_computation | loop fusion | flops 442368 | bytes 196609 | tf_op jit(solution)/shard_map/query_grad_end/jit(_where)/select_n | solution.py:261
  (14 shorter events, 0.0 us)
Async XLA Ops:
  0.6 3.2 %collective-permute-start.1 = (bf16[256,2048]{1,0:T(8,128)(2,1)}, bf16[256,2048]{1,0:T(8,128)(2,1)S(1)}, u32[]{:S(2)}, u32[]{:S(2)}) collective-permute-start(bf16[256,2048]{1,0:T(8,128)(2,1)} %bitcast.11), channel_id=1, source_target_pairs={{0,1},{1,0},{2,3},{3,2},{4,5},{5,4},{6,7},{7,6},{8,9},{9,8},{10,11... | collective-permute-start | bytes 3145736 | tf_op jit(solution)/shard_map/query_gather/ppermute | solution.py:38
  1.1 2.6 %collective-permute-start = (bf16[24,2048]{1,0:T(8,128)(2,1)}, bf16[24,2048]{1,0:T(8,128)(2,1)S(1)}, u32[]{:S(2)}, u32[]{:S(2)}) collective-permute-start(bf16[24,2048]{1,0:T(8,128)(2,1)} %bitcast.14), channel_id=1, source_target_pairs={{0,1},{1,0},{2,3},{3,2},{4,5},{5,4},{6,7},{7,6},{8,9},{9,8},{10,11... | collective-permute-start | bytes 294920 | tf_op jit(solution)/shard_map/sibling_exchange/ppermute | solution.py:38
  1.2 2.6 %copy-start.2 = (bf16[1,24,2048]{2,1,0:T(8,128)(2,1)S(1)}, bf16[1,24,2048]{2,1,0:T(8,128)(2,1)}, u32[]{:S(2)}) copy-start(bf16[1,24,2048]{2,1,0:T(8,128)(2,1)} %param.8) | copy-start | bytes 294916
  3.0 1.6 %collective-permute-start.2 = (bf16[24,1152]{1,0:T(8,128)(2,1)}, bf16[24,1152]{1,0:T(8,128)(2,1)S(1)}, u32[]{:S(2)}, u32[]{:S(2)}) collective-permute-start(bf16[24,1152]{1,0:T(8,128)(2,1)} %get-tuple-element.37), channel_id=1, source_target_pairs={{0,1},{1,0},{2,3},{3,2},{4,5},{5,4},{6,7},{7,6},{8,9},{9,8},{10,11... | collective-permute-start | bytes 165896 | tf_op jit(solution)/shard_map/sibling_exchange/ppermute | solution.py:38
  3.8 0.8 %copy-start.3 = (bf16[24,1152]{1,0:T(8,128)(2,1)S(1)}, bf16[24,1152]{1,0:T(8,128)(2,1)}, u32[]{:S(2)}) copy-start(bf16[24,1152]{1,0:T(8,128)(2,1)} %get-tuple-element.32.own_ref) | copy-start | bytes 165892
  4.8 10.5 %collective-permute-start.7 = (bf16[48,1024]{1,0:T(8,128)(2,1)S(1)}, bf16[48,1024]{1,0:T(8,128)(2,1)S(1)}, u32[]{:S(2)}, u32[]{:S(2)}) collective-permute-start(bf16[48,1024]{1,0:T(8,128)(2,1)S(1)} %get-tuple-element.45.refs_8_), channel_id=1, source_target_pairs={{0,4},{1,5},{2,6},{3,7},{4,0},{5,1},{6,2},{7,3},{8,12},{9,13},{10,... | collective-permute-start | bytes 294920 | tf_op jit(solution)/shard_map/cotangent_gather/ppermute | solution.py:43
  8.7 8.6 %collective-permute-start.6 = (bf16[48,1024]{1,0:T(8,128)(2,1)S(1)}, bf16[48,1024]{1,0:T(8,128)(2,1)S(1)}, u32[]{:S(2)}, u32[]{:S(2)}) collective-permute-start(bf16[48,1024]{1,0:T(8,128)(2,1)S(1)} %get-tuple-element.45.refs_8_), channel_id=1, source_target_pairs={{0,2},{1,3},{2,0},{3,1},{4,6},{5,7},{6,4},{7,5},{8,10},{9,11},{10,... | collective-permute-start | bytes 294920 | tf_op jit(solution)/shard_map/cotangent_gather/ppermute | solution.py:43
  10.3 8.2 %collective-permute-start.5 = (bf16[48,1024]{1,0:T(8,128)(2,1)S(1)}, bf16[48,1024]{1,0:T(8,128)(2,1)S(1)}, u32[]{:S(2)}, u32[]{:S(2)}) collective-permute-start(bf16[48,1024]{1,0:T(8,128)(2,1)S(1)} %join_queries.1.refs_1_.refs_4_), channel_id=1, source_target_pairs={{0,2},{1,3},{2,0},{3,1},{4,6},{5,7},{6,4},{7,5},{8,10},{9,11},{10,... | collective-permute-start | bytes 294920 | tf_op jit(solution)/shard_map/query_gather/ppermute | solution.py:43
  10.8 7.7 %collective-permute-start.3 = (bf16[48,1024]{1,0:T(8,128)(2,1)S(1)}, bf16[48,1024]{1,0:T(8,128)(2,1)S(1)}, u32[]{:S(2)}, u32[]{:S(2)}) collective-permute-start(bf16[48,1024]{1,0:T(8,128)(2,1)S(1)} %join_queries.1.refs_1_.refs_4_), channel_id=1, source_target_pairs={{0,4},{1,5},{2,6},{3,7},{4,0},{5,1},{6,2},{7,3},{8,12},{9,13},{10,... | collective-permute-start | bytes 294920 | tf_op jit(solution)/shard_map/query_gather/ppermute | solution.py:43
  10.8 4.5 %collective-permute-start.4 = (f32[8,128]{1,0:T(8,128)S(1)}, f32[8,128]{1,0:T(8,128)S(1)}, u32[]{:S(2)}, u32[]{:S(2)}) collective-permute-start(f32[8,128]{1,0:T(8,128)S(1)} %get-tuple-element.43), channel_id=1, source_target_pairs={{0,8},{8,0},{16,24},{24,16},{1,9},{9,1},{17,25},{25,17},{2,10},{10... | collective-permute-start | bytes 12296 | tf_op jit(solution)/shard_map/mask_count/ppermute | solution.py:357
  12.6 0.7 %copy-start.4 = (s32[1,1,4]{2,1,0:T(1,128)S(1)}, s32[1,1,4]{2,1,0:T(1,128)}, u32[]{:S(2)}) copy-start(s32[1,1,4]{2,1,0:T(1,128)} %param.14) | copy-start | bytes 52
  12.6 0.7 %copy-start.5 = (s32[1,1,4]{2,1,0:T(1,128)S(1)}, s32[1,1,4]{2,1,0:T(1,128)}, u32[]{:S(2)}) copy-start(s32[1,1,4]{2,1,0:T(1,128)} %param.15) | copy-start | bytes 52
  13.3 1.2 %copy-start.1 = (bf16[1,256,2048]{2,1,0:T(8,128)(2,1)S(1)}, bf16[1,256,2048]{2,1,0:T(8,128)(2,1)}, u32[]{:S(2)}) copy-start(bf16[1,256,2048]{2,1,0:T(8,128)(2,1)} %param.9) | copy-start | bytes 3145732
  15.2 18.3 %copy-start = (bf16[1,256,2048]{2,1,0:T(8,128)(2,1)S(1)}, bf16[1,256,2048]{2,1,0:T(8,128)(2,1)}, u32[]{:S(2)}) copy-start(bf16[1,256,2048]{2,1,0:T(8,128)(2,1)} %param.10) | copy-start | bytes 3145732
  18.5 5.6 %collective-permute-start.8 = (bf16[256,1024]{1,0:T(8,128)(2,1)S(1)}, bf16[256,1024]{1,0:T(8,128)(2,1)S(1)}, u32[]{:S(2)}, u32[]{:S(2)}) collective-permute-start(bf16[256,1024]{1,0:T(8,128)(2,1)S(1)} %get-tuple-element.47), channel_id=1, source_target_pairs={{0,1},{1,0},{2,3},{3,2},{4,5},{5,4},{6,7},{7,6},{8,9},{9,8},{10,11... | collective-permute-start | bytes 1572872 | tf_op jit(solution)/shard_map/key_exchange/ppermute | solution.py:38
  18.5 5.6 %collective-permute-start.9 = (bf16[48,1024]{1,0:T(8,128)(2,1)S(1)}, bf16[48,1024]{1,0:T(8,128)(2,1)S(1)}, u32[]{:S(2)}, u32[]{:S(2)}) collective-permute-start(bf16[48,1024]{1,0:T(8,128)(2,1)S(1)} %collective-permute-done.3.refs_2_.refs_5_), channel_id=1, source_target_pairs={{0,2},{1,3},{2,0},{3,1},{4,6},{5,7},{6,4},{7,5},{8,10},{9,11},{10,... | collective-permute-start | bytes 294920 | tf_op jit(solution)/shard_map/forward/ppermute | solution.py:43
  19.8 9.6 %collective-permute-start.13 = (bf16[48,1024]{1,0:T(8,128)(2,1)S(1)}, bf16[48,1024]{1,0:T(8,128)(2,1)S(1)}, u32[]{:S(2)}, u32[]{:S(2)}) collective-permute-start(bf16[48,1024]{1,0:T(8,128)(2,1)S(1)} %collective-permute-done.7.refs_9_), channel_id=1, source_target_pairs={{0,2},{1,3},{2,0},{3,1},{4,6},{5,7},{6,4},{7,5},{8,10},{9,11},{10,... | collective-permute-start | bytes 294920 | tf_op jit(solution)/shard_map/forward/ppermute | solution.py:43
  25.0 4.6 %collective-permute-start.10 = (f32[8,256]{1,0:T(8,128)S(1)}, f32[8,256]{1,0:T(8,128)S(1)}, u32[]{:S(2)}, u32[]{:S(2)}) collective-permute-start(f32[8,256]{1,0:T(8,128)S(1)} %scores.1.refs_0_), channel_id=1, source_target_pairs={{0,4},{1,5},{2,6},{3,7},{4,0},{5,1},{6,2},{7,3},{8,12},{9,13},{10,... | collective-permute-start | bytes 24584 | tf_op jit(solution)/shard_map/stats_exchange/ppermute | solution.py:43
  27.4 3.7 %collective-permute-start.11 = (f32[8,256]{1,0:T(8,128)S(1)}, f32[8,256]{1,0:T(8,128)S(1)}, u32[]{:S(2)}, u32[]{:S(2)}) collective-permute-start(f32[8,256]{1,0:T(8,128)S(1)} %scores.1.refs_0_), channel_id=1, source_target_pairs={{0,2},{1,3},{2,0},{3,1},{4,6},{5,7},{6,4},{7,5},{8,10},{9,11},{10,... | collective-permute-start | bytes 24584 | tf_op jit(solution)/shard_map/stats_exchange/ppermute | solution.py:43
  28.1 5.4 %collective-permute-start.12 = (f32[8,256]{1,0:T(8,128)S(1)}, f32[8,256]{1,0:T(8,128)S(1)}, u32[]{:S(2)}, u32[]{:S(2)}) collective-permute-start(f32[8,256]{1,0:T(8,128)S(1)} %scores.1.refs_0_), channel_id=1, source_target_pairs={{0,6},{1,7},{2,4},{3,5},{4,2},{5,3},{6,0},{7,1},{8,14},{9,15},{10,... | collective-permute-start | bytes 24584 | tf_op jit(solution)/shard_map/stats_exchange/ppermute | solution.py:43
  36.1 8.1 %collective-permute-start.14 = (bf16[256,2048]{1,0:T(8,128)(2,1)S(1)}, bf16[256,2048]{1,0:T(8,128)(2,1)S(1)}, u32[]{:S(2)}, u32[]{:S(2)}) collective-permute-start(bf16[256,2048]{1,0:T(8,128)(2,1)S(1)} %get-tuple-element.50), channel_id=1, source_target_pairs={{0,1},{1,0},{2,3},{3,2},{4,5},{5,4},{6,7},{7,6},{8,9},{9,8},{10,11... | collective-permute-start | bytes 3145736 | tf_op jit(solution)/shard_map/key_grad_end/ppermute | solution.py:38
  36.2 9.9 %collective-permute-start.16 = (bf16[48,1024]{1,0:T(8,128)(2,1)S(1)}, bf16[48,1024]{1,0:T(8,128)(2,1)S(1)}, u32[]{:S(2)}, u32[]{:S(2)}) collective-permute-start(bf16[48,1024]{1,0:T(8,128)(2,1)S(1)} %get-tuple-element.54), channel_id=1, source_target_pairs={{0,6},{1,7},{2,4},{3,5},{4,2},{5,3},{6,0},{7,1},{8,14},{9,15},{10,... | collective-permute-start | bytes 294920 | tf_op jit(solution)/shard_map/query_grad_sum/ppermute | solution.py:43
  37.6 9.8 %collective-permute-start.17 = (bf16[48,1024]{1,0:T(8,128)(2,1)S(1)}, bf16[48,1024]{1,0:T(8,128)(2,1)S(1)}, u32[]{:S(2)}, u32[]{:S(2)}) collective-permute-start(bf16[48,1024]{1,0:T(8,128)(2,1)S(1)} %get-tuple-element.55), channel_id=1, source_target_pairs={{0,4},{1,5},{2,6},{3,7},{4,0},{5,1},{6,2},{7,3},{8,12},{9,13},{10,... | collective-permute-start | bytes 294920 | tf_op jit(solution)/shard_map/query_grad_sum/ppermute | solution.py:43
  37.6 9.8 %collective-permute-start.18 = (bf16[48,1024]{1,0:T(8,128)(2,1)S(1)}, bf16[48,1024]{1,0:T(8,128)(2,1)S(1)}, u32[]{:S(2)}, u32[]{:S(2)}) collective-permute-start(bf16[48,1024]{1,0:T(8,128)(2,1)S(1)} %get-tuple-element.56), channel_id=1, source_target_pairs={{0,2},{1,3},{2,0},{3,1},{4,6},{5,7},{6,4},{7,5},{8,10},{9,11},{10,... | collective-permute-start | bytes 294920 | tf_op jit(solution)/shard_map/query_grad_sum/ppermute | solution.py:43
  40.7 3.6 %collective-permute-start.15 = (f32[8,128]{1,0:T(8,128)S(1)}, f32[8,128]{1,0:T(8,128)S(1)}, u32[]{:S(2)}, u32[]{:S(2)}) collective-permute-start(f32[8,128]{1,0:T(8,128)S(1)} %get-tuple-element.51.refs_0_), channel_id=1, source_target_pairs={{0,16},{8,24},{16,0},{24,8},{1,17},{9,25},{17,1},{25,9},{2,18},{10... | collective-permute-start | bytes 12296 | tf_op jit(solution)/shard_map/key_grad_end/ppermute | solution.py:357
  47.5 1.3 %collective-permute-start.19 = (bf16[24,1024]{1,0:T(8,128)(2,1)S(1)}, bf16[24,1024]{1,0:T(8,128)(2,1)S(1)}, u32[]{:S(2)}, u32[]{:S(2)}) collective-permute-start(bf16[24,1024]{1,0:T(8,128)(2,1)S(1)} %get-tuple-element.58), channel_id=1, source_target_pairs={{0,1},{1,0},{2,3},{3,2},{4,5},{5,4},{6,7},{7,6},{8,9},{9,8},{10,11... | collective-permute-start | bytes 147464 | tf_op jit(solution)/shard_map/query_grad_end/ppermute | solution.py:38

commit v4 on v2

--- a/solution.py
+++ b/solution.py
@@ -363,12 +363,11 @@
         rows_in_all = float(data_groups * dec_rows)
 
     with jax.named_scope("query_forward"):
-        q_far = [q_far[0], *(after(one, bias_own, count, q_near)[0] for one in q_far[1:])]
+        q_far = [q_far[0], *(after(one, bias_own, count)[0] for one in q_far[1:])]
         q_blocks = [*q_far, q_near, *forwarded(q_far)]
 
     with jax.named_scope("cotangent_gather"):
-        sent = after(g_block, *q_far, q_near)[0]
-        g_blocks = [g_block] + [across(sent, offset) for offset in offsets[1:]]
+        g_far, g_near = gather(after(g_block, *q_far, q_near)[0])
 
     with jax.named_scope("key_exchange"):
         v_recv = to_sibling(value_rows)
@@ -390,6 +389,11 @@
 
     with jax.named_scope("stats_exchange"):
         all_stats = [stats] + [across(stats, offset) for offset in offsets[1:]]
+        near_stats = all_stats[offsets.index(1)]
+
+    with jax.named_scope("cotangent_forward"):
+        g_far = [g_far[0], *(after(one, near_stats)[0] for one in g_far[1:])]
+        g_blocks = [*g_far, g_near, *forwarded(g_far)]
 
     with jax.named_scope("grads"):
         both = shaped(enc_local, 2 * HALF)

time: 46.8 us -> 50 us (1.068)
  waiting for transfers between devices: 12 us -> 16.8 us
  starting transfers between devices: 23.2 us -> 21.6 us
    ppermute x12, waiting for transfers between devices: 6.65 us -> 11.4 us  [across(): lax.ppermute(block, 'seq', [(i, i ^ 2 * apart) for i in range(count)])]
    ppermute x12, starting transfers between devices: 19.4 us -> 17.7 us  [across(): lax.ppermute(block, 'seq', [(i, i ^ 2 * apart) for i in range(count)])]
  transfers between devices with their start and end apart: 20 -> 20, of which waited for: 8 -> 9; matrix products, arithmetic and copies ran while one was open for 0% -> 0% of each run, Pallas kernels for 12% -> 11%
where the time goes in v4:
time: 50 us; the launch traced here: 49.8 us
  starting transfers between devices  21.6 us (43%)
  waiting for transfers between devices  16.8 us (34%)
  Pallas kernels  8.08 us (16%)
  local copies, waits for them, and re-layouts  1.91 us (4%)
  between operations  0.77 us (2%)
  other arithmetic  0.67 us (1%)
    ppermute x12, starting transfers between devices, across(): lax.ppermute(block, 'seq', [(i, i ^ 2 * apart) for i in range(count)])  17.7 us
    ppermute x12, waiting for transfers between devices, across(): lax.ppermute(block, 'seq', [(i, i ^ 2 * apart) for i in range(count)])  11.4 us
    ppermute x6, waiting for transfers between devices, to_sibling(): return lax.ppermute(block, 'seq', [(i, i ^ 1) for i in range(count)])  3.23 us
    ppermute x2, starting transfers between devices, over_groups(): lax.ppermute(count, 'dp', [(i, i ^ apart) for i in range(data_groups)])  3.01 us
    pallas_call x1, Pallas kernels, local(): kernel_call(functools.partial(grads_kernel, offsets), (block,) * chips +...  2.58 us
    ppermute x2, waiting for transfers between devices, over_groups(): lax.ppermute(count, 'dp', [(i, i ^ apart) for i in range(data_groups)])  2.09 us
    unnamed x14, local copies, waits for them, and re-layouts  1.91 us
    pallas_call x1, Pallas kernels, local(): kernel_call(functools.partial(key_end_kernel, rows_in_all), (whole, whole...  1.84 us
  transfers between devices with their start and end apart: 20, of which 9 were waited for; matrix products, arithmetic and copies ran while one was open for 0% of the time, Pallas kernels for 11%

profile of v4, /device:TPU:0, one launch (start us, length us, event | category | flops | bytes accessed | tf_op | source)
XLA Modules:
  0.0 49.8 jit_solution(868092812835172327)
XLA Ops:
  0.6 0.5 %collective-permute-start.2 = (bf16[256,2048]{1,0:T(8,128)(2,1)}, bf16[256,2048]{1,0:T(8,128)(2,1)S(1)}, u32[]{:S(2)}, u32[]{:S(2)}) collective-permute-start(bf16[256,2048]{1,0:T(8,128)(2,1)} %bitcast.11), channel_id=1, source_target_pairs={{0,1},{1,0},{2,3},{3,2},{4,5},{5,4},{6,7},{7,6},{8,9},{9,8},{10,11... | collective-permute-start | bytes 3145736 | tf_op jit(solution)/shard_map/key_exchange/ppermute | solution.py:38
  1.1 0.1 collective-permute-start
  1.2 1.8 %prepare.1 = (bf16[24,1152]{1,0:T(8,128)(2,1)}, bf16[24,1152]{1,0:T(8,128)(2,1)}) custom-call(bf16[24,2048]{1,0:T(8,128)(2,1)} %bitcast.19, bf16[24,2048]{1,0:T(8,128)(2,1)} %bitcast.20, s32[1,24]{1,0:T(1,128)} %mask_ref.1), custom_call_target="tpu_custom_call" | custom-call | flops 100000 | bytes 1000000 | tf_op jit(solution)/shard_map/sibling_exchange/prepare/pallas_call | solution.py:303
  3.0 0.8 %collective-permute-done.other_ref = bf16[24,2048]{1,0:T(8,128)(2,1)S(1)} collective-permute-done((bf16[24,2048]{1,0:T(8,128)(2,1)}, bf16[24,2048]{1,0:T(8,128)(2,1)S(1)}, u32[]{:S(2)}, u32[]{:S(2)}) %collective-permute-start) | collective-permute-done | bytes 98336 | tf_op jit(solution)/shard_map/sibling_exchange/ppermute | solution.py:38
  3.8 4.0 %collective-permute-start.3 = (bf16[48,1024]{1,0:T(8,128)(2,1)S(1)}, bf16[48,1024]{1,0:T(8,128)(2,1)S(1)}, u32[]{:S(2)}, u32[]{:S(2)}) collective-permute-start(bf16[48,1024]{1,0:T(8,128)(2,1)S(1)} %join_queries.1.refs_1_.refs_4_), channel_id=1, source_target_pairs={{0,4},{1,5},{2,6},{3,7},{4,0},{5,1},{6,2},{7,3},{8,12},{9,13},{10,... | collective-permute-start | bytes 294920 | tf_op jit(solution)/shard_map/query_gather/ppermute | solution.py:43
  7.8 1.6 %collective-permute-start.5 = (bf16[48,1024]{1,0:T(8,128)(2,1)S(1)}, bf16[48,1024]{1,0:T(8,128)(2,1)S(1)}, u32[]{:S(2)}, u32[]{:S(2)}) collective-permute-start(bf16[48,1024]{1,0:T(8,128)(2,1)S(1)} %join_queries.1.refs_1_.refs_4_), channel_id=1, source_target_pairs={{0,2},{1,3},{2,0},{3,1},{4,6},{5,7},{6,4},{7,5},{8,10},{9,11},{10,... | collective-permute-start | bytes 294920 | tf_op jit(solution)/shard_map/query_gather/ppermute | solution.py:43
  9.4 0.0 collective-permute-start.1
  9.4 1.2 %collective-permute-done.1.other_ref = bf16[24,1152]{1,0:T(8,128)(2,1)S(1)} collective-permute-done((bf16[24,1152]{1,0:T(8,128)(2,1)S(1)}, bf16[24,1152]{1,0:T(8,128)(2,1)S(1)}, u32[]{:S(2)}, u32[]{:S(2)}) %collective-permute-start.1) | collective-permute-done | bytes 55328 | tf_op jit(solution)/shard_map/sibling_exchange/ppermute | solution.py:38
  10.7 0.2 join_cotangents.1
  10.8 1.5 %collective-permute-start.4 = (f32[8,128]{1,0:T(8,128)S(1)}, f32[8,128]{1,0:T(8,128)S(1)}, u32[]{:S(2)}, u32[]{:S(2)}) collective-permute-start(f32[8,128]{1,0:T(8,128)S(1)} %get-tuple-element.41), channel_id=1, source_target_pairs={{0,8},{8,0},{16,24},{24,16},{1,9},{9,1},{17,25},{25,17},{2,10},{10... | collective-permute-start | bytes 12296 | tf_op jit(solution)/shard_map/mask_count/ppermute | solution.py:356
  12.3 0.7 %copy-done.4 = s32[1,1,4]{2,1,0:T(1,128)S(1)} copy-done((s32[1,1,4]{2,1,0:T(1,128)S(1)}, s32[1,1,4]{2,1,0:T(1,128)}, u32[]{:S(2)}) %copy-start.4) | copy-done | bytes 40
  13.0 0.0 copy-done.5
  13.0 1.2 %copy-done.1 = bf16[1,256,2048]{2,1,0:T(8,128)(2,1)S(1)} copy-done((bf16[1,256,2048]{2,1,0:T(8,128)(2,1)S(1)}, bf16[1,256,2048]{2,1,0:T(8,128)(2,1)}, u32[]{:S(2)}) %copy-start.1) | copy-done | bytes 1048600
  14.2 0.7 %setup.1 = (bf16[256,1024]{1,0:T(8,128)(2,1)S(1)}, bf16[256,1024]{1,0:T(8,128)(2,1)S(1)}, f32[256,192]{1,0:T(8,128)S(1)}, f32[256,192]{1,0:T(8,128)S(1)}) custom-call(s32[1,4]{1,0:T(1,128)S(1)} %bitcast.17, s32[1,4]{1,0:T(1,128)S(1)} %bitcast.18, bf16[256,2048]{1,0:T(8,128)(2,1)S(1)} %bitcast.13), custom_call_target="tpu_custom_call" | custom-call | flops 1000000 | bytes 4194304 | tf_op jit(solution)/shard_map/setup/setup/pallas_call | solution.py:331
  15.0 0.0 copy-start
  15.0 0.0 collective-permute-done.4
  15.0 0.0 collective-permute-done.5.refs_3_.refs_6_
  15.0 0.0 collective-permute-done.2.refs_15_
  15.0 0.1 collective-permute-start.6
  15.1 0.5 %collective-permute-start.7 = (bf16[48,1024]{1,0:T(8,128)(2,1)S(1)}, bf16[48,1024]{1,0:T(8,128)(2,1)S(1)}, u32[]{:S(2)}, u32[]{:S(2)}) collective-permute-start(bf16[48,1024]{1,0:T(8,128)(2,1)S(1)} %collective-permute-done.3.refs_2_.refs_5_), channel_id=1, source_target_pairs={{0,2},{1,3},{2,0},{3,1},{4,6},{5,7},{6,4},{7,5},{8,10},{9,11},{10,... | collective-permute-start | bytes 294920 | tf_op jit(solution)/shard_map/query_forward/ppermute | solution.py:43
  15.6 1.6 %collective-permute-start.11 = (bf16[48,1024]{1,0:T(8,128)(2,1)S(1)}, bf16[48,1024]{1,0:T(8,128)(2,1)S(1)}, u32[]{:S(2)}, u32[]{:S(2)}) collective-permute-start(bf16[48,1024]{1,0:T(8,128)(2,1)S(1)} %get-tuple-element.46.refs_8_), channel_id=1, source_target_pairs={{0,4},{1,5},{2,6},{3,7},{4,0},{5,1},{6,2},{7,3},{8,12},{9,13},{10,... | collective-permute-start | bytes 294920 | tf_op jit(solution)/shard_map/cotangent_gather/ppermute | solution.py:43
  17.2 4.2 %collective-permute-done.7.refs_4_.refs_7_ = bf16[48,1024]{1,0:T(8,128)(2,1)S(1)} collective-permute-done((bf16[48,1024]{1,0:T(8,128)(2,1)S(1)}, bf16[48,1024]{1,0:T(8,128)(2,1)S(1)}, u32[]{:S(2)}, u32[]{:S(2)}) %collective-permute-start.7) | collective-permute-done | bytes 98336 | tf_op jit(solution)/shard_map/query_forward/ppermute | solution.py:43
  21.4 0.0 collective-permute-done.6.other_ref.refs_13_
  21.4 0.9 %scores.1.refs_0_ = f32[8,256]{1,0:T(8,128)S(1)} custom-call(f32[8,48]{1,0:T(8,128)S(1)} %get-tuple-element.38.delta_ref, f32[256,192]{1,0:T(8,128)S(1)} %get-tuple-element.35.bias_own, f32[256,192]{1,0:T(8,128)S(1)} %get-tuple-element.36.bias_other, bf16[256,1024]{1,0:T(8,128)(2,1)S(1)} %get-tuple-element.39.key_ref.refs_12_, ...), custom_call_target="tpu_custom_call" | custom-call | flops 201326592 | bytes 1441792 | tf_op jit(solution)/shard_map/scores/scores/pallas_call | solution.py:379
  22.3 0.1 collective-permute-start.9
  22.4 2.0 %collective-permute-start.12 = (bf16[48,1024]{1,0:T(8,128)(2,1)S(1)}, bf16[48,1024]{1,0:T(8,128)(2,1)S(1)}, u32[]{:S(2)}, u32[]{:S(2)}) collective-permute-start(bf16[48,1024]{1,0:T(8,128)(2,1)S(1)} %get-tuple-element.46.refs_8_), channel_id=1, source_target_pairs={{0,2},{1,3},{2,0},{3,1},{4,6},{5,7},{6,4},{7,5},{8,10},{9,11},{10,... | collective-permute-start | bytes 294920 | tf_op jit(solution)/shard_map/cotangent_gather/ppermute | solution.py:43
  24.4 1.6 %collective-permute-done.9.refs_2_ = f32[8,256]{1,0:T(8,128)S(1)} collective-permute-done((f32[8,256]{1,0:T(8,128)S(1)}, f32[8,256]{1,0:T(8,128)S(1)}, u32[]{:S(2)}, u32[]{:S(2)}) %collective-permute-start.9) | collective-permute-done | bytes 8224 | tf_op jit(solution)/shard_map/stats_exchange/ppermute | solution.py:43
  26.0 0.0 collective-permute-start.13
  26.0 2.4 %collective-permute-start.10 = (f32[8,256]{1,0:T(8,128)S(1)}, f32[8,256]{1,0:T(8,128)S(1)}, u32[]{:S(2)}, u32[]{:S(2)}) collective-permute-start(f32[8,256]{1,0:T(8,128)S(1)} %scores.1.refs_0_), channel_id=1, source_target_pairs={{0,6},{1,7},{2,4},{3,5},{4,2},{5,3},{6,0},{7,1},{8,14},{9,15},{10,... | collective-permute-start | bytes 24584 | tf_op jit(solution)/shard_map/stats_exchange/ppermute | solution.py:43
  28.4 1.1 %collective-permute-start.8 = (f32[8,256]{1,0:T(8,128)S(1)}, f32[8,256]{1,0:T(8,128)S(1)}, u32[]{:S(2)}, u32[]{:S(2)}) collective-permute-start(f32[8,256]{1,0:T(8,128)S(1)} %scores.1.refs_0_), channel_id=1, source_target_pairs={{0,4},{1,5},{2,6},{3,7},{4,0},{5,1},{6,2},{7,3},{8,12},{9,13},{10,... | collective-permute-start | bytes 24584 | tf_op jit(solution)/shard_map/stats_exchange/ppermute | solution.py:43
  29.5 0.0 collective-permute-done.12.refs_10_
  29.5 2.0 %collective-permute-done.10.refs_3_ = f32[8,256]{1,0:T(8,128)S(1)} collective-permute-done((f32[8,256]{1,0:T(8,128)S(1)}, f32[8,256]{1,0:T(8,128)S(1)}, u32[]{:S(2)}, u32[]{:S(2)}) %collective-permute-start.10) | collective-permute-done | bytes 8224 | tf_op jit(solution)/shard_map/stats_exchange/ppermute | solution.py:43
  31.4 1.5 %collective-permute-done.8.refs_1_ = f32[8,256]{1,0:T(8,128)S(1)} collective-permute-done((f32[8,256]{1,0:T(8,128)S(1)}, f32[8,256]{1,0:T(8,128)S(1)}, u32[]{:S(2)}, u32[]{:S(2)}) %collective-permute-start.8) | collective-permute-done | bytes 8224 | tf_op jit(solution)/shard_map/stats_exchange/ppermute | solution.py:43
  33.0 2.6 %grads.1 = (bf16[48,1024]{1,0:T(8,128)(2,1)S(1)}, bf16[48,1024]{1,0:T(8,128)(2,1)S(1)}, bf16[48,1024]{1,0:T(8,128)(2,1)S(1)}, bf16[48,1024]{1,0:T(8,128)(2,1)S(1...) custom-call(f32[256,192]{1,0:T(8,128)S(1)} %get-tuple-element.35.bias_own, ...), custom_call_target="tpu_custom_call" | custom-call | flops 1006632960 | bytes 4980736 | tf_op jit(solution)/shard_map/grads/grads/pallas_call | solution.py:400
  35.6 0.1 collective-permute-start.14
  35.6 1.5 %collective-permute-start.16 = (bf16[48,1024]{1,0:T(8,128)(2,1)S(1)}, bf16[48,1024]{1,0:T(8,128)(2,1)S(1)}, u32[]{:S(2)}, u32[]{:S(2)}) collective-permute-start(bf16[48,1024]{1,0:T(8,128)(2,1)S(1)} %get-tuple-element.54), channel_id=1, source_target_pairs={{0,6},{1,7},{2,4},{3,5},{4,2},{5,3},{6,0},{7,1},{8,14},{9,15},{10,... | collective-permute-start | bytes 294920 | tf_op jit(solution)/shard_map/query_grad_sum/ppermute | solution.py:43
  37.1 1.2 %collective-permute-start.17 = (bf16[48,1024]{1,0:T(8,128)(2,1)S(1)}, bf16[48,1024]{1,0:T(8,128)(2,1)S(1)}, u32[]{:S(2)}, u32[]{:S(2)}) collective-permute-start(bf16[48,1024]{1,0:T(8,128)(2,1)S(1)} %get-tuple-element.55), channel_id=1, source_target_pairs={{0,4},{1,5},{2,6},{3,7},{4,0},{5,1},{6,2},{7,3},{8,12},{9,13},{10,... | collective-permute-start | bytes 294920 | tf_op jit(solution)/shard_map/query_grad_sum/ppermute | solution.py:43
  38.3 1.8 %collective-permute-start.18 = (bf16[48,1024]{1,0:T(8,128)(2,1)S(1)}, bf16[48,1024]{1,0:T(8,128)(2,1)S(1)}, u32[]{:S(2)}, u32[]{:S(2)}) collective-permute-start(bf16[48,1024]{1,0:T(8,128)(2,1)S(1)} %get-tuple-element.56), channel_id=1, source_target_pairs={{0,2},{1,3},{2,0},{3,1},{4,6},{5,7},{6,4},{7,5},{8,10},{9,11},{10,... | collective-permute-start | bytes 294920 | tf_op jit(solution)/shard_map/query_grad_sum/ppermute | solution.py:43
  40.1 1.5 %collective-permute-start.15 = (f32[8,128]{1,0:T(8,128)S(1)}, f32[8,128]{1,0:T(8,128)S(1)}, u32[]{:S(2)}, u32[]{:S(2)}) collective-permute-start(f32[8,128]{1,0:T(8,128)S(1)} %get-tuple-element.51.refs_0_), channel_id=1, source_target_pairs={{0,16},{8,24},{16,0},{24,8},{1,17},{9,25},{17,1},{25,9},{2,18},{10... | collective-permute-start | bytes 12296 | tf_op jit(solution)/shard_map/key_grad_end/ppermute | solution.py:356
  41.6 2.1 %collective-permute-done.15.refs_1_ = f32[8,128]{1,0:T(8,128)S(1)} collective-permute-done((f32[8,128]{1,0:T(8,128)S(1)}, f32[8,128]{1,0:T(8,128)S(1)}, u32[]{:S(2)}, u32[]{:S(2)}) %collective-permute-start.15) | collective-permute-done | bytes 4128 | tf_op jit(solution)/shard_map/key_grad_end/ppermute | solution.py:356
  43.7 0.0 collective-permute-done.14.other_ref
  43.7 1.8 %key_end.1 = (bf16[256,2048]{1,0:T(8,128)(2,1)}, bf16[256,2048]{1,0:T(8,128)(2,1)}, f32[8,128]{1,0:T(8,128)S(1)}) custom-call(bf16[256,2048]{1,0:T(8,128)(2,1)S(1)} %get-tuple-element.49.keep_ref, bf16[256,2048]{1,0:T(8,128)(2,1)S(1)} %collective-permute-done.14.other_ref, f32[8,128]{1,0:T(8,128)S(1)} %get-tuple-element.51.refs_0_, ...), custom_call_target="tpu_custom_call" | custom-call | flops 1000000 | bytes 4194304 | tf_op jit(solution)/shard_map/key_grad_end/key_end/pallas_call | solution.py:420
  45.5 0.0 collective-permute-done.16.refs_1_
  45.5 2.2 %collective-permute-done.17.refs_2_ = bf16[48,1024]{1,0:T(8,128)(2,1)S(1)} collective-permute-done((bf16[48,1024]{1,0:T(8,128)(2,1)S(1)}, bf16[48,1024]{1,0:T(8,128)(2,1)S(1)}, u32[]{:S(2)}, u32[]{:S(2)}) %collective-permute-start.17) | collective-permute-done | bytes 98336 | tf_op jit(solution)/shard_map/query_grad_sum/ppermute | solution.py:43
  47.7 0.1 query_end.1
  47.8 0.1 collective-permute-start.19
  47.9 1.2 %collective-permute-done.19 = bf16[24,1024]{1,0:T(8,128)(2,1)S(1)} collective-permute-done((bf16[24,1024]{1,0:T(8,128)(2,1)S(1)}, bf16[24,1024]{1,0:T(8,128)(2,1)S(1)}, u32[]{:S(2)}, u32[]{:S(2)}) %collective-permute-start.19) | collective-permute-done | bytes 49184 | tf_op jit(solution)/shard_map/query_grad_end/ppermute | solution.py:38
  49.1 0.7 %maximum_select_fusion = bf16[1,24,2048]{2,1,0:T(8,128)(2,1)} fusion(bf16[1,24,1024]{2,1,0:T(8,128)(2,1)S(1)} %bitcast.21, bf16[1,24,1024]{2,1,0:T(8,128)(2,1)S(1)} %bitcast.16, pred[]{:T(512)S(6)} %eq.3), kind=kLoop, calls=%fused_computation | loop fusion | flops 442368 | bytes 196609 | tf_op jit(solution)/shard_map/query_grad_end/jit(_where)/select_n | solution.py:261
  (16 shorter events, 0.1 us)
Async XLA Ops:
  0.6 14.4 %collective-permute-start.2 = (bf16[256,2048]{1,0:T(8,128)(2,1)}, bf16[256,2048]{1,0:T(8,128)(2,1)S(1)}, u32[]{:S(2)}, u32[]{:S(2)}) collective-permute-start(bf16[256,2048]{1,0:T(8,128)(2,1)} %bitcast.11), channel_id=1, source_target_pairs={{0,1},{1,0},{2,3},{3,2},{4,5},{5,4},{6,7},{7,6},{8,9},{9,8},{10,11... | collective-permute-start | bytes 3145736 | tf_op jit(solution)/shard_map/key_exchange/ppermute | solution.py:38
  1.1 2.6 %collective-permute-start = (bf16[24,2048]{1,0:T(8,128)(2,1)}, bf16[24,2048]{1,0:T(8,128)(2,1)S(1)}, u32[]{:S(2)}, u32[]{:S(2)}) collective-permute-start(bf16[24,2048]{1,0:T(8,128)(2,1)} %bitcast.14), channel_id=1, source_target_pairs={{0,1},{1,0},{2,3},{3,2},{4,5},{5,4},{6,7},{7,6},{8,9},{9,8},{10,11... | collective-permute-start | bytes 294920 | tf_op jit(solution)/shard_map/sibling_exchange/ppermute | solution.py:38
  1.2 2.6 %copy-start.2 = (bf16[1,24,2048]{2,1,0:T(8,128)(2,1)S(1)}, bf16[1,24,2048]{2,1,0:T(8,128)(2,1)}, u32[]{:S(2)}) copy-start(bf16[1,24,2048]{2,1,0:T(8,128)(2,1)} %param.8) | copy-start | bytes 294916
  3.8 5.6 %copy-start.6 = (bf16[24,1152]{1,0:T(8,128)(2,1)S(1)}, bf16[24,1152]{1,0:T(8,128)(2,1)}, u32[]{:S(2)}) copy-start(bf16[24,1152]{1,0:T(8,128)(2,1)} %get-tuple-element.37) | copy-start | bytes 165892
  3.8 6.9 %copy-start.3 = (bf16[24,1152]{1,0:T(8,128)(2,1)S(1)}, bf16[24,1152]{1,0:T(8,128)(2,1)}, u32[]{:S(2)}) copy-start(bf16[24,1152]{1,0:T(8,128)(2,1)} %get-tuple-element.32.own_ref) | copy-start | bytes 165892
  3.8 11.2 %collective-permute-start.3 = (bf16[48,1024]{1,0:T(8,128)(2,1)S(1)}, bf16[48,1024]{1,0:T(8,128)(2,1)S(1)}, u32[]{:S(2)}, u32[]{:S(2)}) collective-permute-start(bf16[48,1024]{1,0:T(8,128)(2,1)S(1)} %join_queries.1.refs_1_.refs_4_), channel_id=1, source_target_pairs={{0,4},{1,5},{2,6},{3,7},{4,0},{5,1},{6,2},{7,3},{8,12},{9,13},{10,... | collective-permute-start | bytes 294920 | tf_op jit(solution)/shard_map/query_gather/ppermute | solution.py:43
  7.8 7.2 %collective-permute-start.5 = (bf16[48,1024]{1,0:T(8,128)(2,1)S(1)}, bf16[48,1024]{1,0:T(8,128)(2,1)S(1)}, u32[]{:S(2)}, u32[]{:S(2)}) collective-permute-start(bf16[48,1024]{1,0:T(8,128)(2,1)S(1)} %join_queries.1.refs_1_.refs_4_), channel_id=1, source_target_pairs={{0,2},{1,3},{2,0},{3,1},{4,6},{5,7},{6,4},{7,5},{8,10},{9,11},{10,... | collective-permute-start | bytes 294920 | tf_op jit(solution)/shard_map/query_gather/ppermute | solution.py:43
  9.4 1.2 %collective-permute-start.1 = (bf16[24,1152]{1,0:T(8,128)(2,1)S(1)}, bf16[24,1152]{1,0:T(8,128)(2,1)S(1)}, u32[]{:S(2)}, u32[]{:S(2)}) collective-permute-start(bf16[24,1152]{1,0:T(8,128)(2,1)S(1)} %copy-done.6), channel_id=1, source_target_pairs={{0,1},{1,0},{2,3},{3,2},{4,5},{5,4},{6,7},{7,6},{8,9},{9,8},{10,11... | collective-permute-start | bytes 165896 | tf_op jit(solution)/shard_map/sibling_exchange/ppermute | solution.py:38
  10.8 4.1 %collective-permute-start.4 = (f32[8,128]{1,0:T(8,128)S(1)}, f32[8,128]{1,0:T(8,128)S(1)}, u32[]{:S(2)}, u32[]{:S(2)}) collective-permute-start(f32[8,128]{1,0:T(8,128)S(1)} %get-tuple-element.41), channel_id=1, source_target_pairs={{0,8},{8,0},{16,24},{24,16},{1,9},{9,1},{17,25},{25,17},{2,10},{10... | collective-permute-start | bytes 12296 | tf_op jit(solution)/shard_map/mask_count/ppermute | solution.py:356
  12.3 0.7 %copy-start.4 = (s32[1,1,4]{2,1,0:T(1,128)S(1)}, s32[1,1,4]{2,1,0:T(1,128)}, u32[]{:S(2)}) copy-start(s32[1,1,4]{2,1,0:T(1,128)} %param.14) | copy-start | bytes 52
  12.3 0.7 %copy-start.5 = (s32[1,1,4]{2,1,0:T(1,128)S(1)}, s32[1,1,4]{2,1,0:T(1,128)}, u32[]{:S(2)}) copy-start(s32[1,1,4]{2,1,0:T(1,128)} %param.15) | copy-start | bytes 52
  13.0 1.2 %copy-start.1 = (bf16[1,256,2048]{2,1,0:T(8,128)(2,1)S(1)}, bf16[1,256,2048]{2,1,0:T(8,128)(2,1)}, u32[]{:S(2)}) copy-start(bf16[1,256,2048]{2,1,0:T(8,128)(2,1)} %param.9) | copy-start | bytes 3145732
  15.0 18.0 %copy-start = (bf16[1,256,2048]{2,1,0:T(8,128)(2,1)S(1)}, bf16[1,256,2048]{2,1,0:T(8,128)(2,1)}, u32[]{:S(2)}) copy-start(bf16[1,256,2048]{2,1,0:T(8,128)(2,1)} %param.10) | copy-start | bytes 3145732
  15.0 6.4 %collective-permute-start.6 = (bf16[256,1024]{1,0:T(8,128)(2,1)S(1)}, bf16[256,1024]{1,0:T(8,128)(2,1)S(1)}, u32[]{:S(2)}, u32[]{:S(2)}) collective-permute-start(bf16[256,1024]{1,0:T(8,128)(2,1)S(1)} %get-tuple-element.44), channel_id=1, source_target_pairs={{0,1},{1,0},{2,3},{3,2},{4,5},{5,4},{6,7},{7,6},{8,9},{9,8},{10,11... | collective-permute-start | bytes 1572872 | tf_op jit(solution)/shard_map/key_exchange/ppermute | solution.py:38
  15.1 6.3 %collective-permute-start.7 = (bf16[48,1024]{1,0:T(8,128)(2,1)S(1)}, bf16[48,1024]{1,0:T(8,128)(2,1)S(1)}, u32[]{:S(2)}, u32[]{:S(2)}) collective-permute-start(bf16[48,1024]{1,0:T(8,128)(2,1)S(1)} %collective-permute-done.3.refs_2_.refs_5_), channel_id=1, source_target_pairs={{0,2},{1,3},{2,0},{3,1},{4,6},{5,7},{6,4},{7,5},{8,10},{9,11},{10,... | collective-permute-start | bytes 294920 | tf_op jit(solution)/shard_map/query_forward/ppermute | solution.py:43
  15.6 8.8 %collective-permute-start.11 = (bf16[48,1024]{1,0:T(8,128)(2,1)S(1)}, bf16[48,1024]{1,0:T(8,128)(2,1)S(1)}, u32[]{:S(2)}, u32[]{:S(2)}) collective-permute-start(bf16[48,1024]{1,0:T(8,128)(2,1)S(1)} %get-tuple-element.46.refs_8_), channel_id=1, source_target_pairs={{0,4},{1,5},{2,6},{3,7},{4,0},{5,1},{6,2},{7,3},{8,12},{9,13},{10,... | collective-permute-start | bytes 294920 | tf_op jit(solution)/shard_map/cotangent_gather/ppermute | solution.py:43
  22.3 3.7 %collective-permute-start.9 = (f32[8,256]{1,0:T(8,128)S(1)}, f32[8,256]{1,0:T(8,128)S(1)}, u32[]{:S(2)}, u32[]{:S(2)}) collective-permute-start(f32[8,256]{1,0:T(8,128)S(1)} %scores.1.refs_0_), channel_id=1, source_target_pairs={{0,2},{1,3},{2,0},{3,1},{4,6},{5,7},{6,4},{7,5},{8,10},{9,11},{10,... | collective-permute-start | bytes 24584 | tf_op jit(solution)/shard_map/stats_exchange/ppermute | solution.py:43
  22.4 7.1 %collective-permute-start.12 = (bf16[48,1024]{1,0:T(8,128)(2,1)S(1)}, bf16[48,1024]{1,0:T(8,128)(2,1)S(1)}, u32[]{:S(2)}, u32[]{:S(2)}) collective-permute-start(bf16[48,1024]{1,0:T(8,128)(2,1)S(1)} %get-tuple-element.46.refs_8_), channel_id=1, source_target_pairs={{0,2},{1,3},{2,0},{3,1},{4,6},{5,7},{6,4},{7,5},{8,10},{9,11},{10,... | collective-permute-start | bytes 294920 | tf_op jit(solution)/shard_map/cotangent_gather/ppermute | solution.py:43
  26.0 7.0 %collective-permute-start.13 = (bf16[48,1024]{1,0:T(8,128)(2,1)S(1)}, bf16[48,1024]{1,0:T(8,128)(2,1)S(1)}, u32[]{:S(2)}, u32[]{:S(2)}) collective-permute-start(bf16[48,1024]{1,0:T(8,128)(2,1)S(1)} %collective-permute-done.11.refs_9_), channel_id=1, source_target_pairs={{0,2},{1,3},{2,0},{3,1},{4,6},{5,7},{6,4},{7,5},{8,10},{9,11},{10,... | collective-permute-start | bytes 294920 | tf_op jit(solution)/shard_map/cotangent_forward/ppermute | solution.py:43
  26.0 5.4 %collective-permute-start.10 = (f32[8,256]{1,0:T(8,128)S(1)}, f32[8,256]{1,0:T(8,128)S(1)}, u32[]{:S(2)}, u32[]{:S(2)}) collective-permute-start(f32[8,256]{1,0:T(8,128)S(1)} %scores.1.refs_0_), channel_id=1, source_target_pairs={{0,6},{1,7},{2,4},{3,5},{4,2},{5,3},{6,0},{7,1},{8,14},{9,15},{10,... | collective-permute-start | bytes 24584 | tf_op jit(solution)/shard_map/stats_exchange/ppermute | solution.py:43
  28.4 4.5 %collective-permute-start.8 = (f32[8,256]{1,0:T(8,128)S(1)}, f32[8,256]{1,0:T(8,128)S(1)}, u32[]{:S(2)}, u32[]{:S(2)}) collective-permute-start(f32[8,256]{1,0:T(8,128)S(1)} %scores.1.refs_0_), channel_id=1, source_target_pairs={{0,4},{1,5},{2,6},{3,7},{4,0},{5,1},{6,2},{7,3},{8,12},{9,13},{10,... | collective-permute-start | bytes 24584 | tf_op jit(solution)/shard_map/stats_exchange/ppermute | solution.py:43
  35.6 8.1 %collective-permute-start.14 = (bf16[256,2048]{1,0:T(8,128)(2,1)S(1)}, bf16[256,2048]{1,0:T(8,128)(2,1)S(1)}, u32[]{:S(2)}, u32[]{:S(2)}) collective-permute-start(bf16[256,2048]{1,0:T(8,128)(2,1)S(1)} %get-tuple-element.50), channel_id=1, source_target_pairs={{0,1},{1,0},{2,3},{3,2},{4,5},{5,4},{6,7},{7,6},{8,9},{9,8},{10,11... | collective-permute-start | bytes 3145736 | tf_op jit(solution)/shard_map/key_grad_end/ppermute | solution.py:38
  35.6 9.9 %collective-permute-start.16 = (bf16[48,1024]{1,0:T(8,128)(2,1)S(1)}, bf16[48,1024]{1,0:T(8,128)(2,1)S(1)}, u32[]{:S(2)}, u32[]{:S(2)}) collective-permute-start(bf16[48,1024]{1,0:T(8,128)(2,1)S(1)} %get-tuple-element.54), channel_id=1, source_target_pairs={{0,6},{1,7},{2,4},{3,5},{4,2},{5,3},{6,0},{7,1},{8,14},{9,15},{10,... | collective-permute-start | bytes 294920 | tf_op jit(solution)/shard_map/query_grad_sum/ppermute | solution.py:43
  37.1 10.6 %collective-permute-start.17 = (bf16[48,1024]{1,0:T(8,128)(2,1)S(1)}, bf16[48,1024]{1,0:T(8,128)(2,1)S(1)}, u32[]{:S(2)}, u32[]{:S(2)}) collective-permute-start(bf16[48,1024]{1,0:T(8,128)(2,1)S(1)} %get-tuple-element.55), channel_id=1, source_target_pairs={{0,4},{1,5},{2,6},{3,7},{4,0},{5,1},{6,2},{7,3},{8,12},{9,13},{10,... | collective-permute-start | bytes 294920 | tf_op jit(solution)/shard_map/query_grad_sum/ppermute | solution.py:43
  38.3 9.4 %collective-permute-start.18 = (bf16[48,1024]{1,0:T(8,128)(2,1)S(1)}, bf16[48,1024]{1,0:T(8,128)(2,1)S(1)}, u32[]{:S(2)}, u32[]{:S(2)}) collective-permute-start(bf16[48,1024]{1,0:T(8,128)(2,1)S(1)} %get-tuple-element.56), channel_id=1, source_target_pairs={{0,2},{1,3},{2,0},{3,1},{4,6},{5,7},{6,4},{7,5},{8,10},{9,11},{10,... | collective-permute-start | bytes 294920 | tf_op jit(solution)/shard_map/query_grad_sum/ppermute | solution.py:43
  40.1 3.6 %collective-permute-start.15 = (f32[8,128]{1,0:T(8,128)S(1)}, f32[8,128]{1,0:T(8,128)S(1)}, u32[]{:S(2)}, u32[]{:S(2)}) collective-permute-start(f32[8,128]{1,0:T(8,128)S(1)} %get-tuple-element.51.refs_0_), channel_id=1, source_target_pairs={{0,16},{8,24},{16,0},{24,8},{1,17},{9,25},{17,1},{25,9},{2,18},{10... | collective-permute-start | bytes 12296 | tf_op jit(solution)/shard_map/key_grad_end/ppermute | solution.py:356
  47.8 1.3 %collective-permute-start.19 = (bf16[24,1024]{1,0:T(8,128)(2,1)S(1)}, bf16[24,1024]{1,0:T(8,128)(2,1)S(1)}, u32[]{:S(2)}, u32[]{:S(2)}) collective-permute-start(bf16[24,1024]{1,0:T(8,128)(2,1)S(1)} %get-tuple-element.58), channel_id=1, source_target_pairs={{0,1},{1,0},{2,3},{3,2},{4,5},{5,4},{6,7},{7,6},{8,9},{9,8},{10,11... | collective-permute-start | bytes 147464 | tf_op jit(solution)/shard_map/query_grad_end/ppermute | solution.py:38

commit v5 on v2

--- a/solution.py
+++ b/solution.py
@@ -176,6 +176,7 @@
     rows = blocks[0].shape[0]
     dec_rows = rows * len(offsets)
     stats_ref[...] = jnp.broadcast_to(count_ref[0:1, 0:1], stats_ref.shape)
+    stats_ref[HALF_HEADS:, :dec_rows] = jnp.zeros((HALF_HEADS, dec_rows), F32)
     stats_ref[HALF_HEADS:, :rows] = delta_ref[:HALF_HEADS]
     for head in range(HALF_HEADS):
         q = rows_of(blocks, head)
@@ -191,29 +192,36 @@
         )
 
 
-def gathered_stats(offsets, stats, rows):
-    logs = []
-    for sender, ref in zip(offsets, stats):
-        order = [offsets.index(offset ^ sender) for offset in offsets]
-        logs.append(
-            jnp.concatenate([ref[:HALF_HEADS, j * rows : (j + 1) * rows] for j in order], 1)
-        )
-    top = functools.reduce(jnp.maximum, logs)
-    log_total = top + jnp.log(sum(jnp.exp(log - top) for log in logs))
-    delta = jnp.concatenate([ref[HALF_HEADS:, :rows] for ref in stats], 1)
-    last = stats[0].shape[1] - 1
-    return log_total, delta, sum(ref[0:1, last:] for ref in stats)
+def merged_stats(offsets, apart, own_ref, other_ref, dec_rows):
+    rows = dec_rows // len(offsets)
+    order = [offsets.index(offset ^ apart) for offset in offsets]
+    own = own_ref[:, :dec_rows]
+    other = jnp.concatenate([other_ref[:, j * rows : (j + 1) * rows] for j in order], 1)
+    logs = own[:HALF_HEADS], other[:HALF_HEADS]
+    top = jnp.maximum(jnp.maximum(*logs), -1e20)
+    total = sum(jnp.exp(log - top) for log in logs)
+    log_total = jnp.where(total > 0, top + jnp.log(jnp.maximum(total, 1e-30)), NEVER)
+    last = own_ref.shape[1] - 1
+    count = own_ref[0:1, last:] + other_ref[0:1, last:]
+    return log_total, own[HALF_HEADS:] + other[HALF_HEADS:], count
+
+
+def merge_kernel(offsets, apart, dec_rows, own_ref, other_ref, stats_ref):
+    log_total, delta, count = merged_stats(offsets, apart, own_ref, other_ref, dec_rows)
+    stats_ref[...] = jnp.broadcast_to(count, stats_ref.shape)
+    stats_ref[:HALF_HEADS, :dec_rows] = log_total
+    stats_ref[HALF_HEADS:, :dec_rows] = delta
 
 
 def grads_kernel(offsets, bias_own, bias_other, *refs):
     chips = len(offsets)
-    stats, refs = refs[:chips], refs[chips:]
+    stats, refs = refs[:2], refs[2:]
     q_blocks, refs = refs[:chips], refs[chips:]
     g_blocks, refs = refs[:chips], refs[chips:]
     (key_ref, key_other, value_ref, value_other), refs = refs[:4], refs[4:]
     dq_blocks, (keep_ref, send_ref, count_ref) = refs[:chips], refs[chips:]
     rows = q_blocks[0].shape[0]
-    log_total, delta, count = gathered_stats(offsets, stats, rows)
+    log_total, delta, count = merged_stats(offsets, chips // 2, *stats, rows * chips)
     count_ref[...] = jnp.broadcast_to(count, count_ref.shape)
     for head in range(HALF_HEADS):
         columns = slice(head * HEAD_SIZE, (head + 1) * HEAD_SIZE)
@@ -389,14 +397,27 @@
         )(delta, bias_own, bias_other, k_own, k_recv, count, *q_blocks)
 
     with jax.named_scope("stats_exchange"):
-        all_stats = [stats] + [across(stats, offset) for offset in offsets[1:]]
+        apart = 1
+        while apart < chips // 2:
+            stats = kernel_call(
+                functools.partial(merge_kernel, offsets, apart, dec_rows),
+                shaped(2 * HALF_HEADS, width, dtype=F32),
+                [VMEM] * 2,
+                VMEM,
+                [],
+                1,
+                1,
+                "merge_stats",
+            )(stats, across(stats, apart))
+            apart *= 2
+        all_stats = stats, across(stats, apart)
 
     with jax.named_scope("grads"):
         both = shaped(enc_local, 2 * HALF)
         *dq_blocks, dkv_keep, dkv_send, count = kernel_call(
             functools.partial(grads_kernel, offsets),
             (block,) * chips + (both, both, shaped(8, EXTRA, dtype=F32)),
-            [VMEM] * (3 * chips + 6),
+            [VMEM] * (2 * chips + 8),
             (VMEM,) * (chips + 3),
             [],
             10 * dec_rows * enc_rows * HALF,

time: 46.8 us -> 47.9 us (1.024)
  waiting for transfers between devices: 12 us -> 16.6 us
  starting transfers between devices: 23.2 us -> 19.6 us
    ppermute x12 -> x11, waiting for transfers between devices: 6.65 us -> 11.4 us  [across(): lax.ppermute(block, 'seq', [(i, i ^ 2 * apart) for i in range(count)])]
    ppermute x12 -> x11, starting transfers between devices: 19.4 us -> 15.6 us  [across(): lax.ppermute(block, 'seq', [(i, i ^ 2 * apart) for i in range(count)])]
  transfers between devices with their start and end apart: 20 -> 19, of which waited for: 8 -> 8; matrix products, arithmetic and copies ran while one was open for 0% -> 0% of each run, Pallas kernels for 12% -> 12%
where the time goes in v5:
time: 47.9 us; the launch traced here: 47.7 us
  starting transfers between devices  19.6 us (41%)
  waiting for transfers between devices  16.6 us (35%)
  Pallas kernels  8.2 us (17%)
  local copies, waits for them, and re-layouts  1.91 us (4%)
  between operations  0.76 us (2%)
  other arithmetic  0.67 us (1%)
    ppermute x11, starting transfers between devices, across(): lax.ppermute(block, 'seq', [(i, i ^ 2 * apart) for i in range(count)])  15.6 us
    ppermute x11, waiting for transfers between devices, across(): lax.ppermute(block, 'seq', [(i, i ^ 2 * apart) for i in range(count)])  11.4 us
    ppermute x6, waiting for transfers between devices, to_sibling(): return lax.ppermute(block, 'seq', [(i, i ^ 1) for i in range(count)])  3.13 us
    ppermute x2, starting transfers between devices, over_groups(): lax.ppermute(count, 'dp', [(i, i ^ apart) for i in range(data_groups)])  3.02 us
    pallas_call x1, Pallas kernels, local(): kernel_call(functools.partial(grads_kernel, offsets), (block,) * chips +...  2.58 us
    ppermute x2, waiting for transfers between devices, over_groups(): lax.ppermute(count, 'dp', [(i, i ^ apart) for i in range(data_groups)])  2.09 us
    unnamed x14, local copies, waits for them, and re-layouts  1.91 us
    pallas_call x1, Pallas kernels, local(): kernel_call(functools.partial(key_end_kernel, rows_in_all), (whole, whole...  1.84 us
  transfers between devices with their start and end apart: 19, of which 8 were waited for; matrix products, arithmetic and copies ran while one was open for 0% of the time, Pallas kernels for 12%

profile of v5, /device:TPU:0, one launch (start us, length us, event | category | flops | bytes accessed | tf_op | source)
XLA Modules:
  0.0 47.7 jit_solution(16590502466635110813)
XLA Ops:
  0.6 0.5 %collective-permute-start.2 = (bf16[256,2048]{1,0:T(8,128)(2,1)}, bf16[256,2048]{1,0:T(8,128)(2,1)S(1)}, u32[]{:S(2)}, u32[]{:S(2)}) collective-permute-start(bf16[256,2048]{1,0:T(8,128)(2,1)} %bitcast.11), channel_id=1, source_target_pairs={{0,1},{1,0},{2,3},{3,2},{4,5},{5,4},{6,7},{7,6},{8,9},{9,8},{10,11... | collective-permute-start | bytes 3145736 | tf_op jit(solution)/shard_map/key_exchange/ppermute | solution.py:38
  1.1 0.1 collective-permute-start
  1.2 1.8 %prepare.1 = (bf16[24,1152]{1,0:T(8,128)(2,1)}, bf16[24,1152]{1,0:T(8,128)(2,1)}) custom-call(bf16[24,2048]{1,0:T(8,128)(2,1)} %bitcast.19, bf16[24,2048]{1,0:T(8,128)(2,1)} %bitcast.20, s32[1,24]{1,0:T(1,128)} %mask_ref.1), custom_call_target="tpu_custom_call" | custom-call | flops 100000 | bytes 1000000 | tf_op jit(solution)/shard_map/sibling_exchange/prepare/pallas_call | solution.py:311
  3.0 0.8 %collective-permute-done.other_ref = bf16[24,2048]{1,0:T(8,128)(2,1)S(1)} collective-permute-done((bf16[24,2048]{1,0:T(8,128)(2,1)}, bf16[24,2048]{1,0:T(8,128)(2,1)S(1)}, u32[]{:S(2)}, u32[]{:S(2)}) %collective-permute-start) | collective-permute-done | bytes 98336 | tf_op jit(solution)/shard_map/sibling_exchange/ppermute | solution.py:38
  3.8 3.0 %collective-permute-start.5 = (bf16[48,1024]{1,0:T(8,128)(2,1)S(1)}, bf16[48,1024]{1,0:T(8,128)(2,1)S(1)}, u32[]{:S(2)}, u32[]{:S(2)}) collective-permute-start(bf16[48,1024]{1,0:T(8,128)(2,1)S(1)} %join_queries.1.refs_1_.refs_2_), channel_id=1, source_target_pairs={{0,2},{1,3},{2,0},{3,1},{4,6},{5,7},{6,4},{7,5},{8,10},{9,11},{10,... | collective-permute-start | bytes 294920 | tf_op jit(solution)/shard_map/query_gather/ppermute | solution.py:43
  6.8 2.6 %collective-permute-start.3 = (bf16[48,1024]{1,0:T(8,128)(2,1)S(1)}, bf16[48,1024]{1,0:T(8,128)(2,1)S(1)}, u32[]{:S(2)}, u32[]{:S(2)}) collective-permute-start(bf16[48,1024]{1,0:T(8,128)(2,1)S(1)} %join_queries.1.refs_1_.refs_2_), channel_id=1, source_target_pairs={{0,4},{1,5},{2,6},{3,7},{4,0},{5,1},{6,2},{7,3},{8,12},{9,13},{10,... | collective-permute-start | bytes 294920 | tf_op jit(solution)/shard_map/query_gather/ppermute | solution.py:43
  9.4 0.0 collective-permute-start.1
  9.4 1.2 %collective-permute-done.1.other_ref = bf16[24,1152]{1,0:T(8,128)(2,1)S(1)} collective-permute-done((bf16[24,1152]{1,0:T(8,128)(2,1)S(1)}, bf16[24,1152]{1,0:T(8,128)(2,1)S(1)}, u32[]{:S(2)}, u32[]{:S(2)}) %collective-permute-start.1) | collective-permute-done | bytes 55328 | tf_op jit(solution)/shard_map/sibling_exchange/ppermute | solution.py:38
  10.7 0.2 join_cotangents.1
  10.8 1.5 %collective-permute-start.4 = (f32[8,128]{1,0:T(8,128)S(1)}, f32[8,128]{1,0:T(8,128)S(1)}, u32[]{:S(2)}, u32[]{:S(2)}) collective-permute-start(f32[8,128]{1,0:T(8,128)S(1)} %get-tuple-element.40), channel_id=1, source_target_pairs={{0,8},{8,0},{16,24},{24,16},{1,9},{9,1},{17,25},{25,17},{2,10},{10... | collective-permute-start | bytes 12296 | tf_op jit(solution)/shard_map/mask_count/ppermute | solution.py:364
  12.3 0.7 %copy-done.4 = s32[1,1,4]{2,1,0:T(1,128)S(1)} copy-done((s32[1,1,4]{2,1,0:T(1,128)S(1)}, s32[1,1,4]{2,1,0:T(1,128)}, u32[]{:S(2)}) %copy-start.4) | copy-done | bytes 40
  13.0 0.0 copy-done.5
  13.0 1.2 %copy-done.1 = bf16[1,256,2048]{2,1,0:T(8,128)(2,1)S(1)} copy-done((bf16[1,256,2048]{2,1,0:T(8,128)(2,1)S(1)}, bf16[1,256,2048]{2,1,0:T(8,128)(2,1)}, u32[]{:S(2)}) %copy-start.1) | copy-done | bytes 1048600
  14.2 0.7 %setup.1 = (bf16[256,1024]{1,0:T(8,128)(2,1)S(1)}, bf16[256,1024]{1,0:T(8,128)(2,1)S(1)}, f32[256,192]{1,0:T(8,128)S(1)}, f32[256,192]{1,0:T(8,128)S(1)}) custom-call(s32[1,4]{1,0:T(1,128)S(1)} %bitcast.17, s32[1,4]{1,0:T(1,128)S(1)} %bitcast.18, bf16[256,2048]{1,0:T(8,128)(2,1)S(1)} %bitcast.13), custom_call_target="tpu_custom_call" | custom-call | flops 1000000 | bytes 4194304 | tf_op jit(solution)/shard_map/setup/setup/pallas_call | solution.py:339
  15.0 0.0 copy-start
  15.0 0.0 collective-permute-done.4
  15.0 0.0 collective-permute-done.5.refs_3_.refs_4_
  15.0 0.0 collective-permute-done.3.refs_2_.refs_3_
  15.0 0.0 collective-permute-done.2.refs_13_
  15.0 0.1 collective-permute-start.6
  15.1 0.5 %collective-permute-start.7 = (bf16[48,1024]{1,0:T(8,128)(2,1)S(1)}, bf16[48,1024]{1,0:T(8,128)(2,1)S(1)}, u32[]{:S(2)}, u32[]{:S(2)}) collective-permute-start(bf16[48,1024]{1,0:T(8,128)(2,1)S(1)} %collective-permute-done.3.refs_2_.refs_3_), channel_id=1, source_target_pairs={{0,2},{1,3},{2,0},{3,1},{4,6},{5,7},{6,4},{7,5},{8,10},{9,11},{10,... | collective-permute-start | bytes 294920 | tf_op jit(solution)/shard_map/query_forward/ppermute | solution.py:43
  15.6 1.9 %collective-permute-start.10 = (bf16[48,1024]{1,0:T(8,128)(2,1)S(1)}, bf16[48,1024]{1,0:T(8,128)(2,1)S(1)}, u32[]{:S(2)}, u32[]{:S(2)}) collective-permute-start(bf16[48,1024]{1,0:T(8,128)(2,1)S(1)} %get-tuple-element.45.refs_6_), channel_id=1, source_target_pairs={{0,4},{1,5},{2,6},{3,7},{4,0},{5,1},{6,2},{7,3},{8,12},{9,13},{10,... | collective-permute-start | bytes 294920 | tf_op jit(solution)/shard_map/cotangent_gather/ppermute | solution.py:43
  17.5 0.1 collective-permute-start.11
  17.6 2.4 %collective-permute-start.12 = (bf16[48,1024]{1,0:T(8,128)(2,1)S(1)}, bf16[48,1024]{1,0:T(8,128)(2,1)S(1)}, u32[]{:S(2)}, u32[]{:S(2)}) collective-permute-start(bf16[48,1024]{1,0:T(8,128)(2,1)S(1)} %get-tuple-element.45.refs_6_), channel_id=1, source_target_pairs={{0,6},{1,7},{2,4},{3,5},{4,2},{5,3},{6,0},{7,1},{8,14},{9,15},{10,... | collective-permute-start | bytes 294920 | tf_op jit(solution)/shard_map/cotangent_gather/ppermute | solution.py:43
  20.0 1.9 %collective-permute-done.7.refs_4_.refs_5_ = bf16[48,1024]{1,0:T(8,128)(2,1)S(1)} collective-permute-done((bf16[48,1024]{1,0:T(8,128)(2,1)S(1)}, bf16[48,1024]{1,0:T(8,128)(2,1)S(1)}, u32[]{:S(2)}, u32[]{:S(2)}) %collective-permute-start.7) | collective-permute-done | bytes 98336 | tf_op jit(solution)/shard_map/query_forward/ppermute | solution.py:43
  21.9 0.0 collective-permute-done.6.other_ref.refs_11_
  21.9 0.9 %scores.1.own_ref = f32[8,256]{1,0:T(8,128)S(1)} custom-call(f32[8,48]{1,0:T(8,128)S(1)} %get-tuple-element.37.delta_ref, f32[256,192]{1,0:T(8,128)S(1)} %get-tuple-element.34.bias_own, f32[256,192]{1,0:T(8,128)S(1)} %get-tuple-element.35.bias_other, bf16[256,1024]{1,0:T(8,128)(2,1)S(1)} %get-tuple-element.38.key_ref.refs_10_, ...), custom_call_target="tpu_custom_call" | custom-call | flops 201326592 | bytes 1441792 | tf_op jit(solution)/shard_map/scores/scores/pallas_call | solution.py:388
  22.9 0.1 collective-permute-start.8
  22.9 4.0 %collective-permute-done.8.other_ref = f32[8,256]{1,0:T(8,128)S(1)} collective-permute-done((f32[8,256]{1,0:T(8,128)S(1)}, f32[8,256]{1,0:T(8,128)S(1)}, u32[]{:S(2)}, u32[]{:S(2)}) %collective-permute-start.8) | collective-permute-done | bytes 8224 | tf_op jit(solution)/shard_map/stats_exchange/ppermute | solution.py:43
  27.0 0.1 merge_stats.1.refs_0_
  27.1 0.6 %collective-permute-start.9 = (f32[8,256]{1,0:T(8,128)S(1)}, f32[8,256]{1,0:T(8,128)S(1)}, u32[]{:S(2)}, u32[]{:S(2)}) collective-permute-start(f32[8,256]{1,0:T(8,128)S(1)} %merge_stats.1.refs_0_), channel_id=1, source_target_pairs={{0,4},{1,5},{2,6},{3,7},{4,0},{5,1},{6,2},{7,3},{8,12},{9,13},{10,... | collective-permute-start | bytes 24584 | tf_op jit(solution)/shard_map/stats_exchange/ppermute | solution.py:43
  27.6 0.0 collective-permute-done.10.refs_7_
  27.6 0.0 collective-permute-done.11.refs_8_
  27.6 0.0 collective-permute-done.12.refs_9_
  27.7 4.0 %collective-permute-done.9.refs_1_ = f32[8,256]{1,0:T(8,128)S(1)} collective-permute-done((f32[8,256]{1,0:T(8,128)S(1)}, f32[8,256]{1,0:T(8,128)S(1)}, u32[]{:S(2)}, u32[]{:S(2)}) %collective-permute-start.9) | collective-permute-done | bytes 8224 | tf_op jit(solution)/shard_map/stats_exchange/ppermute | solution.py:43
  31.7 2.6 %grads.1 = (bf16[48,1024]{1,0:T(8,128)(2,1)S(1)}, bf16[48,1024]{1,0:T(8,128)(2,1)S(1)}, bf16[48,1024]{1,0:T(8,128)(2,1)S(1)}, bf16[48,1024]{1,0:T(8,128)(2,1)S(1...) custom-call(f32[256,192]{1,0:T(8,128)S(1)} %get-tuple-element.34.bias_own, ...), custom_call_target="tpu_custom_call" | custom-call | flops 1006632960 | bytes 4980736 | tf_op jit(solution)/shard_map/grads/grads/pallas_call | solution.py:417
  34.3 0.1 collective-permute-start.13
  34.3 2.3 %collective-permute-start.15 = (bf16[48,1024]{1,0:T(8,128)(2,1)S(1)}, bf16[48,1024]{1,0:T(8,128)(2,1)S(1)}, u32[]{:S(2)}, u32[]{:S(2)}) collective-permute-start(bf16[48,1024]{1,0:T(8,128)(2,1)S(1)} %get-tuple-element.52), channel_id=1, source_target_pairs={{0,6},{1,7},{2,4},{3,5},{4,2},{5,3},{6,0},{7,1},{8,14},{9,15},{10,... | collective-permute-start | bytes 294920 | tf_op jit(solution)/shard_map/query_grad_sum/ppermute | solution.py:43
  36.6 2.2 %collective-permute-start.17 = (bf16[48,1024]{1,0:T(8,128)(2,1)S(1)}, bf16[48,1024]{1,0:T(8,128)(2,1)S(1)}, u32[]{:S(2)}, u32[]{:S(2)}) collective-permute-start(bf16[48,1024]{1,0:T(8,128)(2,1)S(1)} %get-tuple-element.54), channel_id=1, source_target_pairs={{0,2},{1,3},{2,0},{3,1},{4,6},{5,7},{6,4},{7,5},{8,10},{9,11},{10,... | collective-permute-start | bytes 294920 | tf_op jit(solution)/shard_map/query_grad_sum/ppermute | solution.py:43
  38.8 1.5 %collective-permute-start.14 = (f32[8,128]{1,0:T(8,128)S(1)}, f32[8,128]{1,0:T(8,128)S(1)}, u32[]{:S(2)}, u32[]{:S(2)}) collective-permute-start(f32[8,128]{1,0:T(8,128)S(1)} %get-tuple-element.49.refs_0_), channel_id=1, source_target_pairs={{0,16},{8,24},{16,0},{24,8},{1,17},{9,25},{17,1},{25,9},{2,18},{10... | collective-permute-start | bytes 12296 | tf_op jit(solution)/shard_map/key_grad_end/ppermute | solution.py:364
  40.3 2.1 %collective-permute-done.14.refs_1_ = f32[8,128]{1,0:T(8,128)S(1)} collective-permute-done((f32[8,128]{1,0:T(8,128)S(1)}, f32[8,128]{1,0:T(8,128)S(1)}, u32[]{:S(2)}, u32[]{:S(2)}) %collective-permute-start.14) | collective-permute-done | bytes 4128 | tf_op jit(solution)/shard_map/key_grad_end/ppermute | solution.py:364
  42.4 0.0 collective-permute-done.13.other_ref
  42.4 1.8 %key_end.1 = (bf16[256,2048]{1,0:T(8,128)(2,1)}, bf16[256,2048]{1,0:T(8,128)(2,1)}, f32[8,128]{1,0:T(8,128)S(1)}) custom-call(bf16[256,2048]{1,0:T(8,128)(2,1)S(1)} %get-tuple-element.47.keep_ref, bf16[256,2048]{1,0:T(8,128)(2,1)S(1)} %collective-permute-done.13.other_ref, f32[8,128]{1,0:T(8,128)S(1)} %get-tuple-element.49.refs_0_, ...), custom_call_target="tpu_custom_call" | custom-call | flops 1000000 | bytes 4194304 | tf_op jit(solution)/shard_map/key_grad_end/key_end/pallas_call | solution.py:437
  44.2 1.4 %collective-permute-done.16.refs_2_ = bf16[48,1024]{1,0:T(8,128)(2,1)S(1)} collective-permute-done((bf16[48,1024]{1,0:T(8,128)(2,1)S(1)}, bf16[48,1024]{1,0:T(8,128)(2,1)S(1)}, u32[]{:S(2)}, u32[]{:S(2)}) %collective-permute-start.16) | collective-permute-done | bytes 98336 | tf_op jit(solution)/shard_map/query_grad_sum/ppermute | solution.py:43
  45.7 0.1 query_end.1
  45.8 0.2 collective-permute-start.18
  45.9 1.1 %collective-permute-done.18 = bf16[24,1024]{1,0:T(8,128)(2,1)S(1)} collective-permute-done((bf16[24,1024]{1,0:T(8,128)(2,1)S(1)}, bf16[24,1024]{1,0:T(8,128)(2,1)S(1)}, u32[]{:S(2)}, u32[]{:S(2)}) %collective-permute-start.18) | collective-permute-done | bytes 49184 | tf_op jit(solution)/shard_map/query_grad_end/ppermute | solution.py:38
  47.0 0.7 %maximum_select_fusion = bf16[1,24,2048]{2,1,0:T(8,128)(2,1)} fusion(bf16[1,24,1024]{2,1,0:T(8,128)(2,1)S(1)} %bitcast.21, bf16[1,24,1024]{2,1,0:T(8,128)(2,1)S(1)} %bitcast.16, pred[]{:T(512)S(6)} %eq.3), kind=kLoop, calls=%fused_computation | loop fusion | flops 442368 | bytes 196609 | tf_op jit(solution)/shard_map/query_grad_end/jit(_where)/select_n | solution.py:269
  (15 shorter events, 0.1 us)
Async XLA Ops:
  0.6 14.4 %collective-permute-start.2 = (bf16[256,2048]{1,0:T(8,128)(2,1)}, bf16[256,2048]{1,0:T(8,128)(2,1)S(1)}, u32[]{:S(2)}, u32[]{:S(2)}) collective-permute-start(bf16[256,2048]{1,0:T(8,128)(2,1)} %bitcast.11), channel_id=1, source_target_pairs={{0,1},{1,0},{2,3},{3,2},{4,5},{5,4},{6,7},{7,6},{8,9},{9,8},{10,11... | collective-permute-start | bytes 3145736 | tf_op jit(solution)/shard_map/key_exchange/ppermute | solution.py:38
  1.1 2.6 %collective-permute-start = (bf16[24,2048]{1,0:T(8,128)(2,1)}, bf16[24,2048]{1,0:T(8,128)(2,1)S(1)}, u32[]{:S(2)}, u32[]{:S(2)}) collective-permute-start(bf16[24,2048]{1,0:T(8,128)(2,1)} %bitcast.14), channel_id=1, source_target_pairs={{0,1},{1,0},{2,3},{3,2},{4,5},{5,4},{6,7},{7,6},{8,9},{9,8},{10,11... | collective-permute-start | bytes 294920 | tf_op jit(solution)/shard_map/sibling_exchange/ppermute | solution.py:38
  1.2 2.6 %copy-start.2 = (bf16[1,24,2048]{2,1,0:T(8,128)(2,1)S(1)}, bf16[1,24,2048]{2,1,0:T(8,128)(2,1)}, u32[]{:S(2)}) copy-start(bf16[1,24,2048]{2,1,0:T(8,128)(2,1)} %param.8) | copy-start | bytes 294916
  3.8 5.6 %copy-start.6 = (bf16[24,1152]{1,0:T(8,128)(2,1)S(1)}, bf16[24,1152]{1,0:T(8,128)(2,1)}, u32[]{:S(2)}) copy-start(bf16[24,1152]{1,0:T(8,128)(2,1)} %get-tuple-element.36) | copy-start | bytes 165892
  3.8 6.9 %copy-start.3 = (bf16[24,1152]{1,0:T(8,128)(2,1)S(1)}, bf16[24,1152]{1,0:T(8,128)(2,1)}, u32[]{:S(2)}) copy-start(bf16[24,1152]{1,0:T(8,128)(2,1)} %get-tuple-element.31.own_ref) | copy-start | bytes 165892
  3.8 11.2 %collective-permute-start.5 = (bf16[48,1024]{1,0:T(8,128)(2,1)S(1)}, bf16[48,1024]{1,0:T(8,128)(2,1)S(1)}, u32[]{:S(2)}, u32[]{:S(2)}) collective-permute-start(bf16[48,1024]{1,0:T(8,128)(2,1)S(1)} %join_queries.1.refs_1_.refs_2_), channel_id=1, source_target_pairs={{0,2},{1,3},{2,0},{3,1},{4,6},{5,7},{6,4},{7,5},{8,10},{9,11},{10,... | collective-permute-start | bytes 294920 | tf_op jit(solution)/shard_map/query_gather/ppermute | solution.py:43
  6.8 8.2 %collective-permute-start.3 = (bf16[48,1024]{1,0:T(8,128)(2,1)S(1)}, bf16[48,1024]{1,0:T(8,128)(2,1)S(1)}, u32[]{:S(2)}, u32[]{:S(2)}) collective-permute-start(bf16[48,1024]{1,0:T(8,128)(2,1)S(1)} %join_queries.1.refs_1_.refs_2_), channel_id=1, source_target_pairs={{0,4},{1,5},{2,6},{3,7},{4,0},{5,1},{6,2},{7,3},{8,12},{9,13},{10,... | collective-permute-start | bytes 294920 | tf_op jit(solution)/shard_map/query_gather/ppermute | solution.py:43
  9.4 1.2 %collective-permute-start.1 = (bf16[24,1152]{1,0:T(8,128)(2,1)S(1)}, bf16[24,1152]{1,0:T(8,128)(2,1)S(1)}, u32[]{:S(2)}, u32[]{:S(2)}) collective-permute-start(bf16[24,1152]{1,0:T(8,128)(2,1)S(1)} %copy-done.6), channel_id=1, source_target_pairs={{0,1},{1,0},{2,3},{3,2},{4,5},{5,4},{6,7},{7,6},{8,9},{9,8},{10,11... | collective-permute-start | bytes 165896 | tf_op jit(solution)/shard_map/sibling_exchange/ppermute | solution.py:38
  10.8 4.1 %collective-permute-start.4 = (f32[8,128]{1,0:T(8,128)S(1)}, f32[8,128]{1,0:T(8,128)S(1)}, u32[]{:S(2)}, u32[]{:S(2)}) collective-permute-start(f32[8,128]{1,0:T(8,128)S(1)} %get-tuple-element.40), channel_id=1, source_target_pairs={{0,8},{8,0},{16,24},{24,16},{1,9},{9,1},{17,25},{25,17},{2,10},{10... | collective-permute-start | bytes 12296 | tf_op jit(solution)/shard_map/mask_count/ppermute | solution.py:364
  12.3 0.7 %copy-start.4 = (s32[1,1,4]{2,1,0:T(1,128)S(1)}, s32[1,1,4]{2,1,0:T(1,128)}, u32[]{:S(2)}) copy-start(s32[1,1,4]{2,1,0:T(1,128)} %param.14) | copy-start | bytes 52
  12.3 0.7 %copy-start.5 = (s32[1,1,4]{2,1,0:T(1,128)S(1)}, s32[1,1,4]{2,1,0:T(1,128)}, u32[]{:S(2)}) copy-start(s32[1,1,4]{2,1,0:T(1,128)} %param.15) | copy-start | bytes 52
  13.0 1.2 %copy-start.1 = (bf16[1,256,2048]{2,1,0:T(8,128)(2,1)S(1)}, bf16[1,256,2048]{2,1,0:T(8,128)(2,1)}, u32[]{:S(2)}) copy-start(bf16[1,256,2048]{2,1,0:T(8,128)(2,1)} %param.9) | copy-start | bytes 3145732
  15.0 16.7 %copy-start = (bf16[1,256,2048]{2,1,0:T(8,128)(2,1)S(1)}, bf16[1,256,2048]{2,1,0:T(8,128)(2,1)}, u32[]{:S(2)}) copy-start(bf16[1,256,2048]{2,1,0:T(8,128)(2,1)} %param.10) | copy-start | bytes 3145732
  15.0 6.9 %collective-permute-start.6 = (bf16[256,1024]{1,0:T(8,128)(2,1)S(1)}, bf16[256,1024]{1,0:T(8,128)(2,1)S(1)}, u32[]{:S(2)}, u32[]{:S(2)}) collective-permute-start(bf16[256,1024]{1,0:T(8,128)(2,1)S(1)} %get-tuple-element.43), channel_id=1, source_target_pairs={{0,1},{1,0},{2,3},{3,2},{4,5},{5,4},{6,7},{7,6},{8,9},{9,8},{10,11... | collective-permute-start | bytes 1572872 | tf_op jit(solution)/shard_map/key_exchange/ppermute | solution.py:38
  15.1 6.8 %collective-permute-start.7 = (bf16[48,1024]{1,0:T(8,128)(2,1)S(1)}, bf16[48,1024]{1,0:T(8,128)(2,1)S(1)}, u32[]{:S(2)}, u32[]{:S(2)}) collective-permute-start(bf16[48,1024]{1,0:T(8,128)(2,1)S(1)} %collective-permute-done.3.refs_2_.refs_3_), channel_id=1, source_target_pairs={{0,2},{1,3},{2,0},{3,1},{4,6},{5,7},{6,4},{7,5},{8,10},{9,11},{10,... | collective-permute-start | bytes 294920 | tf_op jit(solution)/shard_map/query_forward/ppermute | solution.py:43
  15.6 12.0 %collective-permute-start.10 = (bf16[48,1024]{1,0:T(8,128)(2,1)S(1)}, bf16[48,1024]{1,0:T(8,128)(2,1)S(1)}, u32[]{:S(2)}, u32[]{:S(2)}) collective-permute-start(bf16[48,1024]{1,0:T(8,128)(2,1)S(1)} %get-tuple-element.45.refs_6_), channel_id=1, source_target_pairs={{0,4},{1,5},{2,6},{3,7},{4,0},{5,1},{6,2},{7,3},{8,12},{9,13},{10,... | collective-permute-start | bytes 294920 | tf_op jit(solution)/shard_map/cotangent_gather/ppermute | solution.py:43
  17.5 10.2 %collective-permute-start.11 = (bf16[48,1024]{1,0:T(8,128)(2,1)S(1)}, bf16[48,1024]{1,0:T(8,128)(2,1)S(1)}, u32[]{:S(2)}, u32[]{:S(2)}) collective-permute-start(bf16[48,1024]{1,0:T(8,128)(2,1)S(1)} %get-tuple-element.45.refs_6_), channel_id=1, source_target_pairs={{0,2},{1,3},{2,0},{3,1},{4,6},{5,7},{6,4},{7,5},{8,10},{9,11},{10,... | collective-permute-start | bytes 294920 | tf_op jit(solution)/shard_map/cotangent_gather/ppermute | solution.py:43
  17.6 10.1 %collective-permute-start.12 = (bf16[48,1024]{1,0:T(8,128)(2,1)S(1)}, bf16[48,1024]{1,0:T(8,128)(2,1)S(1)}, u32[]{:S(2)}, u32[]{:S(2)}) collective-permute-start(bf16[48,1024]{1,0:T(8,128)(2,1)S(1)} %get-tuple-element.45.refs_6_), channel_id=1, source_target_pairs={{0,6},{1,7},{2,4},{3,5},{4,2},{5,3},{6,0},{7,1},{8,14},{9,15},{10,... | collective-permute-start | bytes 294920 | tf_op jit(solution)/shard_map/cotangent_gather/ppermute | solution.py:43
  22.9 4.1 %collective-permute-start.8 = (f32[8,256]{1,0:T(8,128)S(1)}, f32[8,256]{1,0:T(8,128)S(1)}, u32[]{:S(2)}, u32[]{:S(2)}) collective-permute-start(f32[8,256]{1,0:T(8,128)S(1)} %scores.1.own_ref), channel_id=1, source_target_pairs={{0,2},{1,3},{2,0},{3,1},{4,6},{5,7},{6,4},{7,5},{8,10},{9,11},{10,... | collective-permute-start | bytes 24584 | tf_op jit(solution)/shard_map/stats_exchange/ppermute | solution.py:43
  27.1 4.6 %collective-permute-start.9 = (f32[8,256]{1,0:T(8,128)S(1)}, f32[8,256]{1,0:T(8,128)S(1)}, u32[]{:S(2)}, u32[]{:S(2)}) collective-permute-start(f32[8,256]{1,0:T(8,128)S(1)} %merge_stats.1.refs_0_), channel_id=1, source_target_pairs={{0,4},{1,5},{2,6},{3,7},{4,0},{5,1},{6,2},{7,3},{8,12},{9,13},{10,... | collective-permute-start | bytes 24584 | tf_op jit(solution)/shard_map/stats_exchange/ppermute | solution.py:43
  34.3 8.1 %collective-permute-start.13 = (bf16[256,2048]{1,0:T(8,128)(2,1)S(1)}, bf16[256,2048]{1,0:T(8,128)(2,1)S(1)}, u32[]{:S(2)}, u32[]{:S(2)}) collective-permute-start(bf16[256,2048]{1,0:T(8,128)(2,1)S(1)} %get-tuple-element.48), channel_id=1, source_target_pairs={{0,1},{1,0},{2,3},{3,2},{4,5},{5,4},{6,7},{7,6},{8,9},{9,8},{10,11... | collective-permute-start | bytes 3145736 | tf_op jit(solution)/shard_map/key_grad_end/ppermute | solution.py:38
  34.3 9.9 %collective-permute-start.15 = (bf16[48,1024]{1,0:T(8,128)(2,1)S(1)}, bf16[48,1024]{1,0:T(8,128)(2,1)S(1)}, u32[]{:S(2)}, u32[]{:S(2)}) collective-permute-start(bf16[48,1024]{1,0:T(8,128)(2,1)S(1)} %get-tuple-element.52), channel_id=1, source_target_pairs={{0,6},{1,7},{2,4},{3,5},{4,2},{5,3},{6,0},{7,1},{8,14},{9,15},{10,... | collective-permute-start | bytes 294920 | tf_op jit(solution)/shard_map/query_grad_sum/ppermute | solution.py:43
  36.6 9.1 %collective-permute-start.16 = (bf16[48,1024]{1,0:T(8,128)(2,1)S(1)}, bf16[48,1024]{1,0:T(8,128)(2,1)S(1)}, u32[]{:S(2)}, u32[]{:S(2)}) collective-permute-start(bf16[48,1024]{1,0:T(8,128)(2,1)S(1)} %get-tuple-element.53), channel_id=1, source_target_pairs={{0,4},{1,5},{2,6},{3,7},{4,0},{5,1},{6,2},{7,3},{8,12},{9,13},{10,... | collective-permute-start | bytes 294920 | tf_op jit(solution)/shard_map/query_grad_sum/ppermute | solution.py:43
  36.6 9.1 %collective-permute-start.17 = (bf16[48,1024]{1,0:T(8,128)(2,1)S(1)}, bf16[48,1024]{1,0:T(8,128)(2,1)S(1)}, u32[]{:S(2)}, u32[]{:S(2)}) collective-permute-start(bf16[48,1024]{1,0:T(8,128)(2,1)S(1)} %get-tuple-element.54), channel_id=1, source_target_pairs={{0,2},{1,3},{2,0},{3,1},{4,6},{5,7},{6,4},{7,5},{8,10},{9,11},{10,... | collective-permute-start | bytes 294920 | tf_op jit(solution)/shard_map/query_grad_sum/ppermute | solution.py:43
  38.8 3.6 %collective-permute-start.14 = (f32[8,128]{1,0:T(8,128)S(1)}, f32[8,128]{1,0:T(8,128)S(1)}, u32[]{:S(2)}, u32[]{:S(2)}) collective-permute-start(f32[8,128]{1,0:T(8,128)S(1)} %get-tuple-element.49.refs_0_), channel_id=1, source_target_pairs={{0,16},{8,24},{16,0},{24,8},{1,17},{9,25},{17,1},{25,9},{2,18},{10... | collective-permute-start | bytes 12296 | tf_op jit(solution)/shard_map/key_grad_end/ppermute | solution.py:364
  45.8 1.3 %collective-permute-start.18 = (bf16[24,1024]{1,0:T(8,128)(2,1)S(1)}, bf16[24,1024]{1,0:T(8,128)(2,1)S(1)}, u32[]{:S(2)}, u32[]{:S(2)}) collective-permute-start(bf16[24,1024]{1,0:T(8,128)(2,1)S(1)} %get-tuple-element.56), channel_id=1, source_target_pairs={{0,1},{1,0},{2,3},{3,2},{4,5},{5,4},{6,7},{7,6},{8,9},{9,8},{10,11... | collective-permute-start | bytes 147464 | tf_op jit(solution)/shard_map/query_grad_end/ppermute | solution.py:38

commit v6 on v2

--- a/solution.py
+++ b/solution.py
@@ -106,7 +106,8 @@
 def join_queries_kernel(own_ref, other_ref, joined_ref):
     _, core = position()
     mine = pl.ds(pl.multiple_of(core * HALF, HALF), HALF)
-    joined_ref[...] = in_core_order(own_ref[:, mine], other_ref[:, mine], core)
+    joined = in_core_order(own_ref[:, mine], other_ref[:, mine], core)
+    joined_ref[...] = (joined.astype(F32) * ROOT).astype(BF16)
 
 
 def join_cotangents_kernel(own_ref, other_ref, joined_ref, delta_ref, count_ref):
@@ -180,7 +181,7 @@
     for head in range(HALF_HEADS):
         q = rows_of(blocks, head)
         scores = [
-            dot(k[:, columns_of(head)], q, NT) * ROOT + bias[...]
+            dot(k[:, columns_of(head)], q, NT) + bias[...]
             for k, bias in ((key_ref, bias_own), (other_ref, bias_other))
         ]
         top = functools.reduce(jnp.maximum, [jnp.max(s, axis=0, keepdims=True) for s in scores])
@@ -226,12 +227,12 @@
             (key_other, value_other, bias_other, send_ref),
         ):
             k, v = key[:, columns], value[:, value_columns_of(head)]
-            probs = jnp.exp(dot(k, q, NT) * ROOT + bias[...] - log_total[line])
+            probs = jnp.exp(dot(k, q, NT) + bias[...] - log_total[line])
             dscore = (probs * (dot(v, g, NT) - delta[line])).astype(BF16)
             dq += dot(dscore, k, TN)
-            out_ref[:, columns] = (dot(dscore, q, NN) * ROOT).astype(BF16)
+            out_ref[:, columns] = dot(dscore, q, NN).astype(BF16)
             out_ref[:, value_columns] = dot(probs.astype(BF16), g, NN).astype(BF16)
-        dq = (dq * ROOT).astype(BF16)
+        dq = dq.astype(BF16)
         for j, block in enumerate(dq_blocks):
             block[:, columns] = dq[j * rows : (j + 1) * rows]
 
@@ -250,7 +251,7 @@
 def query_end_kernel(factor_ref, *refs):
     parts, (send_ref, keep_ref) = refs[:-2], refs[-2:]
     _, core = position()
-    summed = factor_ref[0:1, 0:1] * sum(part[...].astype(F32) for part in parts)
+    summed = (factor_ref[0:1, 0:1] * ROOT) * sum(part[...].astype(F32) for part in parts)
     half = summed.shape[0] // 2
     low, high = summed[:half], summed[half:]
     send_ref[...] = jnp.where(core == 0, high, low).astype(BF16)
@@ -283,7 +284,7 @@
         while apart > 1:
             blocks += [across(one, apart) for one in blocks]
             apart //= 2
-        return blocks, across(block, 1)
+        return blocks, across(after(block, g_recv)[0], 1)
 
     def forwarded(blocks):
         return [across(one, 1) for one in blocks[1:]]
@@ -363,16 +364,16 @@
         rows_in_all = float(data_groups * dec_rows)
 
     with jax.named_scope("query_forward"):
-        q_far = [q_far[0], *(after(one, bias_own, count, q_near)[0] for one in q_far[1:])]
+        q_far = [q_far[0], *(after(one, bias_own, count)[0] for one in q_far[1:])]
         q_blocks = [*q_far, q_near, *forwarded(q_far)]
 
     with jax.named_scope("cotangent_gather"):
-        sent = after(g_block, *q_far, q_near)[0]
+        sent = after(g_block, *q_far)[0]
         g_blocks = [g_block] + [across(sent, offset) for offset in offsets[1:]]
 
     with jax.named_scope("key_exchange"):
         v_recv = to_sibling(value_rows)
-        k_send, v_recv, *_ = after(k_send, v_recv, *q_far, q_near)
+        k_send, v_recv, *_ = after(k_send, v_recv, *q_far)
         k_recv = to_sibling(k_send)
 
     with jax.named_scope("scores"):

time: 46.8 us -> 48.8 us (1.043)
  starting transfers between devices: 23.2 us -> 25.1 us
    ppermute x12, starting transfers between devices: 19.4 us -> 21.3 us  [across(): lax.ppermute(block, 'seq', [(i, i ^ 2 * apart) for i in range(count)])]
  transfers between devices with their start and end apart: 20 -> 20, of which waited for: 8 -> 8; matrix products, arithmetic and copies ran while one was open for 0% -> 0% of each run, Pallas kernels for 12% -> 11%
where the time goes in v6:
time: 48.8 us; the launch traced here: 48.6 us
  starting transfers between devices  25.1 us (51%)
  waiting for transfers between devices  12.1 us (25%)
  Pallas kernels  8.05 us (16%)
  local copies, waits for them, and re-layouts  1.91 us (4%)
  between operations  0.76 us (2%)
  other arithmetic  0.67 us (1%)
    ppermute x12, starting transfers between devices, across(): lax.ppermute(block, 'seq', [(i, i ^ 2 * apart) for i in range(count)])  21.3 us
    ppermute x12, waiting for transfers between devices, across(): lax.ppermute(block, 'seq', [(i, i ^ 2 * apart) for i in range(count)])  6.79 us
    ppermute x6, waiting for transfers between devices, to_sibling(): return lax.ppermute(block, 'seq', [(i, i ^ 1) for i in range(count)])  3.23 us
    ppermute x2, starting transfers between devices, over_groups(): lax.ppermute(count, 'dp', [(i, i ^ apart) for i in range(data_groups)])  3.01 us
    pallas_call x1, Pallas kernels, local(): kernel_call(functools.partial(grads_kernel, offsets), (block,) * chips +...  2.58 us
    ppermute x2, waiting for transfers between devices, over_groups(): lax.ppermute(count, 'dp', [(i, i ^ apart) for i in range(data_groups)])  2.09 us
    unnamed x14, local copies, waits for them, and re-layouts  1.91 us
    pallas_call x1, Pallas kernels, local(): kernel_call(functools.partial(key_end_kernel, rows_in_all), (whole, whole...  1.84 us
  transfers between devices with their start and end apart: 20, of which 8 were waited for; matrix products, arithmetic and copies ran while one was open for 0% of the time, Pallas kernels for 11%

profile of v6, /device:TPU:0, one launch (start us, length us, event | category | flops | bytes accessed | tf_op | source)
XLA Modules:
  0.0 48.6 jit_solution(6468734763013164775)
XLA Ops:
  0.6 0.5 %collective-permute-start.2 = (bf16[256,2048]{1,0:T(8,128)(2,1)}, bf16[256,2048]{1,0:T(8,128)(2,1)S(1)}, u32[]{:S(2)}, u32[]{:S(2)}) collective-permute-start(bf16[256,2048]{1,0:T(8,128)(2,1)} %bitcast.11), channel_id=1, source_target_pairs={{0,1},{1,0},{2,3},{3,2},{4,5},{5,4},{6,7},{7,6},{8,9},{9,8},{10,11... | collective-permute-start | bytes 3145736 | tf_op jit(solution)/shard_map/key_exchange/ppermute | solution.py:38
  1.1 0.1 collective-permute-start
  1.2 1.8 %prepare.1 = (bf16[24,1152]{1,0:T(8,128)(2,1)}, bf16[24,1152]{1,0:T(8,128)(2,1)}) custom-call(bf16[24,2048]{1,0:T(8,128)(2,1)} %bitcast.19, bf16[24,2048]{1,0:T(8,128)(2,1)} %bitcast.20, s32[1,24]{1,0:T(1,128)} %mask_ref.1), custom_call_target="tpu_custom_call" | custom-call | flops 100000 | bytes 1000000 | tf_op jit(solution)/shard_map/sibling_exchange/prepare/pallas_call | solution.py:304
  3.0 0.8 %collective-permute-done.other_ref = bf16[24,2048]{1,0:T(8,128)(2,1)S(1)} collective-permute-done((bf16[24,2048]{1,0:T(8,128)(2,1)}, bf16[24,2048]{1,0:T(8,128)(2,1)S(1)}, u32[]{:S(2)}, u32[]{:S(2)}) %collective-permute-start) | collective-permute-done | bytes 98336 | tf_op jit(solution)/shard_map/sibling_exchange/ppermute | solution.py:38
  3.8 4.0 %collective-permute-start.3 = (bf16[48,1024]{1,0:T(8,128)(2,1)S(1)}, bf16[48,1024]{1,0:T(8,128)(2,1)S(1)}, u32[]{:S(2)}, u32[]{:S(2)}) collective-permute-start(bf16[48,1024]{1,0:T(8,128)(2,1)S(1)} %join_queries.1.refs_1_.refs_4_), channel_id=1, source_target_pairs={{0,4},{1,5},{2,6},{3,7},{4,0},{5,1},{6,2},{7,3},{8,12},{9,13},{10,... | collective-permute-start | bytes 294920 | tf_op jit(solution)/shard_map/query_gather/ppermute | solution.py:43
  7.9 0.0 collective-permute-start.1
  7.9 1.2 %collective-permute-done.1.other_ref = bf16[24,1152]{1,0:T(8,128)(2,1)S(1)} collective-permute-done((bf16[24,1152]{1,0:T(8,128)(2,1)S(1)}, bf16[24,1152]{1,0:T(8,128)(2,1)S(1)}, u32[]{:S(2)}, u32[]{:S(2)}) %collective-permute-start.1) | collective-permute-done | bytes 55328 | tf_op jit(solution)/shard_map/sibling_exchange/ppermute | solution.py:38
  9.1 0.2 join_cotangents.1
  9.3 1.5 %collective-permute-start.4 = (f32[8,128]{1,0:T(8,128)S(1)}, f32[8,128]{1,0:T(8,128)S(1)}, u32[]{:S(2)}, u32[]{:S(2)}) collective-permute-start(f32[8,128]{1,0:T(8,128)S(1)} %get-tuple-element.41), channel_id=1, source_target_pairs={{0,8},{8,0},{16,24},{24,16},{1,9},{9,1},{17,25},{25,17},{2,10},{10... | collective-permute-start | bytes 12296 | tf_op jit(solution)/shard_map/mask_count/ppermute | solution.py:357
  10.8 0.7 %copy-done.4 = s32[1,1,4]{2,1,0:T(1,128)S(1)} copy-done((s32[1,1,4]{2,1,0:T(1,128)S(1)}, s32[1,1,4]{2,1,0:T(1,128)}, u32[]{:S(2)}) %copy-start.4) | copy-done | bytes 40
  11.4 0.0 copy-done.5
  11.4 1.2 %copy-done.1 = bf16[1,256,2048]{2,1,0:T(8,128)(2,1)S(1)} copy-done((bf16[1,256,2048]{2,1,0:T(8,128)(2,1)S(1)}, bf16[1,256,2048]{2,1,0:T(8,128)(2,1)}, u32[]{:S(2)}) %copy-start.1) | copy-done | bytes 1048600
  12.7 0.7 %setup.1 = (bf16[256,1024]{1,0:T(8,128)(2,1)S(1)}, bf16[256,1024]{1,0:T(8,128)(2,1)S(1)}, f32[256,192]{1,0:T(8,128)S(1)}, f32[256,192]{1,0:T(8,128)S(1)}) custom-call(s32[1,4]{1,0:T(1,128)S(1)} %bitcast.17, s32[1,4]{1,0:T(1,128)S(1)} %bitcast.18, bf16[256,2048]{1,0:T(8,128)(2,1)S(1)} %bitcast.13), custom_call_target="tpu_custom_call" | custom-call | flops 1000000 | bytes 4194304 | tf_op jit(solution)/shard_map/setup/setup/pallas_call | solution.py:332
  13.4 0.0 copy-start
  13.4 0.0 collective-permute-done.4
  13.4 0.0 collective-permute-done.3.refs_2_.refs_5_
  13.4 0.0 collective-permute-done.2.refs_15_
  13.4 0.1 collective-permute-start.5
  13.5 1.6 %collective-permute-start.6 = (bf16[48,1024]{1,0:T(8,128)(2,1)S(1)}, bf16[48,1024]{1,0:T(8,128)(2,1)S(1)}, u32[]{:S(2)}, u32[]{:S(2)}) collective-permute-start(bf16[48,1024]{1,0:T(8,128)(2,1)S(1)} %join_queries.1.refs_1_.refs_4_), channel_id=1, source_target_pairs={{0,2},{1,3},{2,0},{3,1},{4,6},{5,7},{6,4},{7,5},{8,10},{9,11},{10,... | collective-permute-start | bytes 294920 | tf_op jit(solution)/shard_map/query_gather/ppermute | solution.py:43
  15.2 0.4 collective-permute-start.7
  15.6 1.6 %collective-permute-start.11 = (bf16[48,1024]{1,0:T(8,128)(2,1)S(1)}, bf16[48,1024]{1,0:T(8,128)(2,1)S(1)}, u32[]{:S(2)}, u32[]{:S(2)}) collective-permute-start(bf16[48,1024]{1,0:T(8,128)(2,1)S(1)} %get-tuple-element.47.refs_8_), channel_id=1, source_target_pairs={{0,4},{1,5},{2,6},{3,7},{4,0},{5,1},{6,2},{7,3},{8,12},{9,13},{10,... | collective-permute-start | bytes 294920 | tf_op jit(solution)/shard_map/cotangent_gather/ppermute | solution.py:43
  17.2 2.0 %collective-permute-start.12 = (bf16[48,1024]{1,0:T(8,128)(2,1)S(1)}, bf16[48,1024]{1,0:T(8,128)(2,1)S(1)}, u32[]{:S(2)}, u32[]{:S(2)}) collective-permute-start(bf16[48,1024]{1,0:T(8,128)(2,1)S(1)} %get-tuple-element.47.refs_8_), channel_id=1, source_target_pairs={{0,2},{1,3},{2,0},{3,1},{4,6},{5,7},{6,4},{7,5},{8,10},{9,11},{10,... | collective-permute-start | bytes 294920 | tf_op jit(solution)/shard_map/cotangent_gather/ppermute | solution.py:43
  19.2 2.1 %collective-permute-done.6.refs_3_.refs_6_ = bf16[48,1024]{1,0:T(8,128)(2,1)S(1)} collective-permute-done((bf16[48,1024]{1,0:T(8,128)(2,1)S(1)}, bf16[48,1024]{1,0:T(8,128)(2,1)S(1)}, u32[]{:S(2)}, u32[]{:S(2)}) %collective-permute-start.6) | collective-permute-done | bytes 98336 | tf_op jit(solution)/shard_map/query_gather/ppermute | solution.py:43
  21.3 2.7 %collective-permute-start.13 = (bf16[48,1024]{1,0:T(8,128)(2,1)S(1)}, bf16[48,1024]{1,0:T(8,128)(2,1)S(1)}, u32[]{:S(2)}, u32[]{:S(2)}) collective-permute-start(bf16[48,1024]{1,0:T(8,128)(2,1)S(1)} %get-tuple-element.47.refs_8_), channel_id=1, source_target_pairs={{0,6},{1,7},{2,4},{3,5},{4,2},{5,3},{6,0},{7,1},{8,14},{9,15},{10,... | collective-permute-start | bytes 294920 | tf_op jit(solution)/shard_map/cotangent_gather/ppermute | solution.py:43
  23.9 0.0 collective-permute-done.7.refs_4_.refs_7_
  24.0 0.0 collective-permute-done.5.other_ref.refs_13_
  24.0 0.9 %scores.1.refs_0_ = f32[8,256]{1,0:T(8,128)S(1)} custom-call(f32[8,48]{1,0:T(8,128)S(1)} %get-tuple-element.38.delta_ref, f32[256,192]{1,0:T(8,128)S(1)} %get-tuple-element.35.bias_own, f32[256,192]{1,0:T(8,128)S(1)} %get-tuple-element.36.bias_other, bf16[256,1024]{1,0:T(8,128)(2,1)S(1)} %get-tuple-element.39.key_ref.refs_12_, ...), custom_call_target="tpu_custom_call" | custom-call | flops 201326592 | bytes 1441792 | tf_op jit(solution)/shard_map/scores/scores/pallas_call | solution.py:381
  24.8 2.5 %collective-permute-start.10 = (f32[8,256]{1,0:T(8,128)S(1)}, f32[8,256]{1,0:T(8,128)S(1)}, u32[]{:S(2)}, u32[]{:S(2)}) collective-permute-start(f32[8,256]{1,0:T(8,128)S(1)} %scores.1.refs_0_), channel_id=1, source_target_pairs={{0,6},{1,7},{2,4},{3,5},{4,2},{5,3},{6,0},{7,1},{8,14},{9,15},{10,... | collective-permute-start | bytes 24584 | tf_op jit(solution)/shard_map/stats_exchange/ppermute | solution.py:43
  27.3 0.0 collective-permute-start.8
  27.3 0.0 collective-permute-done.11.refs_9_
  27.3 2.0 %collective-permute-start.9 = (f32[8,256]{1,0:T(8,128)S(1)}, f32[8,256]{1,0:T(8,128)S(1)}, u32[]{:S(2)}, u32[]{:S(2)}) collective-permute-start(f32[8,256]{1,0:T(8,128)S(1)} %scores.1.refs_0_), channel_id=1, source_target_pairs={{0,2},{1,3},{2,0},{3,1},{4,6},{5,7},{6,4},{7,5},{8,10},{9,11},{10,... | collective-permute-start | bytes 24584 | tf_op jit(solution)/shard_map/stats_exchange/ppermute | solution.py:43
  29.3 1.1 %collective-permute-done.10.refs_3_ = f32[8,256]{1,0:T(8,128)S(1)} collective-permute-done((f32[8,256]{1,0:T(8,128)S(1)}, f32[8,256]{1,0:T(8,128)S(1)}, u32[]{:S(2)}, u32[]{:S(2)}) %collective-permute-start.10) | collective-permute-done | bytes 8224 | tf_op jit(solution)/shard_map/stats_exchange/ppermute | solution.py:43
  30.3 1.5 %collective-permute-done.8.refs_1_ = f32[8,256]{1,0:T(8,128)S(1)} collective-permute-done((f32[8,256]{1,0:T(8,128)S(1)}, f32[8,256]{1,0:T(8,128)S(1)}, u32[]{:S(2)}, u32[]{:S(2)}) %collective-permute-start.8) | collective-permute-done | bytes 8224 | tf_op jit(solution)/shard_map/stats_exchange/ppermute | solution.py:43
  31.9 2.6 %grads.1 = (bf16[48,1024]{1,0:T(8,128)(2,1)S(1)}, bf16[48,1024]{1,0:T(8,128)(2,1)S(1)}, bf16[48,1024]{1,0:T(8,128)(2,1)S(1)}, bf16[48,1024]{1,0:T(8,128)(2,1)S(1...) custom-call(f32[256,192]{1,0:T(8,128)S(1)} %get-tuple-element.35.bias_own, ...), custom_call_target="tpu_custom_call" | custom-call | flops 1006632960 | bytes 4980736 | tf_op jit(solution)/shard_map/grads/grads/pallas_call | solution.py:397
  34.4 0.1 collective-permute-start.14
  34.5 1.5 %collective-permute-start.16 = (bf16[48,1024]{1,0:T(8,128)(2,1)S(1)}, bf16[48,1024]{1,0:T(8,128)(2,1)S(1)}, u32[]{:S(2)}, u32[]{:S(2)}) collective-permute-start(bf16[48,1024]{1,0:T(8,128)(2,1)S(1)} %get-tuple-element.54), channel_id=1, source_target_pairs={{0,6},{1,7},{2,4},{3,5},{4,2},{5,3},{6,0},{7,1},{8,14},{9,15},{10,... | collective-permute-start | bytes 294920 | tf_op jit(solution)/shard_map/query_grad_sum/ppermute | solution.py:43
  36.1 1.0 %collective-permute-start.17 = (bf16[48,1024]{1,0:T(8,128)(2,1)S(1)}, bf16[48,1024]{1,0:T(8,128)(2,1)S(1)}, u32[]{:S(2)}, u32[]{:S(2)}) collective-permute-start(bf16[48,1024]{1,0:T(8,128)(2,1)S(1)} %get-tuple-element.55), channel_id=1, source_target_pairs={{0,4},{1,5},{2,6},{3,7},{4,0},{5,1},{6,2},{7,3},{8,12},{9,13},{10,... | collective-permute-start | bytes 294920 | tf_op jit(solution)/shard_map/query_grad_sum/ppermute | solution.py:43
  37.1 1.9 %collective-permute-start.18 = (bf16[48,1024]{1,0:T(8,128)(2,1)S(1)}, bf16[48,1024]{1,0:T(8,128)(2,1)S(1)}, u32[]{:S(2)}, u32[]{:S(2)}) collective-permute-start(bf16[48,1024]{1,0:T(8,128)(2,1)S(1)} %get-tuple-element.56), channel_id=1, source_target_pairs={{0,2},{1,3},{2,0},{3,1},{4,6},{5,7},{6,4},{7,5},{8,10},{9,11},{10,... | collective-permute-start | bytes 294920 | tf_op jit(solution)/shard_map/query_grad_sum/ppermute | solution.py:43
  39.0 1.5 %collective-permute-start.15 = (f32[8,128]{1,0:T(8,128)S(1)}, f32[8,128]{1,0:T(8,128)S(1)}, u32[]{:S(2)}, u32[]{:S(2)}) collective-permute-start(f32[8,128]{1,0:T(8,128)S(1)} %get-tuple-element.51.refs_0_), channel_id=1, source_target_pairs={{0,16},{8,24},{16,0},{24,8},{1,17},{9,25},{17,1},{25,9},{2,18},{10... | collective-permute-start | bytes 12296 | tf_op jit(solution)/shard_map/key_grad_end/ppermute | solution.py:357
  40.5 2.1 %collective-permute-done.15.refs_1_ = f32[8,128]{1,0:T(8,128)S(1)} collective-permute-done((f32[8,128]{1,0:T(8,128)S(1)}, f32[8,128]{1,0:T(8,128)S(1)}, u32[]{:S(2)}, u32[]{:S(2)}) %collective-permute-start.15) | collective-permute-done | bytes 4128 | tf_op jit(solution)/shard_map/key_grad_end/ppermute | solution.py:357
  42.6 0.0 collective-permute-done.14.other_ref
  42.6 1.8 %key_end.1 = (bf16[256,2048]{1,0:T(8,128)(2,1)}, bf16[256,2048]{1,0:T(8,128)(2,1)}, f32[8,128]{1,0:T(8,128)S(1)}) custom-call(bf16[256,2048]{1,0:T(8,128)(2,1)S(1)} %get-tuple-element.49.keep_ref, bf16[256,2048]{1,0:T(8,128)(2,1)S(1)} %collective-permute-done.14.other_ref, f32[8,128]{1,0:T(8,128)S(1)} %get-tuple-element.51.refs_0_, ...), custom_call_target="tpu_custom_call" | custom-call | flops 1000000 | bytes 4194304 | tf_op jit(solution)/shard_map/key_grad_end/key_end/pallas_call | solution.py:417
  44.4 0.0 collective-permute-done.16.refs_1_
  44.4 2.1 %collective-permute-done.17.refs_2_ = bf16[48,1024]{1,0:T(8,128)(2,1)S(1)} collective-permute-done((bf16[48,1024]{1,0:T(8,128)(2,1)S(1)}, bf16[48,1024]{1,0:T(8,128)(2,1)S(1)}, u32[]{:S(2)}, u32[]{:S(2)}) %collective-permute-start.17) | collective-permute-done | bytes 98336 | tf_op jit(solution)/shard_map/query_grad_sum/ppermute | solution.py:43
  46.6 0.1 query_end.1
  46.6 0.1 collective-permute-start.19
  46.7 1.2 %collective-permute-done.19 = bf16[24,1024]{1,0:T(8,128)(2,1)S(1)} collective-permute-done((bf16[24,1024]{1,0:T(8,128)(2,1)S(1)}, bf16[24,1024]{1,0:T(8,128)(2,1)S(1)}, u32[]{:S(2)}, u32[]{:S(2)}) %collective-permute-start.19) | collective-permute-done | bytes 49184 | tf_op jit(solution)/shard_map/query_grad_end/ppermute | solution.py:38
  47.9 0.7 %maximum_select_fusion = bf16[1,24,2048]{2,1,0:T(8,128)(2,1)} fusion(bf16[1,24,1024]{2,1,0:T(8,128)(2,1)S(1)} %bitcast.21, bf16[1,24,1024]{2,1,0:T(8,128)(2,1)S(1)} %bitcast.16, pred[]{:T(512)S(6)} %eq.3), kind=kLoop, calls=%fused_computation | loop fusion | flops 442368 | bytes 196609 | tf_op jit(solution)/shard_map/query_grad_end/jit(_where)/select_n | solution.py:262
  (16 shorter events, 0.1 us)
Async XLA Ops:
  0.6 12.8 %collective-permute-start.2 = (bf16[256,2048]{1,0:T(8,128)(2,1)}, bf16[256,2048]{1,0:T(8,128)(2,1)S(1)}, u32[]{:S(2)}, u32[]{:S(2)}) collective-permute-start(bf16[256,2048]{1,0:T(8,128)(2,1)} %bitcast.11), channel_id=1, source_target_pairs={{0,1},{1,0},{2,3},{3,2},{4,5},{5,4},{6,7},{7,6},{8,9},{9,8},{10,11... | collective-permute-start | bytes 3145736 | tf_op jit(solution)/shard_map/key_exchange/ppermute | solution.py:38
  1.1 2.6 %collective-permute-start = (bf16[24,2048]{1,0:T(8,128)(2,1)}, bf16[24,2048]{1,0:T(8,128)(2,1)S(1)}, u32[]{:S(2)}, u32[]{:S(2)}) collective-permute-start(bf16[24,2048]{1,0:T(8,128)(2,1)} %bitcast.14), channel_id=1, source_target_pairs={{0,1},{1,0},{2,3},{3,2},{4,5},{5,4},{6,7},{7,6},{8,9},{9,8},{10,11... | collective-permute-start | bytes 294920 | tf_op jit(solution)/shard_map/sibling_exchange/ppermute | solution.py:38
  1.2 2.6 %copy-start.2 = (bf16[1,24,2048]{2,1,0:T(8,128)(2,1)S(1)}, bf16[1,24,2048]{2,1,0:T(8,128)(2,1)}, u32[]{:S(2)}) copy-start(bf16[1,24,2048]{2,1,0:T(8,128)(2,1)} %param.8) | copy-start | bytes 294916
  3.8 4.1 %copy-start.6 = (bf16[24,1152]{1,0:T(8,128)(2,1)S(1)}, bf16[24,1152]{1,0:T(8,128)(2,1)}, u32[]{:S(2)}) copy-start(bf16[24,1152]{1,0:T(8,128)(2,1)} %get-tuple-element.37) | copy-start | bytes 165892
  3.8 5.3 %copy-start.3 = (bf16[24,1152]{1,0:T(8,128)(2,1)S(1)}, bf16[24,1152]{1,0:T(8,128)(2,1)}, u32[]{:S(2)}) copy-start(bf16[24,1152]{1,0:T(8,128)(2,1)} %get-tuple-element.32.own_ref) | copy-start | bytes 165892
  3.8 9.6 %collective-permute-start.3 = (bf16[48,1024]{1,0:T(8,128)(2,1)S(1)}, bf16[48,1024]{1,0:T(8,128)(2,1)S(1)}, u32[]{:S(2)}, u32[]{:S(2)}) collective-permute-start(bf16[48,1024]{1,0:T(8,128)(2,1)S(1)} %join_queries.1.refs_1_.refs_4_), channel_id=1, source_target_pairs={{0,4},{1,5},{2,6},{3,7},{4,0},{5,1},{6,2},{7,3},{8,12},{9,13},{10,... | collective-permute-start | bytes 294920 | tf_op jit(solution)/shard_map/query_gather/ppermute | solution.py:43
  7.9 1.2 %collective-permute-start.1 = (bf16[24,1152]{1,0:T(8,128)(2,1)S(1)}, bf16[24,1152]{1,0:T(8,128)(2,1)S(1)}, u32[]{:S(2)}, u32[]{:S(2)}) collective-permute-start(bf16[24,1152]{1,0:T(8,128)(2,1)S(1)} %copy-done.6), channel_id=1, source_target_pairs={{0,1},{1,0},{2,3},{3,2},{4,5},{5,4},{6,7},{7,6},{8,9},{9,8},{10,11... | collective-permute-start | bytes 165896 | tf_op jit(solution)/shard_map/sibling_exchange/ppermute | solution.py:38
  9.3 4.1 %collective-permute-start.4 = (f32[8,128]{1,0:T(8,128)S(1)}, f32[8,128]{1,0:T(8,128)S(1)}, u32[]{:S(2)}, u32[]{:S(2)}) collective-permute-start(f32[8,128]{1,0:T(8,128)S(1)} %get-tuple-element.41), channel_id=1, source_target_pairs={{0,8},{8,0},{16,24},{24,16},{1,9},{9,1},{17,25},{25,17},{2,10},{10... | collective-permute-start | bytes 12296 | tf_op jit(solution)/shard_map/mask_count/ppermute | solution.py:357
  10.8 0.7 %copy-start.4 = (s32[1,1,4]{2,1,0:T(1,128)S(1)}, s32[1,1,4]{2,1,0:T(1,128)}, u32[]{:S(2)}) copy-start(s32[1,1,4]{2,1,0:T(1,128)} %param.14) | copy-start | bytes 52
  10.8 0.7 %copy-start.5 = (s32[1,1,4]{2,1,0:T(1,128)S(1)}, s32[1,1,4]{2,1,0:T(1,128)}, u32[]{:S(2)}) copy-start(s32[1,1,4]{2,1,0:T(1,128)} %param.15) | copy-start | bytes 52
  11.4 1.2 %copy-start.1 = (bf16[1,256,2048]{2,1,0:T(8,128)(2,1)S(1)}, bf16[1,256,2048]{2,1,0:T(8,128)(2,1)}, u32[]{:S(2)}) copy-start(bf16[1,256,2048]{2,1,0:T(8,128)(2,1)} %param.9) | copy-start | bytes 3145732
  13.4 18.5 %copy-start = (bf16[1,256,2048]{2,1,0:T(8,128)(2,1)S(1)}, bf16[1,256,2048]{2,1,0:T(8,128)(2,1)}, u32[]{:S(2)}) copy-start(bf16[1,256,2048]{2,1,0:T(8,128)(2,1)} %param.10) | copy-start | bytes 3145732
  13.4 10.5 %collective-permute-start.5 = (bf16[256,1024]{1,0:T(8,128)(2,1)S(1)}, bf16[256,1024]{1,0:T(8,128)(2,1)S(1)}, u32[]{:S(2)}, u32[]{:S(2)}) collective-permute-start(bf16[256,1024]{1,0:T(8,128)(2,1)S(1)} %get-tuple-element.44), channel_id=1, source_target_pairs={{0,1},{1,0},{2,3},{3,2},{4,5},{5,4},{6,7},{7,6},{8,9},{9,8},{10,11... | collective-permute-start | bytes 1572872 | tf_op jit(solution)/shard_map/key_exchange/ppermute | solution.py:38
  13.5 7.8 %collective-permute-start.6 = (bf16[48,1024]{1,0:T(8,128)(2,1)S(1)}, bf16[48,1024]{1,0:T(8,128)(2,1)S(1)}, u32[]{:S(2)}, u32[]{:S(2)}) collective-permute-start(bf16[48,1024]{1,0:T(8,128)(2,1)S(1)} %join_queries.1.refs_1_.refs_4_), channel_id=1, source_target_pairs={{0,2},{1,3},{2,0},{3,1},{4,6},{5,7},{6,4},{7,5},{8,10},{9,11},{10,... | collective-permute-start | bytes 294920 | tf_op jit(solution)/shard_map/query_gather/ppermute | solution.py:43
  15.2 8.8 %collective-permute-start.7 = (bf16[48,1024]{1,0:T(8,128)(2,1)S(1)}, bf16[48,1024]{1,0:T(8,128)(2,1)S(1)}, u32[]{:S(2)}, u32[]{:S(2)}) collective-permute-start(bf16[48,1024]{1,0:T(8,128)(2,1)S(1)} %collective-permute-done.3.refs_2_.refs_5_), channel_id=1, source_target_pairs={{0,2},{1,3},{2,0},{3,1},{4,6},{5,7},{6,4},{7,5},{8,10},{9,11},{10,... | collective-permute-start | bytes 294920 | tf_op jit(solution)/shard_map/query_forward/ppermute | solution.py:43
  15.6 11.7 %collective-permute-start.11 = (bf16[48,1024]{1,0:T(8,128)(2,1)S(1)}, bf16[48,1024]{1,0:T(8,128)(2,1)S(1)}, u32[]{:S(2)}, u32[]{:S(2)}) collective-permute-start(bf16[48,1024]{1,0:T(8,128)(2,1)S(1)} %get-tuple-element.47.refs_8_), channel_id=1, source_target_pairs={{0,4},{1,5},{2,6},{3,7},{4,0},{5,1},{6,2},{7,3},{8,12},{9,13},{10,... | collective-permute-start | bytes 294920 | tf_op jit(solution)/shard_map/cotangent_gather/ppermute | solution.py:43
  17.2 12.0 %collective-permute-start.12 = (bf16[48,1024]{1,0:T(8,128)(2,1)S(1)}, bf16[48,1024]{1,0:T(8,128)(2,1)S(1)}, u32[]{:S(2)}, u32[]{:S(2)}) collective-permute-start(bf16[48,1024]{1,0:T(8,128)(2,1)S(1)} %get-tuple-element.47.refs_8_), channel_id=1, source_target_pairs={{0,2},{1,3},{2,0},{3,1},{4,6},{5,7},{6,4},{7,5},{8,10},{9,11},{10,... | collective-permute-start | bytes 294920 | tf_op jit(solution)/shard_map/cotangent_gather/ppermute | solution.py:43
  21.3 8.0 %collective-permute-start.13 = (bf16[48,1024]{1,0:T(8,128)(2,1)S(1)}, bf16[48,1024]{1,0:T(8,128)(2,1)S(1)}, u32[]{:S(2)}, u32[]{:S(2)}) collective-permute-start(bf16[48,1024]{1,0:T(8,128)(2,1)S(1)} %get-tuple-element.47.refs_8_), channel_id=1, source_target_pairs={{0,6},{1,7},{2,4},{3,5},{4,2},{5,3},{6,0},{7,1},{8,14},{9,15},{10,... | collective-permute-start | bytes 294920 | tf_op jit(solution)/shard_map/cotangent_gather/ppermute | solution.py:43
  24.8 5.5 %collective-permute-start.10 = (f32[8,256]{1,0:T(8,128)S(1)}, f32[8,256]{1,0:T(8,128)S(1)}, u32[]{:S(2)}, u32[]{:S(2)}) collective-permute-start(f32[8,256]{1,0:T(8,128)S(1)} %scores.1.refs_0_), channel_id=1, source_target_pairs={{0,6},{1,7},{2,4},{3,5},{4,2},{5,3},{6,0},{7,1},{8,14},{9,15},{10,... | collective-permute-start | bytes 24584 | tf_op jit(solution)/shard_map/stats_exchange/ppermute | solution.py:43
  27.3 4.5 %collective-permute-start.8 = (f32[8,256]{1,0:T(8,128)S(1)}, f32[8,256]{1,0:T(8,128)S(1)}, u32[]{:S(2)}, u32[]{:S(2)}) collective-permute-start(f32[8,256]{1,0:T(8,128)S(1)} %scores.1.refs_0_), channel_id=1, source_target_pairs={{0,4},{1,5},{2,6},{3,7},{4,0},{5,1},{6,2},{7,3},{8,12},{9,13},{10,... | collective-permute-start | bytes 24584 | tf_op jit(solution)/shard_map/stats_exchange/ppermute | solution.py:43
  27.3 4.5 %collective-permute-start.9 = (f32[8,256]{1,0:T(8,128)S(1)}, f32[8,256]{1,0:T(8,128)S(1)}, u32[]{:S(2)}, u32[]{:S(2)}) collective-permute-start(f32[8,256]{1,0:T(8,128)S(1)} %scores.1.refs_0_), channel_id=1, source_target_pairs={{0,2},{1,3},{2,0},{3,1},{4,6},{5,7},{6,4},{7,5},{8,10},{9,11},{10,... | collective-permute-start | bytes 24584 | tf_op jit(solution)/shard_map/stats_exchange/ppermute | solution.py:43
  34.4 8.1 %collective-permute-start.14 = (bf16[256,2048]{1,0:T(8,128)(2,1)S(1)}, bf16[256,2048]{1,0:T(8,128)(2,1)S(1)}, u32[]{:S(2)}, u32[]{:S(2)}) collective-permute-start(bf16[256,2048]{1,0:T(8,128)(2,1)S(1)} %get-tuple-element.50), channel_id=1, source_target_pairs={{0,1},{1,0},{2,3},{3,2},{4,5},{5,4},{6,7},{7,6},{8,9},{9,8},{10,11... | collective-permute-start | bytes 3145736 | tf_op jit(solution)/shard_map/key_grad_end/ppermute | solution.py:38
  34.5 9.9 %collective-permute-start.16 = (bf16[48,1024]{1,0:T(8,128)(2,1)S(1)}, bf16[48,1024]{1,0:T(8,128)(2,1)S(1)}, u32[]{:S(2)}, u32[]{:S(2)}) collective-permute-start(bf16[48,1024]{1,0:T(8,128)(2,1)S(1)} %get-tuple-element.54), channel_id=1, source_target_pairs={{0,6},{1,7},{2,4},{3,5},{4,2},{5,3},{6,0},{7,1},{8,14},{9,15},{10,... | collective-permute-start | bytes 294920 | tf_op jit(solution)/shard_map/query_grad_sum/ppermute | solution.py:43
  36.1 10.5 %collective-permute-start.17 = (bf16[48,1024]{1,0:T(8,128)(2,1)S(1)}, bf16[48,1024]{1,0:T(8,128)(2,1)S(1)}, u32[]{:S(2)}, u32[]{:S(2)}) collective-permute-start(bf16[48,1024]{1,0:T(8,128)(2,1)S(1)} %get-tuple-element.55), channel_id=1, source_target_pairs={{0,4},{1,5},{2,6},{3,7},{4,0},{5,1},{6,2},{7,3},{8,12},{9,13},{10,... | collective-permute-start | bytes 294920 | tf_op jit(solution)/shard_map/query_grad_sum/ppermute | solution.py:43
  37.1 9.4 %collective-permute-start.18 = (bf16[48,1024]{1,0:T(8,128)(2,1)S(1)}, bf16[48,1024]{1,0:T(8,128)(2,1)S(1)}, u32[]{:S(2)}, u32[]{:S(2)}) collective-permute-start(bf16[48,1024]{1,0:T(8,128)(2,1)S(1)} %get-tuple-element.56), channel_id=1, source_target_pairs={{0,2},{1,3},{2,0},{3,1},{4,6},{5,7},{6,4},{7,5},{8,10},{9,11},{10,... | collective-permute-start | bytes 294920 | tf_op jit(solution)/shard_map/query_grad_sum/ppermute | solution.py:43
  39.0 3.6 %collective-permute-start.15 = (f32[8,128]{1,0:T(8,128)S(1)}, f32[8,128]{1,0:T(8,128)S(1)}, u32[]{:S(2)}, u32[]{:S(2)}) collective-permute-start(f32[8,128]{1,0:T(8,128)S(1)} %get-tuple-element.51.refs_0_), channel_id=1, source_target_pairs={{0,16},{8,24},{16,0},{24,8},{1,17},{9,25},{17,1},{25,9},{2,18},{10... | collective-permute-start | bytes 12296 | tf_op jit(solution)/shard_map/key_grad_end/ppermute | solution.py:357
  46.6 1.3 %collective-permute-start.19 = (bf16[24,1024]{1,0:T(8,128)(2,1)S(1)}, bf16[24,1024]{1,0:T(8,128)(2,1)S(1)}, u32[]{:S(2)}, u32[]{:S(2)}) collective-permute-start(bf16[24,1024]{1,0:T(8,128)(2,1)S(1)} %get-tuple-element.58), channel_id=1, source_target_pairs={{0,1},{1,0},{2,3},{3,2},{4,5},{5,4},{6,7},{7,6},{8,9},{9,8},{10,11... | collective-permute-start | bytes 147464 | tf_op jit(solution)/shard_map/query_grad_end/ppermute | solution.py:38

commit v7 on v2

--- a/solution.py
+++ b/solution.py
@@ -207,7 +207,8 @@
 
 def grads_kernel(offsets, bias_own, bias_other, *refs):
     chips = len(offsets)
-    stats, refs = refs[:chips], refs[chips:]
+    order = [0, *sorted(offsets[1:], reverse=True)]
+    stats, refs = [refs[order.index(offset)] for offset in offsets], refs[chips:]
     q_blocks, refs = refs[:chips], refs[chips:]
     g_blocks, refs = refs[:chips], refs[chips:]
     (key_ref, key_other, value_ref, value_other), refs = refs[:4], refs[4:]
@@ -389,7 +390,8 @@
         )(delta, bias_own, bias_other, k_own, k_recv, count, *q_blocks)
 
     with jax.named_scope("stats_exchange"):
-        all_stats = [stats] + [across(stats, offset) for offset in offsets[1:]]
+        order = [0, *sorted(offsets[1:], reverse=True)]
+        all_stats = [stats] + [across(stats, offset) for offset in order[1:]]
 
     with jax.named_scope("grads"):
         both = shaped(enc_local, 2 * HALF)

time: 46.8 us -> 46.7 us (level)
  starting transfers between devices: 23.2 us -> 22.3 us
  waiting for transfers between devices: 12 us -> 12.8 us
    ppermute x12, starting transfers between devices: 19.4 us -> 18.5 us  [across(): lax.ppermute(block, 'seq', [(i, i ^ 2 * apart) for i in range(count)])]
    ppermute x12, waiting for transfers between devices: 6.65 us -> 7.46 us  [across(): lax.ppermute(block, 'seq', [(i, i ^ 2 * apart) for i in range(count)])]
  transfers between devices with their start and end apart: 20 -> 20, of which waited for: 8 -> 9; matrix products, arithmetic and copies ran while one was open for 0% -> 0% of each run, Pallas kernels for 12% -> 12%
where the time goes in v7:
time: 46.7 us; the launch traced here: 46.5 us
  starting transfers between devices  22.3 us (48%)
  waiting for transfers between devices  12.8 us (27%)
  Pallas kernels  8.08 us (17%)
  local copies, waits for them, and re-layouts  1.91 us (4%)
  between operations  0.77 us (2%)
  other arithmetic  0.67 us (1%)
    ppermute x12, starting transfers between devices, across(): lax.ppermute(block, 'seq', [(i, i ^ 2 * apart) for i in range(count)])  18.5 us
    ppermute x12, waiting for transfers between devices, across(): lax.ppermute(block, 'seq', [(i, i ^ 2 * apart) for i in range(count)])  7.46 us
    ppermute x6, waiting for transfers between devices, to_sibling(): return lax.ppermute(block, 'seq', [(i, i ^ 1) for i in range(count)])  3.23 us
    ppermute x2, starting transfers between devices, over_groups(): lax.ppermute(count, 'dp', [(i, i ^ apart) for i in range(data_groups)])  3.02 us
    pallas_call x1, Pallas kernels, local(): kernel_call(functools.partial(grads_kernel, offsets), (block,) * chips +...  2.58 us
    ppermute x2, waiting for transfers between devices, over_groups(): lax.ppermute(count, 'dp', [(i, i ^ apart) for i in range(data_groups)])  2.09 us
    unnamed x14, local copies, waits for them, and re-layouts  1.91 us
    pallas_call x1, Pallas kernels, local(): kernel_call(functools.partial(key_end_kernel, rows_in_all), (whole, whole...  1.84 us
  transfers between devices with their start and end apart: 20, of which 9 were waited for; matrix products, arithmetic and copies ran while one was open for 0% of the time, Pallas kernels for 12%

profile of v7, /device:TPU:0, one launch (start us, length us, event | category | flops | bytes accessed | tf_op | source)
XLA Modules:
  0.0 46.5 jit_solution(3133625887994837437)
XLA Ops:
  0.6 0.5 %collective-permute-start.2 = (bf16[256,2048]{1,0:T(8,128)(2,1)}, bf16[256,2048]{1,0:T(8,128)(2,1)S(1)}, u32[]{:S(2)}, u32[]{:S(2)}) collective-permute-start(bf16[256,2048]{1,0:T(8,128)(2,1)} %bitcast.11), channel_id=1, source_target_pairs={{0,1},{1,0},{2,3},{3,2},{4,5},{5,4},{6,7},{7,6},{8,9},{9,8},{10,11... | collective-permute-start | bytes 3145736 | tf_op jit(solution)/shard_map/key_exchange/ppermute | solution.py:38
  1.1 0.1 collective-permute-start
  1.2 1.8 %prepare.1 = (bf16[24,1152]{1,0:T(8,128)(2,1)}, bf16[24,1152]{1,0:T(8,128)(2,1)}) custom-call(bf16[24,2048]{1,0:T(8,128)(2,1)} %bitcast.19, bf16[24,2048]{1,0:T(8,128)(2,1)} %bitcast.20, s32[1,24]{1,0:T(1,128)} %mask_ref.1), custom_call_target="tpu_custom_call" | custom-call | flops 100000 | bytes 1000000 | tf_op jit(solution)/shard_map/sibling_exchange/prepare/pallas_call | solution.py:304
  3.0 0.8 %collective-permute-done.other_ref = bf16[24,2048]{1,0:T(8,128)(2,1)S(1)} collective-permute-done((bf16[24,2048]{1,0:T(8,128)(2,1)}, bf16[24,2048]{1,0:T(8,128)(2,1)S(1)}, u32[]{:S(2)}, u32[]{:S(2)}) %collective-permute-start) | collective-permute-done | bytes 98336 | tf_op jit(solution)/shard_map/sibling_exchange/ppermute | solution.py:38
  3.8 3.0 %collective-permute-start.5 = (bf16[48,1024]{1,0:T(8,128)(2,1)S(1)}, bf16[48,1024]{1,0:T(8,128)(2,1)S(1)}, u32[]{:S(2)}, u32[]{:S(2)}) collective-permute-start(bf16[48,1024]{1,0:T(8,128)(2,1)S(1)} %join_queries.1.refs_1_.refs_4_), channel_id=1, source_target_pairs={{0,2},{1,3},{2,0},{3,1},{4,6},{5,7},{6,4},{7,5},{8,10},{9,11},{10,... | collective-permute-start | bytes 294920 | tf_op jit(solution)/shard_map/query_gather/ppermute | solution.py:43
  6.8 2.6 %collective-permute-start.3 = (bf16[48,1024]{1,0:T(8,128)(2,1)S(1)}, bf16[48,1024]{1,0:T(8,128)(2,1)S(1)}, u32[]{:S(2)}, u32[]{:S(2)}) collective-permute-start(bf16[48,1024]{1,0:T(8,128)(2,1)S(1)} %join_queries.1.refs_1_.refs_4_), channel_id=1, source_target_pairs={{0,4},{1,5},{2,6},{3,7},{4,0},{5,1},{6,2},{7,3},{8,12},{9,13},{10,... | collective-permute-start | bytes 294920 | tf_op jit(solution)/shard_map/query_gather/ppermute | solution.py:43
  9.4 1.2 %collective-permute-done.1.other_ref = bf16[24,1152]{1,0:T(8,128)(2,1)S(1)} collective-permute-done((bf16[24,1152]{1,0:T(8,128)(2,1)S(1)}, bf16[24,1152]{1,0:T(8,128)(2,1)S(1)}, u32[]{:S(2)}, u32[]{:S(2)}) %collective-permute-start.1) | collective-permute-done | bytes 55328 | tf_op jit(solution)/shard_map/sibling_exchange/ppermute | solution.py:38
  10.7 0.2 join_cotangents.1
  10.8 1.5 %collective-permute-start.4 = (f32[8,128]{1,0:T(8,128)S(1)}, f32[8,128]{1,0:T(8,128)S(1)}, u32[]{:S(2)}, u32[]{:S(2)}) collective-permute-start(f32[8,128]{1,0:T(8,128)S(1)} %get-tuple-element.40), channel_id=1, source_target_pairs={{0,8},{8,0},{16,24},{24,16},{1,9},{9,1},{17,25},{25,17},{2,10},{10... | collective-permute-start | bytes 12296 | tf_op jit(solution)/shard_map/mask_count/ppermute | solution.py:357
  12.3 0.7 %copy-done.4 = s32[1,1,4]{2,1,0:T(1,128)S(1)} copy-done((s32[1,1,4]{2,1,0:T(1,128)S(1)}, s32[1,1,4]{2,1,0:T(1,128)}, u32[]{:S(2)}) %copy-start.4) | copy-done | bytes 40
  13.0 0.0 copy-done.5
  13.0 1.2 %copy-done.1 = bf16[1,256,2048]{2,1,0:T(8,128)(2,1)S(1)} copy-done((bf16[1,256,2048]{2,1,0:T(8,128)(2,1)S(1)}, bf16[1,256,2048]{2,1,0:T(8,128)(2,1)}, u32[]{:S(2)}) %copy-start.1) | copy-done | bytes 1048600
  14.2 0.7 %setup.1 = (bf16[256,1024]{1,0:T(8,128)(2,1)S(1)}, bf16[256,1024]{1,0:T(8,128)(2,1)S(1)}, f32[256,192]{1,0:T(8,128)S(1)}, f32[256,192]{1,0:T(8,128)S(1)}) custom-call(s32[1,4]{1,0:T(1,128)S(1)} %bitcast.17, s32[1,4]{1,0:T(1,128)S(1)} %bitcast.18, bf16[256,2048]{1,0:T(8,128)(2,1)S(1)} %bitcast.13), custom_call_target="tpu_custom_call" | custom-call | flops 1000000 | bytes 4194304 | tf_op jit(solution)/shard_map/setup/setup/pallas_call | solution.py:332
  15.0 0.0 copy-start
  15.0 0.0 collective-permute-done.5.refs_3_.refs_6_
  15.0 0.0 collective-permute-done.2.refs_15_
  15.0 0.1 collective-permute-start.6
  15.1 0.5 %collective-permute-start.7 = (bf16[48,1024]{1,0:T(8,128)(2,1)S(1)}, bf16[48,1024]{1,0:T(8,128)(2,1)S(1)}, u32[]{:S(2)}, u32[]{:S(2)}) collective-permute-start(bf16[48,1024]{1,0:T(8,128)(2,1)S(1)} %collective-permute-done.3.refs_2_.refs_5_), channel_id=1, source_target_pairs={{0,2},{1,3},{2,0},{3,1},{4,6},{5,7},{6,4},{7,5},{8,10},{9,11},{10,... | collective-permute-start | bytes 294920 | tf_op jit(solution)/shard_map/query_forward/ppermute | solution.py:43
  15.6 1.9 %collective-permute-start.11 = (bf16[48,1024]{1,0:T(8,128)(2,1)S(1)}, bf16[48,1024]{1,0:T(8,128)(2,1)S(1)}, u32[]{:S(2)}, u32[]{:S(2)}) collective-permute-start(bf16[48,1024]{1,0:T(8,128)(2,1)S(1)} %get-tuple-element.45.refs_8_), channel_id=1, source_target_pairs={{0,4},{1,5},{2,6},{3,7},{4,0},{5,1},{6,2},{7,3},{8,12},{9,13},{10,... | collective-permute-start | bytes 294920 | tf_op jit(solution)/shard_map/cotangent_gather/ppermute | solution.py:43
  17.5 0.1 collective-permute-start.12
  17.6 2.4 %collective-permute-start.13 = (bf16[48,1024]{1,0:T(8,128)(2,1)S(1)}, bf16[48,1024]{1,0:T(8,128)(2,1)S(1)}, u32[]{:S(2)}, u32[]{:S(2)}) collective-permute-start(bf16[48,1024]{1,0:T(8,128)(2,1)S(1)} %get-tuple-element.45.refs_8_), channel_id=1, source_target_pairs={{0,6},{1,7},{2,4},{3,5},{4,2},{5,3},{6,0},{7,1},{8,14},{9,15},{10,... | collective-permute-start | bytes 294920 | tf_op jit(solution)/shard_map/cotangent_gather/ppermute | solution.py:43
  20.0 1.9 %collective-permute-done.7.refs_4_.refs_7_ = bf16[48,1024]{1,0:T(8,128)(2,1)S(1)} collective-permute-done((bf16[48,1024]{1,0:T(8,128)(2,1)S(1)}, bf16[48,1024]{1,0:T(8,128)(2,1)S(1)}, u32[]{:S(2)}, u32[]{:S(2)}) %collective-permute-start.7) | collective-permute-done | bytes 98336 | tf_op jit(solution)/shard_map/query_forward/ppermute | solution.py:43
  21.9 0.0 collective-permute-done.6.other_ref.refs_13_
  21.9 0.9 %scores.1.refs_0_ = f32[8,256]{1,0:T(8,128)S(1)} custom-call(f32[8,48]{1,0:T(8,128)S(1)} %get-tuple-element.37.delta_ref, f32[256,192]{1,0:T(8,128)S(1)} %get-tuple-element.34.bias_own, f32[256,192]{1,0:T(8,128)S(1)} %get-tuple-element.35.bias_other, bf16[256,1024]{1,0:T(8,128)(2,1)S(1)} %get-tuple-element.38.key_ref.refs_12_, ...), custom_call_target="tpu_custom_call" | custom-call | flops 201326592 | bytes 1441792 | tf_op jit(solution)/shard_map/scores/scores/pallas_call | solution.py:381
  22.8 0.1 collective-permute-start.10
  22.9 2.3 %collective-permute-start.8 = (f32[8,256]{1,0:T(8,128)S(1)}, f32[8,256]{1,0:T(8,128)S(1)}, u32[]{:S(2)}, u32[]{:S(2)}) collective-permute-start(f32[8,256]{1,0:T(8,128)S(1)} %scores.1.refs_0_), channel_id=1, source_target_pairs={{0,6},{1,7},{2,4},{3,5},{4,2},{5,3},{6,0},{7,1},{8,14},{9,15},{10,... | collective-permute-start | bytes 24584 | tf_op jit(solution)/shard_map/stats_exchange/ppermute | solution.py:43
  25.2 0.0 collective-permute-done.11.refs_9_
  25.2 1.1 %collective-permute-start.9 = (f32[8,256]{1,0:T(8,128)S(1)}, f32[8,256]{1,0:T(8,128)S(1)}, u32[]{:S(2)}, u32[]{:S(2)}) collective-permute-start(f32[8,256]{1,0:T(8,128)S(1)} %scores.1.refs_0_), channel_id=1, source_target_pairs={{0,4},{1,5},{2,6},{3,7},{4,0},{5,1},{6,2},{7,3},{8,12},{9,13},{10,... | collective-permute-start | bytes 24584 | tf_op jit(solution)/shard_map/stats_exchange/ppermute | solution.py:43
  26.4 0.0 collective-permute-done.12.refs_10_
  26.4 0.6 %collective-permute-done.13.refs_11_ = bf16[48,1024]{1,0:T(8,128)(2,1)S(1)} collective-permute-done((bf16[48,1024]{1,0:T(8,128)(2,1)S(1)}, bf16[48,1024]{1,0:T(8,128)(2,1)S(1)}, u32[]{:S(2)}, u32[]{:S(2)}) %collective-permute-start.13) | collective-permute-done | bytes 98336 | tf_op jit(solution)/shard_map/cotangent_gather/ppermute | solution.py:43
  27.0 0.0 collective-permute-done.10.refs_3_
  27.0 1.4 %collective-permute-done.8.refs_1_ = f32[8,256]{1,0:T(8,128)S(1)} collective-permute-done((f32[8,256]{1,0:T(8,128)S(1)}, f32[8,256]{1,0:T(8,128)S(1)}, u32[]{:S(2)}, u32[]{:S(2)}) %collective-permute-start.8) | collective-permute-done | bytes 8224 | tf_op jit(solution)/shard_map/stats_exchange/ppermute | solution.py:43
  28.4 1.4 %collective-permute-done.9.refs_2_ = f32[8,256]{1,0:T(8,128)S(1)} collective-permute-done((f32[8,256]{1,0:T(8,128)S(1)}, f32[8,256]{1,0:T(8,128)S(1)}, u32[]{:S(2)}, u32[]{:S(2)}) %collective-permute-start.9) | collective-permute-done | bytes 8224 | tf_op jit(solution)/shard_map/stats_exchange/ppermute | solution.py:43
  29.8 2.6 %grads.1 = (bf16[48,1024]{1,0:T(8,128)(2,1)S(1)}, bf16[48,1024]{1,0:T(8,128)(2,1)S(1)}, bf16[48,1024]{1,0:T(8,128)(2,1)S(1)}, bf16[48,1024]{1,0:T(8,128)(2,1)S(1...) custom-call(f32[256,192]{1,0:T(8,128)S(1)} %get-tuple-element.34.bias_own, ...), custom_call_target="tpu_custom_call" | custom-call | flops 1006632960 | bytes 4980736 | tf_op jit(solution)/shard_map/grads/grads/pallas_call | solution.py:398
  32.4 0.1 collective-permute-start.14
  32.5 1.6 %collective-permute-start.16 = (bf16[48,1024]{1,0:T(8,128)(2,1)S(1)}, bf16[48,1024]{1,0:T(8,128)(2,1)S(1)}, u32[]{:S(2)}, u32[]{:S(2)}) collective-permute-start(bf16[48,1024]{1,0:T(8,128)(2,1)S(1)} %get-tuple-element.52), channel_id=1, source_target_pairs={{0,6},{1,7},{2,4},{3,5},{4,2},{5,3},{6,0},{7,1},{8,14},{9,15},{10,... | collective-permute-start | bytes 294920 | tf_op jit(solution)/shard_map/query_grad_sum/ppermute | solution.py:43
  34.1 1.0 %collective-permute-start.17 = (bf16[48,1024]{1,0:T(8,128)(2,1)S(1)}, bf16[48,1024]{1,0:T(8,128)(2,1)S(1)}, u32[]{:S(2)}, u32[]{:S(2)}) collective-permute-start(bf16[48,1024]{1,0:T(8,128)(2,1)S(1)} %get-tuple-element.53), channel_id=1, source_target_pairs={{0,4},{1,5},{2,6},{3,7},{4,0},{5,1},{6,2},{7,3},{8,12},{9,13},{10,... | collective-permute-start | bytes 294920 | tf_op jit(solution)/shard_map/query_grad_sum/ppermute | solution.py:43
  35.1 1.9 %collective-permute-start.18 = (bf16[48,1024]{1,0:T(8,128)(2,1)S(1)}, bf16[48,1024]{1,0:T(8,128)(2,1)S(1)}, u32[]{:S(2)}, u32[]{:S(2)}) collective-permute-start(bf16[48,1024]{1,0:T(8,128)(2,1)S(1)} %get-tuple-element.54), channel_id=1, source_target_pairs={{0,2},{1,3},{2,0},{3,1},{4,6},{5,7},{6,4},{7,5},{8,10},{9,11},{10,... | collective-permute-start | bytes 294920 | tf_op jit(solution)/shard_map/query_grad_sum/ppermute | solution.py:43
  36.9 1.5 %collective-permute-start.15 = (f32[8,128]{1,0:T(8,128)S(1)}, f32[8,128]{1,0:T(8,128)S(1)}, u32[]{:S(2)}, u32[]{:S(2)}) collective-permute-start(f32[8,128]{1,0:T(8,128)S(1)} %get-tuple-element.49.refs_0_), channel_id=1, source_target_pairs={{0,16},{8,24},{16,0},{24,8},{1,17},{9,25},{17,1},{25,9},{2,18},{10... | collective-permute-start | bytes 12296 | tf_op jit(solution)/shard_map/key_grad_end/ppermute | solution.py:357
  38.4 2.1 %collective-permute-done.15.refs_1_ = f32[8,128]{1,0:T(8,128)S(1)} collective-permute-done((f32[8,128]{1,0:T(8,128)S(1)}, f32[8,128]{1,0:T(8,128)S(1)}, u32[]{:S(2)}, u32[]{:S(2)}) %collective-permute-start.15) | collective-permute-done | bytes 4128 | tf_op jit(solution)/shard_map/key_grad_end/ppermute | solution.py:357
  40.5 0.0 collective-permute-done.14.other_ref
  40.5 1.8 %key_end.1 = (bf16[256,2048]{1,0:T(8,128)(2,1)}, bf16[256,2048]{1,0:T(8,128)(2,1)}, f32[8,128]{1,0:T(8,128)S(1)}) custom-call(bf16[256,2048]{1,0:T(8,128)(2,1)S(1)} %get-tuple-element.47.keep_ref, bf16[256,2048]{1,0:T(8,128)(2,1)S(1)} %collective-permute-done.14.other_ref, f32[8,128]{1,0:T(8,128)S(1)} %get-tuple-element.49.refs_0_, ...), custom_call_target="tpu_custom_call" | custom-call | flops 1000000 | bytes 4194304 | tf_op jit(solution)/shard_map/key_grad_end/key_end/pallas_call | solution.py:418
  42.4 0.0 collective-permute-done.16.refs_1_
  42.4 2.1 %collective-permute-done.17.refs_2_ = bf16[48,1024]{1,0:T(8,128)(2,1)S(1)} collective-permute-done((bf16[48,1024]{1,0:T(8,128)(2,1)S(1)}, bf16[48,1024]{1,0:T(8,128)(2,1)S(1)}, u32[]{:S(2)}, u32[]{:S(2)}) %collective-permute-start.17) | collective-permute-done | bytes 98336 | tf_op jit(solution)/shard_map/query_grad_sum/ppermute | solution.py:43
  44.5 0.1 query_end.1
  44.6 0.1 collective-permute-start.19
  44.7 1.2 %collective-permute-done.19 = bf16[24,1024]{1,0:T(8,128)(2,1)S(1)} collective-permute-done((bf16[24,1024]{1,0:T(8,128)(2,1)S(1)}, bf16[24,1024]{1,0:T(8,128)(2,1)S(1)}, u32[]{:S(2)}, u32[]{:S(2)}) %collective-permute-start.19) | collective-permute-done | bytes 49184 | tf_op jit(solution)/shard_map/query_grad_end/ppermute | solution.py:38
  45.9 0.7 %maximum_select_fusion = bf16[1,24,2048]{2,1,0:T(8,128)(2,1)} fusion(bf16[1,24,1024]{2,1,0:T(8,128)(2,1)S(1)} %bitcast.21, bf16[1,24,1024]{2,1,0:T(8,128)(2,1)S(1)} %bitcast.16, pred[]{:T(512)S(6)} %eq.3), kind=kLoop, calls=%fused_computation | loop fusion | flops 442368 | bytes 196609 | tf_op jit(solution)/shard_map/query_grad_end/jit(_where)/select_n | solution.py:262
  (16 shorter events, 0.1 us)
Async XLA Ops:
  0.6 14.4 %collective-permute-start.2 = (bf16[256,2048]{1,0:T(8,128)(2,1)}, bf16[256,2048]{1,0:T(8,128)(2,1)S(1)}, u32[]{:S(2)}, u32[]{:S(2)}) collective-permute-start(bf16[256,2048]{1,0:T(8,128)(2,1)} %bitcast.11), channel_id=1, source_target_pairs={{0,1},{1,0},{2,3},{3,2},{4,5},{5,4},{6,7},{7,6},{8,9},{9,8},{10,11... | collective-permute-start | bytes 3145736 | tf_op jit(solution)/shard_map/key_exchange/ppermute | solution.py:38
  1.1 2.6 %collective-permute-start = (bf16[24,2048]{1,0:T(8,128)(2,1)}, bf16[24,2048]{1,0:T(8,128)(2,1)S(1)}, u32[]{:S(2)}, u32[]{:S(2)}) collective-permute-start(bf16[24,2048]{1,0:T(8,128)(2,1)} %bitcast.14), channel_id=1, source_target_pairs={{0,1},{1,0},{2,3},{3,2},{4,5},{5,4},{6,7},{7,6},{8,9},{9,8},{10,11... | collective-permute-start | bytes 294920 | tf_op jit(solution)/shard_map/sibling_exchange/ppermute | solution.py:38
  1.2 2.6 %copy-start.2 = (bf16[1,24,2048]{2,1,0:T(8,128)(2,1)S(1)}, bf16[1,24,2048]{2,1,0:T(8,128)(2,1)}, u32[]{:S(2)}) copy-start(bf16[1,24,2048]{2,1,0:T(8,128)(2,1)} %param.8) | copy-start | bytes 294916
  3.8 5.6 %copy-start.6 = (bf16[24,1152]{1,0:T(8,128)(2,1)S(1)}, bf16[24,1152]{1,0:T(8,128)(2,1)}, u32[]{:S(2)}) copy-start(bf16[24,1152]{1,0:T(8,128)(2,1)} %get-tuple-element.36) | copy-start | bytes 165892
  3.8 6.9 %copy-start.3 = (bf16[24,1152]{1,0:T(8,128)(2,1)S(1)}, bf16[24,1152]{1,0:T(8,128)(2,1)}, u32[]{:S(2)}) copy-start(bf16[24,1152]{1,0:T(8,128)(2,1)} %get-tuple-element.31.own_ref) | copy-start | bytes 165892
  3.8 11.2 %collective-permute-start.5 = (bf16[48,1024]{1,0:T(8,128)(2,1)S(1)}, bf16[48,1024]{1,0:T(8,128)(2,1)S(1)}, u32[]{:S(2)}, u32[]{:S(2)}) collective-permute-start(bf16[48,1024]{1,0:T(8,128)(2,1)S(1)} %join_queries.1.refs_1_.refs_4_), channel_id=1, source_target_pairs={{0,2},{1,3},{2,0},{3,1},{4,6},{5,7},{6,4},{7,5},{8,10},{9,11},{10,... | collective-permute-start | bytes 294920 | tf_op jit(solution)/shard_map/query_gather/ppermute | solution.py:43
  6.8 8.2 %collective-permute-start.3 = (bf16[48,1024]{1,0:T(8,128)(2,1)S(1)}, bf16[48,1024]{1,0:T(8,128)(2,1)S(1)}, u32[]{:S(2)}, u32[]{:S(2)}) collective-permute-start(bf16[48,1024]{1,0:T(8,128)(2,1)S(1)} %join_queries.1.refs_1_.refs_4_), channel_id=1, source_target_pairs={{0,4},{1,5},{2,6},{3,7},{4,0},{5,1},{6,2},{7,3},{8,12},{9,13},{10,... | collective-permute-start | bytes 294920 | tf_op jit(solution)/shard_map/query_gather/ppermute | solution.py:43
  9.4 1.2 %collective-permute-start.1 = (bf16[24,1152]{1,0:T(8,128)(2,1)S(1)}, bf16[24,1152]{1,0:T(8,128)(2,1)S(1)}, u32[]{:S(2)}, u32[]{:S(2)}) collective-permute-start(bf16[24,1152]{1,0:T(8,128)(2,1)S(1)} %copy-done.6), channel_id=1, source_target_pairs={{0,1},{1,0},{2,3},{3,2},{4,5},{5,4},{6,7},{7,6},{8,9},{9,8},{10,11... | collective-permute-start | bytes 165896 | tf_op jit(solution)/shard_map/sibling_exchange/ppermute | solution.py:38
  10.8 4.1 %collective-permute-start.4 = (f32[8,128]{1,0:T(8,128)S(1)}, f32[8,128]{1,0:T(8,128)S(1)}, u32[]{:S(2)}, u32[]{:S(2)}) collective-permute-start(f32[8,128]{1,0:T(8,128)S(1)} %get-tuple-element.40), channel_id=1, source_target_pairs={{0,8},{8,0},{16,24},{24,16},{1,9},{9,1},{17,25},{25,17},{2,10},{10... | collective-permute-start | bytes 12296 | tf_op jit(solution)/shard_map/mask_count/ppermute | solution.py:357
  12.3 0.7 %copy-start.4 = (s32[1,1,4]{2,1,0:T(1,128)S(1)}, s32[1,1,4]{2,1,0:T(1,128)}, u32[]{:S(2)}) copy-start(s32[1,1,4]{2,1,0:T(1,128)} %param.14) | copy-start | bytes 52
  12.3 0.7 %copy-start.5 = (s32[1,1,4]{2,1,0:T(1,128)S(1)}, s32[1,1,4]{2,1,0:T(1,128)}, u32[]{:S(2)}) copy-start(s32[1,1,4]{2,1,0:T(1,128)} %param.15) | copy-start | bytes 52
  13.0 1.2 %copy-start.1 = (bf16[1,256,2048]{2,1,0:T(8,128)(2,1)S(1)}, bf16[1,256,2048]{2,1,0:T(8,128)(2,1)}, u32[]{:S(2)}) copy-start(bf16[1,256,2048]{2,1,0:T(8,128)(2,1)} %param.9) | copy-start | bytes 3145732
  15.0 14.8 %copy-start = (bf16[1,256,2048]{2,1,0:T(8,128)(2,1)S(1)}, bf16[1,256,2048]{2,1,0:T(8,128)(2,1)}, u32[]{:S(2)}) copy-start(bf16[1,256,2048]{2,1,0:T(8,128)(2,1)} %param.10) | copy-start | bytes 3145732
  15.0 6.9 %collective-permute-start.6 = (bf16[256,1024]{1,0:T(8,128)(2,1)S(1)}, bf16[256,1024]{1,0:T(8,128)(2,1)S(1)}, u32[]{:S(2)}, u32[]{:S(2)}) collective-permute-start(bf16[256,1024]{1,0:T(8,128)(2,1)S(1)} %get-tuple-element.43), channel_id=1, source_target_pairs={{0,1},{1,0},{2,3},{3,2},{4,5},{5,4},{6,7},{7,6},{8,9},{9,8},{10,11... | collective-permute-start | bytes 1572872 | tf_op jit(solution)/shard_map/key_exchange/ppermute | solution.py:38
  15.1 6.8 %collective-permute-start.7 = (bf16[48,1024]{1,0:T(8,128)(2,1)S(1)}, bf16[48,1024]{1,0:T(8,128)(2,1)S(1)}, u32[]{:S(2)}, u32[]{:S(2)}) collective-permute-start(bf16[48,1024]{1,0:T(8,128)(2,1)S(1)} %collective-permute-done.3.refs_2_.refs_5_), channel_id=1, source_target_pairs={{0,2},{1,3},{2,0},{3,1},{4,6},{5,7},{6,4},{7,5},{8,10},{9,11},{10,... | collective-permute-start | bytes 294920 | tf_op jit(solution)/shard_map/query_forward/ppermute | solution.py:43
  15.6 9.6 %collective-permute-start.11 = (bf16[48,1024]{1,0:T(8,128)(2,1)S(1)}, bf16[48,1024]{1,0:T(8,128)(2,1)S(1)}, u32[]{:S(2)}, u32[]{:S(2)}) collective-permute-start(bf16[48,1024]{1,0:T(8,128)(2,1)S(1)} %get-tuple-element.45.refs_8_), channel_id=1, source_target_pairs={{0,4},{1,5},{2,6},{3,7},{4,0},{5,1},{6,2},{7,3},{8,12},{9,13},{10,... | collective-permute-start | bytes 294920 | tf_op jit(solution)/shard_map/cotangent_gather/ppermute | solution.py:43
  17.5 8.9 %collective-permute-start.12 = (bf16[48,1024]{1,0:T(8,128)(2,1)S(1)}, bf16[48,1024]{1,0:T(8,128)(2,1)S(1)}, u32[]{:S(2)}, u32[]{:S(2)}) collective-permute-start(bf16[48,1024]{1,0:T(8,128)(2,1)S(1)} %get-tuple-element.45.refs_8_), channel_id=1, source_target_pairs={{0,2},{1,3},{2,0},{3,1},{4,6},{5,7},{6,4},{7,5},{8,10},{9,11},{10,... | collective-permute-start | bytes 294920 | tf_op jit(solution)/shard_map/cotangent_gather/ppermute | solution.py:43
  17.6 9.5 %collective-permute-start.13 = (bf16[48,1024]{1,0:T(8,128)(2,1)S(1)}, bf16[48,1024]{1,0:T(8,128)(2,1)S(1)}, u32[]{:S(2)}, u32[]{:S(2)}) collective-permute-start(bf16[48,1024]{1,0:T(8,128)(2,1)S(1)} %get-tuple-element.45.refs_8_), channel_id=1, source_target_pairs={{0,6},{1,7},{2,4},{3,5},{4,2},{5,3},{6,0},{7,1},{8,14},{9,15},{10,... | collective-permute-start | bytes 294920 | tf_op jit(solution)/shard_map/cotangent_gather/ppermute | solution.py:43
  22.8 4.2 %collective-permute-start.10 = (f32[8,256]{1,0:T(8,128)S(1)}, f32[8,256]{1,0:T(8,128)S(1)}, u32[]{:S(2)}, u32[]{:S(2)}) collective-permute-start(f32[8,256]{1,0:T(8,128)S(1)} %scores.1.refs_0_), channel_id=1, source_target_pairs={{0,2},{1,3},{2,0},{3,1},{4,6},{5,7},{6,4},{7,5},{8,10},{9,11},{10,... | collective-permute-start | bytes 24584 | tf_op jit(solution)/shard_map/stats_exchange/ppermute | solution.py:43
  22.9 5.5 %collective-permute-start.8 = (f32[8,256]{1,0:T(8,128)S(1)}, f32[8,256]{1,0:T(8,128)S(1)}, u32[]{:S(2)}, u32[]{:S(2)}) collective-permute-start(f32[8,256]{1,0:T(8,128)S(1)} %scores.1.refs_0_), channel_id=1, source_target_pairs={{0,6},{1,7},{2,4},{3,5},{4,2},{5,3},{6,0},{7,1},{8,14},{9,15},{10,... | collective-permute-start | bytes 24584 | tf_op jit(solution)/shard_map/stats_exchange/ppermute | solution.py:43
  25.2 4.6 %collective-permute-start.9 = (f32[8,256]{1,0:T(8,128)S(1)}, f32[8,256]{1,0:T(8,128)S(1)}, u32[]{:S(2)}, u32[]{:S(2)}) collective-permute-start(f32[8,256]{1,0:T(8,128)S(1)} %scores.1.refs_0_), channel_id=1, source_target_pairs={{0,4},{1,5},{2,6},{3,7},{4,0},{5,1},{6,2},{7,3},{8,12},{9,13},{10,... | collective-permute-start | bytes 24584 | tf_op jit(solution)/shard_map/stats_exchange/ppermute | solution.py:43
  32.4 8.1 %collective-permute-start.14 = (bf16[256,2048]{1,0:T(8,128)(2,1)S(1)}, bf16[256,2048]{1,0:T(8,128)(2,1)S(1)}, u32[]{:S(2)}, u32[]{:S(2)}) collective-permute-start(bf16[256,2048]{1,0:T(8,128)(2,1)S(1)} %get-tuple-element.48), channel_id=1, source_target_pairs={{0,1},{1,0},{2,3},{3,2},{4,5},{5,4},{6,7},{7,6},{8,9},{9,8},{10,11... | collective-permute-start | bytes 3145736 | tf_op jit(solution)/shard_map/key_grad_end/ppermute | solution.py:38
  32.5 9.9 %collective-permute-start.16 = (bf16[48,1024]{1,0:T(8,128)(2,1)S(1)}, bf16[48,1024]{1,0:T(8,128)(2,1)S(1)}, u32[]{:S(2)}, u32[]{:S(2)}) collective-permute-start(bf16[48,1024]{1,0:T(8,128)(2,1)S(1)} %get-tuple-element.52), channel_id=1, source_target_pairs={{0,6},{1,7},{2,4},{3,5},{4,2},{5,3},{6,0},{7,1},{8,14},{9,15},{10,... | collective-permute-start | bytes 294920 | tf_op jit(solution)/shard_map/query_grad_sum/ppermute | solution.py:43
  34.1 10.4 %collective-permute-start.17 = (bf16[48,1024]{1,0:T(8,128)(2,1)S(1)}, bf16[48,1024]{1,0:T(8,128)(2,1)S(1)}, u32[]{:S(2)}, u32[]{:S(2)}) collective-permute-start(bf16[48,1024]{1,0:T(8,128)(2,1)S(1)} %get-tuple-element.53), channel_id=1, source_target_pairs={{0,4},{1,5},{2,6},{3,7},{4,0},{5,1},{6,2},{7,3},{8,12},{9,13},{10,... | collective-permute-start | bytes 294920 | tf_op jit(solution)/shard_map/query_grad_sum/ppermute | solution.py:43
  35.1 9.4 %collective-permute-start.18 = (bf16[48,1024]{1,0:T(8,128)(2,1)S(1)}, bf16[48,1024]{1,0:T(8,128)(2,1)S(1)}, u32[]{:S(2)}, u32[]{:S(2)}) collective-permute-start(bf16[48,1024]{1,0:T(8,128)(2,1)S(1)} %get-tuple-element.54), channel_id=1, source_target_pairs={{0,2},{1,3},{2,0},{3,1},{4,6},{5,7},{6,4},{7,5},{8,10},{9,11},{10,... | collective-permute-start | bytes 294920 | tf_op jit(solution)/shard_map/query_grad_sum/ppermute | solution.py:43
  36.9 3.6 %collective-permute-start.15 = (f32[8,128]{1,0:T(8,128)S(1)}, f32[8,128]{1,0:T(8,128)S(1)}, u32[]{:S(2)}, u32[]{:S(2)}) collective-permute-start(f32[8,128]{1,0:T(8,128)S(1)} %get-tuple-element.49.refs_0_), channel_id=1, source_target_pairs={{0,16},{8,24},{16,0},{24,8},{1,17},{9,25},{17,1},{25,9},{2,18},{10... | collective-permute-start | bytes 12296 | tf_op jit(solution)/shard_map/key_grad_end/ppermute | solution.py:357
  44.6 1.3 %collective-permute-start.19 = (bf16[24,1024]{1,0:T(8,128)(2,1)S(1)}, bf16[24,1024]{1,0:T(8,128)(2,1)S(1)}, u32[]{:S(2)}, u32[]{:S(2)}) collective-permute-start(bf16[24,1024]{1,0:T(8,128)(2,1)S(1)} %get-tuple-element.56), channel_id=1, source_target_pairs={{0,1},{1,0},{2,3},{3,2},{4,5},{5,4},{6,7},{7,6},{8,9},{9,8},{10,11... | collective-permute-start | bytes 147464 | tf_op jit(solution)/shard_map/query_grad_end/ppermute | solution.py:38

commit v8 on v7

--- a/solution.py
+++ b/solution.py
@@ -62,14 +62,43 @@
     )
 
 
+def document_of(positions, lengths_ref):
+    end = 0
+    document = jnp.zeros_like(positions)
+    for i in range(lengths_ref.shape[1]):
+        end = end + lengths_ref[0, i]
+        document += (positions >= end).astype(jnp.int32)
+    return document
+
+
 def prepare_kernel(
-    grad_ref, out_ref, mask_ref, send_ref, keep_ref, grad_held, out_held, mask_held, sems
+    offsets,
+    dec_rows,
+    enc_rows,
+    in_ref,
+    target_ref,
+    grad_ref,
+    out_ref,
+    mask_ref,
+    send_ref,
+    keep_ref,
+    docs_ref,
+    grad_held, out_held, mask_held, sems
 ):
-    _, core = position()
+    chip, core = position()
     rows = grad_ref.shape[0]
     copies = start_all(
         [(mask_ref, mask_held), (grad_ref, grad_held), (out_ref, out_held)], sems
     )
+    lane = lax.broadcasted_iota(jnp.int32, (1, docs_ref.shape[1]), 1)
+    block = dec_rows // len(offsets)
+    dec = lane + chip * block
+    for j, offset in enumerate(offsets[1:], 1):
+        dec = jnp.where(lane >= j * block, lane + ((chip ^ offset) - j) * block, dec)
+    docs = [document_of(dec, target_ref)]
+    for side in (core, 1 - core):
+        docs.append(document_of(lane + (2 * chip + side) * enc_rows, in_ref))
+    docs_ref[...] = jnp.concatenate(docs + docs + docs[:2], 0).astype(F32)
     copies[0].wait()
     mask_row = mask_held[...].astype(F32)
     here = lax.broadcasted_iota(jnp.int32, (rows, rows), 0) == lax.broadcasted_iota(
@@ -124,28 +153,13 @@
         ref[...] = rows_ref[:, pl.ds(pl.multiple_of(half * HALF, HALF), HALF)]
 
 
-def document_of(positions, lengths_ref):
-    end = 0
-    document = jnp.zeros_like(positions)
-    for i in range(lengths_ref.shape[1]):
-        end = end + lengths_ref[0, i]
-        document += (positions >= end).astype(jnp.int32)
-    return document
-
-
-def setup_kernel(offsets, in_ref, target_ref, key_ref, k_ref, send_ref, bias_own, bias_other):
-    chip, core = position()
+def setup_kernel(docs_ref, key_ref, k_ref, send_ref, bias_own, bias_other):
     split_kernel(key_ref, k_ref, send_ref)
     enc_rows, dec_rows = bias_own.shape
-    block = dec_rows // len(offsets)
-    lane = lax.broadcasted_iota(jnp.int32, (1, dec_rows), 1)
-    dec = lane + chip * block
-    for j, offset in enumerate(offsets[1:], 1):
-        dec = jnp.where(lane >= j * block, lane + ((chip ^ offset) - j) * block, dec)
-    dec = document_of(dec, target_ref)
-    for ref, side in ((bias_own, core), (bias_other, 1 - core)):
-        enc = lax.broadcasted_iota(jnp.int32, (enc_rows, 1), 0) + (2 * chip + side) * enc_rows
-        ref[...] = jnp.where(document_of(enc, in_ref) == dec, 0.0, NEVER)
+    dec = docs_ref[0:1, :dec_rows]
+    columns = jnp.transpose(docs_ref[:, :enc_rows])
+    for ref, column in ((bias_own, 1), (bias_other, 2)):
+        ref[...] = jnp.where(columns[:, column : column + 1] == dec, 0.0, NEVER)
 
 
 def start_all(pairs, sems):
@@ -301,11 +315,12 @@
 
     with jax.named_scope("sibling_exchange"):
         q_recv = to_sibling(query_rows)
-        g_send, g_keep = kernel_call(
-            prepare_kernel,
-            (sent, sent),
-            [ANY] * 3,
-            (VMEM, VMEM),
+        docs = shaped(8, pl.cdiv(max(dec_rows, enc_local), 128) * 128, dtype=F32)
+        g_send, g_keep, docs = kernel_call(
+            functools.partial(prepare_kernel, offsets, dec_rows, enc_local),
+            (sent, sent, docs),
+            [SMEM] * 2 + [ANY] * 3,
+            (VMEM, VMEM, VMEM),
             [
                 pltpu.VMEM((dec_local, features), BF16),
                 pltpu.VMEM((dec_local, features), BF16),
@@ -316,7 +331,7 @@
             10**6,
             "prepare",
             60 * 1024 * 1024,
-        )(out_grad[0], attn_out[0], loss_mask)
+        )(*lengths, out_grad[0], attn_out[0], loss_mask)
         g_recv = to_sibling(g_send)
 
     with jax.named_scope("query_gather"):
@@ -330,15 +345,15 @@
         half_rows = shaped(enc_local, HALF)
         bias = shaped(enc_local, dec_rows, dtype=F32)
         k_own, k_send, bias_own, bias_other = kernel_call(
-            functools.partial(setup_kernel, offsets),
+            setup_kernel,
             (half_rows, half_rows, bias, bias),
-            [SMEM] * 2 + [VMEM],
+            [VMEM] * 2,
             (VMEM,) * 4,
             [],
             10**6,
             2**22,
             "setup",
-        )(*lengths, after(key_rows, q_block)[0])
+        )(docs, after(key_rows, q_block)[0])
 
     with jax.named_scope("cotangent_gather"):
         small = shaped(8, 2 * dec_local, dtype=F32)

time: 46.7 us -> 46.5 us (level)
  local copies, waits for them, and re-layouts: 1.91 us -> 1.25 us
    ppermute x6, waiting for transfers between devices: 3.23 us -> 2.46 us  [to_sibling(): return lax.ppermute(block, 'seq', [(i, i ^ 1) for i in range(count)])]
    unnamed x14 -> x12, local copies, waits for them, and re-layouts: 1.91 us -> 1.25 us
    ppermute x2, waiting for transfers between devices: 2.09 us -> 2.66 us  [over_groups(): lax.ppermute(count, 'dp', [(i, i ^ apart) for i in range(data_groups)])]
where the time goes in v8:
time: 46.5 us; the launch traced here: 46.2 us
  starting transfers between devices  22.4 us (48%)
  waiting for transfers between devices  12.7 us (27%)
  Pallas kernels  8.44 us (18%)
  local copies, waits for them, and re-layouts  1.25 us (3%)
  between operations  0.78 us (2%)
  other arithmetic  0.66 us (1%)
    ppermute x12, starting transfers between devices, across(): lax.ppermute(block, 'seq', [(i, i ^ 2 * apart) for i in range(count)])  18.6 us
    ppermute x12, waiting for transfers between devices, across(): lax.ppermute(block, 'seq', [(i, i ^ 2 * apart) for i in range(count)])  7.58 us
    ppermute x2, starting transfers between devices, over_groups(): lax.ppermute(count, 'dp', [(i, i ^ apart) for i in range(data_groups)])  3.01 us
    ppermute x2, waiting for transfers between devices, over_groups(): lax.ppermute(count, 'dp', [(i, i ^ apart) for i in range(data_groups)])  2.66 us
    pallas_call x1, Pallas kernels, local(): kernel_call(functools.partial(grads_kernel, offsets), (block,) * chips +...  2.58 us
    pallas_call x1, Pallas kernels, local(): kernel_call(functools.partial(prepare_kernel, offsets, dec_rows, enc_loca...  2.55 us
    ppermute x6, waiting for transfers between devices, to_sibling(): return lax.ppermute(block, 'seq', [(i, i ^ 1) for i in range(count)])  2.46 us
    pallas_call x1, Pallas kernels, local(): kernel_call(functools.partial(key_end_kernel, rows_in_all), (whole, whole...  1.84 us
  transfers between devices with their start and end apart: 20, of which 9 were waited for; matrix products, arithmetic and copies ran while one was open for 0% of the time, Pallas kernels for 12%

profile of v8, /device:TPU:0, one launch (start us, length us, event | category | flops | bytes accessed | tf_op | source)
XLA Modules:
  0.0 46.2 jit_solution(12903246074781627760)
XLA Ops:
  0.6 0.5 %collective-permute-start.2 = (bf16[256,2048]{1,0:T(8,128)(2,1)}, bf16[256,2048]{1,0:T(8,128)(2,1)S(1)}, u32[]{:S(2)}, u32[]{:S(2)}) collective-permute-start(bf16[256,2048]{1,0:T(8,128)(2,1)} %bitcast.11), channel_id=1, source_target_pairs={{0,1},{1,0},{2,3},{3,2},{4,5},{5,4},{6,7},{7,6},{8,9},{9,8},{10,11... | collective-permute-start | bytes 3145736 | tf_op jit(solution)/shard_map/key_exchange/ppermute | solution.py:38
  1.1 0.1 collective-permute-start
  1.2 2.6 %prepare.1 = (bf16[24,1152]{1,0:T(8,128)(2,1)}, bf16[24,1152]{1,0:T(8,128)(2,1)}, f32[8,256]{1,0:T(8,128)}) custom-call(s32[1,4]{1,0:T(1,128)} %bitcast.20, s32[1,4]{1,0:T(1,128)} %bitcast.21, bf16[24,2048]{1,0:T(8,128)(2,1)} %bitcast.17, bf16[24,2048]{1,0:T(8,128)(2,1)} %bitcast.18, s32[1,24]{1,0:T(1,128)} %mask_ref.1), custom_call_target="tpu_custom_call" | custom-call | flops 100000 | bytes 1000000 | tf_op jit(solution)/shard_map/sibling_exchange/prepare/pallas_call | solution.py:319
  3.8 0.0 collective-permute-done.other_ref
  3.8 0.0 copy-start.5
  3.8 0.0 copy-start.3
  3.9 3.1 %collective-permute-start.5 = (bf16[48,1024]{1,0:T(8,128)(2,1)S(1)}, bf16[48,1024]{1,0:T(8,128)(2,1)S(1)}, u32[]{:S(2)}, u32[]{:S(2)}) collective-permute-start(bf16[48,1024]{1,0:T(8,128)(2,1)S(1)} %join_queries.1.refs_1_.refs_4_), channel_id=1, source_target_pairs={{0,2},{1,3},{2,0},{3,1},{4,6},{5,7},{6,4},{7,5},{8,10},{9,11},{10,... | collective-permute-start | bytes 294920 | tf_op jit(solution)/shard_map/query_gather/ppermute | solution.py:43
  6.9 2.6 %collective-permute-start.3 = (bf16[48,1024]{1,0:T(8,128)(2,1)S(1)}, bf16[48,1024]{1,0:T(8,128)(2,1)S(1)}, u32[]{:S(2)}, u32[]{:S(2)}) collective-permute-start(bf16[48,1024]{1,0:T(8,128)(2,1)S(1)} %join_queries.1.refs_1_.refs_4_), channel_id=1, source_target_pairs={{0,4},{1,5},{2,6},{3,7},{4,0},{5,1},{6,2},{7,3},{8,12},{9,13},{10,... | collective-permute-start | bytes 294920 | tf_op jit(solution)/shard_map/query_gather/ppermute | solution.py:43
  9.5 0.0 collective-permute-start.1
  9.5 1.2 %collective-permute-done.1.other_ref = bf16[24,1152]{1,0:T(8,128)(2,1)S(1)} collective-permute-done((bf16[24,1152]{1,0:T(8,128)(2,1)S(1)}, bf16[24,1152]{1,0:T(8,128)(2,1)S(1)}, u32[]{:S(2)}, u32[]{:S(2)}) %collective-permute-start.1) | collective-permute-done | bytes 55328 | tf_op jit(solution)/shard_map/sibling_exchange/ppermute | solution.py:38
  10.8 0.2 join_cotangents.1
  10.9 1.5 %collective-permute-start.4 = (f32[8,128]{1,0:T(8,128)S(1)}, f32[8,128]{1,0:T(8,128)S(1)}, u32[]{:S(2)}, u32[]{:S(2)}) collective-permute-start(f32[8,128]{1,0:T(8,128)S(1)} %get-tuple-element.42), channel_id=1, source_target_pairs={{0,8},{8,0},{16,24},{24,16},{1,9},{9,1},{17,25},{25,17},{2,10},{10... | collective-permute-start | bytes 12296 | tf_op jit(solution)/shard_map/mask_count/ppermute | solution.py:372
  12.4 1.2 %copy-done.1 = bf16[1,256,2048]{2,1,0:T(8,128)(2,1)S(1)} copy-done((bf16[1,256,2048]{2,1,0:T(8,128)(2,1)S(1)}, bf16[1,256,2048]{2,1,0:T(8,128)(2,1)}, u32[]{:S(2)}) %copy-start.1) | copy-done | bytes 1048600
  13.7 0.3 setup.1
  14.0 0.0 copy-start
  14.0 0.6 %collective-permute-done.4 = f32[8,128]{1,0:T(8,128)S(1)} collective-permute-done((f32[8,128]{1,0:T(8,128)S(1)}, f32[8,128]{1,0:T(8,128)S(1)}, u32[]{:S(2)}, u32[]{:S(2)}) %collective-permute-start.4) | collective-permute-done | bytes 4128 | tf_op jit(solution)/shard_map/mask_count/ppermute | solution.py:372
  14.6 0.0 collective-permute-done.5.refs_3_.refs_6_
  14.6 0.0 collective-permute-done.3.refs_2_.refs_5_
  14.6 0.0 collective-permute-done.2.refs_15_
  14.6 0.1 collective-permute-start.6
  14.7 0.5 %collective-permute-start.7 = (bf16[48,1024]{1,0:T(8,128)(2,1)S(1)}, bf16[48,1024]{1,0:T(8,128)(2,1)S(1)}, u32[]{:S(2)}, u32[]{:S(2)}) collective-permute-start(bf16[48,1024]{1,0:T(8,128)(2,1)S(1)} %collective-permute-done.3.refs_2_.refs_5_), channel_id=1, source_target_pairs={{0,2},{1,3},{2,0},{3,1},{4,6},{5,7},{6,4},{7,5},{8,10},{9,11},{10,... | collective-permute-start | bytes 294920 | tf_op jit(solution)/shard_map/query_forward/ppermute | solution.py:43
  15.2 2.4 %collective-permute-start.11 = (bf16[48,1024]{1,0:T(8,128)(2,1)S(1)}, bf16[48,1024]{1,0:T(8,128)(2,1)S(1)}, u32[]{:S(2)}, u32[]{:S(2)}) collective-permute-start(bf16[48,1024]{1,0:T(8,128)(2,1)S(1)} %get-tuple-element.47.refs_8_), channel_id=1, source_target_pairs={{0,4},{1,5},{2,6},{3,7},{4,0},{5,1},{6,2},{7,3},{8,12},{9,13},{10,... | collective-permute-start | bytes 294920 | tf_op jit(solution)/shard_map/cotangent_gather/ppermute | solution.py:43
  17.5 0.1 collective-permute-start.12
  17.6 1.9 %collective-permute-start.13 = (bf16[48,1024]{1,0:T(8,128)(2,1)S(1)}, bf16[48,1024]{1,0:T(8,128)(2,1)S(1)}, u32[]{:S(2)}, u32[]{:S(2)}) collective-permute-start(bf16[48,1024]{1,0:T(8,128)(2,1)S(1)} %get-tuple-element.47.refs_8_), channel_id=1, source_target_pairs={{0,6},{1,7},{2,4},{3,5},{4,2},{5,3},{6,0},{7,1},{8,14},{9,15},{10,... | collective-permute-start | bytes 294920 | tf_op jit(solution)/shard_map/cotangent_gather/ppermute | solution.py:43
  19.6 2.4 %collective-permute-done.7.refs_4_.refs_7_ = bf16[48,1024]{1,0:T(8,128)(2,1)S(1)} collective-permute-done((bf16[48,1024]{1,0:T(8,128)(2,1)S(1)}, bf16[48,1024]{1,0:T(8,128)(2,1)S(1)}, u32[]{:S(2)}, u32[]{:S(2)}) %collective-permute-start.7) | collective-permute-done | bytes 98336 | tf_op jit(solution)/shard_map/query_forward/ppermute | solution.py:43
  22.0 0.0 collective-permute-done.6.other_ref.refs_13_
  22.0 0.9 %scores.1.refs_0_ = f32[8,256]{1,0:T(8,128)S(1)} custom-call(f32[8,48]{1,0:T(8,128)S(1)} %get-tuple-element.39.delta_ref, f32[256,192]{1,0:T(8,128)S(1)} %get-tuple-element.36.bias_own, f32[256,192]{1,0:T(8,128)S(1)} %get-tuple-element.37.bias_other, bf16[256,1024]{1,0:T(8,128)(2,1)S(1)} %get-tuple-element.40.key_ref.refs_12_, ...), custom_call_target="tpu_custom_call" | custom-call | flops 201326592 | bytes 1441792 | tf_op jit(solution)/shard_map/scores/scores/pallas_call | solution.py:396
  22.9 0.1 collective-permute-start.10
  23.0 2.0 %collective-permute-start.8 = (f32[8,256]{1,0:T(8,128)S(1)}, f32[8,256]{1,0:T(8,128)S(1)}, u32[]{:S(2)}, u32[]{:S(2)}) collective-permute-start(f32[8,256]{1,0:T(8,128)S(1)} %scores.1.refs_0_), channel_id=1, source_target_pairs={{0,6},{1,7},{2,4},{3,5},{4,2},{5,3},{6,0},{7,1},{8,14},{9,15},{10,... | collective-permute-start | bytes 24584 | tf_op jit(solution)/shard_map/stats_exchange/ppermute | solution.py:43
  24.9 0.0 collective-permute-done.11.refs_9_
  24.9 1.5 %collective-permute-start.9 = (f32[8,256]{1,0:T(8,128)S(1)}, f32[8,256]{1,0:T(8,128)S(1)}, u32[]{:S(2)}, u32[]{:S(2)}) collective-permute-start(f32[8,256]{1,0:T(8,128)S(1)} %scores.1.refs_0_), channel_id=1, source_target_pairs={{0,4},{1,5},{2,6},{3,7},{4,0},{5,1},{6,2},{7,3},{8,12},{9,13},{10,... | collective-permute-start | bytes 24584 | tf_op jit(solution)/shard_map/stats_exchange/ppermute | solution.py:43
  26.4 0.6 %collective-permute-done.13.refs_11_ = bf16[48,1024]{1,0:T(8,128)(2,1)S(1)} collective-permute-done((bf16[48,1024]{1,0:T(8,128)(2,1)S(1)}, bf16[48,1024]{1,0:T(8,128)(2,1)S(1)}, u32[]{:S(2)}, u32[]{:S(2)}) %collective-permute-start.13) | collective-permute-done | bytes 98336 | tf_op jit(solution)/shard_map/cotangent_gather/ppermute | solution.py:43
  27.0 0.0 collective-permute-done.10.refs_3_
  27.1 1.4 %collective-permute-done.8.refs_1_ = f32[8,256]{1,0:T(8,128)S(1)} collective-permute-done((f32[8,256]{1,0:T(8,128)S(1)}, f32[8,256]{1,0:T(8,128)S(1)}, u32[]{:S(2)}, u32[]{:S(2)}) %collective-permute-start.8) | collective-permute-done | bytes 8224 | tf_op jit(solution)/shard_map/stats_exchange/ppermute | solution.py:43
  28.5 1.0 %collective-permute-done.9.refs_2_ = f32[8,256]{1,0:T(8,128)S(1)} collective-permute-done((f32[8,256]{1,0:T(8,128)S(1)}, f32[8,256]{1,0:T(8,128)S(1)}, u32[]{:S(2)}, u32[]{:S(2)}) %collective-permute-start.9) | collective-permute-done | bytes 8224 | tf_op jit(solution)/shard_map/stats_exchange/ppermute | solution.py:43
  29.5 2.6 %grads.1 = (bf16[48,1024]{1,0:T(8,128)(2,1)S(1)}, bf16[48,1024]{1,0:T(8,128)(2,1)S(1)}, bf16[48,1024]{1,0:T(8,128)(2,1)S(1)}, bf16[48,1024]{1,0:T(8,128)(2,1)S(1...) custom-call(f32[256,192]{1,0:T(8,128)S(1)} %get-tuple-element.36.bias_own, ...), custom_call_target="tpu_custom_call" | custom-call | flops 1006632960 | bytes 4980736 | tf_op jit(solution)/shard_map/grads/grads/pallas_call | solution.py:413
  32.1 0.1 collective-permute-start.14
  32.2 2.0 %collective-permute-start.16 = (bf16[48,1024]{1,0:T(8,128)(2,1)S(1)}, bf16[48,1024]{1,0:T(8,128)(2,1)S(1)}, u32[]{:S(2)}, u32[]{:S(2)}) collective-permute-start(bf16[48,1024]{1,0:T(8,128)(2,1)S(1)} %get-tuple-element.54), channel_id=1, source_target_pairs={{0,6},{1,7},{2,4},{3,5},{4,2},{5,3},{6,0},{7,1},{8,14},{9,15},{10,... | collective-permute-start | bytes 294920 | tf_op jit(solution)/shard_map/query_grad_sum/ppermute | solution.py:43
  34.1 0.6 %collective-permute-start.17 = (bf16[48,1024]{1,0:T(8,128)(2,1)S(1)}, bf16[48,1024]{1,0:T(8,128)(2,1)S(1)}, u32[]{:S(2)}, u32[]{:S(2)}) collective-permute-start(bf16[48,1024]{1,0:T(8,128)(2,1)S(1)} %get-tuple-element.55), channel_id=1, source_target_pairs={{0,4},{1,5},{2,6},{3,7},{4,0},{5,1},{6,2},{7,3},{8,12},{9,13},{10,... | collective-permute-start | bytes 294920 | tf_op jit(solution)/shard_map/query_grad_sum/ppermute | solution.py:43
  34.7 1.9 %collective-permute-start.18 = (bf16[48,1024]{1,0:T(8,128)(2,1)S(1)}, bf16[48,1024]{1,0:T(8,128)(2,1)S(1)}, u32[]{:S(2)}, u32[]{:S(2)}) collective-permute-start(bf16[48,1024]{1,0:T(8,128)(2,1)S(1)} %get-tuple-element.56), channel_id=1, source_target_pairs={{0,2},{1,3},{2,0},{3,1},{4,6},{5,7},{6,4},{7,5},{8,10},{9,11},{10,... | collective-permute-start | bytes 294920 | tf_op jit(solution)/shard_map/query_grad_sum/ppermute | solution.py:43
  36.6 1.5 %collective-permute-start.15 = (f32[8,128]{1,0:T(8,128)S(1)}, f32[8,128]{1,0:T(8,128)S(1)}, u32[]{:S(2)}, u32[]{:S(2)}) collective-permute-start(f32[8,128]{1,0:T(8,128)S(1)} %get-tuple-element.51.refs_0_), channel_id=1, source_target_pairs={{0,16},{8,24},{16,0},{24,8},{1,17},{9,25},{17,1},{25,9},{2,18},{10... | collective-permute-start | bytes 12296 | tf_op jit(solution)/shard_map/key_grad_end/ppermute | solution.py:372
  38.1 2.1 %collective-permute-done.15.refs_1_ = f32[8,128]{1,0:T(8,128)S(1)} collective-permute-done((f32[8,128]{1,0:T(8,128)S(1)}, f32[8,128]{1,0:T(8,128)S(1)}, u32[]{:S(2)}, u32[]{:S(2)}) %collective-permute-start.15) | collective-permute-done | bytes 4128 | tf_op jit(solution)/shard_map/key_grad_end/ppermute | solution.py:372
  40.2 1.8 %key_end.1 = (bf16[256,2048]{1,0:T(8,128)(2,1)}, bf16[256,2048]{1,0:T(8,128)(2,1)}, f32[8,128]{1,0:T(8,128)S(1)}) custom-call(bf16[256,2048]{1,0:T(8,128)(2,1)S(1)} %get-tuple-element.49.keep_ref, bf16[256,2048]{1,0:T(8,128)(2,1)S(1)} %collective-permute-done.14.other_ref, f32[8,128]{1,0:T(8,128)S(1)} %get-tuple-element.51.refs_0_, ...), custom_call_target="tpu_custom_call" | custom-call | flops 1000000 | bytes 4194304 | tf_op jit(solution)/shard_map/key_grad_end/key_end/pallas_call | solution.py:433
  42.1 2.1 %collective-permute-done.17.refs_2_ = bf16[48,1024]{1,0:T(8,128)(2,1)S(1)} collective-permute-done((bf16[48,1024]{1,0:T(8,128)(2,1)S(1)}, bf16[48,1024]{1,0:T(8,128)(2,1)S(1)}, u32[]{:S(2)}, u32[]{:S(2)}) %collective-permute-start.17) | collective-permute-done | bytes 98336 | tf_op jit(solution)/shard_map/query_grad_sum/ppermute | solution.py:43
  44.2 0.1 query_end.1
  44.3 0.1 collective-permute-start.19
  44.3 1.2 %collective-permute-done.19 = bf16[24,1024]{1,0:T(8,128)(2,1)S(1)} collective-permute-done((bf16[24,1024]{1,0:T(8,128)(2,1)S(1)}, bf16[24,1024]{1,0:T(8,128)(2,1)S(1)}, u32[]{:S(2)}, u32[]{:S(2)}) %collective-permute-start.19) | collective-permute-done | bytes 49184 | tf_op jit(solution)/shard_map/query_grad_end/ppermute | solution.py:38
  45.6 0.7 %maximum_select_fusion = bf16[1,24,2048]{2,1,0:T(8,128)(2,1)} fusion(bf16[1,24,1024]{2,1,0:T(8,128)(2,1)S(1)} %bitcast.19, bf16[1,24,1024]{2,1,0:T(8,128)(2,1)S(1)} %bitcast.16, pred[]{:T(512)S(6)} %eq.3), kind=kLoop, calls=%fused_computation | loop fusion | flops 442368 | bytes 196609 | tf_op jit(solution)/shard_map/query_grad_end/jit(_where)/select_n | solution.py:276
  (14 shorter events, 0.1 us)
Async XLA Ops:
  0.6 13.9 %collective-permute-start.2 = (bf16[256,2048]{1,0:T(8,128)(2,1)}, bf16[256,2048]{1,0:T(8,128)(2,1)S(1)}, u32[]{:S(2)}, u32[]{:S(2)}) collective-permute-start(bf16[256,2048]{1,0:T(8,128)(2,1)} %bitcast.11), channel_id=1, source_target_pairs={{0,1},{1,0},{2,3},{3,2},{4,5},{5,4},{6,7},{7,6},{8,9},{9,8},{10,11... | collective-permute-start | bytes 3145736 | tf_op jit(solution)/shard_map/key_exchange/ppermute | solution.py:38
  1.1 2.6 %collective-permute-start = (bf16[24,2048]{1,0:T(8,128)(2,1)}, bf16[24,2048]{1,0:T(8,128)(2,1)S(1)}, u32[]{:S(2)}, u32[]{:S(2)}) collective-permute-start(bf16[24,2048]{1,0:T(8,128)(2,1)} %bitcast.14), channel_id=1, source_target_pairs={{0,1},{1,0},{2,3},{3,2},{4,5},{5,4},{6,7},{7,6},{8,9},{9,8},{10,11... | collective-permute-start | bytes 294920 | tf_op jit(solution)/shard_map/sibling_exchange/ppermute | solution.py:38
  1.2 2.6 %copy-start.2 = (bf16[1,24,2048]{2,1,0:T(8,128)(2,1)S(1)}, bf16[1,24,2048]{2,1,0:T(8,128)(2,1)}, u32[]{:S(2)}) copy-start(bf16[1,24,2048]{2,1,0:T(8,128)(2,1)} %param.8) | copy-start | bytes 294916
  3.8 5.7 %copy-start.5 = (bf16[24,1152]{1,0:T(8,128)(2,1)S(1)}, bf16[24,1152]{1,0:T(8,128)(2,1)}, u32[]{:S(2)}) copy-start(bf16[24,1152]{1,0:T(8,128)(2,1)} %get-tuple-element.38) | copy-start | bytes 165892
  3.8 7.0 %copy-start.3 = (bf16[24,1152]{1,0:T(8,128)(2,1)S(1)}, bf16[24,1152]{1,0:T(8,128)(2,1)}, u32[]{:S(2)}) copy-start(bf16[24,1152]{1,0:T(8,128)(2,1)} %get-tuple-element.33.own_ref) | copy-start | bytes 165892
  3.9 10.7 %collective-permute-start.5 = (bf16[48,1024]{1,0:T(8,128)(2,1)S(1)}, bf16[48,1024]{1,0:T(8,128)(2,1)S(1)}, u32[]{:S(2)}, u32[]{:S(2)}) collective-permute-start(bf16[48,1024]{1,0:T(8,128)(2,1)S(1)} %join_queries.1.refs_1_.refs_4_), channel_id=1, source_target_pairs={{0,2},{1,3},{2,0},{3,1},{4,6},{5,7},{6,4},{7,5},{8,10},{9,11},{10,... | collective-permute-start | bytes 294920 | tf_op jit(solution)/shard_map/query_gather/ppermute | solution.py:43
  6.9 7.6 %collective-permute-start.3 = (bf16[48,1024]{1,0:T(8,128)(2,1)S(1)}, bf16[48,1024]{1,0:T(8,128)(2,1)S(1)}, u32[]{:S(2)}, u32[]{:S(2)}) collective-permute-start(bf16[48,1024]{1,0:T(8,128)(2,1)S(1)} %join_queries.1.refs_1_.refs_4_), channel_id=1, source_target_pairs={{0,4},{1,5},{2,6},{3,7},{4,0},{5,1},{6,2},{7,3},{8,12},{9,13},{10,... | collective-permute-start | bytes 294920 | tf_op jit(solution)/shard_map/query_gather/ppermute | solution.py:43
  9.5 1.2 %collective-permute-start.1 = (bf16[24,1152]{1,0:T(8,128)(2,1)S(1)}, bf16[24,1152]{1,0:T(8,128)(2,1)S(1)}, u32[]{:S(2)}, u32[]{:S(2)}) collective-permute-start(bf16[24,1152]{1,0:T(8,128)(2,1)S(1)} %copy-done.5), channel_id=1, source_target_pairs={{0,1},{1,0},{2,3},{3,2},{4,5},{5,4},{6,7},{7,6},{8,9},{9,8},{10,11... | collective-permute-start | bytes 165896 | tf_op jit(solution)/shard_map/sibling_exchange/ppermute | solution.py:38
  10.8 1.7 %copy-start.4 = (f32[8,256]{1,0:T(8,128)S(1)}, f32[8,256]{1,0:T(8,128)}, u32[]{:S(2)}) copy-start(f32[8,256]{1,0:T(8,128)} %get-tuple-element.32.docs_ref) | copy-start | bytes 24580
  10.9 3.6 %collective-permute-start.4 = (f32[8,128]{1,0:T(8,128)S(1)}, f32[8,128]{1,0:T(8,128)S(1)}, u32[]{:S(2)}, u32[]{:S(2)}) collective-permute-start(f32[8,128]{1,0:T(8,128)S(1)} %get-tuple-element.42), channel_id=1, source_target_pairs={{0,8},{8,0},{16,24},{24,16},{1,9},{9,1},{17,25},{25,17},{2,10},{10... | collective-permute-start | bytes 12296 | tf_op jit(solution)/shard_map/mask_count/ppermute | solution.py:372
  12.4 1.2 %copy-start.1 = (bf16[1,256,2048]{2,1,0:T(8,128)(2,1)S(1)}, bf16[1,256,2048]{2,1,0:T(8,128)(2,1)}, u32[]{:S(2)}) copy-start(bf16[1,256,2048]{2,1,0:T(8,128)(2,1)} %param.9) | copy-start | bytes 3145732
  14.0 15.5 %copy-start = (bf16[1,256,2048]{2,1,0:T(8,128)(2,1)S(1)}, bf16[1,256,2048]{2,1,0:T(8,128)(2,1)}, u32[]{:S(2)}) copy-start(bf16[1,256,2048]{2,1,0:T(8,128)(2,1)} %param.10) | copy-start | bytes 3145732
  14.6 7.4 %collective-permute-start.6 = (bf16[256,1024]{1,0:T(8,128)(2,1)S(1)}, bf16[256,1024]{1,0:T(8,128)(2,1)S(1)}, u32[]{:S(2)}, u32[]{:S(2)}) collective-permute-start(bf16[256,1024]{1,0:T(8,128)(2,1)S(1)} %get-tuple-element.45), channel_id=1, source_target_pairs={{0,1},{1,0},{2,3},{3,2},{4,5},{5,4},{6,7},{7,6},{8,9},{9,8},{10,11... | collective-permute-start | bytes 1572872 | tf_op jit(solution)/shard_map/key_exchange/ppermute | solution.py:38
  14.7 7.3 %collective-permute-start.7 = (bf16[48,1024]{1,0:T(8,128)(2,1)S(1)}, bf16[48,1024]{1,0:T(8,128)(2,1)S(1)}, u32[]{:S(2)}, u32[]{:S(2)}) collective-permute-start(bf16[48,1024]{1,0:T(8,128)(2,1)S(1)} %collective-permute-done.3.refs_2_.refs_5_), channel_id=1, source_target_pairs={{0,2},{1,3},{2,0},{3,1},{4,6},{5,7},{6,4},{7,5},{8,10},{9,11},{10,... | collective-permute-start | bytes 294920 | tf_op jit(solution)/shard_map/query_forward/ppermute | solution.py:43
  15.2 9.8 %collective-permute-start.11 = (bf16[48,1024]{1,0:T(8,128)(2,1)S(1)}, bf16[48,1024]{1,0:T(8,128)(2,1)S(1)}, u32[]{:S(2)}, u32[]{:S(2)}) collective-permute-start(bf16[48,1024]{1,0:T(8,128)(2,1)S(1)} %get-tuple-element.47.refs_8_), channel_id=1, source_target_pairs={{0,4},{1,5},{2,6},{3,7},{4,0},{5,1},{6,2},{7,3},{8,12},{9,13},{10,... | collective-permute-start | bytes 294920 | tf_op jit(solution)/shard_map/cotangent_gather/ppermute | solution.py:43
  17.5 8.9 %collective-permute-start.12 = (bf16[48,1024]{1,0:T(8,128)(2,1)S(1)}, bf16[48,1024]{1,0:T(8,128)(2,1)S(1)}, u32[]{:S(2)}, u32[]{:S(2)}) collective-permute-start(bf16[48,1024]{1,0:T(8,128)(2,1)S(1)} %get-tuple-element.47.refs_8_), channel_id=1, source_target_pairs={{0,2},{1,3},{2,0},{3,1},{4,6},{5,7},{6,4},{7,5},{8,10},{9,11},{10,... | collective-permute-start | bytes 294920 | tf_op jit(solution)/shard_map/cotangent_gather/ppermute | solution.py:43
  17.6 9.4 %collective-permute-start.13 = (bf16[48,1024]{1,0:T(8,128)(2,1)S(1)}, bf16[48,1024]{1,0:T(8,128)(2,1)S(1)}, u32[]{:S(2)}, u32[]{:S(2)}) collective-permute-start(bf16[48,1024]{1,0:T(8,128)(2,1)S(1)} %get-tuple-element.47.refs_8_), channel_id=1, source_target_pairs={{0,6},{1,7},{2,4},{3,5},{4,2},{5,3},{6,0},{7,1},{8,14},{9,15},{10,... | collective-permute-start | bytes 294920 | tf_op jit(solution)/shard_map/cotangent_gather/ppermute | solution.py:43
  22.9 4.2 %collective-permute-start.10 = (f32[8,256]{1,0:T(8,128)S(1)}, f32[8,256]{1,0:T(8,128)S(1)}, u32[]{:S(2)}, u32[]{:S(2)}) collective-permute-start(f32[8,256]{1,0:T(8,128)S(1)} %scores.1.refs_0_), channel_id=1, source_target_pairs={{0,2},{1,3},{2,0},{3,1},{4,6},{5,7},{6,4},{7,5},{8,10},{9,11},{10,... | collective-permute-start | bytes 24584 | tf_op jit(solution)/shard_map/stats_exchange/ppermute | solution.py:43
  23.0 5.5 %collective-permute-start.8 = (f32[8,256]{1,0:T(8,128)S(1)}, f32[8,256]{1,0:T(8,128)S(1)}, u32[]{:S(2)}, u32[]{:S(2)}) collective-permute-start(f32[8,256]{1,0:T(8,128)S(1)} %scores.1.refs_0_), channel_id=1, source_target_pairs={{0,6},{1,7},{2,4},{3,5},{4,2},{5,3},{6,0},{7,1},{8,14},{9,15},{10,... | collective-permute-start | bytes 24584 | tf_op jit(solution)/shard_map/stats_exchange/ppermute | solution.py:43
  24.9 4.6 %collective-permute-start.9 = (f32[8,256]{1,0:T(8,128)S(1)}, f32[8,256]{1,0:T(8,128)S(1)}, u32[]{:S(2)}, u32[]{:S(2)}) collective-permute-start(f32[8,256]{1,0:T(8,128)S(1)} %scores.1.refs_0_), channel_id=1, source_target_pairs={{0,4},{1,5},{2,6},{3,7},{4,0},{5,1},{6,2},{7,3},{8,12},{9,13},{10,... | collective-permute-start | bytes 24584 | tf_op jit(solution)/shard_map/stats_exchange/ppermute | solution.py:43
  32.1 8.1 %collective-permute-start.14 = (bf16[256,2048]{1,0:T(8,128)(2,1)S(1)}, bf16[256,2048]{1,0:T(8,128)(2,1)S(1)}, u32[]{:S(2)}, u32[]{:S(2)}) collective-permute-start(bf16[256,2048]{1,0:T(8,128)(2,1)S(1)} %get-tuple-element.50), channel_id=1, source_target_pairs={{0,1},{1,0},{2,3},{3,2},{4,5},{5,4},{6,7},{7,6},{8,9},{9,8},{10,11... | collective-permute-start | bytes 3145736 | tf_op jit(solution)/shard_map/key_grad_end/ppermute | solution.py:38
  32.2 9.9 %collective-permute-start.16 = (bf16[48,1024]{1,0:T(8,128)(2,1)S(1)}, bf16[48,1024]{1,0:T(8,128)(2,1)S(1)}, u32[]{:S(2)}, u32[]{:S(2)}) collective-permute-start(bf16[48,1024]{1,0:T(8,128)(2,1)S(1)} %get-tuple-element.54), channel_id=1, source_target_pairs={{0,6},{1,7},{2,4},{3,5},{4,2},{5,3},{6,0},{7,1},{8,14},{9,15},{10,... | collective-permute-start | bytes 294920 | tf_op jit(solution)/shard_map/query_grad_sum/ppermute | solution.py:43
  34.1 10.0 %collective-permute-start.17 = (bf16[48,1024]{1,0:T(8,128)(2,1)S(1)}, bf16[48,1024]{1,0:T(8,128)(2,1)S(1)}, u32[]{:S(2)}, u32[]{:S(2)}) collective-permute-start(bf16[48,1024]{1,0:T(8,128)(2,1)S(1)} %get-tuple-element.55), channel_id=1, source_target_pairs={{0,4},{1,5},{2,6},{3,7},{4,0},{5,1},{6,2},{7,3},{8,12},{9,13},{10,... | collective-permute-start | bytes 294920 | tf_op jit(solution)/shard_map/query_grad_sum/ppermute | solution.py:43
  34.7 9.4 %collective-permute-start.18 = (bf16[48,1024]{1,0:T(8,128)(2,1)S(1)}, bf16[48,1024]{1,0:T(8,128)(2,1)S(1)}, u32[]{:S(2)}, u32[]{:S(2)}) collective-permute-start(bf16[48,1024]{1,0:T(8,128)(2,1)S(1)} %get-tuple-element.56), channel_id=1, source_target_pairs={{0,2},{1,3},{2,0},{3,1},{4,6},{5,7},{6,4},{7,5},{8,10},{9,11},{10,... | collective-permute-start | bytes 294920 | tf_op jit(solution)/shard_map/query_grad_sum/ppermute | solution.py:43
  36.6 3.6 %collective-permute-start.15 = (f32[8,128]{1,0:T(8,128)S(1)}, f32[8,128]{1,0:T(8,128)S(1)}, u32[]{:S(2)}, u32[]{:S(2)}) collective-permute-start(f32[8,128]{1,0:T(8,128)S(1)} %get-tuple-element.51.refs_0_), channel_id=1, source_target_pairs={{0,16},{8,24},{16,0},{24,8},{1,17},{9,25},{17,1},{25,9},{2,18},{10... | collective-permute-start | bytes 12296 | tf_op jit(solution)/shard_map/key_grad_end/ppermute | solution.py:372
  44.3 1.3 %collective-permute-start.19 = (bf16[24,1024]{1,0:T(8,128)(2,1)S(1)}, bf16[24,1024]{1,0:T(8,128)(2,1)S(1)}, u32[]{:S(2)}, u32[]{:S(2)}) collective-permute-start(bf16[24,1024]{1,0:T(8,128)(2,1)S(1)} %get-tuple-element.58), channel_id=1, source_target_pairs={{0,1},{1,0},{2,3},{3,2},{4,5},{5,4},{6,7},{7,6},{8,9},{9,8},{10,11... | collective-permute-start | bytes 147464 | tf_op jit(solution)/shard_map/query_grad_end/ppermute | solution.py:38

commit v9 on v8

--- a/solution.py
+++ b/solution.py
@@ -18,7 +18,6 @@
 BF16 = jnp.bfloat16
 ANY = pl.BlockSpec(memory_space=pl.ANY)
 VMEM = pl.BlockSpec(memory_space=pltpu.VMEM)
-SMEM = pl.BlockSpec(memory_space=pltpu.SMEM)
 NT = (((1,), (1,)), ((), ()))
 TN = (((0,), (0,)), ((), ()))
 NN = (((1,), (0,)), ((), ()))
@@ -75,21 +74,35 @@
     offsets,
     dec_rows,
     enc_rows,
-    in_ref,
-    target_ref,
+    in_any,
+    target_any,
     grad_ref,
     out_ref,
     mask_ref,
     send_ref,
     keep_ref,
     docs_ref,
-    grad_held, out_held, mask_held, sems
+    in_ref,
+    target_ref,
+    grad_held,
+    out_held,
+    mask_held,
+    sems,
 ):
     chip, core = position()
     rows = grad_ref.shape[0]
     copies = start_all(
-        [(mask_ref, mask_held), (grad_ref, grad_held), (out_ref, out_held)], sems
-    )
+        [
+            (in_any, in_ref),
+            (target_any, target_ref),
+            (mask_ref, mask_held),
+            (grad_ref, grad_held),
+            (out_ref, out_held),
+        ],
+        sems,
+    )
+    for copy in copies[:3]:
+        copy.wait()
     lane = lax.broadcasted_iota(jnp.int32, (1, docs_ref.shape[1]), 1)
     block = dec_rows // len(offsets)
     dec = lane + chip * block
@@ -99,14 +112,13 @@
     for side in (core, 1 - core):
         docs.append(document_of(lane + (2 * chip + side) * enc_rows, in_ref))
     docs_ref[...] = jnp.concatenate(docs + docs + docs[:2], 0).astype(F32)
-    copies[0].wait()
     mask_row = mask_held[...].astype(F32)
     here = lax.broadcasted_iota(jnp.int32, (rows, rows), 0) == lax.broadcasted_iota(
         jnp.int32, (rows, rows), 1
     )
     mask = jnp.sum(jnp.where(here, mask_row, 0.0), axis=1, keepdims=True)
     lane = lax.broadcasted_iota(jnp.int32, (rows, EXTRA), 1)
-    for copy in copies[1:]:
+    for copy in copies[3:]:
         copy.wait()
     masked = grad_held[...].astype(F32) * mask
     products = masked * out_held[...].astype(F32)
@@ -319,13 +331,15 @@
         g_send, g_keep, docs = kernel_call(
             functools.partial(prepare_kernel, offsets, dec_rows, enc_local),
             (sent, sent, docs),
-            [SMEM] * 2 + [ANY] * 3,
+            [ANY] * 5,
             (VMEM, VMEM, VMEM),
             [
+                pltpu.SMEM(lengths[0].shape, jnp.int32),
+                pltpu.SMEM(lengths[1].shape, jnp.int32),
                 pltpu.VMEM((dec_local, features), BF16),
                 pltpu.VMEM((dec_local, features), BF16),
                 pltpu.VMEM((1, dec_local), jnp.int32),
-                pltpu.SemaphoreType.DMA((3,)),
+                pltpu.SemaphoreType.DMA((5,)),
             ],
             10**5,
             10**6,
@@ -387,7 +401,7 @@
         g_blocks = [g_block] + [across(sent, offset) for offset in offsets[1:]]
 
     with jax.named_scope("key_exchange"):
-        v_recv = to_sibling(value_rows)
+        v_recv = to_sibling(after(value_rows, q_recv)[0])
         k_send, v_recv, *_ = after(k_send, v_recv, *q_far, q_near)
         k_recv = to_sibling(k_send)
 

time: 46.5 us -> 45.7 us (0.983)
  Pallas kernels: 8.44 us -> 7.67 us
    pallas_call x1, Pallas kernels: 2.55 us -> 1.8 us  [local(): kernel_call(functools.partial(prepare_kernel, offsets, dec_rows, enc_loca...]
  transfers between devices with their start and end apart: 20 -> 20, of which waited for: 9 -> 9; matrix products, arithmetic and copies ran while one was open for 0% -> 0% of each run, Pallas kernels for 12% -> 11%
where the time goes in v9:
time: 45.7 us; the launch traced here: 45.5 us
  starting transfers between devices  22.5 us (49%)
  waiting for transfers between devices  12.7 us (28%)
  Pallas kernels  7.67 us (17%)
  local copies, waits for them, and re-layouts  1.25 us (3%)
  between operations  0.77 us (2%)
  other arithmetic  0.66 us (1%)
    ppermute x12, starting transfers between devices, across(): lax.ppermute(block, 'seq', [(i, i ^ 2 * apart) for i in range(count)])  18.6 us
    ppermute x12, waiting for transfers between devices, across(): lax.ppermute(block, 'seq', [(i, i ^ 2 * apart) for i in range(count)])  7.54 us
    ppermute x2, starting transfers between devices, over_groups(): lax.ppermute(count, 'dp', [(i, i ^ apart) for i in range(data_groups)])  3.02 us
    ppermute x2, waiting for transfers between devices, over_groups(): lax.ppermute(count, 'dp', [(i, i ^ apart) for i in range(data_groups)])  2.65 us
    pallas_call x1, Pallas kernels, local(): kernel_call(functools.partial(grads_kernel, offsets), (block,) * chips +...  2.58 us
    ppermute x6, waiting for transfers between devices, to_sibling(): return lax.ppermute(block, 'seq', [(i, i ^ 1) for i in range(count)])  2.46 us
    pallas_call x1, Pallas kernels, local(): kernel_call(functools.partial(key_end_kernel, rows_in_all), (whole, whole...  1.84 us
    pallas_call x1, Pallas kernels, local(): kernel_call(functools.partial(prepare_kernel, offsets, dec_rows, enc_loca...  1.8 us
  transfers between devices with their start and end apart: 20, of which 9 were waited for; matrix products, arithmetic and copies ran while one was open for 0% of the time, Pallas kernels for 11%

profile of v9, /device:TPU:0, one launch (start us, length us, event | category | flops | bytes accessed | tf_op | source)
XLA Modules:
  0.0 45.5 jit_solution(2597876865392503808)
XLA Ops:
  0.6 0.5 %collective-permute-start = (bf16[24,2048]{1,0:T(8,128)(2,1)}, bf16[24,2048]{1,0:T(8,128)(2,1)S(1)}, u32[]{:S(2)}, u32[]{:S(2)}) collective-permute-start(bf16[24,2048]{1,0:T(8,128)(2,1)} %bitcast.14), channel_id=1, source_target_pairs={{0,1},{1,0},{2,3},{3,2},{4,5},{5,4},{6,7},{7,6},{8,9},{9,8},{10,11... | collective-permute-start | bytes 294920 | tf_op jit(solution)/shard_map/sibling_exchange/ppermute | solution.py:37
  1.2 1.8 %prepare.1 = (bf16[24,1152]{1,0:T(8,128)(2,1)}, bf16[24,1152]{1,0:T(8,128)(2,1)}, f32[8,256]{1,0:T(8,128)}) custom-call(s32[1,4]{1,0:T(1,128)} %bitcast.20, s32[1,4]{1,0:T(1,128)} %bitcast.21, bf16[24,2048]{1,0:T(8,128)(2,1)} %bitcast.17, bf16[24,2048]{1,0:T(8,128)(2,1)} %bitcast.18, s32[1,24]{1,0:T(1,128)} %mask_ref.1), custom_call_target="tpu_custom_call" | custom-call | flops 100000 | bytes 1000000 | tf_op jit(solution)/shard_map/sibling_exchange/prepare/pallas_call | solution.py:331
  3.0 0.0 collective-permute-done.other_ref
  3.0 0.0 copy-start.5
  3.0 0.0 copy-start.3
  3.0 0.1 collective-permute-start.2
  3.1 3.1 %collective-permute-start.5 = (bf16[48,1024]{1,0:T(8,128)(2,1)S(1)}, bf16[48,1024]{1,0:T(8,128)(2,1)S(1)}, u32[]{:S(2)}, u32[]{:S(2)}) collective-permute-start(bf16[48,1024]{1,0:T(8,128)(2,1)S(1)} %join_queries.1.refs_1_.refs_4_), channel_id=1, source_target_pairs={{0,2},{1,3},{2,0},{3,1},{4,6},{5,7},{6,4},{7,5},{8,10},{9,11},{10,... | collective-permute-start | bytes 294920 | tf_op jit(solution)/shard_map/query_gather/ppermute | solution.py:42
  6.2 2.6 %collective-permute-start.3 = (bf16[48,1024]{1,0:T(8,128)(2,1)S(1)}, bf16[48,1024]{1,0:T(8,128)(2,1)S(1)}, u32[]{:S(2)}, u32[]{:S(2)}) collective-permute-start(bf16[48,1024]{1,0:T(8,128)(2,1)S(1)} %join_queries.1.refs_1_.refs_4_), channel_id=1, source_target_pairs={{0,4},{1,5},{2,6},{3,7},{4,0},{5,1},{6,2},{7,3},{8,12},{9,13},{10,... | collective-permute-start | bytes 294920 | tf_op jit(solution)/shard_map/query_gather/ppermute | solution.py:42
  8.8 0.0 collective-permute-start.1
  8.8 1.2 %collective-permute-done.1.other_ref = bf16[24,1152]{1,0:T(8,128)(2,1)S(1)} collective-permute-done((bf16[24,1152]{1,0:T(8,128)(2,1)S(1)}, bf16[24,1152]{1,0:T(8,128)(2,1)S(1)}, u32[]{:S(2)}, u32[]{:S(2)}) %collective-permute-start.1) | collective-permute-done | bytes 55328 | tf_op jit(solution)/shard_map/sibling_exchange/ppermute | solution.py:37
  10.1 0.2 join_cotangents.1
  10.2 1.5 %collective-permute-start.4 = (f32[8,128]{1,0:T(8,128)S(1)}, f32[8,128]{1,0:T(8,128)S(1)}, u32[]{:S(2)}, u32[]{:S(2)}) collective-permute-start(f32[8,128]{1,0:T(8,128)S(1)} %get-tuple-element.44), channel_id=1, source_target_pairs={{0,8},{8,0},{16,24},{24,16},{1,9},{9,1},{17,25},{25,17},{2,10},{10... | collective-permute-start | bytes 12296 | tf_op jit(solution)/shard_map/mask_count/ppermute | solution.py:386
  11.7 1.2 %copy-done.1 = bf16[1,256,2048]{2,1,0:T(8,128)(2,1)S(1)} copy-done((bf16[1,256,2048]{2,1,0:T(8,128)(2,1)S(1)}, bf16[1,256,2048]{2,1,0:T(8,128)(2,1)}, u32[]{:S(2)}) %copy-start.1) | copy-done | bytes 1048600
  13.0 0.3 setup.1
  13.3 0.0 copy-start
  13.3 0.6 %collective-permute-done.4 = f32[8,128]{1,0:T(8,128)S(1)} collective-permute-done((f32[8,128]{1,0:T(8,128)S(1)}, f32[8,128]{1,0:T(8,128)S(1)}, u32[]{:S(2)}, u32[]{:S(2)}) %collective-permute-start.4) | collective-permute-done | bytes 4128 | tf_op jit(solution)/shard_map/mask_count/ppermute | solution.py:386
  13.8 0.0 collective-permute-done.5.refs_3_.refs_6_
  13.9 0.0 collective-permute-done.2.refs_15_
  13.9 0.1 collective-permute-start.6
  13.9 0.5 %collective-permute-start.7 = (bf16[48,1024]{1,0:T(8,128)(2,1)S(1)}, bf16[48,1024]{1,0:T(8,128)(2,1)S(1)}, u32[]{:S(2)}, u32[]{:S(2)}) collective-permute-start(bf16[48,1024]{1,0:T(8,128)(2,1)S(1)} %collective-permute-done.3.refs_2_.refs_5_), channel_id=1, source_target_pairs={{0,2},{1,3},{2,0},{3,1},{4,6},{5,7},{6,4},{7,5},{8,10},{9,11},{10,... | collective-permute-start | bytes 294920 | tf_op jit(solution)/shard_map/query_forward/ppermute | solution.py:42
  14.5 2.3 %collective-permute-start.11 = (bf16[48,1024]{1,0:T(8,128)(2,1)S(1)}, bf16[48,1024]{1,0:T(8,128)(2,1)S(1)}, u32[]{:S(2)}, u32[]{:S(2)}) collective-permute-start(bf16[48,1024]{1,0:T(8,128)(2,1)S(1)} %get-tuple-element.49.refs_8_), channel_id=1, source_target_pairs={{0,4},{1,5},{2,6},{3,7},{4,0},{5,1},{6,2},{7,3},{8,12},{9,13},{10,... | collective-permute-start | bytes 294920 | tf_op jit(solution)/shard_map/cotangent_gather/ppermute | solution.py:42
  16.8 0.1 collective-permute-start.12
  16.9 2.0 %collective-permute-start.13 = (bf16[48,1024]{1,0:T(8,128)(2,1)S(1)}, bf16[48,1024]{1,0:T(8,128)(2,1)S(1)}, u32[]{:S(2)}, u32[]{:S(2)}) collective-permute-start(bf16[48,1024]{1,0:T(8,128)(2,1)S(1)} %get-tuple-element.49.refs_8_), channel_id=1, source_target_pairs={{0,6},{1,7},{2,4},{3,5},{4,2},{5,3},{6,0},{7,1},{8,14},{9,15},{10,... | collective-permute-start | bytes 294920 | tf_op jit(solution)/shard_map/cotangent_gather/ppermute | solution.py:42
  18.9 2.4 %collective-permute-done.7.refs_4_.refs_7_ = bf16[48,1024]{1,0:T(8,128)(2,1)S(1)} collective-permute-done((bf16[48,1024]{1,0:T(8,128)(2,1)S(1)}, bf16[48,1024]{1,0:T(8,128)(2,1)S(1)}, u32[]{:S(2)}, u32[]{:S(2)}) %collective-permute-start.7) | collective-permute-done | bytes 98336 | tf_op jit(solution)/shard_map/query_forward/ppermute | solution.py:42
  21.2 0.0 collective-permute-done.6.other_ref.refs_13_
  21.2 0.9 %scores.1.refs_0_ = f32[8,256]{1,0:T(8,128)S(1)} custom-call(f32[8,48]{1,0:T(8,128)S(1)} %get-tuple-element.40.delta_ref, f32[256,192]{1,0:T(8,128)S(1)} %get-tuple-element.37.bias_own, f32[256,192]{1,0:T(8,128)S(1)} %get-tuple-element.38.bias_other, bf16[256,1024]{1,0:T(8,128)(2,1)S(1)} %get-tuple-element.41.key_ref.refs_12_, ...), custom_call_target="tpu_custom_call" | custom-call | flops 201326592 | bytes 1441792 | tf_op jit(solution)/shard_map/scores/scores/pallas_call | solution.py:410
  22.1 0.1 collective-permute-start.10
  22.2 2.0 %collective-permute-start.8 = (f32[8,256]{1,0:T(8,128)S(1)}, f32[8,256]{1,0:T(8,128)S(1)}, u32[]{:S(2)}, u32[]{:S(2)}) collective-permute-start(f32[8,256]{1,0:T(8,128)S(1)} %scores.1.refs_0_), channel_id=1, source_target_pairs={{0,6},{1,7},{2,4},{3,5},{4,2},{5,3},{6,0},{7,1},{8,14},{9,15},{10,... | collective-permute-start | bytes 24584 | tf_op jit(solution)/shard_map/stats_exchange/ppermute | solution.py:42
  24.2 0.0 collective-permute-done.11.refs_9_
  24.2 1.5 %collective-permute-start.9 = (f32[8,256]{1,0:T(8,128)S(1)}, f32[8,256]{1,0:T(8,128)S(1)}, u32[]{:S(2)}, u32[]{:S(2)}) collective-permute-start(f32[8,256]{1,0:T(8,128)S(1)} %scores.1.refs_0_), channel_id=1, source_target_pairs={{0,4},{1,5},{2,6},{3,7},{4,0},{5,1},{6,2},{7,3},{8,12},{9,13},{10,... | collective-permute-start | bytes 24584 | tf_op jit(solution)/shard_map/stats_exchange/ppermute | solution.py:42
  25.7 0.0 collective-permute-done.12.refs_10_
  25.7 0.6 %collective-permute-done.13.refs_11_ = bf16[48,1024]{1,0:T(8,128)(2,1)S(1)} collective-permute-done((bf16[48,1024]{1,0:T(8,128)(2,1)S(1)}, bf16[48,1024]{1,0:T(8,128)(2,1)S(1)}, u32[]{:S(2)}, u32[]{:S(2)}) %collective-permute-start.13) | collective-permute-done | bytes 98336 | tf_op jit(solution)/shard_map/cotangent_gather/ppermute | solution.py:42
  26.3 0.0 collective-permute-done.10.refs_3_
  26.3 1.4 %collective-permute-done.8.refs_1_ = f32[8,256]{1,0:T(8,128)S(1)} collective-permute-done((f32[8,256]{1,0:T(8,128)S(1)}, f32[8,256]{1,0:T(8,128)S(1)}, u32[]{:S(2)}, u32[]{:S(2)}) %collective-permute-start.8) | collective-permute-done | bytes 8224 | tf_op jit(solution)/shard_map/stats_exchange/ppermute | solution.py:42
  27.7 1.0 %collective-permute-done.9.refs_2_ = f32[8,256]{1,0:T(8,128)S(1)} collective-permute-done((f32[8,256]{1,0:T(8,128)S(1)}, f32[8,256]{1,0:T(8,128)S(1)}, u32[]{:S(2)}, u32[]{:S(2)}) %collective-permute-start.9) | collective-permute-done | bytes 8224 | tf_op jit(solution)/shard_map/stats_exchange/ppermute | solution.py:42
  28.7 2.6 %grads.1 = (bf16[48,1024]{1,0:T(8,128)(2,1)S(1)}, bf16[48,1024]{1,0:T(8,128)(2,1)S(1)}, bf16[48,1024]{1,0:T(8,128)(2,1)S(1)}, bf16[48,1024]{1,0:T(8,128)(2,1)S(1...) custom-call(f32[256,192]{1,0:T(8,128)S(1)} %get-tuple-element.37.bias_own, ...), custom_call_target="tpu_custom_call" | custom-call | flops 1006632960 | bytes 4980736 | tf_op jit(solution)/shard_map/grads/grads/pallas_call | solution.py:427
  31.3 0.1 collective-permute-start.14
  31.4 2.0 %collective-permute-start.16 = (bf16[48,1024]{1,0:T(8,128)(2,1)S(1)}, bf16[48,1024]{1,0:T(8,128)(2,1)S(1)}, u32[]{:S(2)}, u32[]{:S(2)}) collective-permute-start(bf16[48,1024]{1,0:T(8,128)(2,1)S(1)} %get-tuple-element.56), channel_id=1, source_target_pairs={{0,6},{1,7},{2,4},{3,5},{4,2},{5,3},{6,0},{7,1},{8,14},{9,15},{10,... | collective-permute-start | bytes 294920 | tf_op jit(solution)/shard_map/query_grad_sum/ppermute | solution.py:42
  33.4 0.6 %collective-permute-start.17 = (bf16[48,1024]{1,0:T(8,128)(2,1)S(1)}, bf16[48,1024]{1,0:T(8,128)(2,1)S(1)}, u32[]{:S(2)}, u32[]{:S(2)}) collective-permute-start(bf16[48,1024]{1,0:T(8,128)(2,1)S(1)} %get-tuple-element.57), channel_id=1, source_target_pairs={{0,4},{1,5},{2,6},{3,7},{4,0},{5,1},{6,2},{7,3},{8,12},{9,13},{10,... | collective-permute-start | bytes 294920 | tf_op jit(solution)/shard_map/query_grad_sum/ppermute | solution.py:42
  34.0 1.9 %collective-permute-start.18 = (bf16[48,1024]{1,0:T(8,128)(2,1)S(1)}, bf16[48,1024]{1,0:T(8,128)(2,1)S(1)}, u32[]{:S(2)}, u32[]{:S(2)}) collective-permute-start(bf16[48,1024]{1,0:T(8,128)(2,1)S(1)} %get-tuple-element.58), channel_id=1, source_target_pairs={{0,2},{1,3},{2,0},{3,1},{4,6},{5,7},{6,4},{7,5},{8,10},{9,11},{10,... | collective-permute-start | bytes 294920 | tf_op jit(solution)/shard_map/query_grad_sum/ppermute | solution.py:42
  35.8 1.5 %collective-permute-start.15 = (f32[8,128]{1,0:T(8,128)S(1)}, f32[8,128]{1,0:T(8,128)S(1)}, u32[]{:S(2)}, u32[]{:S(2)}) collective-permute-start(f32[8,128]{1,0:T(8,128)S(1)} %get-tuple-element.53.refs_0_), channel_id=1, source_target_pairs={{0,16},{8,24},{16,0},{24,8},{1,17},{9,25},{17,1},{25,9},{2,18},{10... | collective-permute-start | bytes 12296 | tf_op jit(solution)/shard_map/key_grad_end/ppermute | solution.py:386
  37.4 2.1 %collective-permute-done.15.refs_1_ = f32[8,128]{1,0:T(8,128)S(1)} collective-permute-done((f32[8,128]{1,0:T(8,128)S(1)}, f32[8,128]{1,0:T(8,128)S(1)}, u32[]{:S(2)}, u32[]{:S(2)}) %collective-permute-start.15) | collective-permute-done | bytes 4128 | tf_op jit(solution)/shard_map/key_grad_end/ppermute | solution.py:386
  39.5 1.8 %key_end.1 = (bf16[256,2048]{1,0:T(8,128)(2,1)}, bf16[256,2048]{1,0:T(8,128)(2,1)}, f32[8,128]{1,0:T(8,128)S(1)}) custom-call(bf16[256,2048]{1,0:T(8,128)(2,1)S(1)} %get-tuple-element.51.keep_ref, bf16[256,2048]{1,0:T(8,128)(2,1)S(1)} %collective-permute-done.14.other_ref, f32[8,128]{1,0:T(8,128)S(1)} %get-tuple-element.53.refs_0_, ...), custom_call_target="tpu_custom_call" | custom-call | flops 1000000 | bytes 4194304 | tf_op jit(solution)/shard_map/key_grad_end/key_end/pallas_call | solution.py:447
  41.3 2.1 %collective-permute-done.17.refs_2_ = bf16[48,1024]{1,0:T(8,128)(2,1)S(1)} collective-permute-done((bf16[48,1024]{1,0:T(8,128)(2,1)S(1)}, bf16[48,1024]{1,0:T(8,128)(2,1)S(1)}, u32[]{:S(2)}, u32[]{:S(2)}) %collective-permute-start.17) | collective-permute-done | bytes 98336 | tf_op jit(solution)/shard_map/query_grad_sum/ppermute | solution.py:42
  43.4 0.1 query_end.1
  43.5 0.1 collective-permute-start.19
  43.6 1.2 %collective-permute-done.19 = bf16[24,1024]{1,0:T(8,128)(2,1)S(1)} collective-permute-done((bf16[24,1024]{1,0:T(8,128)(2,1)S(1)}, bf16[24,1024]{1,0:T(8,128)(2,1)S(1)}, u32[]{:S(2)}, u32[]{:S(2)}) %collective-permute-start.19) | collective-permute-done | bytes 49184 | tf_op jit(solution)/shard_map/query_grad_end/ppermute | solution.py:37
  44.8 0.7 %maximum_select_fusion = bf16[1,24,2048]{2,1,0:T(8,128)(2,1)} fusion(bf16[1,24,1024]{2,1,0:T(8,128)(2,1)S(1)} %bitcast.19, bf16[1,24,1024]{2,1,0:T(8,128)(2,1)S(1)} %bitcast.16, pred[]{:T(512)S(6)} %eq.3), kind=kLoop, calls=%fused_computation | loop fusion | flops 442368 | bytes 196609 | tf_op jit(solution)/shard_map/query_grad_end/jit(_where)/select_n | solution.py:288
  (14 shorter events, 0.0 us)
Async XLA Ops:
  0.6 2.3 %collective-permute-start = (bf16[24,2048]{1,0:T(8,128)(2,1)}, bf16[24,2048]{1,0:T(8,128)(2,1)S(1)}, u32[]{:S(2)}, u32[]{:S(2)}) collective-permute-start(bf16[24,2048]{1,0:T(8,128)(2,1)} %bitcast.14), channel_id=1, source_target_pairs={{0,1},{1,0},{2,3},{3,2},{4,5},{5,4},{6,7},{7,6},{8,9},{9,8},{10,11... | collective-permute-start | bytes 294920 | tf_op jit(solution)/shard_map/sibling_exchange/ppermute | solution.py:37
  1.1 2.0 %copy-start.2 = (bf16[1,24,2048]{2,1,0:T(8,128)(2,1)S(1)}, bf16[1,24,2048]{2,1,0:T(8,128)(2,1)}, u32[]{:S(2)}) copy-start(bf16[1,24,2048]{2,1,0:T(8,128)(2,1)} %param.8) | copy-start | bytes 294916
  3.0 5.9 %copy-start.5 = (bf16[24,1152]{1,0:T(8,128)(2,1)S(1)}, bf16[24,1152]{1,0:T(8,128)(2,1)}, u32[]{:S(2)}) copy-start(bf16[24,1152]{1,0:T(8,128)(2,1)} %get-tuple-element.39) | copy-start | bytes 165892
  3.0 7.1 %copy-start.3 = (bf16[24,1152]{1,0:T(8,128)(2,1)S(1)}, bf16[24,1152]{1,0:T(8,128)(2,1)}, u32[]{:S(2)}) copy-start(bf16[24,1152]{1,0:T(8,128)(2,1)} %get-tuple-element.34.own_ref) | copy-start | bytes 165892
  3.0 10.9 %collective-permute-start.2 = (bf16[256,2048]{1,0:T(8,128)(2,1)}, bf16[256,2048]{1,0:T(8,128)(2,1)S(1)}, u32[]{:S(2)}, u32[]{:S(2)}) collective-permute-start(bf16[256,2048]{1,0:T(8,128)(2,1)} %bitcast.11), channel_id=1, source_target_pairs={{0,1},{1,0},{2,3},{3,2},{4,5},{5,4},{6,7},{7,6},{8,9},{9,8},{10,11... | collective-permute-start | bytes 3145736 | tf_op jit(solution)/shard_map/key_exchange/ppermute | solution.py:37
  3.1 10.7 %collective-permute-start.5 = (bf16[48,1024]{1,0:T(8,128)(2,1)S(1)}, bf16[48,1024]{1,0:T(8,128)(2,1)S(1)}, u32[]{:S(2)}, u32[]{:S(2)}) collective-permute-start(bf16[48,1024]{1,0:T(8,128)(2,1)S(1)} %join_queries.1.refs_1_.refs_4_), channel_id=1, source_target_pairs={{0,2},{1,3},{2,0},{3,1},{4,6},{5,7},{6,4},{7,5},{8,10},{9,11},{10,... | collective-permute-start | bytes 294920 | tf_op jit(solution)/shard_map/query_gather/ppermute | solution.py:42
  6.2 7.6 %collective-permute-start.3 = (bf16[48,1024]{1,0:T(8,128)(2,1)S(1)}, bf16[48,1024]{1,0:T(8,128)(2,1)S(1)}, u32[]{:S(2)}, u32[]{:S(2)}) collective-permute-start(bf16[48,1024]{1,0:T(8,128)(2,1)S(1)} %join_queries.1.refs_1_.refs_4_), channel_id=1, source_target_pairs={{0,4},{1,5},{2,6},{3,7},{4,0},{5,1},{6,2},{7,3},{8,12},{9,13},{10,... | collective-permute-start | bytes 294920 | tf_op jit(solution)/shard_map/query_gather/ppermute | solution.py:42
  8.8 1.2 %collective-permute-start.1 = (bf16[24,1152]{1,0:T(8,128)(2,1)S(1)}, bf16[24,1152]{1,0:T(8,128)(2,1)S(1)}, u32[]{:S(2)}, u32[]{:S(2)}) collective-permute-start(bf16[24,1152]{1,0:T(8,128)(2,1)S(1)} %copy-done.5), channel_id=1, source_target_pairs={{0,1},{1,0},{2,3},{3,2},{4,5},{5,4},{6,7},{7,6},{8,9},{9,8},{10,11... | collective-permute-start | bytes 165896 | tf_op jit(solution)/shard_map/sibling_exchange/ppermute | solution.py:37
  10.1 1.7 %copy-start.4 = (f32[8,256]{1,0:T(8,128)S(1)}, f32[8,256]{1,0:T(8,128)}, u32[]{:S(2)}) copy-start(f32[8,256]{1,0:T(8,128)} %get-tuple-element.33.docs_ref) | copy-start | bytes 24580
  10.2 3.6 %collective-permute-start.4 = (f32[8,128]{1,0:T(8,128)S(1)}, f32[8,128]{1,0:T(8,128)S(1)}, u32[]{:S(2)}, u32[]{:S(2)}) collective-permute-start(f32[8,128]{1,0:T(8,128)S(1)} %get-tuple-element.44), channel_id=1, source_target_pairs={{0,8},{8,0},{16,24},{24,16},{1,9},{9,1},{17,25},{25,17},{2,10},{10... | collective-permute-start | bytes 12296 | tf_op jit(solution)/shard_map/mask_count/ppermute | solution.py:386
  11.7 1.2 %copy-start.1 = (bf16[1,256,2048]{2,1,0:T(8,128)(2,1)S(1)}, bf16[1,256,2048]{2,1,0:T(8,128)(2,1)}, u32[]{:S(2)}) copy-start(bf16[1,256,2048]{2,1,0:T(8,128)(2,1)} %param.9) | copy-start | bytes 3145732
  13.3 15.5 %copy-start = (bf16[1,256,2048]{2,1,0:T(8,128)(2,1)S(1)}, bf16[1,256,2048]{2,1,0:T(8,128)(2,1)}, u32[]{:S(2)}) copy-start(bf16[1,256,2048]{2,1,0:T(8,128)(2,1)} %param.10) | copy-start | bytes 3145732
  13.9 7.4 %collective-permute-start.6 = (bf16[256,1024]{1,0:T(8,128)(2,1)S(1)}, bf16[256,1024]{1,0:T(8,128)(2,1)S(1)}, u32[]{:S(2)}, u32[]{:S(2)}) collective-permute-start(bf16[256,1024]{1,0:T(8,128)(2,1)S(1)} %get-tuple-element.47), channel_id=1, source_target_pairs={{0,1},{1,0},{2,3},{3,2},{4,5},{5,4},{6,7},{7,6},{8,9},{9,8},{10,11... | collective-permute-start | bytes 1572872 | tf_op jit(solution)/shard_map/key_exchange/ppermute | solution.py:37
  13.9 7.3 %collective-permute-start.7 = (bf16[48,1024]{1,0:T(8,128)(2,1)S(1)}, bf16[48,1024]{1,0:T(8,128)(2,1)S(1)}, u32[]{:S(2)}, u32[]{:S(2)}) collective-permute-start(bf16[48,1024]{1,0:T(8,128)(2,1)S(1)} %collective-permute-done.3.refs_2_.refs_5_), channel_id=1, source_target_pairs={{0,2},{1,3},{2,0},{3,1},{4,6},{5,7},{6,4},{7,5},{8,10},{9,11},{10,... | collective-permute-start | bytes 294920 | tf_op jit(solution)/shard_map/query_forward/ppermute | solution.py:42
  14.5 9.7 %collective-permute-start.11 = (bf16[48,1024]{1,0:T(8,128)(2,1)S(1)}, bf16[48,1024]{1,0:T(8,128)(2,1)S(1)}, u32[]{:S(2)}, u32[]{:S(2)}) collective-permute-start(bf16[48,1024]{1,0:T(8,128)(2,1)S(1)} %get-tuple-element.49.refs_8_), channel_id=1, source_target_pairs={{0,4},{1,5},{2,6},{3,7},{4,0},{5,1},{6,2},{7,3},{8,12},{9,13},{10,... | collective-permute-start | bytes 294920 | tf_op jit(solution)/shard_map/cotangent_gather/ppermute | solution.py:42
  16.8 8.9 %collective-permute-start.12 = (bf16[48,1024]{1,0:T(8,128)(2,1)S(1)}, bf16[48,1024]{1,0:T(8,128)(2,1)S(1)}, u32[]{:S(2)}, u32[]{:S(2)}) collective-permute-start(bf16[48,1024]{1,0:T(8,128)(2,1)S(1)} %get-tuple-element.49.refs_8_), channel_id=1, source_target_pairs={{0,2},{1,3},{2,0},{3,1},{4,6},{5,7},{6,4},{7,5},{8,10},{9,11},{10,... | collective-permute-start | bytes 294920 | tf_op jit(solution)/shard_map/cotangent_gather/ppermute | solution.py:42
  16.9 9.4 %collective-permute-start.13 = (bf16[48,1024]{1,0:T(8,128)(2,1)S(1)}, bf16[48,1024]{1,0:T(8,128)(2,1)S(1)}, u32[]{:S(2)}, u32[]{:S(2)}) collective-permute-start(bf16[48,1024]{1,0:T(8,128)(2,1)S(1)} %get-tuple-element.49.refs_8_), channel_id=1, source_target_pairs={{0,6},{1,7},{2,4},{3,5},{4,2},{5,3},{6,0},{7,1},{8,14},{9,15},{10,... | collective-permute-start | bytes 294920 | tf_op jit(solution)/shard_map/cotangent_gather/ppermute | solution.py:42
  22.1 4.2 %collective-permute-start.10 = (f32[8,256]{1,0:T(8,128)S(1)}, f32[8,256]{1,0:T(8,128)S(1)}, u32[]{:S(2)}, u32[]{:S(2)}) collective-permute-start(f32[8,256]{1,0:T(8,128)S(1)} %scores.1.refs_0_), channel_id=1, source_target_pairs={{0,2},{1,3},{2,0},{3,1},{4,6},{5,7},{6,4},{7,5},{8,10},{9,11},{10,... | collective-permute-start | bytes 24584 | tf_op jit(solution)/shard_map/stats_exchange/ppermute | solution.py:42
  22.2 5.5 %collective-permute-start.8 = (f32[8,256]{1,0:T(8,128)S(1)}, f32[8,256]{1,0:T(8,128)S(1)}, u32[]{:S(2)}, u32[]{:S(2)}) collective-permute-start(f32[8,256]{1,0:T(8,128)S(1)} %scores.1.refs_0_), channel_id=1, source_target_pairs={{0,6},{1,7},{2,4},{3,5},{4,2},{5,3},{6,0},{7,1},{8,14},{9,15},{10,... | collective-permute-start | bytes 24584 | tf_op jit(solution)/shard_map/stats_exchange/ppermute | solution.py:42
  24.2 4.6 %collective-permute-start.9 = (f32[8,256]{1,0:T(8,128)S(1)}, f32[8,256]{1,0:T(8,128)S(1)}, u32[]{:S(2)}, u32[]{:S(2)}) collective-permute-start(f32[8,256]{1,0:T(8,128)S(1)} %scores.1.refs_0_), channel_id=1, source_target_pairs={{0,4},{1,5},{2,6},{3,7},{4,0},{5,1},{6,2},{7,3},{8,12},{9,13},{10,... | collective-permute-start | bytes 24584 | tf_op jit(solution)/shard_map/stats_exchange/ppermute | solution.py:42
  31.3 8.1 %collective-permute-start.14 = (bf16[256,2048]{1,0:T(8,128)(2,1)S(1)}, bf16[256,2048]{1,0:T(8,128)(2,1)S(1)}, u32[]{:S(2)}, u32[]{:S(2)}) collective-permute-start(bf16[256,2048]{1,0:T(8,128)(2,1)S(1)} %get-tuple-element.52), channel_id=1, source_target_pairs={{0,1},{1,0},{2,3},{3,2},{4,5},{5,4},{6,7},{7,6},{8,9},{9,8},{10,11... | collective-permute-start | bytes 3145736 | tf_op jit(solution)/shard_map/key_grad_end/ppermute | solution.py:37
  31.4 9.9 %collective-permute-start.16 = (bf16[48,1024]{1,0:T(8,128)(2,1)S(1)}, bf16[48,1024]{1,0:T(8,128)(2,1)S(1)}, u32[]{:S(2)}, u32[]{:S(2)}) collective-permute-start(bf16[48,1024]{1,0:T(8,128)(2,1)S(1)} %get-tuple-element.56), channel_id=1, source_target_pairs={{0,6},{1,7},{2,4},{3,5},{4,2},{5,3},{6,0},{7,1},{8,14},{9,15},{10,... | collective-permute-start | bytes 294920 | tf_op jit(solution)/shard_map/query_grad_sum/ppermute | solution.py:42
  33.4 10.0 %collective-permute-start.17 = (bf16[48,1024]{1,0:T(8,128)(2,1)S(1)}, bf16[48,1024]{1,0:T(8,128)(2,1)S(1)}, u32[]{:S(2)}, u32[]{:S(2)}) collective-permute-start(bf16[48,1024]{1,0:T(8,128)(2,1)S(1)} %get-tuple-element.57), channel_id=1, source_target_pairs={{0,4},{1,5},{2,6},{3,7},{4,0},{5,1},{6,2},{7,3},{8,12},{9,13},{10,... | collective-permute-start | bytes 294920 | tf_op jit(solution)/shard_map/query_grad_sum/ppermute | solution.py:42
  34.0 9.4 %collective-permute-start.18 = (bf16[48,1024]{1,0:T(8,128)(2,1)S(1)}, bf16[48,1024]{1,0:T(8,128)(2,1)S(1)}, u32[]{:S(2)}, u32[]{:S(2)}) collective-permute-start(bf16[48,1024]{1,0:T(8,128)(2,1)S(1)} %get-tuple-element.58), channel_id=1, source_target_pairs={{0,2},{1,3},{2,0},{3,1},{4,6},{5,7},{6,4},{7,5},{8,10},{9,11},{10,... | collective-permute-start | bytes 294920 | tf_op jit(solution)/shard_map/query_grad_sum/ppermute | solution.py:42
  35.8 3.6 %collective-permute-start.15 = (f32[8,128]{1,0:T(8,128)S(1)}, f32[8,128]{1,0:T(8,128)S(1)}, u32[]{:S(2)}, u32[]{:S(2)}) collective-permute-start(f32[8,128]{1,0:T(8,128)S(1)} %get-tuple-element.53.refs_0_), channel_id=1, source_target_pairs={{0,16},{8,24},{16,0},{24,8},{1,17},{9,25},{17,1},{25,9},{2,18},{10... | collective-permute-start | bytes 12296 | tf_op jit(solution)/shard_map/key_grad_end/ppermute | solution.py:386
  43.5 1.3 %collective-permute-start.19 = (bf16[24,1024]{1,0:T(8,128)(2,1)S(1)}, bf16[24,1024]{1,0:T(8,128)(2,1)S(1)}, u32[]{:S(2)}, u32[]{:S(2)}) collective-permute-start(bf16[24,1024]{1,0:T(8,128)(2,1)S(1)} %get-tuple-element.60), channel_id=1, source_target_pairs={{0,1},{1,0},{2,3},{3,2},{4,5},{5,4},{6,7},{7,6},{8,9},{9,8},{10,11... | collective-permute-start | bytes 147464 | tf_op jit(solution)/shard_map/query_grad_end/ppermute | solution.py:37

commit v10 on v9

--- a/solution.py
+++ b/solution.py
@@ -393,7 +393,7 @@
         rows_in_all = float(data_groups * dec_rows)
 
     with jax.named_scope("query_forward"):
-        q_far = [q_far[0], *(after(one, bias_own, count, q_near)[0] for one in q_far[1:])]
+        q_far = [q_far[0], *(after(one, bias_own, count)[0] for one in q_far[1:])]
         q_blocks = [*q_far, q_near, *forwarded(q_far)]
 
     with jax.named_scope("cotangent_gather"):

time: 45.7 us -> 45.7 us (level)
  no operation moved by 1% of the time
where the time goes in v10:
time: 45.7 us; the launch traced here: 45.5 us
  starting transfers between devices  22.4 us (49%)
  waiting for transfers between devices  12.7 us (28%)
  Pallas kernels  7.67 us (17%)
  local copies, waits for them, and re-layouts  1.25 us (3%)
  between operations  0.77 us (2%)
  other arithmetic  0.66 us (1%)
    ppermute x12, starting transfers between devices, across(): lax.ppermute(block, 'seq', [(i, i ^ 2 * apart) for i in range(count)])  18.6 us
    ppermute x12, waiting for transfers between devices, across(): lax.ppermute(block, 'seq', [(i, i ^ 2 * apart) for i in range(count)])  7.54 us
    ppermute x2, starting transfers between devices, over_groups(): lax.ppermute(count, 'dp', [(i, i ^ apart) for i in range(data_groups)])  3.01 us
    ppermute x2, waiting for transfers between devices, over_groups(): lax.ppermute(count, 'dp', [(i, i ^ apart) for i in range(data_groups)])  2.66 us
    pallas_call x1, Pallas kernels, local(): kernel_call(functools.partial(grads_kernel, offsets), (block,) * chips +...  2.58 us
    ppermute x6, waiting for transfers between devices, to_sibling(): return lax.ppermute(block, 'seq', [(i, i ^ 1) for i in range(count)])  2.46 us
    pallas_call x1, Pallas kernels, local(): kernel_call(functools.partial(key_end_kernel, rows_in_all), (whole, whole...  1.84 us
    pallas_call x1, Pallas kernels, local(): kernel_call(functools.partial(prepare_kernel, offsets, dec_rows, enc_loca...  1.8 us
  transfers between devices with their start and end apart: 20, of which 9 were waited for; matrix products, arithmetic and copies ran while one was open for 0% of the time, Pallas kernels for 11%

profile of v10, /device:TPU:0, one launch (start us, length us, event | category | flops | bytes accessed | tf_op | source)
XLA Modules:
  0.0 45.5 jit_solution(1940063342535100003)
XLA Ops:
  0.6 0.5 %collective-permute-start = (bf16[24,2048]{1,0:T(8,128)(2,1)}, bf16[24,2048]{1,0:T(8,128)(2,1)S(1)}, u32[]{:S(2)}, u32[]{:S(2)}) collective-permute-start(bf16[24,2048]{1,0:T(8,128)(2,1)} %bitcast.14), channel_id=1, source_target_pairs={{0,1},{1,0},{2,3},{3,2},{4,5},{5,4},{6,7},{7,6},{8,9},{9,8},{10,11... | collective-permute-start | bytes 294920 | tf_op jit(solution)/shard_map/sibling_exchange/ppermute | solution.py:37
  1.2 1.8 %prepare.1 = (bf16[24,1152]{1,0:T(8,128)(2,1)}, bf16[24,1152]{1,0:T(8,128)(2,1)}, f32[8,256]{1,0:T(8,128)}) custom-call(s32[1,4]{1,0:T(1,128)} %bitcast.20, s32[1,4]{1,0:T(1,128)} %bitcast.21, bf16[24,2048]{1,0:T(8,128)(2,1)} %bitcast.17, bf16[24,2048]{1,0:T(8,128)(2,1)} %bitcast.18, s32[1,24]{1,0:T(1,128)} %mask_ref.1), custom_call_target="tpu_custom_call" | custom-call | flops 100000 | bytes 1000000 | tf_op jit(solution)/shard_map/sibling_exchange/prepare/pallas_call | solution.py:331
  3.0 0.0 collective-permute-done.other_ref
  3.0 0.0 copy-start.5
  3.0 0.0 copy-start.3
  3.0 0.1 collective-permute-start.2
  3.1 4.1 %collective-permute-start.3 = (bf16[48,1024]{1,0:T(8,128)(2,1)S(1)}, bf16[48,1024]{1,0:T(8,128)(2,1)S(1)}, u32[]{:S(2)}, u32[]{:S(2)}) collective-permute-start(bf16[48,1024]{1,0:T(8,128)(2,1)S(1)} %join_queries.1.refs_1_.refs_4_), channel_id=1, source_target_pairs={{0,4},{1,5},{2,6},{3,7},{4,0},{5,1},{6,2},{7,3},{8,12},{9,13},{10,... | collective-permute-start | bytes 294920 | tf_op jit(solution)/shard_map/query_gather/ppermute | solution.py:42
  7.2 1.6 %collective-permute-start.5 = (bf16[48,1024]{1,0:T(8,128)(2,1)S(1)}, bf16[48,1024]{1,0:T(8,128)(2,1)S(1)}, u32[]{:S(2)}, u32[]{:S(2)}) collective-permute-start(bf16[48,1024]{1,0:T(8,128)(2,1)S(1)} %join_queries.1.refs_1_.refs_4_), channel_id=1, source_target_pairs={{0,2},{1,3},{2,0},{3,1},{4,6},{5,7},{6,4},{7,5},{8,10},{9,11},{10,... | collective-permute-start | bytes 294920 | tf_op jit(solution)/shard_map/query_gather/ppermute | solution.py:42
  8.8 0.0 collective-permute-start.1
  8.8 1.2 %collective-permute-done.1.other_ref = bf16[24,1152]{1,0:T(8,128)(2,1)S(1)} collective-permute-done((bf16[24,1152]{1,0:T(8,128)(2,1)S(1)}, bf16[24,1152]{1,0:T(8,128)(2,1)S(1)}, u32[]{:S(2)}, u32[]{:S(2)}) %collective-permute-start.1) | collective-permute-done | bytes 55328 | tf_op jit(solution)/shard_map/sibling_exchange/ppermute | solution.py:37
  10.1 0.2 join_cotangents.1
  10.2 1.5 %collective-permute-start.4 = (f32[8,128]{1,0:T(8,128)S(1)}, f32[8,128]{1,0:T(8,128)S(1)}, u32[]{:S(2)}, u32[]{:S(2)}) collective-permute-start(f32[8,128]{1,0:T(8,128)S(1)} %get-tuple-element.44), channel_id=1, source_target_pairs={{0,8},{8,0},{16,24},{24,16},{1,9},{9,1},{17,25},{25,17},{2,10},{10... | collective-permute-start | bytes 12296 | tf_op jit(solution)/shard_map/mask_count/ppermute | solution.py:386
  11.7 1.2 %copy-done.1 = bf16[1,256,2048]{2,1,0:T(8,128)(2,1)S(1)} copy-done((bf16[1,256,2048]{2,1,0:T(8,128)(2,1)S(1)}, bf16[1,256,2048]{2,1,0:T(8,128)(2,1)}, u32[]{:S(2)}) %copy-start.1) | copy-done | bytes 1048600
  13.0 0.3 setup.1
  13.3 0.0 copy-start
  13.3 0.6 %collective-permute-done.4 = f32[8,128]{1,0:T(8,128)S(1)} collective-permute-done((f32[8,128]{1,0:T(8,128)S(1)}, f32[8,128]{1,0:T(8,128)S(1)}, u32[]{:S(2)}, u32[]{:S(2)}) %collective-permute-start.4) | collective-permute-done | bytes 4128 | tf_op jit(solution)/shard_map/mask_count/ppermute | solution.py:386
  13.8 0.0 collective-permute-done.3.refs_2_.refs_5_
  13.9 0.0 collective-permute-done.2.refs_15_
  13.9 0.1 collective-permute-start.6
  13.9 0.5 %collective-permute-start.7 = (bf16[48,1024]{1,0:T(8,128)(2,1)S(1)}, bf16[48,1024]{1,0:T(8,128)(2,1)S(1)}, u32[]{:S(2)}, u32[]{:S(2)}) collective-permute-start(bf16[48,1024]{1,0:T(8,128)(2,1)S(1)} %collective-permute-done.3.refs_2_.refs_5_), channel_id=1, source_target_pairs={{0,2},{1,3},{2,0},{3,1},{4,6},{5,7},{6,4},{7,5},{8,10},{9,11},{10,... | collective-permute-start | bytes 294920 | tf_op jit(solution)/shard_map/query_forward/ppermute | solution.py:42
  14.5 2.1 %collective-permute-start.11 = (bf16[48,1024]{1,0:T(8,128)(2,1)S(1)}, bf16[48,1024]{1,0:T(8,128)(2,1)S(1)}, u32[]{:S(2)}, u32[]{:S(2)}) collective-permute-start(bf16[48,1024]{1,0:T(8,128)(2,1)S(1)} %get-tuple-element.49.refs_8_), channel_id=1, source_target_pairs={{0,4},{1,5},{2,6},{3,7},{4,0},{5,1},{6,2},{7,3},{8,12},{9,13},{10,... | collective-permute-start | bytes 294920 | tf_op jit(solution)/shard_map/cotangent_gather/ppermute | solution.py:42
  16.5 0.1 collective-permute-start.12
  16.6 2.2 %collective-permute-start.13 = (bf16[48,1024]{1,0:T(8,128)(2,1)S(1)}, bf16[48,1024]{1,0:T(8,128)(2,1)S(1)}, u32[]{:S(2)}, u32[]{:S(2)}) collective-permute-start(bf16[48,1024]{1,0:T(8,128)(2,1)S(1)} %get-tuple-element.49.refs_8_), channel_id=1, source_target_pairs={{0,6},{1,7},{2,4},{3,5},{4,2},{5,3},{6,0},{7,1},{8,14},{9,15},{10,... | collective-permute-start | bytes 294920 | tf_op jit(solution)/shard_map/cotangent_gather/ppermute | solution.py:42
  18.9 2.1 %collective-permute-done.7.refs_4_.refs_7_ = bf16[48,1024]{1,0:T(8,128)(2,1)S(1)} collective-permute-done((bf16[48,1024]{1,0:T(8,128)(2,1)S(1)}, bf16[48,1024]{1,0:T(8,128)(2,1)S(1)}, u32[]{:S(2)}, u32[]{:S(2)}) %collective-permute-start.7) | collective-permute-done | bytes 98336 | tf_op jit(solution)/shard_map/query_forward/ppermute | solution.py:42
  20.9 0.9 %scores.1.refs_0_ = f32[8,256]{1,0:T(8,128)S(1)} custom-call(f32[8,48]{1,0:T(8,128)S(1)} %get-tuple-element.40.delta_ref, f32[256,192]{1,0:T(8,128)S(1)} %get-tuple-element.37.bias_own, f32[256,192]{1,0:T(8,128)S(1)} %get-tuple-element.38.bias_other, bf16[256,1024]{1,0:T(8,128)(2,1)S(1)} %get-tuple-element.41.key_ref.refs_12_, ...), custom_call_target="tpu_custom_call" | custom-call | flops 201326592 | bytes 1441792 | tf_op jit(solution)/shard_map/scores/scores/pallas_call | solution.py:410
  21.8 0.1 collective-permute-start.10
  21.9 2.3 %collective-permute-start.8 = (f32[8,256]{1,0:T(8,128)S(1)}, f32[8,256]{1,0:T(8,128)S(1)}, u32[]{:S(2)}, u32[]{:S(2)}) collective-permute-start(f32[8,256]{1,0:T(8,128)S(1)} %scores.1.refs_0_), channel_id=1, source_target_pairs={{0,6},{1,7},{2,4},{3,5},{4,2},{5,3},{6,0},{7,1},{8,14},{9,15},{10,... | collective-permute-start | bytes 24584 | tf_op jit(solution)/shard_map/stats_exchange/ppermute | solution.py:42
  24.2 1.2 %collective-permute-start.9 = (f32[8,256]{1,0:T(8,128)S(1)}, f32[8,256]{1,0:T(8,128)S(1)}, u32[]{:S(2)}, u32[]{:S(2)}) collective-permute-start(f32[8,256]{1,0:T(8,128)S(1)} %scores.1.refs_0_), channel_id=1, source_target_pairs={{0,4},{1,5},{2,6},{3,7},{4,0},{5,1},{6,2},{7,3},{8,12},{9,13},{10,... | collective-permute-start | bytes 24584 | tf_op jit(solution)/shard_map/stats_exchange/ppermute | solution.py:42
  25.4 0.6 %collective-permute-done.13.refs_11_ = bf16[48,1024]{1,0:T(8,128)(2,1)S(1)} collective-permute-done((bf16[48,1024]{1,0:T(8,128)(2,1)S(1)}, bf16[48,1024]{1,0:T(8,128)(2,1)S(1)}, u32[]{:S(2)}, u32[]{:S(2)}) %collective-permute-start.13) | collective-permute-done | bytes 98336 | tf_op jit(solution)/shard_map/cotangent_gather/ppermute | solution.py:42
  26.0 0.0 collective-permute-done.10.refs_3_
  26.0 1.4 %collective-permute-done.8.refs_1_ = f32[8,256]{1,0:T(8,128)S(1)} collective-permute-done((f32[8,256]{1,0:T(8,128)S(1)}, f32[8,256]{1,0:T(8,128)S(1)}, u32[]{:S(2)}, u32[]{:S(2)}) %collective-permute-start.8) | collective-permute-done | bytes 8224 | tf_op jit(solution)/shard_map/stats_exchange/ppermute | solution.py:42
  27.4 1.3 %collective-permute-done.9.refs_2_ = f32[8,256]{1,0:T(8,128)S(1)} collective-permute-done((f32[8,256]{1,0:T(8,128)S(1)}, f32[8,256]{1,0:T(8,128)S(1)}, u32[]{:S(2)}, u32[]{:S(2)}) %collective-permute-start.9) | collective-permute-done | bytes 8224 | tf_op jit(solution)/shard_map/stats_exchange/ppermute | solution.py:42
  28.7 2.6 %grads.1 = (bf16[48,1024]{1,0:T(8,128)(2,1)S(1)}, bf16[48,1024]{1,0:T(8,128)(2,1)S(1)}, bf16[48,1024]{1,0:T(8,128)(2,1)S(1)}, bf16[48,1024]{1,0:T(8,128)(2,1)S(1...) custom-call(f32[256,192]{1,0:T(8,128)S(1)} %get-tuple-element.37.bias_own, ...), custom_call_target="tpu_custom_call" | custom-call | flops 1006632960 | bytes 4980736 | tf_op jit(solution)/shard_map/grads/grads/pallas_call | solution.py:427
  31.3 0.1 collective-permute-start.14
  31.4 1.7 %collective-permute-start.16 = (bf16[48,1024]{1,0:T(8,128)(2,1)S(1)}, bf16[48,1024]{1,0:T(8,128)(2,1)S(1)}, u32[]{:S(2)}, u32[]{:S(2)}) collective-permute-start(bf16[48,1024]{1,0:T(8,128)(2,1)S(1)} %get-tuple-element.56), channel_id=1, source_target_pairs={{0,6},{1,7},{2,4},{3,5},{4,2},{5,3},{6,0},{7,1},{8,14},{9,15},{10,... | collective-permute-start | bytes 294920 | tf_op jit(solution)/shard_map/query_grad_sum/ppermute | solution.py:42
  33.1 0.9 %collective-permute-start.17 = (bf16[48,1024]{1,0:T(8,128)(2,1)S(1)}, bf16[48,1024]{1,0:T(8,128)(2,1)S(1)}, u32[]{:S(2)}, u32[]{:S(2)}) collective-permute-start(bf16[48,1024]{1,0:T(8,128)(2,1)S(1)} %get-tuple-element.57), channel_id=1, source_target_pairs={{0,4},{1,5},{2,6},{3,7},{4,0},{5,1},{6,2},{7,3},{8,12},{9,13},{10,... | collective-permute-start | bytes 294920 | tf_op jit(solution)/shard_map/query_grad_sum/ppermute | solution.py:42
  34.0 1.9 %collective-permute-start.18 = (bf16[48,1024]{1,0:T(8,128)(2,1)S(1)}, bf16[48,1024]{1,0:T(8,128)(2,1)S(1)}, u32[]{:S(2)}, u32[]{:S(2)}) collective-permute-start(bf16[48,1024]{1,0:T(8,128)(2,1)S(1)} %get-tuple-element.58), channel_id=1, source_target_pairs={{0,2},{1,3},{2,0},{3,1},{4,6},{5,7},{6,4},{7,5},{8,10},{9,11},{10,... | collective-permute-start | bytes 294920 | tf_op jit(solution)/shard_map/query_grad_sum/ppermute | solution.py:42
  35.8 1.5 %collective-permute-start.15 = (f32[8,128]{1,0:T(8,128)S(1)}, f32[8,128]{1,0:T(8,128)S(1)}, u32[]{:S(2)}, u32[]{:S(2)}) collective-permute-start(f32[8,128]{1,0:T(8,128)S(1)} %get-tuple-element.53.refs_0_), channel_id=1, source_target_pairs={{0,16},{8,24},{16,0},{24,8},{1,17},{9,25},{17,1},{25,9},{2,18},{10... | collective-permute-start | bytes 12296 | tf_op jit(solution)/shard_map/key_grad_end/ppermute | solution.py:386
  37.4 2.1 %collective-permute-done.15.refs_1_ = f32[8,128]{1,0:T(8,128)S(1)} collective-permute-done((f32[8,128]{1,0:T(8,128)S(1)}, f32[8,128]{1,0:T(8,128)S(1)}, u32[]{:S(2)}, u32[]{:S(2)}) %collective-permute-start.15) | collective-permute-done | bytes 4128 | tf_op jit(solution)/shard_map/key_grad_end/ppermute | solution.py:386
  39.4 0.0 collective-permute-done.14.other_ref
  39.4 1.8 %key_end.1 = (bf16[256,2048]{1,0:T(8,128)(2,1)}, bf16[256,2048]{1,0:T(8,128)(2,1)}, f32[8,128]{1,0:T(8,128)S(1)}) custom-call(bf16[256,2048]{1,0:T(8,128)(2,1)S(1)} %get-tuple-element.51.keep_ref, bf16[256,2048]{1,0:T(8,128)(2,1)S(1)} %collective-permute-done.14.other_ref, f32[8,128]{1,0:T(8,128)S(1)} %get-tuple-element.53.refs_0_, ...), custom_call_target="tpu_custom_call" | custom-call | flops 1000000 | bytes 4194304 | tf_op jit(solution)/shard_map/key_grad_end/key_end/pallas_call | solution.py:447
  41.3 0.0 collective-permute-done.16.refs_1_
  41.3 2.1 %collective-permute-done.17.refs_2_ = bf16[48,1024]{1,0:T(8,128)(2,1)S(1)} collective-permute-done((bf16[48,1024]{1,0:T(8,128)(2,1)S(1)}, bf16[48,1024]{1,0:T(8,128)(2,1)S(1)}, u32[]{:S(2)}, u32[]{:S(2)}) %collective-permute-start.17) | collective-permute-done | bytes 98336 | tf_op jit(solution)/shard_map/query_grad_sum/ppermute | solution.py:42
  43.4 0.0 collective-permute-done.18.refs_3_
  43.4 0.1 query_end.1
  43.5 0.1 collective-permute-start.19
  43.6 1.2 %collective-permute-done.19 = bf16[24,1024]{1,0:T(8,128)(2,1)S(1)} collective-permute-done((bf16[24,1024]{1,0:T(8,128)(2,1)S(1)}, bf16[24,1024]{1,0:T(8,128)(2,1)S(1)}, u32[]{:S(2)}, u32[]{:S(2)}) %collective-permute-start.19) | collective-permute-done | bytes 49184 | tf_op jit(solution)/shard_map/query_grad_end/ppermute | solution.py:37
  44.8 0.7 %maximum_select_fusion = bf16[1,24,2048]{2,1,0:T(8,128)(2,1)} fusion(bf16[1,24,1024]{2,1,0:T(8,128)(2,1)S(1)} %bitcast.19, bf16[1,24,1024]{2,1,0:T(8,128)(2,1)S(1)} %bitcast.16, pred[]{:T(512)S(6)} %eq.3), kind=kLoop, calls=%fused_computation | loop fusion | flops 442368 | bytes 196609 | tf_op jit(solution)/shard_map/query_grad_end/jit(_where)/select_n | solution.py:288
  (14 shorter events, 0.0 us)
Async XLA Ops:
  0.6 2.3 %collective-permute-start = (bf16[24,2048]{1,0:T(8,128)(2,1)}, bf16[24,2048]{1,0:T(8,128)(2,1)S(1)}, u32[]{:S(2)}, u32[]{:S(2)}) collective-permute-start(bf16[24,2048]{1,0:T(8,128)(2,1)} %bitcast.14), channel_id=1, source_target_pairs={{0,1},{1,0},{2,3},{3,2},{4,5},{5,4},{6,7},{7,6},{8,9},{9,8},{10,11... | collective-permute-start | bytes 294920 | tf_op jit(solution)/shard_map/sibling_exchange/ppermute | solution.py:37
  1.1 2.0 %copy-start.2 = (bf16[1,24,2048]{2,1,0:T(8,128)(2,1)S(1)}, bf16[1,24,2048]{2,1,0:T(8,128)(2,1)}, u32[]{:S(2)}) copy-start(bf16[1,24,2048]{2,1,0:T(8,128)(2,1)} %param.8) | copy-start | bytes 294916
  3.0 5.9 %copy-start.5 = (bf16[24,1152]{1,0:T(8,128)(2,1)S(1)}, bf16[24,1152]{1,0:T(8,128)(2,1)}, u32[]{:S(2)}) copy-start(bf16[24,1152]{1,0:T(8,128)(2,1)} %get-tuple-element.39) | copy-start | bytes 165892
  3.0 7.1 %copy-start.3 = (bf16[24,1152]{1,0:T(8,128)(2,1)S(1)}, bf16[24,1152]{1,0:T(8,128)(2,1)}, u32[]{:S(2)}) copy-start(bf16[24,1152]{1,0:T(8,128)(2,1)} %get-tuple-element.34.own_ref) | copy-start | bytes 165892
  3.0 10.9 %collective-permute-start.2 = (bf16[256,2048]{1,0:T(8,128)(2,1)}, bf16[256,2048]{1,0:T(8,128)(2,1)S(1)}, u32[]{:S(2)}, u32[]{:S(2)}) collective-permute-start(bf16[256,2048]{1,0:T(8,128)(2,1)} %bitcast.11), channel_id=1, source_target_pairs={{0,1},{1,0},{2,3},{3,2},{4,5},{5,4},{6,7},{7,6},{8,9},{9,8},{10,11... | collective-permute-start | bytes 3145736 | tf_op jit(solution)/shard_map/key_exchange/ppermute | solution.py:37
  3.1 10.7 %collective-permute-start.3 = (bf16[48,1024]{1,0:T(8,128)(2,1)S(1)}, bf16[48,1024]{1,0:T(8,128)(2,1)S(1)}, u32[]{:S(2)}, u32[]{:S(2)}) collective-permute-start(bf16[48,1024]{1,0:T(8,128)(2,1)S(1)} %join_queries.1.refs_1_.refs_4_), channel_id=1, source_target_pairs={{0,4},{1,5},{2,6},{3,7},{4,0},{5,1},{6,2},{7,3},{8,12},{9,13},{10,... | collective-permute-start | bytes 294920 | tf_op jit(solution)/shard_map/query_gather/ppermute | solution.py:42
  7.2 6.6 %collective-permute-start.5 = (bf16[48,1024]{1,0:T(8,128)(2,1)S(1)}, bf16[48,1024]{1,0:T(8,128)(2,1)S(1)}, u32[]{:S(2)}, u32[]{:S(2)}) collective-permute-start(bf16[48,1024]{1,0:T(8,128)(2,1)S(1)} %join_queries.1.refs_1_.refs_4_), channel_id=1, source_target_pairs={{0,2},{1,3},{2,0},{3,1},{4,6},{5,7},{6,4},{7,5},{8,10},{9,11},{10,... | collective-permute-start | bytes 294920 | tf_op jit(solution)/shard_map/query_gather/ppermute | solution.py:42
  8.8 1.2 %collective-permute-start.1 = (bf16[24,1152]{1,0:T(8,128)(2,1)S(1)}, bf16[24,1152]{1,0:T(8,128)(2,1)S(1)}, u32[]{:S(2)}, u32[]{:S(2)}) collective-permute-start(bf16[24,1152]{1,0:T(8,128)(2,1)S(1)} %copy-done.5), channel_id=1, source_target_pairs={{0,1},{1,0},{2,3},{3,2},{4,5},{5,4},{6,7},{7,6},{8,9},{9,8},{10,11... | collective-permute-start | bytes 165896 | tf_op jit(solution)/shard_map/sibling_exchange/ppermute | solution.py:37
  10.1 1.7 %copy-start.4 = (f32[8,256]{1,0:T(8,128)S(1)}, f32[8,256]{1,0:T(8,128)}, u32[]{:S(2)}) copy-start(f32[8,256]{1,0:T(8,128)} %get-tuple-element.33.docs_ref) | copy-start | bytes 24580
  10.2 3.6 %collective-permute-start.4 = (f32[8,128]{1,0:T(8,128)S(1)}, f32[8,128]{1,0:T(8,128)S(1)}, u32[]{:S(2)}, u32[]{:S(2)}) collective-permute-start(f32[8,128]{1,0:T(8,128)S(1)} %get-tuple-element.44), channel_id=1, source_target_pairs={{0,8},{8,0},{16,24},{24,16},{1,9},{9,1},{17,25},{25,17},{2,10},{10... | collective-permute-start | bytes 12296 | tf_op jit(solution)/shard_map/mask_count/ppermute | solution.py:386
  11.7 1.2 %copy-start.1 = (bf16[1,256,2048]{2,1,0:T(8,128)(2,1)S(1)}, bf16[1,256,2048]{2,1,0:T(8,128)(2,1)}, u32[]{:S(2)}) copy-start(bf16[1,256,2048]{2,1,0:T(8,128)(2,1)} %param.9) | copy-start | bytes 3145732
  13.3 15.5 %copy-start = (bf16[1,256,2048]{2,1,0:T(8,128)(2,1)S(1)}, bf16[1,256,2048]{2,1,0:T(8,128)(2,1)}, u32[]{:S(2)}) copy-start(bf16[1,256,2048]{2,1,0:T(8,128)(2,1)} %param.10) | copy-start | bytes 3145732
  13.9 7.0 %collective-permute-start.6 = (bf16[256,1024]{1,0:T(8,128)(2,1)S(1)}, bf16[256,1024]{1,0:T(8,128)(2,1)S(1)}, u32[]{:S(2)}, u32[]{:S(2)}) collective-permute-start(bf16[256,1024]{1,0:T(8,128)(2,1)S(1)} %get-tuple-element.47), channel_id=1, source_target_pairs={{0,1},{1,0},{2,3},{3,2},{4,5},{5,4},{6,7},{7,6},{8,9},{9,8},{10,11... | collective-permute-start | bytes 1572872 | tf_op jit(solution)/shard_map/key_exchange/ppermute | solution.py:37
  13.9 7.0 %collective-permute-start.7 = (bf16[48,1024]{1,0:T(8,128)(2,1)S(1)}, bf16[48,1024]{1,0:T(8,128)(2,1)S(1)}, u32[]{:S(2)}, u32[]{:S(2)}) collective-permute-start(bf16[48,1024]{1,0:T(8,128)(2,1)S(1)} %collective-permute-done.3.refs_2_.refs_5_), channel_id=1, source_target_pairs={{0,2},{1,3},{2,0},{3,1},{4,6},{5,7},{6,4},{7,5},{8,10},{9,11},{10,... | collective-permute-start | bytes 294920 | tf_op jit(solution)/shard_map/query_forward/ppermute | solution.py:42
  14.5 9.7 %collective-permute-start.11 = (bf16[48,1024]{1,0:T(8,128)(2,1)S(1)}, bf16[48,1024]{1,0:T(8,128)(2,1)S(1)}, u32[]{:S(2)}, u32[]{:S(2)}) collective-permute-start(bf16[48,1024]{1,0:T(8,128)(2,1)S(1)} %get-tuple-element.49.refs_8_), channel_id=1, source_target_pairs={{0,4},{1,5},{2,6},{3,7},{4,0},{5,1},{6,2},{7,3},{8,12},{9,13},{10,... | collective-permute-start | bytes 294920 | tf_op jit(solution)/shard_map/cotangent_gather/ppermute | solution.py:42
  16.5 8.8 %collective-permute-start.12 = (bf16[48,1024]{1,0:T(8,128)(2,1)S(1)}, bf16[48,1024]{1,0:T(8,128)(2,1)S(1)}, u32[]{:S(2)}, u32[]{:S(2)}) collective-permute-start(bf16[48,1024]{1,0:T(8,128)(2,1)S(1)} %get-tuple-element.49.refs_8_), channel_id=1, source_target_pairs={{0,2},{1,3},{2,0},{3,1},{4,6},{5,7},{6,4},{7,5},{8,10},{9,11},{10,... | collective-permute-start | bytes 294920 | tf_op jit(solution)/shard_map/cotangent_gather/ppermute | solution.py:42
  16.6 9.4 %collective-permute-start.13 = (bf16[48,1024]{1,0:T(8,128)(2,1)S(1)}, bf16[48,1024]{1,0:T(8,128)(2,1)S(1)}, u32[]{:S(2)}, u32[]{:S(2)}) collective-permute-start(bf16[48,1024]{1,0:T(8,128)(2,1)S(1)} %get-tuple-element.49.refs_8_), channel_id=1, source_target_pairs={{0,6},{1,7},{2,4},{3,5},{4,2},{5,3},{6,0},{7,1},{8,14},{9,15},{10,... | collective-permute-start | bytes 294920 | tf_op jit(solution)/shard_map/cotangent_gather/ppermute | solution.py:42
  21.8 4.2 %collective-permute-start.10 = (f32[8,256]{1,0:T(8,128)S(1)}, f32[8,256]{1,0:T(8,128)S(1)}, u32[]{:S(2)}, u32[]{:S(2)}) collective-permute-start(f32[8,256]{1,0:T(8,128)S(1)} %scores.1.refs_0_), channel_id=1, source_target_pairs={{0,2},{1,3},{2,0},{3,1},{4,6},{5,7},{6,4},{7,5},{8,10},{9,11},{10,... | collective-permute-start | bytes 24584 | tf_op jit(solution)/shard_map/stats_exchange/ppermute | solution.py:42
  21.9 5.5 %collective-permute-start.8 = (f32[8,256]{1,0:T(8,128)S(1)}, f32[8,256]{1,0:T(8,128)S(1)}, u32[]{:S(2)}, u32[]{:S(2)}) collective-permute-start(f32[8,256]{1,0:T(8,128)S(1)} %scores.1.refs_0_), channel_id=1, source_target_pairs={{0,6},{1,7},{2,4},{3,5},{4,2},{5,3},{6,0},{7,1},{8,14},{9,15},{10,... | collective-permute-start | bytes 24584 | tf_op jit(solution)/shard_map/stats_exchange/ppermute | solution.py:42
  24.2 4.6 %collective-permute-start.9 = (f32[8,256]{1,0:T(8,128)S(1)}, f32[8,256]{1,0:T(8,128)S(1)}, u32[]{:S(2)}, u32[]{:S(2)}) collective-permute-start(f32[8,256]{1,0:T(8,128)S(1)} %scores.1.refs_0_), channel_id=1, source_target_pairs={{0,4},{1,5},{2,6},{3,7},{4,0},{5,1},{6,2},{7,3},{8,12},{9,13},{10,... | collective-permute-start | bytes 24584 | tf_op jit(solution)/shard_map/stats_exchange/ppermute | solution.py:42
  31.3 8.1 %collective-permute-start.14 = (bf16[256,2048]{1,0:T(8,128)(2,1)S(1)}, bf16[256,2048]{1,0:T(8,128)(2,1)S(1)}, u32[]{:S(2)}, u32[]{:S(2)}) collective-permute-start(bf16[256,2048]{1,0:T(8,128)(2,1)S(1)} %get-tuple-element.52), channel_id=1, source_target_pairs={{0,1},{1,0},{2,3},{3,2},{4,5},{5,4},{6,7},{7,6},{8,9},{9,8},{10,11... | collective-permute-start | bytes 3145736 | tf_op jit(solution)/shard_map/key_grad_end/ppermute | solution.py:37
  31.4 9.9 %collective-permute-start.16 = (bf16[48,1024]{1,0:T(8,128)(2,1)S(1)}, bf16[48,1024]{1,0:T(8,128)(2,1)S(1)}, u32[]{:S(2)}, u32[]{:S(2)}) collective-permute-start(bf16[48,1024]{1,0:T(8,128)(2,1)S(1)} %get-tuple-element.56), channel_id=1, source_target_pairs={{0,6},{1,7},{2,4},{3,5},{4,2},{5,3},{6,0},{7,1},{8,14},{9,15},{10,... | collective-permute-start | bytes 294920 | tf_op jit(solution)/shard_map/query_grad_sum/ppermute | solution.py:42
  33.1 10.3 %collective-permute-start.17 = (bf16[48,1024]{1,0:T(8,128)(2,1)S(1)}, bf16[48,1024]{1,0:T(8,128)(2,1)S(1)}, u32[]{:S(2)}, u32[]{:S(2)}) collective-permute-start(bf16[48,1024]{1,0:T(8,128)(2,1)S(1)} %get-tuple-element.57), channel_id=1, source_target_pairs={{0,4},{1,5},{2,6},{3,7},{4,0},{5,1},{6,2},{7,3},{8,12},{9,13},{10,... | collective-permute-start | bytes 294920 | tf_op jit(solution)/shard_map/query_grad_sum/ppermute | solution.py:42
  34.0 9.4 %collective-permute-start.18 = (bf16[48,1024]{1,0:T(8,128)(2,1)S(1)}, bf16[48,1024]{1,0:T(8,128)(2,1)S(1)}, u32[]{:S(2)}, u32[]{:S(2)}) collective-permute-start(bf16[48,1024]{1,0:T(8,128)(2,1)S(1)} %get-tuple-element.58), channel_id=1, source_target_pairs={{0,2},{1,3},{2,0},{3,1},{4,6},{5,7},{6,4},{7,5},{8,10},{9,11},{10,... | collective-permute-start | bytes 294920 | tf_op jit(solution)/shard_map/query_grad_sum/ppermute | solution.py:42
  35.8 3.6 %collective-permute-start.15 = (f32[8,128]{1,0:T(8,128)S(1)}, f32[8,128]{1,0:T(8,128)S(1)}, u32[]{:S(2)}, u32[]{:S(2)}) collective-permute-start(f32[8,128]{1,0:T(8,128)S(1)} %get-tuple-element.53.refs_0_), channel_id=1, source_target_pairs={{0,16},{8,24},{16,0},{24,8},{1,17},{9,25},{17,1},{25,9},{2,18},{10... | collective-permute-start | bytes 12296 | tf_op jit(solution)/shard_map/key_grad_end/ppermute | solution.py:386
  43.5 1.3 %collective-permute-start.19 = (bf16[24,1024]{1,0:T(8,128)(2,1)S(1)}, bf16[24,1024]{1,0:T(8,128)(2,1)S(1)}, u32[]{:S(2)}, u32[]{:S(2)}) collective-permute-start(bf16[24,1024]{1,0:T(8,128)(2,1)S(1)} %get-tuple-element.60), channel_id=1, source_target_pairs={{0,1},{1,0},{2,3},{3,2},{4,5},{5,4},{6,7},{7,6},{8,9},{9,8},{10,11... | collective-permute-start | bytes 147464 | tf_op jit(solution)/shard_map/query_grad_end/ppermute | solution.py:37

commit v11 on v10

--- a/solution.py
+++ b/solution.py
@@ -437,7 +437,7 @@
 
     with jax.named_scope("query_grad_sum"):
         parts = [dq_blocks[0]]
-        for j in sorted(range(1, chips), key=lambda j: -offsets[j]):
+        for j in sorted(range(1, chips), key=lambda j: (offsets[j] == 1, offsets[j])):
             parts.append(across(dq_blocks[j], offsets[j]))
 
     with jax.named_scope("key_grad_end"):

time: 45.7 us -> 45.4 us (level)
  starting transfers between devices: 22.4 us -> 21.5 us
  waiting for transfers between devices: 12.7 us -> 13.2 us
    ppermute x12, starting transfers between devices: 18.6 us -> 17.7 us  [across(): lax.ppermute(block, 'seq', [(i, i ^ 2 * apart) for i in range(count)])]
    ppermute x12, waiting for transfers between devices: 7.54 us -> 8.1 us  [across(): lax.ppermute(block, 'seq', [(i, i ^ 2 * apart) for i in range(count)])]
  transfers between devices with their start and end apart: 20 -> 20, of which waited for: 9 -> 10; matrix products, arithmetic and copies ran while one was open for 0% -> 0% of each run, Pallas kernels for 11% -> 11%
where the time goes in v11:
time: 45.4 us; the launch traced here: 45.1 us
  starting transfers between devices  21.5 us (47%)
  waiting for transfers between devices  13.2 us (29%)
  Pallas kernels  7.67 us (17%)
  local copies, waits for them, and re-layouts  1.25 us (3%)
  between operations  0.77 us (2%)
  other arithmetic  0.66 us (1%)
    ppermute x12, starting transfers between devices, across(): lax.ppermute(block, 'seq', [(i, i ^ 2 * apart) for i in range(count)])  17.7 us
    ppermute x12, waiting for transfers between devices, across(): lax.ppermute(block, 'seq', [(i, i ^ 2 * apart) for i in range(count)])  8.1 us
    ppermute x2, starting transfers between devices, over_groups(): lax.ppermute(count, 'dp', [(i, i ^ apart) for i in range(data_groups)])  3.01 us
    ppermute x2, waiting for transfers between devices, over_groups(): lax.ppermute(count, 'dp', [(i, i ^ apart) for i in range(data_groups)])  2.66 us
    pallas_call x1, Pallas kernels, local(): kernel_call(functools.partial(grads_kernel, offsets), (block,) * chips +...  2.58 us
    ppermute x6, waiting for transfers between devices, to_sibling(): return lax.ppermute(block, 'seq', [(i, i ^ 1) for i in range(count)])  2.46 us
    pallas_call x1, Pallas kernels, local(): kernel_call(functools.partial(key_end_kernel, rows_in_all), (whole, whole...  1.84 us
    pallas_call x1, Pallas kernels, local(): kernel_call(functools.partial(prepare_kernel, offsets, dec_rows, enc_loca...  1.8 us
  transfers between devices with their start and end apart: 20, of which 10 were waited for; matrix products, arithmetic and copies ran while one was open for 0% of the time, Pallas kernels for 11%

profile of v11, /device:TPU:0, one launch (start us, length us, event | category | flops | bytes accessed | tf_op | source)
XLA Modules:
  0.0 45.1 jit_solution(3188783504068715039)
XLA Ops:
  0.6 0.5 %collective-permute-start = (bf16[24,2048]{1,0:T(8,128)(2,1)}, bf16[24,2048]{1,0:T(8,128)(2,1)S(1)}, u32[]{:S(2)}, u32[]{:S(2)}) collective-permute-start(bf16[24,2048]{1,0:T(8,128)(2,1)} %bitcast.14), channel_id=1, source_target_pairs={{0,1},{1,0},{2,3},{3,2},{4,5},{5,4},{6,7},{7,6},{8,9},{9,8},{10,11... | collective-permute-start | bytes 294920 | tf_op jit(solution)/shard_map/sibling_exchange/ppermute | solution.py:37
  1.2 1.8 %prepare.1 = (bf16[24,1152]{1,0:T(8,128)(2,1)}, bf16[24,1152]{1,0:T(8,128)(2,1)}, f32[8,256]{1,0:T(8,128)}) custom-call(s32[1,4]{1,0:T(1,128)} %bitcast.20, s32[1,4]{1,0:T(1,128)} %bitcast.21, bf16[24,2048]{1,0:T(8,128)(2,1)} %bitcast.17, bf16[24,2048]{1,0:T(8,128)(2,1)} %bitcast.18, s32[1,24]{1,0:T(1,128)} %mask_ref.1), custom_call_target="tpu_custom_call" | custom-call | flops 100000 | bytes 1000000 | tf_op jit(solution)/shard_map/sibling_exchange/prepare/pallas_call | solution.py:331
  3.0 0.0 collective-permute-done.other_ref
  3.0 0.0 copy-start.5
  3.0 0.0 copy-start.3
  3.0 0.1 collective-permute-start.2
  3.1 4.1 %collective-permute-start.3 = (bf16[48,1024]{1,0:T(8,128)(2,1)S(1)}, bf16[48,1024]{1,0:T(8,128)(2,1)S(1)}, u32[]{:S(2)}, u32[]{:S(2)}) collective-permute-start(bf16[48,1024]{1,0:T(8,128)(2,1)S(1)} %join_queries.1.refs_1_.refs_4_), channel_id=1, source_target_pairs={{0,4},{1,5},{2,6},{3,7},{4,0},{5,1},{6,2},{7,3},{8,12},{9,13},{10,... | collective-permute-start | bytes 294920 | tf_op jit(solution)/shard_map/query_gather/ppermute | solution.py:42
  7.2 1.6 %collective-permute-start.5 = (bf16[48,1024]{1,0:T(8,128)(2,1)S(1)}, bf16[48,1024]{1,0:T(8,128)(2,1)S(1)}, u32[]{:S(2)}, u32[]{:S(2)}) collective-permute-start(bf16[48,1024]{1,0:T(8,128)(2,1)S(1)} %join_queries.1.refs_1_.refs_4_), channel_id=1, source_target_pairs={{0,2},{1,3},{2,0},{3,1},{4,6},{5,7},{6,4},{7,5},{8,10},{9,11},{10,... | collective-permute-start | bytes 294920 | tf_op jit(solution)/shard_map/query_gather/ppermute | solution.py:42
  8.8 0.0 collective-permute-start.1
  8.8 1.2 %collective-permute-done.1.other_ref = bf16[24,1152]{1,0:T(8,128)(2,1)S(1)} collective-permute-done((bf16[24,1152]{1,0:T(8,128)(2,1)S(1)}, bf16[24,1152]{1,0:T(8,128)(2,1)S(1)}, u32[]{:S(2)}, u32[]{:S(2)}) %collective-permute-start.1) | collective-permute-done | bytes 55328 | tf_op jit(solution)/shard_map/sibling_exchange/ppermute | solution.py:37
  10.1 0.2 join_cotangents.1
  10.2 1.5 %collective-permute-start.4 = (f32[8,128]{1,0:T(8,128)S(1)}, f32[8,128]{1,0:T(8,128)S(1)}, u32[]{:S(2)}, u32[]{:S(2)}) collective-permute-start(f32[8,128]{1,0:T(8,128)S(1)} %get-tuple-element.44), channel_id=1, source_target_pairs={{0,8},{8,0},{16,24},{24,16},{1,9},{9,1},{17,25},{25,17},{2,10},{10... | collective-permute-start | bytes 12296 | tf_op jit(solution)/shard_map/mask_count/ppermute | solution.py:386
  11.7 1.2 %copy-done.1 = bf16[1,256,2048]{2,1,0:T(8,128)(2,1)S(1)} copy-done((bf16[1,256,2048]{2,1,0:T(8,128)(2,1)S(1)}, bf16[1,256,2048]{2,1,0:T(8,128)(2,1)}, u32[]{:S(2)}) %copy-start.1) | copy-done | bytes 1048600
  13.0 0.3 setup.1
  13.3 0.0 copy-start
  13.3 0.6 %collective-permute-done.4 = f32[8,128]{1,0:T(8,128)S(1)} collective-permute-done((f32[8,128]{1,0:T(8,128)S(1)}, f32[8,128]{1,0:T(8,128)S(1)}, u32[]{:S(2)}, u32[]{:S(2)}) %collective-permute-start.4) | collective-permute-done | bytes 4128 | tf_op jit(solution)/shard_map/mask_count/ppermute | solution.py:386
  13.8 0.0 collective-permute-done.3.refs_2_.refs_5_
  13.9 0.0 collective-permute-done.5.refs_3_.refs_6_
  13.9 0.1 collective-permute-start.6
  13.9 0.5 %collective-permute-start.7 = (bf16[48,1024]{1,0:T(8,128)(2,1)S(1)}, bf16[48,1024]{1,0:T(8,128)(2,1)S(1)}, u32[]{:S(2)}, u32[]{:S(2)}) collective-permute-start(bf16[48,1024]{1,0:T(8,128)(2,1)S(1)} %collective-permute-done.3.refs_2_.refs_5_), channel_id=1, source_target_pairs={{0,2},{1,3},{2,0},{3,1},{4,6},{5,7},{6,4},{7,5},{8,10},{9,11},{10,... | collective-permute-start | bytes 294920 | tf_op jit(solution)/shard_map/query_forward/ppermute | solution.py:42
  14.5 2.1 %collective-permute-start.11 = (bf16[48,1024]{1,0:T(8,128)(2,1)S(1)}, bf16[48,1024]{1,0:T(8,128)(2,1)S(1)}, u32[]{:S(2)}, u32[]{:S(2)}) collective-permute-start(bf16[48,1024]{1,0:T(8,128)(2,1)S(1)} %get-tuple-element.49.refs_8_), channel_id=1, source_target_pairs={{0,4},{1,5},{2,6},{3,7},{4,0},{5,1},{6,2},{7,3},{8,12},{9,13},{10,... | collective-permute-start | bytes 294920 | tf_op jit(solution)/shard_map/cotangent_gather/ppermute | solution.py:42
  16.5 0.1 collective-permute-start.12
  16.6 2.2 %collective-permute-start.13 = (bf16[48,1024]{1,0:T(8,128)(2,1)S(1)}, bf16[48,1024]{1,0:T(8,128)(2,1)S(1)}, u32[]{:S(2)}, u32[]{:S(2)}) collective-permute-start(bf16[48,1024]{1,0:T(8,128)(2,1)S(1)} %get-tuple-element.49.refs_8_), channel_id=1, source_target_pairs={{0,6},{1,7},{2,4},{3,5},{4,2},{5,3},{6,0},{7,1},{8,14},{9,15},{10,... | collective-permute-start | bytes 294920 | tf_op jit(solution)/shard_map/cotangent_gather/ppermute | solution.py:42
  18.9 2.1 %collective-permute-done.7.refs_4_.refs_7_ = bf16[48,1024]{1,0:T(8,128)(2,1)S(1)} collective-permute-done((bf16[48,1024]{1,0:T(8,128)(2,1)S(1)}, bf16[48,1024]{1,0:T(8,128)(2,1)S(1)}, u32[]{:S(2)}, u32[]{:S(2)}) %collective-permute-start.7) | collective-permute-done | bytes 98336 | tf_op jit(solution)/shard_map/query_forward/ppermute | solution.py:42
  20.9 0.0 collective-permute-done.6.other_ref.refs_13_
  20.9 0.9 %scores.1.refs_0_ = f32[8,256]{1,0:T(8,128)S(1)} custom-call(f32[8,48]{1,0:T(8,128)S(1)} %get-tuple-element.40.delta_ref, f32[256,192]{1,0:T(8,128)S(1)} %get-tuple-element.37.bias_own, f32[256,192]{1,0:T(8,128)S(1)} %get-tuple-element.38.bias_other, bf16[256,1024]{1,0:T(8,128)(2,1)S(1)} %get-tuple-element.41.key_ref.refs_12_, ...), custom_call_target="tpu_custom_call" | custom-call | flops 201326592 | bytes 1441792 | tf_op jit(solution)/shard_map/scores/scores/pallas_call | solution.py:410
  21.8 0.1 collective-permute-start.10
  21.9 2.3 %collective-permute-start.8 = (f32[8,256]{1,0:T(8,128)S(1)}, f32[8,256]{1,0:T(8,128)S(1)}, u32[]{:S(2)}, u32[]{:S(2)}) collective-permute-start(f32[8,256]{1,0:T(8,128)S(1)} %scores.1.refs_0_), channel_id=1, source_target_pairs={{0,6},{1,7},{2,4},{3,5},{4,2},{5,3},{6,0},{7,1},{8,14},{9,15},{10,... | collective-permute-start | bytes 24584 | tf_op jit(solution)/shard_map/stats_exchange/ppermute | solution.py:42
  24.2 1.2 %collective-permute-start.9 = (f32[8,256]{1,0:T(8,128)S(1)}, f32[8,256]{1,0:T(8,128)S(1)}, u32[]{:S(2)}, u32[]{:S(2)}) collective-permute-start(f32[8,256]{1,0:T(8,128)S(1)} %scores.1.refs_0_), channel_id=1, source_target_pairs={{0,4},{1,5},{2,6},{3,7},{4,0},{5,1},{6,2},{7,3},{8,12},{9,13},{10,... | collective-permute-start | bytes 24584 | tf_op jit(solution)/shard_map/stats_exchange/ppermute | solution.py:42
  25.4 0.6 %collective-permute-done.13.refs_11_ = bf16[48,1024]{1,0:T(8,128)(2,1)S(1)} collective-permute-done((bf16[48,1024]{1,0:T(8,128)(2,1)S(1)}, bf16[48,1024]{1,0:T(8,128)(2,1)S(1)}, u32[]{:S(2)}, u32[]{:S(2)}) %collective-permute-start.13) | collective-permute-done | bytes 98336 | tf_op jit(solution)/shard_map/cotangent_gather/ppermute | solution.py:42
  26.0 0.0 collective-permute-done.10.refs_3_
  26.0 1.4 %collective-permute-done.8.refs_1_ = f32[8,256]{1,0:T(8,128)S(1)} collective-permute-done((f32[8,256]{1,0:T(8,128)S(1)}, f32[8,256]{1,0:T(8,128)S(1)}, u32[]{:S(2)}, u32[]{:S(2)}) %collective-permute-start.8) | collective-permute-done | bytes 8224 | tf_op jit(solution)/shard_map/stats_exchange/ppermute | solution.py:42
  27.4 1.3 %collective-permute-done.9.refs_2_ = f32[8,256]{1,0:T(8,128)S(1)} collective-permute-done((f32[8,256]{1,0:T(8,128)S(1)}, f32[8,256]{1,0:T(8,128)S(1)}, u32[]{:S(2)}, u32[]{:S(2)}) %collective-permute-start.9) | collective-permute-done | bytes 8224 | tf_op jit(solution)/shard_map/stats_exchange/ppermute | solution.py:42
  28.7 2.6 %grads.1 = (bf16[48,1024]{1,0:T(8,128)(2,1)S(1)}, bf16[48,1024]{1,0:T(8,128)(2,1)S(1)}, bf16[48,1024]{1,0:T(8,128)(2,1)S(1)}, bf16[48,1024]{1,0:T(8,128)(2,1)S(1...) custom-call(f32[256,192]{1,0:T(8,128)S(1)} %get-tuple-element.37.bias_own, ...), custom_call_target="tpu_custom_call" | custom-call | flops 1006632960 | bytes 4980736 | tf_op jit(solution)/shard_map/grads/grads/pallas_call | solution.py:427
  31.3 0.1 collective-permute-start.14
  31.4 1.3 %collective-permute-start.16 = (bf16[48,1024]{1,0:T(8,128)(2,1)S(1)}, bf16[48,1024]{1,0:T(8,128)(2,1)S(1)}, u32[]{:S(2)}, u32[]{:S(2)}) collective-permute-start(bf16[48,1024]{1,0:T(8,128)(2,1)S(1)} %get-tuple-element.56), channel_id=1, source_target_pairs={{0,4},{1,5},{2,6},{3,7},{4,0},{5,1},{6,2},{7,3},{8,12},{9,13},{10,... | collective-permute-start | bytes 294920 | tf_op jit(solution)/shard_map/query_grad_sum/ppermute | solution.py:42
  32.7 2.2 %collective-permute-start.17 = (bf16[48,1024]{1,0:T(8,128)(2,1)S(1)}, bf16[48,1024]{1,0:T(8,128)(2,1)S(1)}, u32[]{:S(2)}, u32[]{:S(2)}) collective-permute-start(bf16[48,1024]{1,0:T(8,128)(2,1)S(1)} %get-tuple-element.57), channel_id=1, source_target_pairs={{0,6},{1,7},{2,4},{3,5},{4,2},{5,3},{6,0},{7,1},{8,14},{9,15},{10,... | collective-permute-start | bytes 294920 | tf_op jit(solution)/shard_map/query_grad_sum/ppermute | solution.py:42
  34.9 0.1 collective-permute-start.18
  34.9 1.5 %collective-permute-start.15 = (f32[8,128]{1,0:T(8,128)S(1)}, f32[8,128]{1,0:T(8,128)S(1)}, u32[]{:S(2)}, u32[]{:S(2)}) collective-permute-start(f32[8,128]{1,0:T(8,128)S(1)} %get-tuple-element.53.refs_0_), channel_id=1, source_target_pairs={{0,16},{8,24},{16,0},{24,8},{1,17},{9,25},{17,1},{25,9},{2,18},{10... | collective-permute-start | bytes 12296 | tf_op jit(solution)/shard_map/key_grad_end/ppermute | solution.py:386
  36.5 2.1 %collective-permute-done.15.refs_1_ = f32[8,128]{1,0:T(8,128)S(1)} collective-permute-done((f32[8,128]{1,0:T(8,128)S(1)}, f32[8,128]{1,0:T(8,128)S(1)}, u32[]{:S(2)}, u32[]{:S(2)}) %collective-permute-start.15) | collective-permute-done | bytes 4128 | tf_op jit(solution)/shard_map/key_grad_end/ppermute | solution.py:386
  38.6 1.8 %key_end.1 = (bf16[256,2048]{1,0:T(8,128)(2,1)}, bf16[256,2048]{1,0:T(8,128)(2,1)}, f32[8,128]{1,0:T(8,128)S(1)}) custom-call(bf16[256,2048]{1,0:T(8,128)(2,1)S(1)} %get-tuple-element.51.keep_ref, bf16[256,2048]{1,0:T(8,128)(2,1)S(1)} %collective-permute-done.14.other_ref, f32[8,128]{1,0:T(8,128)S(1)} %get-tuple-element.53.refs_0_, ...), custom_call_target="tpu_custom_call" | custom-call | flops 1000000 | bytes 4194304 | tf_op jit(solution)/shard_map/key_grad_end/key_end/pallas_call | solution.py:447
  40.4 1.8 %collective-permute-done.16.refs_1_ = bf16[48,1024]{1,0:T(8,128)(2,1)S(1)} collective-permute-done((bf16[48,1024]{1,0:T(8,128)(2,1)S(1)}, bf16[48,1024]{1,0:T(8,128)(2,1)S(1)}, u32[]{:S(2)}, u32[]{:S(2)}) %collective-permute-start.16) | collective-permute-done | bytes 98336 | tf_op jit(solution)/shard_map/query_grad_sum/ppermute | solution.py:42
  42.2 0.0 collective-permute-done.17.refs_2_
  42.2 0.9 %collective-permute-done.18.refs_3_ = bf16[48,1024]{1,0:T(8,128)(2,1)S(1)} collective-permute-done((bf16[48,1024]{1,0:T(8,128)(2,1)S(1)}, bf16[48,1024]{1,0:T(8,128)(2,1)S(1)}, u32[]{:S(2)}, u32[]{:S(2)}) %collective-permute-start.18) | collective-permute-done | bytes 98336 | tf_op jit(solution)/shard_map/query_grad_sum/ppermute | solution.py:42
  43.1 0.1 query_end.1
  43.2 0.1 collective-permute-start.19
  43.2 1.2 %collective-permute-done.19 = bf16[24,1024]{1,0:T(8,128)(2,1)S(1)} collective-permute-done((bf16[24,1024]{1,0:T(8,128)(2,1)S(1)}, bf16[24,1024]{1,0:T(8,128)(2,1)S(1)}, u32[]{:S(2)}, u32[]{:S(2)}) %collective-permute-start.19) | collective-permute-done | bytes 49184 | tf_op jit(solution)/shard_map/query_grad_end/ppermute | solution.py:37
  44.5 0.7 %maximum_select_fusion = bf16[1,24,2048]{2,1,0:T(8,128)(2,1)} fusion(bf16[1,24,1024]{2,1,0:T(8,128)(2,1)S(1)} %bitcast.19, bf16[1,24,1024]{2,1,0:T(8,128)(2,1)S(1)} %bitcast.16, pred[]{:T(512)S(6)} %eq.3), kind=kLoop, calls=%fused_computation | loop fusion | flops 442368 | bytes 196609 | tf_op jit(solution)/shard_map/query_grad_end/jit(_where)/select_n | solution.py:288
  (14 shorter events, 0.0 us)
Async XLA Ops:
  0.6 2.3 %collective-permute-start = (bf16[24,2048]{1,0:T(8,128)(2,1)}, bf16[24,2048]{1,0:T(8,128)(2,1)S(1)}, u32[]{:S(2)}, u32[]{:S(2)}) collective-permute-start(bf16[24,2048]{1,0:T(8,128)(2,1)} %bitcast.14), channel_id=1, source_target_pairs={{0,1},{1,0},{2,3},{3,2},{4,5},{5,4},{6,7},{7,6},{8,9},{9,8},{10,11... | collective-permute-start | bytes 294920 | tf_op jit(solution)/shard_map/sibling_exchange/ppermute | solution.py:37
  1.1 2.0 %copy-start.2 = (bf16[1,24,2048]{2,1,0:T(8,128)(2,1)S(1)}, bf16[1,24,2048]{2,1,0:T(8,128)(2,1)}, u32[]{:S(2)}) copy-start(bf16[1,24,2048]{2,1,0:T(8,128)(2,1)} %param.8) | copy-start | bytes 294916
  3.0 5.9 %copy-start.5 = (bf16[24,1152]{1,0:T(8,128)(2,1)S(1)}, bf16[24,1152]{1,0:T(8,128)(2,1)}, u32[]{:S(2)}) copy-start(bf16[24,1152]{1,0:T(8,128)(2,1)} %get-tuple-element.39) | copy-start | bytes 165892
  3.0 7.1 %copy-start.3 = (bf16[24,1152]{1,0:T(8,128)(2,1)S(1)}, bf16[24,1152]{1,0:T(8,128)(2,1)}, u32[]{:S(2)}) copy-start(bf16[24,1152]{1,0:T(8,128)(2,1)} %get-tuple-element.34.own_ref) | copy-start | bytes 165892
  3.0 10.9 %collective-permute-start.2 = (bf16[256,2048]{1,0:T(8,128)(2,1)}, bf16[256,2048]{1,0:T(8,128)(2,1)S(1)}, u32[]{:S(2)}, u32[]{:S(2)}) collective-permute-start(bf16[256,2048]{1,0:T(8,128)(2,1)} %bitcast.11), channel_id=1, source_target_pairs={{0,1},{1,0},{2,3},{3,2},{4,5},{5,4},{6,7},{7,6},{8,9},{9,8},{10,11... | collective-permute-start | bytes 3145736 | tf_op jit(solution)/shard_map/key_exchange/ppermute | solution.py:37
  3.1 10.7 %collective-permute-start.3 = (bf16[48,1024]{1,0:T(8,128)(2,1)S(1)}, bf16[48,1024]{1,0:T(8,128)(2,1)S(1)}, u32[]{:S(2)}, u32[]{:S(2)}) collective-permute-start(bf16[48,1024]{1,0:T(8,128)(2,1)S(1)} %join_queries.1.refs_1_.refs_4_), channel_id=1, source_target_pairs={{0,4},{1,5},{2,6},{3,7},{4,0},{5,1},{6,2},{7,3},{8,12},{9,13},{10,... | collective-permute-start | bytes 294920 | tf_op jit(solution)/shard_map/query_gather/ppermute | solution.py:42
  7.2 6.6 %collective-permute-start.5 = (bf16[48,1024]{1,0:T(8,128)(2,1)S(1)}, bf16[48,1024]{1,0:T(8,128)(2,1)S(1)}, u32[]{:S(2)}, u32[]{:S(2)}) collective-permute-start(bf16[48,1024]{1,0:T(8,128)(2,1)S(1)} %join_queries.1.refs_1_.refs_4_), channel_id=1, source_target_pairs={{0,2},{1,3},{2,0},{3,1},{4,6},{5,7},{6,4},{7,5},{8,10},{9,11},{10,... | collective-permute-start | bytes 294920 | tf_op jit(solution)/shard_map/query_gather/ppermute | solution.py:42
  8.8 1.2 %collective-permute-start.1 = (bf16[24,1152]{1,0:T(8,128)(2,1)S(1)}, bf16[24,1152]{1,0:T(8,128)(2,1)S(1)}, u32[]{:S(2)}, u32[]{:S(2)}) collective-permute-start(bf16[24,1152]{1,0:T(8,128)(2,1)S(1)} %copy-done.5), channel_id=1, source_target_pairs={{0,1},{1,0},{2,3},{3,2},{4,5},{5,4},{6,7},{7,6},{8,9},{9,8},{10,11... | collective-permute-start | bytes 165896 | tf_op jit(solution)/shard_map/sibling_exchange/ppermute | solution.py:37
  10.1 1.7 %copy-start.4 = (f32[8,256]{1,0:T(8,128)S(1)}, f32[8,256]{1,0:T(8,128)}, u32[]{:S(2)}) copy-start(f32[8,256]{1,0:T(8,128)} %get-tuple-element.33.docs_ref) | copy-start | bytes 24580
  10.2 3.6 %collective-permute-start.4 = (f32[8,128]{1,0:T(8,128)S(1)}, f32[8,128]{1,0:T(8,128)S(1)}, u32[]{:S(2)}, u32[]{:S(2)}) collective-permute-start(f32[8,128]{1,0:T(8,128)S(1)} %get-tuple-element.44), channel_id=1, source_target_pairs={{0,8},{8,0},{16,24},{24,16},{1,9},{9,1},{17,25},{25,17},{2,10},{10... | collective-permute-start | bytes 12296 | tf_op jit(solution)/shard_map/mask_count/ppermute | solution.py:386
  11.7 1.2 %copy-start.1 = (bf16[1,256,2048]{2,1,0:T(8,128)(2,1)S(1)}, bf16[1,256,2048]{2,1,0:T(8,128)(2,1)}, u32[]{:S(2)}) copy-start(bf16[1,256,2048]{2,1,0:T(8,128)(2,1)} %param.9) | copy-start | bytes 3145732
  13.3 15.5 %copy-start = (bf16[1,256,2048]{2,1,0:T(8,128)(2,1)S(1)}, bf16[1,256,2048]{2,1,0:T(8,128)(2,1)}, u32[]{:S(2)}) copy-start(bf16[1,256,2048]{2,1,0:T(8,128)(2,1)} %param.10) | copy-start | bytes 3145732
  13.9 7.0 %collective-permute-start.6 = (bf16[256,1024]{1,0:T(8,128)(2,1)S(1)}, bf16[256,1024]{1,0:T(8,128)(2,1)S(1)}, u32[]{:S(2)}, u32[]{:S(2)}) collective-permute-start(bf16[256,1024]{1,0:T(8,128)(2,1)S(1)} %get-tuple-element.47), channel_id=1, source_target_pairs={{0,1},{1,0},{2,3},{3,2},{4,5},{5,4},{6,7},{7,6},{8,9},{9,8},{10,11... | collective-permute-start | bytes 1572872 | tf_op jit(solution)/shard_map/key_exchange/ppermute | solution.py:37
  13.9 7.0 %collective-permute-start.7 = (bf16[48,1024]{1,0:T(8,128)(2,1)S(1)}, bf16[48,1024]{1,0:T(8,128)(2,1)S(1)}, u32[]{:S(2)}, u32[]{:S(2)}) collective-permute-start(bf16[48,1024]{1,0:T(8,128)(2,1)S(1)} %collective-permute-done.3.refs_2_.refs_5_), channel_id=1, source_target_pairs={{0,2},{1,3},{2,0},{3,1},{4,6},{5,7},{6,4},{7,5},{8,10},{9,11},{10,... | collective-permute-start | bytes 294920 | tf_op jit(solution)/shard_map/query_forward/ppermute | solution.py:42
  14.5 9.7 %collective-permute-start.11 = (bf16[48,1024]{1,0:T(8,128)(2,1)S(1)}, bf16[48,1024]{1,0:T(8,128)(2,1)S(1)}, u32[]{:S(2)}, u32[]{:S(2)}) collective-permute-start(bf16[48,1024]{1,0:T(8,128)(2,1)S(1)} %get-tuple-element.49.refs_8_), channel_id=1, source_target_pairs={{0,4},{1,5},{2,6},{3,7},{4,0},{5,1},{6,2},{7,3},{8,12},{9,13},{10,... | collective-permute-start | bytes 294920 | tf_op jit(solution)/shard_map/cotangent_gather/ppermute | solution.py:42
  16.5 8.8 %collective-permute-start.12 = (bf16[48,1024]{1,0:T(8,128)(2,1)S(1)}, bf16[48,1024]{1,0:T(8,128)(2,1)S(1)}, u32[]{:S(2)}, u32[]{:S(2)}) collective-permute-start(bf16[48,1024]{1,0:T(8,128)(2,1)S(1)} %get-tuple-element.49.refs_8_), channel_id=1, source_target_pairs={{0,2},{1,3},{2,0},{3,1},{4,6},{5,7},{6,4},{7,5},{8,10},{9,11},{10,... | collective-permute-start | bytes 294920 | tf_op jit(solution)/shard_map/cotangent_gather/ppermute | solution.py:42
  16.6 9.4 %collective-permute-start.13 = (bf16[48,1024]{1,0:T(8,128)(2,1)S(1)}, bf16[48,1024]{1,0:T(8,128)(2,1)S(1)}, u32[]{:S(2)}, u32[]{:S(2)}) collective-permute-start(bf16[48,1024]{1,0:T(8,128)(2,1)S(1)} %get-tuple-element.49.refs_8_), channel_id=1, source_target_pairs={{0,6},{1,7},{2,4},{3,5},{4,2},{5,3},{6,0},{7,1},{8,14},{9,15},{10,... | collective-permute-start | bytes 294920 | tf_op jit(solution)/shard_map/cotangent_gather/ppermute | solution.py:42
  21.8 4.2 %collective-permute-start.10 = (f32[8,256]{1,0:T(8,128)S(1)}, f32[8,256]{1,0:T(8,128)S(1)}, u32[]{:S(2)}, u32[]{:S(2)}) collective-permute-start(f32[8,256]{1,0:T(8,128)S(1)} %scores.1.refs_0_), channel_id=1, source_target_pairs={{0,2},{1,3},{2,0},{3,1},{4,6},{5,7},{6,4},{7,5},{8,10},{9,11},{10,... | collective-permute-start | bytes 24584 | tf_op jit(solution)/shard_map/stats_exchange/ppermute | solution.py:42
  21.9 5.5 %collective-permute-start.8 = (f32[8,256]{1,0:T(8,128)S(1)}, f32[8,256]{1,0:T(8,128)S(1)}, u32[]{:S(2)}, u32[]{:S(2)}) collective-permute-start(f32[8,256]{1,0:T(8,128)S(1)} %scores.1.refs_0_), channel_id=1, source_target_pairs={{0,6},{1,7},{2,4},{3,5},{4,2},{5,3},{6,0},{7,1},{8,14},{9,15},{10,... | collective-permute-start | bytes 24584 | tf_op jit(solution)/shard_map/stats_exchange/ppermute | solution.py:42
  24.2 4.6 %collective-permute-start.9 = (f32[8,256]{1,0:T(8,128)S(1)}, f32[8,256]{1,0:T(8,128)S(1)}, u32[]{:S(2)}, u32[]{:S(2)}) collective-permute-start(f32[8,256]{1,0:T(8,128)S(1)} %scores.1.refs_0_), channel_id=1, source_target_pairs={{0,4},{1,5},{2,6},{3,7},{4,0},{5,1},{6,2},{7,3},{8,12},{9,13},{10,... | collective-permute-start | bytes 24584 | tf_op jit(solution)/shard_map/stats_exchange/ppermute | solution.py:42
  31.3 7.2 %collective-permute-start.14 = (bf16[256,2048]{1,0:T(8,128)(2,1)S(1)}, bf16[256,2048]{1,0:T(8,128)(2,1)S(1)}, u32[]{:S(2)}, u32[]{:S(2)}) collective-permute-start(bf16[256,2048]{1,0:T(8,128)(2,1)S(1)} %get-tuple-element.52), channel_id=1, source_target_pairs={{0,1},{1,0},{2,3},{3,2},{4,5},{5,4},{6,7},{7,6},{8,9},{9,8},{10,11... | collective-permute-start | bytes 3145736 | tf_op jit(solution)/shard_map/key_grad_end/ppermute | solution.py:37
  31.4 10.8 %collective-permute-start.16 = (bf16[48,1024]{1,0:T(8,128)(2,1)S(1)}, bf16[48,1024]{1,0:T(8,128)(2,1)S(1)}, u32[]{:S(2)}, u32[]{:S(2)}) collective-permute-start(bf16[48,1024]{1,0:T(8,128)(2,1)S(1)} %get-tuple-element.56), channel_id=1, source_target_pairs={{0,4},{1,5},{2,6},{3,7},{4,0},{5,1},{6,2},{7,3},{8,12},{9,13},{10,... | collective-permute-start | bytes 294920 | tf_op jit(solution)/shard_map/query_grad_sum/ppermute | solution.py:42
  32.7 9.5 %collective-permute-start.17 = (bf16[48,1024]{1,0:T(8,128)(2,1)S(1)}, bf16[48,1024]{1,0:T(8,128)(2,1)S(1)}, u32[]{:S(2)}, u32[]{:S(2)}) collective-permute-start(bf16[48,1024]{1,0:T(8,128)(2,1)S(1)} %get-tuple-element.57), channel_id=1, source_target_pairs={{0,6},{1,7},{2,4},{3,5},{4,2},{5,3},{6,0},{7,1},{8,14},{9,15},{10,... | collective-permute-start | bytes 294920 | tf_op jit(solution)/shard_map/query_grad_sum/ppermute | solution.py:42
  34.9 8.2 %collective-permute-start.18 = (bf16[48,1024]{1,0:T(8,128)(2,1)S(1)}, bf16[48,1024]{1,0:T(8,128)(2,1)S(1)}, u32[]{:S(2)}, u32[]{:S(2)}) collective-permute-start(bf16[48,1024]{1,0:T(8,128)(2,1)S(1)} %get-tuple-element.58), channel_id=1, source_target_pairs={{0,2},{1,3},{2,0},{3,1},{4,6},{5,7},{6,4},{7,5},{8,10},{9,11},{10,... | collective-permute-start | bytes 294920 | tf_op jit(solution)/shard_map/query_grad_sum/ppermute | solution.py:42
  34.9 3.6 %collective-permute-start.15 = (f32[8,128]{1,0:T(8,128)S(1)}, f32[8,128]{1,0:T(8,128)S(1)}, u32[]{:S(2)}, u32[]{:S(2)}) collective-permute-start(f32[8,128]{1,0:T(8,128)S(1)} %get-tuple-element.53.refs_0_), channel_id=1, source_target_pairs={{0,16},{8,24},{16,0},{24,8},{1,17},{9,25},{17,1},{25,9},{2,18},{10... | collective-permute-start | bytes 12296 | tf_op jit(solution)/shard_map/key_grad_end/ppermute | solution.py:386
  43.2 1.3 %collective-permute-start.19 = (bf16[24,1024]{1,0:T(8,128)(2,1)S(1)}, bf16[24,1024]{1,0:T(8,128)(2,1)S(1)}, u32[]{:S(2)}, u32[]{:S(2)}) collective-permute-start(bf16[24,1024]{1,0:T(8,128)(2,1)S(1)} %get-tuple-element.60), channel_id=1, source_target_pairs={{0,1},{1,0},{2,3},{3,2},{4,5},{5,4},{6,7},{7,6},{8,9},{9,8},{10,11... | collective-permute-start | bytes 147464 | tf_op jit(solution)/shard_map/query_grad_end/ppermute | solution.py:37
